TPU v7x, 32 devices: a whole 2x2x4 slice. The times are simulated.
32 devices in a mesh: region: 2 (over x), var: 8 (over z, y), samp: 2 (over core).
Axes of the slice: x: 2, y: 2, z: 4, core: 2. Of those that a mesh axis runs over, the one named last changes fastest.
Arguments:
- dosage: bfloat16 [2048, 16384], P('samp', ('region', 'var')), parts along dimension 1, may hold values from 0 to 2
- observed: int32 [2048, 16384], P('samp', ('region', 'var')), parts along dimension 1, may hold values from 0 to 1, as said below
- counts: int32 [16], P(('region', 'var')), parts along dimension 0, may hold values from 1 to 4, as said below
Outputs:
- correlations: bfloat16 [16, 4, 1024, 1024], P(('region', 'var'), None, 'samp'), parts along dimension 0
There are 2 independent parts, one for each index of `region`. A program takes and returns all parts, laid end to end along the dimension named above; each array names one. Nothing has to cross between parts.
Inputs may be any that keep to these rules, and one draw needn't show every extreme that they name: Block b's partners are blocks b to b + counts[b] - 1; counts[b] is at most 8 - b, and counts[0] = 4. `observed`: some variants are missing in every sample.
All inputs are finite; a program needn't handle non-finite values.
Results may differ from a plain program's by a relative error of at most 0.001.
The roundings to bfloat16 on the way count: a program that leaves them out, or rounds other values in their place, can miss the bound.
Values may be sent and summed in bfloat16 or wider, within the bound.
No kernel may reach another device: no remote copies, remote signals or barrier semaphores. Data moves between devices by JAX's collectives and lax.ppermute only.
A program may use at most 128 MiB of HBM per device.

v0:
```python
import jax
import jax.numpy as jnp
from jax import lax
from jax.sharding import PartitionSpec as P

WIN = 4


epsilon = 1e-05


def from_behind(shard, axis, by):
    count = lax.axis_size(axis)
    pairs = [(i, i + by) for i in range(count) if 0 <= i + by < count]
    return lax.ppermute(shard, axis, pairs)


def contract(left, right):
    return lax.dot_general(
        left, right, (((0,), (0,)), ((), ())), preferred_element_type=jnp.float32
    )


def per_device(dosage, observed, counts):
    values = dosage.astype(jnp.float32)
    present = observed.astype(jnp.float32)
    present_count, summed, squares = lax.psum(
        (
            jnp.sum(present, axis=0),
            jnp.sum(present * values, axis=0),
            jnp.sum(present * values * values, axis=0),
        ),
        "samp",
    )
    present_count = jnp.maximum(present_count, 1.0)
    center = summed / present_count
    offsets = present * (values - center)
    spread = squares / present_count - center * center
    scored = (offsets * lax.rsqrt(spread + epsilon)).astype(jnp.bfloat16)
    width = scored.shape[1]
    total_samples = float(scored.shape[0] * lax.axis_size("samp"))
    partner_count = counts[0]
    tiles = []
    for offset in range(WIN):
        if offset == 0:
            partner = scored
        else:
            partner = from_behind(scored, "var", -offset)
        tiles.append(
            lax.cond(
                offset < partner_count,
                lambda other: contract(scored, other),
                lambda other: jnp.zeros((width, width), jnp.float32),
                partner,
            )
        )
    stacked = jnp.stack(tiles)
    reduced = lax.psum_scatter(stacked, "samp", scatter_dimension=1, tiled=True)
    scaled = reduced / total_samples
    keep = jnp.arange(WIN, dtype=jnp.int32)[:, None, None] < partner_count
    result = jnp.where(keep, scaled, jnp.zeros_like(scaled)).astype(jnp.bfloat16)
    return result[None]


def solution(mesh):
    in_specs = (P("samp", ("region", "var")), P("samp", ("region", "var")), P(("region", "var")))
    out_specs = P(("region", "var"), None, "samp", None)
    return jax.shard_map(
        per_device, mesh=mesh, in_specs=in_specs, out_specs=out_specs, check_vma=False
    )
```

profile of v0, /device:TPU:0, one launch (start us, length us, event | category | flops | bytes accessed | tf_op | source)
XLA Modules:
  0.0 262.8 jit_solution(15636543799726126289)
XLA Ops:
  6.5 0.0 copy-start
  6.5 0.0 reduce-scatter.2.cloned.1.call-start
  6.5 4.0 %fusion.5 = (f32[1024]{0:T(1024)S(1)}, f32[1024]{0:T(1024)S(1)}, f32[1024]{0:T(1024)S(1)}) fusion(bf16[1024,1024]{1,0:T(8,128)(2,1)} %param.11, s32[1024,1024]{1,0:T(8,128)} %param.12), kind=kLoop, calls=%fused_computation.15 | loop fusion | flops 7336960 | bytes 6303744 | tf_op jit(solution)/shard_map/reduce_sum | solution.py:30
  10.6 3.6 %all-reduce = (f32[1024]{0:T(1024)S(1)}, f32[1024]{0:T(1024)S(1)}, f32[1024]{0:T(1024)S(1)}) all-reduce(f32[1024]{0:T(1024)S(1)} %get-tuple-element.41, f32[1024]{0:T(1024)S(1)} %get-tuple-element.42, f32[1024]{0:T(1024)S(1)} %get-tuple-element.40), channel_id=1, replica_groups=mesh['region'=2,'var'=8,'samp'=2] {'samp'}, use_global_device_ids=true, to_apply=%region_5.0 | all-reduce | flops 3072 | bytes 24576 | tf_op jit(solution)/shard_map/psum | solution.py:27
  14.2 0.0 copy-done
  14.2 4.4 %fusion.2 = bf16[1024,1024]{1,0:T(8,128)(2,1)} fusion(bf16[1024,1024]{1,0:T(8,128)(2,1)S(1)} %copy-done, s32[1024,1024]{1,0:T(8,128)} %param.12, f32[1024]{0:T(1024)S(1)} %get-tuple-element.47, f32[1024]{0:T(1024)S(1)} %get-tuple-element.46), kind=kLoop, calls=%fused_computation.11 | loop fusion | flops 6291456 | bytes 8396800 | tf_op jit(solution)/shard_map/convert_element_type | solution.py:39
  18.5 1.3 collective-permute-start.2
  19.8 1.3 collective-permute-start.1
  21.1 1.3 collective-permute-start
  23.1 6.6 %conditional.4 = (f32[1,1024,1024]{2,1,0:T(8,128)}) conditional(s32[]{:T(128)} %convert_element_type.27, () %tuple.37, bf16[1024,1024]{1,0:T(8,128)(2,1)} %fusion.2), branch_computations={%region_6.0_spmd, %region_7.0_spmd} | conditional | flops 2147483648 | bytes 6291464 | solution.py:50
  23.1 6.5 %convolution_bitcast_fusion = f32[1,1024,1024]{2,1,0:T(8,128)} fusion(bf16[1024,1024]{1,0:T(8,128)(2,1)} %param.1), kind=kOutput, calls=%fused_computation | convolution fusion | flops 2147483648 | bytes 6291456 | tf_op jit(solution)/shard_map/cond/branch_1_fun/dot_general | solution.py:19
  29.7 41.2 %collective-permute-done.2 = bf16[1024,1024]{1,0:T(8,128)(2,1)} collective-permute-done((bf16[1024,1024]{1,0:T(8,128)(2,1)}, bf16[1024,1024]{1,0:T(8,128)(2,1)}, u32[]{:S(2)}, u32[]{:S(2)}) %collective-permute-start.2) | collective-permute-done | bytes 2097184 | tf_op jit(solution)/shard_map/ppermute | solution.py:15
  70.9 6.6 %conditional.7 = (f32[1,1024,1024]{2,1,0:T(8,128)}) conditional(s32[]{:T(128)} %convert_element_type.33, () %tuple.42, (bf16[1024,1024]{1,0:T(8,128)(2,1)}, bf16[1024,1024]{1,0:T(8,128)(2,1)}) %tuple.43), branch_computations={%region_12.0_spmd, %region_13.0_spmd} | conditional | flops 2147483648 | bytes 8388616 | solution.py:50
  70.9 6.6 %convolution_bitcast_fusion.3 = f32[1,1024,1024]{2,1,0:T(8,128)} fusion(bf16[1024,1024]{1,0:T(8,128)(2,1)} %get-tuple-element.38, bf16[1024,1024]{1,0:T(8,128)(2,1)} %get-tuple-element.39), kind=kOutput, calls=%fused_computation.3 | convolution fusion | flops 2147483648 | bytes 8388608 | tf_op jit(solution)/shard_map/cond/branch_1_fun/dot_general | solution.py:19
  77.5 0.0 collective-permute-done.1
  77.5 6.6 %conditional.6 = (f32[1,1024,1024]{2,1,0:T(8,128)}) conditional(s32[]{:T(128)} %convert_element_type.32, () %tuple.40, (bf16[1024,1024]{1,0:T(8,128)(2,1)}, bf16[1024,1024]{1,0:T(8,128)(2,1)}) %tuple.41), branch_computations={%region_10.0_spmd, %region_11.0_spmd} | conditional | flops 2147483648 | bytes 8388616 | solution.py:50
  77.5 6.6 %convolution_bitcast_fusion.2 = f32[1,1024,1024]{2,1,0:T(8,128)} fusion(bf16[1024,1024]{1,0:T(8,128)(2,1)} %get-tuple-element.36, bf16[1024,1024]{1,0:T(8,128)(2,1)} %get-tuple-element.37), kind=kOutput, calls=%fused_computation.2 | convolution fusion | flops 2147483648 | bytes 8388608 | tf_op jit(solution)/shard_map/cond/branch_1_fun/dot_general | solution.py:19
  84.1 31.4 %collective-permute-done = bf16[1024,1024]{1,0:T(8,128)(2,1)S(1)} collective-permute-done((bf16[1024,1024]{1,0:T(8,128)(2,1)}, bf16[1024,1024]{1,0:T(8,128)(2,1)S(1)}, u32[]{:S(2)}, u32[]{:S(2)}) %collective-permute-start) | collective-permute-done | bytes 2097184 | tf_op jit(solution)/shard_map/ppermute | solution.py:15
  115.4 5.9 %conditional.5 = (f32[1,1024,1024]{2,1,0:T(8,128)}) conditional(s32[]{:T(128)} %convert_element_type.31, () %tuple.38, (bf16[1024,1024]{1,0:T(8,128)(2,1)}, bf16[1024,1024]{1,0:T(8,128)(2,1)S(1)}) %tuple.39), branch_computations={%region_8.0_spmd, %region_9.0_spmd} | conditional | flops 2147483648 | bytes 8388616 | solution.py:50
  115.4 5.9 %convolution_bitcast_fusion.1 = f32[1,1024,1024]{2,1,0:T(8,128)} fusion(bf16[1024,1024]{1,0:T(8,128)(2,1)} %get-tuple-element.34, bf16[1024,1024]{1,0:T(8,128)(2,1)S(1)} %get-tuple-element.35), kind=kOutput, calls=%fused_computation.1 | convolution fusion | flops 2147483648 | bytes 8388608 | tf_op jit(solution)/shard_map/cond/branch_1_fun/dot_general | solution.py:19
  121.4 11.7 %pad_maximum_fusion = f32[4,1024,1024]{2,1,0:T(8,128)} fusion(f32[1,1024,1024]{2,1,0:T(8,128)} %get-tuple-element.51, f32[1,1024,1024]{2,1,0:T(8,128)} %get-tuple-element.50, f32[1,1024,1024]{2,1,0:T(8,128)} %get-tuple-element.49, f32[1,1024,1024]{2,1,0:T(8,128)} %get-tuple-element.48), kind=kLoop, calls=%fused_computation.4 | loop fusion | flops 12582912 | bytes 33554432 | tf_op jit(solution)/shard_map/stack | solution.py:57
  133.1 0.0 reduce-scatter.2.cloned.1.call-update
  133.2 115.6 %reduce-scatter.2.cloned.1.call-done = f32[4,512,1024]{2,1,0:T(8,128)} async-done(((f32[4,1024,1024]{2,1,0:T(8,128)}), f32[4,512,1024]{2,1,0:T(8,128)}) %reduce-scatter.2.cloned.1.call-update) | async-done | bytes 8388624 | tf_op jit(solution)/shard_map/reduce_scatter | solution.py:58
  248.7 7.2 %fusion.4 = bf16[1,4,512,1024]{3,2,1,0:T(8,128)(2,1)} fusion(f32[4,512,1024]{2,1,0:T(8,128)} %reduce-scatter.2.cloned.1.call-done, pred[4]{0:T(512)(128)(4,1)S(1)} %iota_compare_fusion), kind=kLoop, calls=%fused_computation.13 | loop fusion | flops 6291456 | bytes 12582916 | tf_op jit(solution)/shard_map/broadcast_in_dim | solution.py:62
  (2 shorter events, 0.0 us)
Async XLA Ops:
  6.5 7.6 %copy-start = (bf16[1024,1024]{1,0:T(8,128)(2,1)S(1)}, bf16[1024,1024]{1,0:T(8,128)(2,1)}, u32[]{:S(2)}) copy-start(bf16[1024,1024]{1,0:T(8,128)(2,1)} %param.11) | copy-start | bytes 6291460
  6.5 242.2 %reduce-scatter.2.cloned.1.call-start = ((), (), s32[]{:S(2)}) async-start(), calls=%async_computation.1 | async-start | bytes 25165824 | tf_op jit(solution)/shard_map/reduce_scatter | solution.py:58
  18.5 52.3 %collective-permute-start.2 = (bf16[1024,1024]{1,0:T(8,128)(2,1)}, bf16[1024,1024]{1,0:T(8,128)(2,1)}, u32[]{:S(2)}, u32[]{:S(2)}) collective-permute-start(bf16[1024,1024]{1,0:T(8,128)(2,1)} %fusion.2), channel_id=1, source_target_pairs={{6,0},{8,2},{10,4},{12,6},{14,8},{7,1},{9,3},{11,5},{13,7},{15,9},... | collective-permute-start | bytes 6291464 | tf_op jit(solution)/shard_map/ppermute | solution.py:15
  19.8 57.7 %collective-permute-start.1 = (bf16[1024,1024]{1,0:T(8,128)(2,1)}, bf16[1024,1024]{1,0:T(8,128)(2,1)}, u32[]{:S(2)}, u32[]{:S(2)}) collective-permute-start(bf16[1024,1024]{1,0:T(8,128)(2,1)} %fusion.2), channel_id=1, source_target_pairs={{4,0},{6,2},{8,4},{10,6},{12,8},{14,10},{5,1},{7,3},{9,5},{11,7},{... | collective-permute-start | bytes 6291464 | tf_op jit(solution)/shard_map/ppermute | solution.py:15
  21.1 94.3 %collective-permute-start = (bf16[1024,1024]{1,0:T(8,128)(2,1)}, bf16[1024,1024]{1,0:T(8,128)(2,1)S(1)}, u32[]{:S(2)}, u32[]{:S(2)}) collective-permute-start(bf16[1024,1024]{1,0:T(8,128)(2,1)} %fusion.2), channel_id=1, source_target_pairs={{2,0},{4,2},{6,4},{8,6},{10,8},{12,10},{14,12},{3,1},{5,3},{7,5},{... | collective-permute-start | bytes 6291464 | tf_op jit(solution)/shard_map/ppermute | solution.py:15
Sparse Core Ops, SparseCore 0:
  133.3 115.4 reduce-scatter.1
where the time goes:
time: 263 us
  waiting for transfers between devices  188 us (71%)
  other arithmetic  27.3 us (10%)
  matrix products  25.7 us (10%)
  between operations  14.1 us (5%)
  starting transfers between devices  3.87 us (1%)
  blocking collectives  3.57 us (1%)
    reduce_scatter x1, waiting for transfers between devices, per_device(): reduced = lax.psum_scatter(stacked, 'samp', scatter_dimension=1, tiled=True)  116 us
    ppermute x3, waiting for transfers between devices, from_behind(): return lax.ppermute(shard, axis, pairs)  72.6 us
    dot_general x4, matrix products, contract(): lax.dot_general(left, right, (((0,), (0,)), ((), ())), preferred_element_...  25.7 us
    another operation x1, other arithmetic, per_device(): stacked = jnp.stack(tiles)  11.7 us
    broadcast_in_dim x1, other arithmetic, per_device(): return result[None]  7.17 us
  transfers between devices with their start and end apart: 4, of which 3 were waited for; matrix products, arithmetic and copies ran while one was open for 8% of the time, Pallas kernels for 0%

commit v1 on v0

--- a/solution.py
+++ b/solution.py
@@ -4,15 +4,17 @@
 from jax.sharding import PartitionSpec as P
 
 WIN = 4
-
-
 epsilon = 1e-05
 
 
 def from_behind(shard, axis, by):
     count = lax.axis_size(axis)
-    pairs = [(i, i + by) for i in range(count) if 0 <= i + by < count]
+    pairs = [(i + by, i) for i in range(count - by)]
     return lax.ppermute(shard, axis, pairs)
+
+
+def from_mate(shard):
+    return lax.ppermute(shard, "samp", [(0, 1), (1, 0)])
 
 
 def contract(left, right):
@@ -38,28 +40,24 @@
     spread = squares / present_count - center * center
     scored = (offsets * lax.rsqrt(spread + epsilon)).astype(jnp.bfloat16)
     width = scored.shape[1]
+    half = width // lax.axis_size("samp")
     total_samples = float(scored.shape[0] * lax.axis_size("samp"))
     partner_count = counts[0]
+    first = lax.axis_index("samp") * half
+    other = from_mate(scored)
+    left = lax.dynamic_slice_in_dim(scored, first, half, 1)
+    left_other = lax.dynamic_slice_in_dim(other, first, half, 1)
     tiles = []
     for offset in range(WIN):
         if offset == 0:
-            partner = scored
+            partner, partner_other = scored, other
         else:
-            partner = from_behind(scored, "var", -offset)
-        tiles.append(
-            lax.cond(
-                offset < partner_count,
-                lambda other: contract(scored, other),
-                lambda other: jnp.zeros((width, width), jnp.float32),
-                partner,
-            )
-        )
-    stacked = jnp.stack(tiles)
-    reduced = lax.psum_scatter(stacked, "samp", scatter_dimension=1, tiled=True)
-    scaled = reduced / total_samples
-    keep = jnp.arange(WIN, dtype=jnp.int32)[:, None, None] < partner_count
-    result = jnp.where(keep, scaled, jnp.zeros_like(scaled)).astype(jnp.bfloat16)
-    return result[None]
+            partner = from_behind(scored, "var", offset)
+            partner_other = from_mate(partner)
+        tile = contract(left, partner) + contract(left_other, partner_other)
+        tile = jnp.where(offset < partner_count, tile / total_samples, 0.0)
+        tiles.append(tile.astype(jnp.bfloat16))
+    return jnp.stack(tiles)[None]
 
 
 def solution(mesh):

time: 263 us -> 221 us (0.84)
  the two profiles are of different devices: /device:TPU:0 before, /device:TPU:7 now
where the time goes in v1:
time: 221 us
  waiting for transfers between devices  176 us (80%)
  matrix products  21.4 us (10%)
  other arithmetic  9.87 us (4%)
  starting transfers between devices  8.64 us (4%)
  blocking collectives  3.8 us (2%)
    ppermute x3, waiting for transfers between devices, from_behind(): return lax.ppermute(shard, axis, pairs)  176 us
    dot_general x8, matrix products, contract(): lax.dot_general(left, right, (((0,), (0,)), ((), ())), preferred_element_...  21.4 us
    ppermute x3, starting transfers between devices, from_behind(): return lax.ppermute(shard, axis, pairs)  4.72 us
  transfers between devices with their start and end apart: 7, of which 2 were waited for; matrix products, arithmetic and copies ran while one was open for 9% of the time, Pallas kernels for 0%

profile of v1, /device:TPU:7, one launch (start us, length us, event | category | flops | bytes accessed | tf_op | source)
XLA Modules:
  0.0 220.6 jit_solution(2024395957588700416)
XLA Ops:
  0.0 3.9 %fusion.4 = (f32[1024]{0:T(1024)S(1)}, f32[1024]{0:T(1024)S(1)}, f32[1024]{0:T(1024)S(1)}) fusion(bf16[1024,1024]{1,0:T(8,128)(2,1)} %param.3, s32[1024,1024]{1,0:T(8,128)} %param.4), kind=kLoop, calls=%fused_computation.9 | loop fusion | flops 7336960 | bytes 6303744 | tf_op jit(solution)/shard_map/reduce_sum | solution.py:32
  3.9 3.8 %all-reduce = (f32[1024]{0:T(1024)S(1)}, f32[1024]{0:T(1024)S(1)}, f32[1024]{0:T(1024)S(1)}) all-reduce(f32[1024]{0:T(1024)S(1)} %get-tuple-element.6, f32[1024]{0:T(1024)S(1)} %get-tuple-element.7, f32[1024]{0:T(1024)S(1)} %get-tuple-element.5), channel_id=1, replica_groups=mesh['region'=2,'var'=8,'samp'=2] {'samp'}, use_global_device_ids=true, to_apply=%region_5.0 | all-reduce | flops 3072 | bytes 24576 | tf_op jit(solution)/shard_map/psum | solution.py:29
  7.7 3.7 %fusion.2 = bf16[1024,1024]{1,0:T(8,128)(2,1)S(1)} fusion(bf16[1024,1024]{1,0:T(8,128)(2,1)} %param.3, s32[1024,1024]{1,0:T(8,128)} %param.4, f32[1024]{0:T(1024)S(1)} %get-tuple-element.12, f32[1024]{0:T(1024)S(1)} %get-tuple-element.11), kind=kLoop, calls=%fused_computation.5 | loop fusion | flops 6291456 | bytes 8396800 | tf_op jit(solution)/shard_map/convert_element_type | solution.py:41
  11.4 2.1 collective-permute-start.1
  13.5 1.3 collective-permute-start.3
  14.8 1.3 collective-permute-start.5
  16.1 0.5 collective-permute-start
  16.6 44.7 %collective-permute-done.1 = bf16[1024,1024]{1,0:T(8,128)(2,1)} collective-permute-done((bf16[1024,1024]{1,0:T(8,128)(2,1)S(1)}, bf16[1024,1024]{1,0:T(8,128)(2,1)}, u32[]{:S(2)}, u32[]{:S(2)}) %collective-permute-start.1) | collective-permute-done | bytes 2097184 | tf_op jit(solution)/shard_map/ppermute | solution.py:13
  61.4 1.5 collective-permute-start.2
  63.6 0.0 collective-permute-done.3
  63.6 0.9 collective-permute-start.4
  64.5 1.3 fusion.19
  65.8 131.4 %collective-permute-done.5 = bf16[1024,1024]{1,0:T(8,128)(2,1)} collective-permute-done((bf16[1024,1024]{1,0:T(8,128)(2,1)S(1)}, bf16[1024,1024]{1,0:T(8,128)(2,1)}, u32[]{:S(2)}, u32[]{:S(2)}) %collective-permute-start.5) | collective-permute-done | bytes 2097184 | tf_op jit(solution)/shard_map/ppermute | solution.py:13
  197.2 1.0 collective-permute-start.6
  198.2 2.9 %fusion.17 = f32[512,1024]{1,0:T(8,128)S(1)} fusion(bf16[1024,1024]{1,0:T(8,128)(2,1)} %collective-permute-done.1, bf16[1024,1024]{1,0:T(8,128)(2,1)S(1)} %fusion.2, s32[]{:T(128)S(6)} %select_n.31), kind=kOutput, calls=%fused_computation.26 | convolution fusion | flops 1073741824 | bytes 5242884 | tf_op jit(solution)/shard_map/dot_general | solution.py:21
  201.1 2.9 %fusion.15 = f32[512,1024]{1,0:T(8,128)S(1)} fusion(bf16[1024,1024]{1,0:T(8,128)(2,1)} %collective-permute-done.3, bf16[1024,1024]{1,0:T(8,128)(2,1)S(1)} %fusion.2, s32[]{:T(128)S(6)} %select_n.31), kind=kOutput, calls=%fused_computation.24 | convolution fusion | flops 1073741824 | bytes 5242884 | tf_op jit(solution)/shard_map/dot_general | solution.py:21
  203.9 2.9 %fusion.13 = f32[512,1024]{1,0:T(8,128)S(1)} fusion(bf16[1024,1024]{1,0:T(8,128)(2,1)} %collective-permute-done.5, bf16[1024,1024]{1,0:T(8,128)(2,1)S(1)} %fusion.2, s32[]{:T(128)S(6)} %select_n.31), kind=kOutput, calls=%fused_computation.22 | convolution fusion | flops 1073741824 | bytes 5242884 | tf_op jit(solution)/shard_map/dot_general | solution.py:21
  206.8 0.0 collective-permute-done
  206.9 3.2 %fusion.5 = bf16[1,512,1024]{2,1,0:T(8,128)(2,1)S(1)} fusion(f32[512,1024]{1,0:T(8,128)S(1)} %fusion.19, bf16[1024,1024]{1,0:T(8,128)(2,1)} %collective-permute-done, pred[]{:T(512)} %bitcast, s32[]{:T(128)S(6)} %select_n.31), kind=kOutput, calls=%fused_computation.14 | convolution fusion | flops 1075838976 | bytes 6291972 | tf_op jit(solution)/shard_map/dot_general | solution.py:21
  210.1 0.0 collective-permute-done.2
  210.1 3.2 %fusion.6 = bf16[1,512,1024]{2,1,0:T(8,128)(2,1)S(1)} fusion(f32[512,1024]{1,0:T(8,128)S(1)} %fusion.17, bf16[1024,1024]{1,0:T(8,128)(2,1)} %collective-permute-done.2, pred[]{:T(512)} %bitcast.2, bf16[1024,1024]{1,0:T(8,128)(2,1)} %collective-permute-done, s32[]{:T(128)S(6)} %select_n.31), kind=kOutput, calls=%fused_computation.15 | convolution fusion | flops 1075838976 | bytes 6291972 | tf_op jit(solution)/shard_map/dot_general | solution.py:21
  213.3 0.0 collective-permute-done.4
  213.3 2.5 %fusion.7 = bf16[1,512,1024]{2,1,0:T(8,128)(2,1)S(1)} fusion(f32[512,1024]{1,0:T(8,128)S(1)} %fusion.15, bf16[1024,1024]{1,0:T(8,128)(2,1)S(1)} %collective-permute-done.4, pred[]{:T(512)} %bitcast.4, bf16[1024,1024]{1,0:T(8,128)(2,1)} %collective-permute-done, s32[]{:T(128)S(6)} %select_n.31), kind=kOutput, calls=%fused_computation.16 | convolution fusion | flops 1075838976 | bytes 6291972 | tf_op jit(solution)/shard_map/dot_general | solution.py:21
  215.8 0.0 collective-permute-done.6
  215.8 2.5 %fusion.8 = bf16[1,512,1024]{2,1,0:T(8,128)(2,1)S(1)} fusion(f32[512,1024]{1,0:T(8,128)S(1)} %fusion.13, bf16[1024,1024]{1,0:T(8,128)(2,1)S(1)} %collective-permute-done.6, pred[]{:T(512)} %bitcast.6, bf16[1024,1024]{1,0:T(8,128)(2,1)} %collective-permute-done, s32[]{:T(128)S(6)} %select_n.31), kind=kOutput, calls=%fused_computation.17 | convolution fusion | flops 1075838976 | bytes 6291972 | tf_op jit(solution)/shard_map/dot_general | solution.py:21
  218.3 2.3 %maximum_bitcast_fusion = bf16[1,4,512,1024]{3,2,1,0:T(8,128)(2,1)} fusion(bf16[1,512,1024]{2,1,0:T(8,128)(2,1)S(1)} %fusion.8, bf16[1,512,1024]{2,1,0:T(8,128)(2,1)S(1)} %fusion.7, bf16[1,512,1024]{2,1,0:T(8,128)(2,1)S(1)} %fusion.6, bf16[1,512,1024]{2,1,0:T(8,128)(2,1)S(1)} %fusion.5), kind=kLoop, calls=%fused_computation.7 | loop fusion | flops 6291456 | bytes 8388608 | tf_op jit(solution)/shard_map/broadcast_in_dim | solution.py:60
  (1 shorter events, 0.0 us)
Async XLA Ops:
  11.4 50.0 %collective-permute-start.1 = (bf16[1024,1024]{1,0:T(8,128)(2,1)S(1)}, bf16[1024,1024]{1,0:T(8,128)(2,1)}, u32[]{:S(2)}, u32[]{:S(2)}) collective-permute-start(bf16[1024,1024]{1,0:T(8,128)(2,1)S(1)} %fusion.2), channel_id=1, source_target_pairs={{2,0},{4,2},{6,4},{8,6},{10,8},{12,10},{14,12},{3,1},{5,3},{7,5},{... | collective-permute-start | bytes 6291464 | tf_op jit(solution)/shard_map/ppermute | solution.py:13
  13.5 50.0 %collective-permute-start.3 = (bf16[1024,1024]{1,0:T(8,128)(2,1)S(1)}, bf16[1024,1024]{1,0:T(8,128)(2,1)}, u32[]{:S(2)}, u32[]{:S(2)}) collective-permute-start(bf16[1024,1024]{1,0:T(8,128)(2,1)S(1)} %fusion.2), channel_id=1, source_target_pairs={{4,0},{6,2},{8,4},{10,6},{12,8},{14,10},{5,1},{7,3},{9,5},{11,7},{... | collective-permute-start | bytes 6291464 | tf_op jit(solution)/shard_map/ppermute | solution.py:13
  14.8 182.4 %collective-permute-start.5 = (bf16[1024,1024]{1,0:T(8,128)(2,1)S(1)}, bf16[1024,1024]{1,0:T(8,128)(2,1)}, u32[]{:S(2)}, u32[]{:S(2)}) collective-permute-start(bf16[1024,1024]{1,0:T(8,128)(2,1)S(1)} %fusion.2), channel_id=1, source_target_pairs={{6,0},{8,2},{10,4},{12,6},{14,8},{7,1},{9,3},{11,5},{13,7},{15,9},... | collective-permute-start | bytes 6291464 | tf_op jit(solution)/shard_map/ppermute | solution.py:13
  16.1 190.7 %collective-permute-start = (bf16[1024,1024]{1,0:T(8,128)(2,1)S(1)}, bf16[1024,1024]{1,0:T(8,128)(2,1)}, u32[]{:S(2)}, u32[]{:S(2)}) collective-permute-start(bf16[1024,1024]{1,0:T(8,128)(2,1)S(1)} %fusion.2), channel_id=1, source_target_pairs={{0,1},{1,0},{2,3},{3,2},{4,5},{5,4},{6,7},{7,6},{8,9},{9,8},{10,11... | collective-permute-start | bytes 6291464 | tf_op jit(solution)/shard_map/ppermute | solution.py:17
  61.4 148.7 %collective-permute-start.2 = (bf16[1024,1024]{1,0:T(8,128)(2,1)}, bf16[1024,1024]{1,0:T(8,128)(2,1)}, u32[]{:S(2)}, u32[]{:S(2)}) collective-permute-start(bf16[1024,1024]{1,0:T(8,128)(2,1)} %collective-permute-done.1), channel_id=1, source_target_pairs={{0,1},{1,0},{2,3},{3,2},{4,5},{5,4},{6,7},{7,6},{8,9},{9,8},{10,11... | collective-permute-start | bytes 6291464 | tf_op jit(solution)/shard_map/ppermute | solution.py:17
  63.6 149.7 %collective-permute-start.4 = (bf16[1024,1024]{1,0:T(8,128)(2,1)}, bf16[1024,1024]{1,0:T(8,128)(2,1)S(1)}, u32[]{:S(2)}, u32[]{:S(2)}) collective-permute-start(bf16[1024,1024]{1,0:T(8,128)(2,1)} %collective-permute-done.3), channel_id=1, source_target_pairs={{0,1},{1,0},{2,3},{3,2},{4,5},{5,4},{6,7},{7,6},{8,9},{9,8},{10,11... | collective-permute-start | bytes 6291464 | tf_op jit(solution)/shard_map/ppermute | solution.py:17
  197.2 18.6 %collective-permute-start.6 = (bf16[1024,1024]{1,0:T(8,128)(2,1)}, bf16[1024,1024]{1,0:T(8,128)(2,1)S(1)}, u32[]{:S(2)}, u32[]{:S(2)}) collective-permute-start(bf16[1024,1024]{1,0:T(8,128)(2,1)} %collective-permute-done.5), channel_id=1, source_target_pairs={{0,1},{1,0},{2,3},{3,2},{4,5},{5,4},{6,7},{7,6},{8,9},{9,8},{10,11... | collective-permute-start | bytes 6291464 | tf_op jit(solution)/shard_map/ppermute | solution.py:17

commit v2 on v1

v2 whole, which is shorter than its diff:
```python
import functools

import jax
import jax.numpy as jnp
from jax import lax
from jax.experimental import pallas as pl
from jax.experimental.pallas import tpu as pltpu
from jax.sharding import PartitionSpec as P

WIN = 4
QUARTERS = 4
PARTS = 2
epsilon = 1e-05

SMEM = pl.BlockSpec(memory_space=pltpu.SMEM)
VMEM = pl.BlockSpec(memory_space=pltpu.VMEM)
ANY = pl.BlockSpec(memory_space=pl.ANY)
PARAMS = pltpu.CompilerParams(vmem_limit_bytes=32 * 1024 * 1024)
COST = pl.CostEstimate(flops=1000, bytes_accessed=1000, transcendentals=0)


def stats_kernel(dosage_ref, observed_ref, sums_ref, masked_ref):
    @pl.when(pl.program_id(0) == 0)
    def _():
        sums_ref[...] = jnp.zeros_like(sums_ref)

    values = dosage_ref[...].astype(jnp.float32)
    present = observed_ref[...] > 0
    kept = jnp.where(present, values, 0.0)
    masked_ref[...] = jnp.where(present, values, -1.0).astype(masked_ref.dtype)
    rows, width = values.shape

    def fold(terms):
        return jnp.sum(terms.reshape(rows // 8, 8, width), axis=0)

    sums_ref[0] += fold(jnp.where(present, 1.0, 0.0))
    sums_ref[1] += fold(kept)
    sums_ref[2] += fold(kept * kept)


def stats(dosage, observed):
    samples, width = dosage.shape
    block = samples // 8
    return pl.pallas_call(
        stats_kernel,
        grid=(samples // block,),
        in_specs=[pl.BlockSpec((block, width), lambda i: (i, 0))] * 2,
        out_specs=[
            pl.BlockSpec((3, 8, width), lambda i: (0, 0, 0)),
            pl.BlockSpec((block, width), lambda i: (i, 0)),
        ],
        out_shape=[
            jax.ShapeDtypeStruct((3, 8, width), jnp.float32),
            jax.ShapeDtypeStruct((samples, width), jnp.bfloat16),
        ],
        compiler_params=PARAMS,
        cost_estimate=COST,
    )(dosage, observed)


def score_kernel(place_ref, masked_ref, sums_ref, sums_other_ref, *outs):
    pieces, rows_here, rows_away = outs[:QUARTERS], outs[QUARTERS:-PARTS], outs[-PARTS:]
    core = place_ref[1]
    quarter = pieces[0].shape[1]
    per_core = QUARTERS // 2
    for j in range(QUARTERS):
        columns = slice(j * quarter, (j + 1) * quarter)
        totals = [
            jnp.sum(sums_ref[n, :, columns] + sums_other_ref[n, :, columns], axis=0, keepdims=True)
            for n in range(3)
        ]
        count = jnp.maximum(totals[0], 1.0)
        center = totals[1] / count
        spread = totals[2] / count - center * center
        factor = lax.rsqrt(spread + epsilon)
        masked = masked_ref[:, columns].astype(jnp.float32)
        scored = jnp.where(masked >= 0.0, (masked - center) * factor, 0.0)
        scored = scored.astype(jnp.bfloat16)
        pieces[j][...] = scored
        turned = scored.T
        here = core == j // per_core

        @pl.when(here)
        def _():
            rows_here[j % per_core][...] = turned

        @pl.when(jnp.logical_not(here))
        def _():
            rows_away[j % per_core][...] = turned


def score(place, masked, sums, sums_other):
    samples, width = masked.shape
    quarter = width // QUARTERS
    part = width // 2 // PARTS
    return pl.pallas_call(
        score_kernel,
        in_specs=[SMEM, VMEM, VMEM, VMEM],
        out_specs=[VMEM] * (QUARTERS + 2 * PARTS),
        out_shape=[jax.ShapeDtypeStruct((samples, quarter), jnp.bfloat16)] * QUARTERS
        + [jax.ShapeDtypeStruct((part, samples), jnp.bfloat16)] * (2 * PARTS),
        compiler_params=PARAMS,
        cost_estimate=COST,
    )(place, masked, sums, sums_other)


def dots(rows, rights, scale):
    total = None
    for left, right in zip(rows, rights):
        term = jnp.dot(left[...], right[...], preferred_element_type=jnp.float32)
        total = term if total is None else total + term
    return total * scale


def tile_kernel(k, parts, scale, place_ref, *refs):
    rows, out_ref = refs[: 2 * parts], refs[-1]
    rights = refs[2 * parts :]
    keep = k < place_ref[2]
    part = rows[0].shape[0]
    pairs = (out_ref.shape[2] + rights[0].shape[1] - 1) // rights[0].shape[1]
    quarter = rights[0].shape[1]
    for q in range(pairs):
        for r in range(parts):
            block = dots(rows[2 * r : 2 * r + 2], rights[2 * q : 2 * q + 2], scale)
            block = jnp.where(keep, block, 0.0)
            out_ref[0, r * part : (r + 1) * part, q * quarter : (q + 1) * quarter] = block.astype(
                out_ref.dtype
            )


def tile(place, buffer, k, column, rows, rights, samples):
    quarter = rights[0].shape[1]
    part = rows[0].shape[0]
    parts = len(rows) // 2
    pieces = len(rights) // 2
    width = quarter * QUARTERS
    shape = jax.ShapeDtypeStruct((WIN, part * parts, width), jnp.bfloat16)
    operands = [place, *rows, *rights]
    specs = [SMEM] + [VMEM] * (len(operands) - 1)
    kernel = functools.partial(tile_kernel, k, parts, 1.0 / samples)
    aliases = {}
    if buffer is not None:
        aliases = {len(operands): 0}
        operands.append(buffer)
        specs.append(ANY)
        inner = kernel

        def kernel(*refs):
            inner(*refs[:-2], refs[-1])

    return pl.pallas_call(
        kernel,
        grid=(1,),
        in_specs=specs,
        out_specs=pl.BlockSpec(
            (1, part * parts, quarter * pieces), lambda i: (k, 0, column // pieces)
        ),
        out_shape=shape,
        input_output_aliases=aliases,
        compiler_params=PARAMS,
        cost_estimate=COST,
    )(*operands)


def far_kernel(only_odd, scale, parts, place_ref, *refs):
    rows, out_ref = refs[: 2 * parts], refs[-2]
    rights = refs[2 * parts : -3]
    part = rows[0].shape[0]
    quarter = rights[0].shape[1]

    def work():
        for q in range(len(rights) // 2):
            for r in range(parts):
                block = dots(rows[2 * r : 2 * r + 2], rights[2 * q : 2 * q + 2], scale)
                out_ref[r * part : (r + 1) * part, q * quarter : (q + 1) * quarter] = block.astype(
                    out_ref.dtype
                )

    if only_odd:
        pl.when(place_ref[0] == 1)(work)
    else:
        work()


def far(place, buffer, rows, rights, samples, only_odd=False):
    parts = len(rows) // 2
    shape = (rows[0].shape[0] * parts, rights[0].shape[1] * (len(rights) // 2))
    operands = [place, *rows, *rights, buffer]
    return pl.pallas_call(
        functools.partial(far_kernel, only_odd, 1.0 / samples, parts),
        in_specs=[SMEM] + [VMEM] * (len(operands) - 2) + [ANY],
        out_specs=[VMEM, ANY],
        out_shape=[
            jax.ShapeDtypeStruct(shape, jnp.bfloat16),
            jax.ShapeDtypeStruct(buffer.shape, buffer.dtype),
        ],
        input_output_aliases={len(operands) - 1: 1},
        compiler_params=PARAMS,
        cost_estimate=COST,
    )(*operands)


def choose_kernel(place_ref, odd_ref, even_ref, buffer_ref, out_ref, passed_ref):
    @pl.when(place_ref[0] == 1)
    def _():
        out_ref[...] = odd_ref[...]

    @pl.when(place_ref[0] == 0)
    def _():
        out_ref[...] = even_ref[...]


def choose(place, buffer, if_odd, if_even):
    return pl.pallas_call(
        choose_kernel,
        in_specs=[SMEM, VMEM, VMEM, ANY],
        out_specs=[VMEM, ANY],
        out_shape=[
            jax.ShapeDtypeStruct(if_odd.shape, if_odd.dtype),
            jax.ShapeDtypeStruct(buffer.shape, buffer.dtype),
        ],
        input_output_aliases={3: 1},
        compiler_params=PARAMS,
        cost_estimate=COST,
    )(place, if_odd, if_even, buffer)


def last_kernel(scale, place_ref, *refs):
    rows = refs[: 2 * PARTS]
    mine_ref, other_ref = refs[2 * PARTS : 2 * PARTS + 2]
    back2 = refs[2 * PARTS + 2 : 3 * PARTS + 2]
    back3 = refs[3 * PARTS + 2 : -4]
    out_ref, second, third, sems = refs[-4:]
    part = rows[0].shape[0]
    quarter = mine_ref.shape[1]
    keep2, keep3 = 2 < place_ref[2], 3 < place_ref[2]
    odd = place_ref[0] == 1
    row, column = 0, 0
    third[0:part, 0 : 2 * quarter] = jnp.where(keep3, back3[0][...], 0.0).astype(third.dtype)
    third[part:, 0 : 2 * quarter] = jnp.where(keep3, back3[1][...], 0.0).astype(third.dtype)
    third[:, 2 * quarter : 3 * quarter] = jnp.where(keep3, back3[2][...], 0.0).astype(third.dtype)
    third[:, 3 * quarter :] = jnp.where(keep3, back3[3][...], 0.0).astype(third.dtype)
    copy3 = pltpu.make_async_copy(third, out_ref.at[3], sems.at[0])
    copy3.start()

    @pl.when(odd)
    def _():
        for r in range(PARTS):
            second[r * part : (r + 1) * part, :] = jnp.where(keep2, back2[r][...], 0.0).astype(
                second.dtype
            )
        copy = pltpu.make_async_copy(second, out_ref.at[2], sems.at[1])
        copy.start()
        copy.wait()

    @pl.when(jnp.logical_not(odd))
    def _():
        for r in range(PARTS):
            block = dots(rows[2 * r : 2 * r + 2], (mine_ref, other_ref), scale)
            second[r * part : (r + 1) * part, 0:quarter] = jnp.where(keep2, block, 0.0).astype(
                second.dtype
            )
        copy = pltpu.make_async_copy(
            second.at[:, 0:quarter], out_ref.at[2, :, 0:quarter], sems.at[1]
        )
        copy.start()
        copy.wait()

    copy3.wait()


def last(place, buffer, rows, mine, other, back2, back3, samples):
    operands = [place, *rows, mine, other, *back2, *back3, buffer]

    def kernel(*refs):
        count = len(operands)
        last_kernel(1.0 / samples, *refs[: count - 1], *refs[count:])

    return pl.pallas_call(
        kernel,
        in_specs=[SMEM] + [VMEM] * (len(operands) - 2) + [ANY],
        out_specs=ANY,
        out_shape=jax.ShapeDtypeStruct(buffer.shape, buffer.dtype),
        scratch_shapes=[
            pltpu.VMEM(buffer.shape[1:], buffer.dtype),
            pltpu.VMEM(buffer.shape[1:], buffer.dtype),
            pltpu.SemaphoreType.DMA((2,)),
        ],
        input_output_aliases={len(operands) - 1: 0},
        compiler_params=PARAMS,
        cost_estimate=COST,
    )(*operands)


def per_device(dosage, observed, counts):
    places = lax.axis_size("var")
    samples = dosage.shape[0] * lax.axis_size("samp")
    place = jnp.stack(
        [
            (lax.axis_index("var") % 2).astype(jnp.int32),
            lax.axis_index("samp").astype(jnp.int32),
            counts[0],
        ]
    )

    def send(shard, pairs):
        return lax.ppermute(shard, "var", pairs)

    up = [(i, i + 2) for i in range(places - 2)]
    down = [(i + 2, i) for i in range(places - 2)]
    down_even = [pair for pair in down if pair[0] % 2 == 0]
    down_odd = [pair for pair in down if pair[0] % 2 == 1]
    to_even = [(i + 1, i) for i in range(0, places - 1, 2)]
    swap = to_even + [(i, i + 1) for i in range(0, places - 1, 2)]

    def mate(shard):
        return lax.ppermute(shard, "samp", [(0, 1), (1, 0)])

    sums, masked = stats(dosage, observed)
    made = score(place, masked, sums, mate(sums))
    own, here, away = made[:QUARTERS], made[QUARTERS:-PARTS], made[-PARTS:]

    beside = send(own[0], swap)
    above = [None] * QUARTERS
    above[1] = send(own[1], down_even)
    below = [send(here[0], up)]
    arrived = [mate(piece) for piece in away]
    own_other = [mate(piece) for piece in own]
    above[2] = send(own[2], down_even)
    below.append(send(arrived[0], up))
    above[3] = send(own[3], down_even)
    below.append(send(here[1], up))
    below.append(send(arrived[1], up))
    rows = [here[0], arrived[0], here[1], arrived[1]]
    own_rights = [piece for pair in zip(own, own_other) for piece in pair]

    buffer = tile(place, None, 0, 0, rows, own_rights, samples)
    around = send(beside, down_odd)
    next_one = [None] * QUARTERS
    swapped, buffer = choose(place, buffer, own[1], above[1])
    next_one[1] = send(swapped, swap)
    swapped, buffer = choose(place, buffer, own[2], above[2])
    next_one[2] = send(swapped, swap)
    next_one[0], buffer = choose(place, buffer, around, beside)
    above[0] = send(around, to_even)
    next_other = [mate(next_one[0]), mate(next_one[1]), mate(next_one[2]), None]
    swapped, buffer = choose(place, buffer, own[3], above[3])
    next_one[3] = send(swapped, swap)
    next_other[3] = mate(next_one[3])
    above_other = [mate(piece) for piece in above]

    def pair(j):
        return [next_one[j], next_other[j]]

    back2, back3 = [None] * PARTS, [None] * 4
    made, buffer = far(place, buffer, below[:2], own_rights, samples, True)
    back2[0] = send(made, down_odd)
    buffer = tile(place, buffer, 1, 0, rows, pair(0), samples)
    buffer = tile(place, buffer, 1, 1, rows, pair(1), samples)
    made, buffer = far(place, buffer, below[:2], pair(0) + pair(1), samples)
    back3[0] = send(made, down)
    buffer = tile(place, buffer, 2, 1, rows, [above[1], above_other[1]], samples)
    buffer = tile(place, buffer, 2, 2, rows, [above[2], above_other[2]], samples)
    buffer = tile(place, buffer, 1, 2, rows, pair(2), samples)
    made, buffer = far(place, buffer, below[2:], own_rights, samples, True)
    back2[1] = send(made, down_odd)
    made, buffer = far(place, buffer, below[2:], pair(0) + pair(1), samples)
    back3[1] = send(made, down)
    made, buffer = far(place, buffer, below, pair(2), samples)
    back3[2] = send(made, down)
    made, buffer = far(place, buffer, below, pair(3), samples)
    back3[3] = send(made, down)
    buffer = tile(place, buffer, 1, 3, rows, pair(3), samples)
    buffer = tile(place, buffer, 2, 3, rows, [above[3], above_other[3]], samples)
    buffer = last(place, buffer, rows, above[0], above_other[0], back2, back3, samples)
    return buffer[None]


def solution(mesh):
    in_specs = (P("samp", ("region", "var")), P("samp", ("region", "var")), P(("region", "var")))
    out_specs = P(("region", "var"), None, "samp", None)
    return jax.shard_map(
        per_device, mesh=mesh, in_specs=in_specs, out_specs=out_specs, check_vma=False
    )
```

time: 221 us -> 145 us (0.66)
  the two profiles are of different devices: /device:TPU:7 before, /device:TPU:22 now
where the time goes in v2:
time: 145 us
  waiting for transfers between devices  54 us (37%)
  starting transfers between devices  52.1 us (36%)
  Pallas kernels  33.8 us (23%)
  local copies, waits for them, and re-layouts  3.78 us (3%)
    ppermute x19, waiting for transfers between devices, send(): return lax.ppermute(shard, 'var', pairs)  52.1 us
    ppermute x19, starting transfers between devices, send(): return lax.ppermute(shard, 'var', pairs)  49.4 us
    pallas_call x8, Pallas kernels, tile(): pl.pallas_call(kernel, grid=(1,), in_specs=specs, out_specs=pl.BlockSpec(...  17.5 us
    pallas_call x6, Pallas kernels, far(): pl.pallas_call(functools.partial(far_kernel, only_odd, 1.0 / samples, par...  8.75 us
    unnamed x4, local copies, waits for them, and re-layouts  3.78 us
  transfers between devices with their start and end apart: 34, of which 13 were waited for; matrix products, arithmetic and copies ran while one was open for 0% of the time, Pallas kernels for 20%

profile of v2, /device:TPU:22, one launch (start us, length us, event | category | flops | bytes accessed | tf_op | source)
XLA Modules:
  0.0 145.0 jit_solution(16941417465844901391)
XLA Ops:
  0.0 2.2 %copy-done = s32[1024,1024]{1,0:T(8,128)S(1)} copy-done((s32[1024,1024]{1,0:T(8,128)S(1)}, s32[1024,1024]{1,0:T(8,128)}, u32[]{:S(2)}) %copy-start) | copy-done | bytes 4194328
  2.2 1.6 %copy-done.1 = bf16[1024,1024]{1,0:T(8,128)(2,1)S(1)} copy-done((bf16[1024,1024]{1,0:T(8,128)(2,1)S(1)}, bf16[1024,1024]{1,0:T(8,128)(2,1)}, u32[]{:S(2)}) %copy-start.1) | copy-done | bytes 2097176
  3.8 1.4 shard_map.37
  6.0 0.1 pad_add_fusion.place_ref.refs_0_
  6.0 0.6 collective-permute-done.sums_other_ref
  6.6 1.8 %shard_map.38 = (bf16[1024,256]{1,0:T(8,128)(2,1)S(1)}, bf16[1024,256]{1,0:T(8,128)(2,1)S(1)}, bf16[1024,256]{1,0:T(8,128)(2,1)S(1)}, bf16[1024,256]{1,0:T(8,128...) custom-call(s32[3]{0:T(128)S(1)} %pad_add_fusion.place_ref.refs_0_, ...), custom_call_target="tpu_custom_call" | custom-call | flops 1000 | bytes 1000 | tf_op jit(solution)/shard_map/pallas_call | solution.py:96
  8.4 0.2 collective-permute-start.1
  8.6 0.4 collective-permute-start.10
  8.9 0.2 collective-permute-start.11
  9.1 0.4 collective-permute-start.12
  9.4 0.2 collective-permute-start.2
  9.6 0.7 collective-permute-done.1.refs_1_.refs_2_
  10.3 0.2 collective-permute-start.9
  10.5 0.6 collective-permute-done.10.refs_7_.refs_5_
  11.1 0.7 collective-permute-start.15
  11.8 2.2 %collective-permute-start.3 = (bf16[1024,256]{1,0:T(8,128)(2,1)S(1)}, bf16[1024,256]{1,0:T(8,128)(2,1)S(1)}, u32[]{:S(2)}, u32[]{:S(2)}) collective-permute-start(bf16[1024,256]{1,0:T(8,128)(2,1)S(1)} %get-tuple-element.41.refs_4_.refs_2_), channel_id=1, source_target_pairs={{2,0},{6,4},{10,8},{14,12},{0,2},{4,6},{8,10},{12,14},{3,1},{7,5},... | collective-permute-start | bytes 1572872 | tf_op jit(solution)/shard_map/ppermute | solution.py:307
  14.0 0.7 collective-permute-start.14
  14.7 0.7 collective-permute-start.13
  15.4 3.5 %collective-permute-start.7 = (bf16[256,1024]{1,0:T(8,128)(2,1)S(1)}, bf16[256,1024]{1,0:T(8,128)(2,1)S(1)}, u32[]{:S(2)}, u32[]{:S(2)}) collective-permute-start(bf16[256,1024]{1,0:T(8,128)(2,1)S(1)} %get-tuple-element.37.refs_0_.refs_1_), channel_id=1, source_target_pairs={{0,4},{2,6},{4,8},{6,10},{8,12},{10,14},{1,5},{3,7},{5,9},{7,11},{... | collective-permute-start | bytes 1572872 | tf_op jit(solution)/shard_map/ppermute | solution.py:307
  19.0 1.9 %collective-permute-start.17 = (bf16[256,1024]{1,0:T(8,128)(2,1)S(1)}, bf16[256,1024]{1,0:T(8,128)(2,1)S(1)}, u32[]{:S(2)}, u32[]{:S(2)}) collective-permute-start(bf16[256,1024]{1,0:T(8,128)(2,1)S(1)} %get-tuple-element.39.refs_2_.refs_3_), channel_id=1, source_target_pairs={{0,4},{2,6},{4,8},{6,10},{8,12},{10,14},{1,5},{3,7},{5,9},{7,11},{... | collective-permute-start | bytes 1572872 | tf_op jit(solution)/shard_map/ppermute | solution.py:307
  20.9 5.1 %collective-permute-done.3.even_ref = bf16[1024,256]{1,0:T(8,128)(2,1)S(1)} collective-permute-done((bf16[1024,256]{1,0:T(8,128)(2,1)S(1)}, bf16[1024,256]{1,0:T(8,128)(2,1)S(1)}, u32[]{:S(2)}, u32[]{:S(2)}) %collective-permute-start.3) | collective-permute-done | bytes 524320 | tf_op jit(solution)/shard_map/ppermute | solution.py:307
  26.0 2.3 %collective-permute-start.4 = (bf16[1024,256]{1,0:T(8,128)(2,1)S(1)}, bf16[1024,256]{1,0:T(8,128)(2,1)S(1)}, u32[]{:S(2)}, u32[]{:S(2)}) collective-permute-start(bf16[1024,256]{1,0:T(8,128)(2,1)S(1)} %collective-permute-done.3.even_ref), channel_id=1, source_target_pairs={{6,2},{10,6},{14,10},{7,3},{11,7},{15,11},{22,18},{26,22},{30,26},... | collective-permute-start | bytes 1572872 | tf_op jit(solution)/shard_map/ppermute | solution.py:307
  28.3 3.8 %shard_map.39.buffer_ref = bf16[4,512,1024]{2,1,0:T(8,128)(2,1)} custom-call(s32[3]{0:T(128)S(1)} %pad_add_fusion.place_ref.refs_0_, bf16[256,1024]{1,0:T(8,128)(2,1)S(1)} %get-tuple-element.37.refs_0_.refs_1_, bf16[256,1024]{1,0:T(8,128)(2,1)S(1)} %collective-permute-done.1.refs_1_.refs_2_, bf16[256,1024]{1,0:T(8,128)(2,1)S(1)} %get-tuple-element.39.refs_2_.refs_3_, ...), custom_call_target="tpu_custom_call" | custom-call | flops 1000 | bytes 1000 | tf_op jit(solution)/shard_map/pallas_call | solution.py:151
  32.2 0.6 shard_map.40
  32.8 3.5 %collective-permute-start.8 = (bf16[256,1024]{1,0:T(8,128)(2,1)S(1)}, bf16[256,1024]{1,0:T(8,128)(2,1)S(1)}, u32[]{:S(2)}, u32[]{:S(2)}) collective-permute-start(bf16[256,1024]{1,0:T(8,128)(2,1)S(1)} %collective-permute-done.1.refs_1_.refs_2_), channel_id=1, source_target_pairs={{0,4},{2,6},{4,8},{6,10},{8,12},{10,14},{1,5},{3,7},{5,9},{7,11},{... | collective-permute-start | bytes 1572872 | tf_op jit(solution)/shard_map/ppermute | solution.py:307
  36.3 13.6 %collective-permute-start.24 = (bf16[1024,256]{1,0:T(8,128)(2,1)S(1)}, bf16[1024,256]{1,0:T(8,128)(2,1)S(1)}, u32[]{:S(2)}, u32[]{:S(2)}) collective-permute-start(bf16[1024,256]{1,0:T(8,128)(2,1)S(1)} %get-tuple-element.52), channel_id=1, source_target_pairs={{2,0},{6,4},{10,8},{14,12},{0,2},{4,6},{8,10},{12,14},{3,1},{7,5},... | collective-permute-start | bytes 1572872 | tf_op jit(solution)/shard_map/ppermute | solution.py:307
  49.9 0.6 shard_map.41
  50.5 0.1 collective-permute-start.22
  50.6 0.1 collective-permute-start.19
  50.7 0.5 collective-permute-start.21
  51.2 0.6 shard_map.42
  51.8 0.6 shard_map.43
  52.4 0.8 collective-permute-done.8.refs_1_
  53.2 9.5 %collective-permute-done.24.refs_5_.refs_4_ = bf16[1024,256]{1,0:T(8,128)(2,1)S(1)} collective-permute-done((bf16[1024,256]{1,0:T(8,128)(2,1)S(1)}, bf16[1024,256]{1,0:T(8,128)(2,1)S(1)}, u32[]{:S(2)}, u32[]{:S(2)}) %collective-permute-start.24) | collective-permute-done | bytes 524320 | tf_op jit(solution)/shard_map/ppermute | solution.py:307
  62.8 2.0 %collective-permute-start.30 = (bf16[1024,256]{1,0:T(8,128)(2,1)S(1)}, bf16[1024,256]{1,0:T(8,128)(2,1)S(1)}, u32[]{:S(2)}, u32[]{:S(2)}) collective-permute-start(bf16[1024,256]{1,0:T(8,128)(2,1)S(1)} %get-tuple-element.61), channel_id=1, source_target_pairs={{2,0},{6,4},{10,8},{14,12},{0,2},{4,6},{8,10},{12,14},{3,1},{7,5},... | collective-permute-start | bytes 1572872 | tf_op jit(solution)/shard_map/ppermute | solution.py:307
  64.8 9.2 %collective-permute-done.19.refs_5_.refs_4_ = bf16[1024,256]{1,0:T(8,128)(2,1)S(1)} collective-permute-done((bf16[1024,256]{1,0:T(8,128)(2,1)S(1)}, bf16[1024,256]{1,0:T(8,128)(2,1)S(1)}, u32[]{:S(2)}, u32[]{:S(2)}) %collective-permute-start.19) | collective-permute-done | bytes 524320 | tf_op jit(solution)/shard_map/ppermute | solution.py:307
  74.0 1.9 %collective-permute-start.18 = (bf16[256,1024]{1,0:T(8,128)(2,1)S(1)}, bf16[256,1024]{1,0:T(8,128)(2,1)S(1)}, u32[]{:S(2)}, u32[]{:S(2)}) collective-permute-start(bf16[256,1024]{1,0:T(8,128)(2,1)S(1)} %collective-permute-done.2.refs_3_.refs_4_), channel_id=1, source_target_pairs={{0,4},{2,6},{4,8},{6,10},{8,12},{10,14},{1,5},{3,7},{5,9},{7,11},{... | collective-permute-start | bytes 1572872 | tf_op jit(solution)/shard_map/ppermute | solution.py:307
  75.9 4.0 %collective-permute-start.5 = (bf16[1024,256]{1,0:T(8,128)(2,1)S(1)}, bf16[1024,256]{1,0:T(8,128)(2,1)S(1)}, u32[]{:S(2)}, u32[]{:S(2)}) collective-permute-start(bf16[1024,256]{1,0:T(8,128)(2,1)S(1)} %collective-permute-done.4.odd_ref), channel_id=1, source_target_pairs={{2,0},{6,4},{10,8},{14,12},{3,1},{7,5},{11,9},{15,13},{18,16},{22,... | collective-permute-start | bytes 1572872 | tf_op jit(solution)/shard_map/ppermute | solution.py:307
  79.9 4.9 %collective-permute-done.30.refs_4_.refs_5_ = bf16[1024,256]{1,0:T(8,128)(2,1)S(1)} collective-permute-done((bf16[1024,256]{1,0:T(8,128)(2,1)S(1)}, bf16[1024,256]{1,0:T(8,128)(2,1)S(1)}, u32[]{:S(2)}, u32[]{:S(2)}) %collective-permute-start.30) | collective-permute-done | bytes 524320 | tf_op jit(solution)/shard_map/ppermute | solution.py:307
  84.8 1.8 %shard_map.44 = (bf16[256,1024]{1,0:T(8,128)(2,1)S(1)}, bf16[4,512,1024]{2,1,0:T(8,128)(2,1)}) custom-call(s32[3]{0:T(128)S(1)} %pad_add_fusion.place_ref.refs_0_, bf16[256,1024]{1,0:T(8,128)(2,1)S(1)} %collective-permute-done.7.refs_0_, bf16[256,1024]{1,0:T(8,128)(2,1)S(1)} %collective-permute-done.8.refs_1_, ...), custom_call_target="tpu_custom_call", output_to_operand_aliasing={{1}: (11, {})} | custom-call | flops 1000 | bytes 1000 | tf_op jit(solution)/shard_map/pallas_call | solution.py:189
  86.6 0.6 collective-permute-start.33
  87.2 1.9 %collective-permute-start.16 = (bf16[256,1024]{1,0:T(8,128)(2,1)S(1)}, bf16[256,1024]{1,0:T(8,128)(2,1)S(1)}, u32[]{:S(2)}, u32[]{:S(2)}) collective-permute-start(bf16[256,1024]{1,0:T(8,128)(2,1)S(1)} %get-tuple-element.49), channel_id=1, source_target_pairs={{6,2},{10,6},{14,10},{7,3},{11,7},{15,11},{22,18},{26,22},{30,26},... | collective-permute-start | bytes 1572872 | tf_op jit(solution)/shard_map/ppermute | solution.py:307
  89.1 2.0 %shard_map.45.refs_7_ = bf16[4,512,1024]{2,1,0:T(8,128)(2,1)} custom-call(s32[3]{0:T(128)S(1)} %pad_add_fusion.place_ref.refs_0_, bf16[256,1024]{1,0:T(8,128)(2,1)S(1)} %get-tuple-element.37.refs_0_.refs_1_, bf16[256,1024]{1,0:T(8,128)(2,1)S(1)} %collective-permute-done.1.refs_1_.refs_2_, ...), custom_call_target="tpu_custom_call", output_to_operand_aliasing={{}: (7, {})} | custom-call | flops 1000 | bytes 1000 | tf_op jit(solution)/shard_map/pallas_call | solution.py:151
  91.0 2.0 %shard_map.46.refs_6_ = bf16[4,512,1024]{2,1,0:T(8,128)(2,1)} custom-call(s32[3]{0:T(128)S(1)} %pad_add_fusion.place_ref.refs_0_, bf16[256,1024]{1,0:T(8,128)(2,1)S(1)} %get-tuple-element.37.refs_0_.refs_1_, bf16[256,1024]{1,0:T(8,128)(2,1)S(1)} %collective-permute-done.1.refs_1_.refs_2_, ...), custom_call_target="tpu_custom_call", output_to_operand_aliasing={{}: (7, {})} | custom-call | flops 1000 | bytes 1000 | tf_op jit(solution)/shard_map/pallas_call | solution.py:151
  93.0 1.2 shard_map.47
  94.2 2.0 %shard_map.48.refs_7_ = bf16[4,512,1024]{2,1,0:T(8,128)(2,1)} custom-call(s32[3]{0:T(128)S(1)} %pad_add_fusion.place_ref.refs_0_, bf16[256,1024]{1,0:T(8,128)(2,1)S(1)} %get-tuple-element.37.refs_0_.refs_1_, bf16[256,1024]{1,0:T(8,128)(2,1)S(1)} %collective-permute-done.1.refs_1_.refs_2_, ...), custom_call_target="tpu_custom_call", output_to_operand_aliasing={{}: (7, {})} | custom-call | flops 1000 | bytes 1000 | tf_op jit(solution)/shard_map/pallas_call | solution.py:151
  96.2 2.0 %shard_map.49.refs_7_ = bf16[4,512,1024]{2,1,0:T(8,128)(2,1)} custom-call(s32[3]{0:T(128)S(1)} %pad_add_fusion.place_ref.refs_0_, bf16[256,1024]{1,0:T(8,128)(2,1)S(1)} %get-tuple-element.37.refs_0_.refs_1_, bf16[256,1024]{1,0:T(8,128)(2,1)S(1)} %collective-permute-done.1.refs_1_.refs_2_, ...), custom_call_target="tpu_custom_call", output_to_operand_aliasing={{}: (7, {})} | custom-call | flops 1000 | bytes 1000 | tf_op jit(solution)/shard_map/pallas_call | solution.py:151
  98.2 2.0 %shard_map.50.refs_10_ = bf16[4,512,1024]{2,1,0:T(8,128)(2,1)} custom-call(s32[3]{0:T(128)S(1)} %pad_add_fusion.place_ref.refs_0_, bf16[256,1024]{1,0:T(8,128)(2,1)S(1)} %get-tuple-element.37.refs_0_.refs_1_, bf16[256,1024]{1,0:T(8,128)(2,1)S(1)} %collective-permute-done.1.refs_1_.refs_2_, ...), custom_call_target="tpu_custom_call", output_to_operand_aliasing={{}: (7, {})} | custom-call | flops 1000 | bytes 1000 | tf_op jit(solution)/shard_map/pallas_call | solution.py:151
  100.1 2.0 %shard_map.51 = (bf16[256,1024]{1,0:T(8,128)(2,1)S(1)}, bf16[4,512,1024]{2,1,0:T(8,128)(2,1)}) custom-call(s32[3]{0:T(128)S(1)} %pad_add_fusion.place_ref.refs_0_, bf16[256,1024]{1,0:T(8,128)(2,1)S(1)} %collective-permute-done.17.refs_0_.refs_2_, bf16[256,1024]{1,0:T(8,128)(2,1)S(1)} %collective-permute-done.18.refs_1_.refs_3_, ...), custom_call_target="tpu_custom_call", output_to_operand_aliasing={{1}: (11, {})} | custom-call | flops 1000 | bytes 1000 | tf_op jit(solution)/shard_map/pallas_call | solution.py:189
  102.1 1.3 shard_map.52
  103.4 1.2 shard_map.53
  104.6 2.3 %collective-permute-start.29 = (bf16[512,256]{1,0:T(8,128)(2,1)S(1)}, bf16[512,256]{1,0:T(8,128)(2,1)S(1)}, u32[]{:S(2)}, u32[]{:S(2)}) collective-permute-start(bf16[512,256]{1,0:T(8,128)(2,1)S(1)} %get-tuple-element.60), channel_id=1, source_target_pairs={{4,0},{6,2},{8,4},{10,6},{12,8},{14,10},{5,1},{7,3},{9,5},{11,7},{... | collective-permute-start | bytes 786440 | tf_op jit(solution)/shard_map/ppermute | solution.py:307
  106.9 1.9 %collective-permute-start.26 = (bf16[256,1024]{1,0:T(8,128)(2,1)S(1)}, bf16[256,1024]{1,0:T(8,128)(2,1)S(1)}, u32[]{:S(2)}, u32[]{:S(2)}) collective-permute-start(bf16[256,1024]{1,0:T(8,128)(2,1)S(1)} %get-tuple-element.55), channel_id=1, source_target_pairs={{6,2},{10,6},{14,10},{7,3},{11,7},{15,11},{22,18},{26,22},{30,26},... | collective-permute-start | bytes 1572872 | tf_op jit(solution)/shard_map/ppermute | solution.py:307
  109.0 1.2 shard_map.54
  110.2 1.9 %collective-permute-start.28 = (bf16[256,512]{1,0:T(8,128)(2,1)S(1)}, bf16[256,512]{1,0:T(8,128)(2,1)S(1)}, u32[]{:S(2)}, u32[]{:S(2)}) collective-permute-start(bf16[256,512]{1,0:T(8,128)(2,1)S(1)} %get-tuple-element.58), channel_id=1, source_target_pairs={{4,0},{6,2},{8,4},{10,6},{12,8},{14,10},{5,1},{7,3},{9,5},{11,7},{... | collective-permute-start | bytes 786440 | tf_op jit(solution)/shard_map/ppermute | solution.py:307
  112.2 1.9 %collective-permute-start.27 = (bf16[256,512]{1,0:T(8,128)(2,1)S(1)}, bf16[256,512]{1,0:T(8,128)(2,1)S(1)}, u32[]{:S(2)}, u32[]{:S(2)}) collective-permute-start(bf16[256,512]{1,0:T(8,128)(2,1)S(1)} %get-tuple-element.56), channel_id=1, source_target_pairs={{4,0},{6,2},{8,4},{10,6},{12,8},{14,10},{5,1},{7,3},{9,5},{11,7},{... | collective-permute-start | bytes 786440 | tf_op jit(solution)/shard_map/ppermute | solution.py:307
  114.1 1.6 %collective-permute-done.29.refs_11_ = bf16[512,256]{1,0:T(8,128)(2,1)S(1)} collective-permute-done((bf16[512,256]{1,0:T(8,128)(2,1)S(1)}, bf16[512,256]{1,0:T(8,128)(2,1)S(1)}, u32[]{:S(2)}, u32[]{:S(2)}) %collective-permute-start.29) | collective-permute-done | bytes 262176 | tf_op jit(solution)/shard_map/ppermute | solution.py:307
  115.7 2.3 %collective-permute-start.32 = (bf16[512,256]{1,0:T(8,128)(2,1)S(1)}, bf16[512,256]{1,0:T(8,128)(2,1)S(1)}, u32[]{:S(2)}, u32[]{:S(2)}) collective-permute-start(bf16[512,256]{1,0:T(8,128)(2,1)S(1)} %get-tuple-element.63), channel_id=1, source_target_pairs={{4,0},{6,2},{8,4},{10,6},{12,8},{14,10},{5,1},{7,3},{9,5},{11,7},{... | collective-permute-start | bytes 786440 | tf_op jit(solution)/shard_map/ppermute | solution.py:307
  118.0 2.0 %shard_map.55.refs_7_ = bf16[4,512,1024]{2,1,0:T(8,128)(2,1)} custom-call(s32[3]{0:T(128)S(1)} %pad_add_fusion.place_ref.refs_0_, bf16[256,1024]{1,0:T(8,128)(2,1)S(1)} %get-tuple-element.37.refs_0_.refs_1_, bf16[256,1024]{1,0:T(8,128)(2,1)S(1)} %collective-permute-done.1.refs_1_.refs_2_, ...), custom_call_target="tpu_custom_call", output_to_operand_aliasing={{}: (7, {})} | custom-call | flops 1000 | bytes 1000 | tf_op jit(solution)/shard_map/pallas_call | solution.py:151
  119.9 2.0 %shard_map.56.refs_13_ = bf16[4,512,1024]{2,1,0:T(8,128)(2,1)} custom-call(s32[3]{0:T(128)S(1)} %pad_add_fusion.place_ref.refs_0_, bf16[256,1024]{1,0:T(8,128)(2,1)S(1)} %get-tuple-element.37.refs_0_.refs_1_, bf16[256,1024]{1,0:T(8,128)(2,1)S(1)} %collective-permute-done.1.refs_1_.refs_2_, ...), custom_call_target="tpu_custom_call", output_to_operand_aliasing={{}: (7, {})} | custom-call | flops 1000 | bytes 1000 | tf_op jit(solution)/shard_map/pallas_call | solution.py:151
  121.9 10.6 %collective-permute-done.28.refs_10_ = bf16[256,512]{1,0:T(8,128)(2,1)S(1)} collective-permute-done((bf16[256,512]{1,0:T(8,128)(2,1)S(1)}, bf16[256,512]{1,0:T(8,128)(2,1)S(1)}, u32[]{:S(2)}, u32[]{:S(2)}) %collective-permute-start.28) | collective-permute-done | bytes 262176 | tf_op jit(solution)/shard_map/ppermute | solution.py:307
  132.5 5.6 %collective-permute-done.27.refs_9_ = bf16[256,512]{1,0:T(8,128)(2,1)S(1)} collective-permute-done((bf16[256,512]{1,0:T(8,128)(2,1)S(1)}, bf16[256,512]{1,0:T(8,128)(2,1)S(1)}, u32[]{:S(2)}, u32[]{:S(2)}) %collective-permute-start.27) | collective-permute-done | bytes 262176 | tf_op jit(solution)/shard_map/ppermute | solution.py:307
  138.1 4.7 %collective-permute-done.32.refs_12_ = bf16[512,256]{1,0:T(8,128)(2,1)S(1)} collective-permute-done((bf16[512,256]{1,0:T(8,128)(2,1)S(1)}, bf16[512,256]{1,0:T(8,128)(2,1)S(1)}, u32[]{:S(2)}, u32[]{:S(2)}) %collective-permute-start.32) | collective-permute-done | bytes 262176 | tf_op jit(solution)/shard_map/ppermute | solution.py:307
  142.8 2.0 %shard_map.57 = bf16[4,512,1024]{2,1,0:T(8,128)(2,1)} custom-call(s32[3]{0:T(128)S(1)} %pad_add_fusion.place_ref.refs_0_, bf16[256,1024]{1,0:T(8,128)(2,1)S(1)} %get-tuple-element.37.refs_0_.refs_1_, bf16[256,1024]{1,0:T(8,128)(2,1)S(1)} %collective-permute-done.1.refs_1_.refs_2_, ...), custom_call_target="tpu_custom_call", output_to_operand_aliasing={{}: (13, {})} | custom-call | flops 1000 | bytes 1000 | tf_op jit(solution)/shard_map/pallas_call | solution.py:279
  (30 shorter events, 0.3 us)
Async XLA Ops:
  0.0 2.2 %copy-start = (s32[1024,1024]{1,0:T(8,128)S(1)}, s32[1024,1024]{1,0:T(8,128)}, u32[]{:S(2)}) copy-start(s32[1024,1024]{1,0:T(8,128)} %observed_ref.1) | copy-start | bytes 12582916
  2.2 1.6 %copy-start.1 = (bf16[1024,1024]{1,0:T(8,128)(2,1)S(1)}, bf16[1024,1024]{1,0:T(8,128)(2,1)}, u32[]{:S(2)}) copy-start(bf16[1024,1024]{1,0:T(8,128)(2,1)} %dosage_ref.1) | copy-start | bytes 6291460
  5.2 1.4 collective-permute-start
  8.4 2.0 %collective-permute-start.1 = (bf16[256,1024]{1,0:T(8,128)(2,1)S(1)}, bf16[256,1024]{1,0:T(8,128)(2,1)S(1)}, u32[]{:S(2)}, u32[]{:S(2)}) collective-permute-start(bf16[256,1024]{1,0:T(8,128)(2,1)S(1)} %get-tuple-element.38), channel_id=1, source_target_pairs={{0,1},{1,0},{2,3},{3,2},{4,5},{5,4},{6,7},{7,6},{8,9},{9,8},{10,11... | collective-permute-start | bytes 1572872 | tf_op jit(solution)/shard_map/ppermute | solution.py:317
  8.6 2.5 %collective-permute-start.10 = (bf16[1024,256]{1,0:T(8,128)(2,1)S(1)}, bf16[1024,256]{1,0:T(8,128)(2,1)S(1)}, u32[]{:S(2)}, u32[]{:S(2)}) collective-permute-start(bf16[1024,256]{1,0:T(8,128)(2,1)S(1)} %get-tuple-element.42.refs_6_.odd_ref.refs_4_), channel_id=1, source_target_pairs={{0,1},{1,0},{2,3},{3,2},{4,5},{5,4},{6,7},{7,6},{8,9},{9,8},{10,11... | collective-permute-start | bytes 1572872 | tf_op jit(solution)/shard_map/ppermute | solution.py:317
  8.9 2.9 %collective-permute-start.11 = (bf16[1024,256]{1,0:T(8,128)(2,1)S(1)}, bf16[1024,256]{1,0:T(8,128)(2,1)S(1)}, u32[]{:S(2)}, u32[]{:S(2)}) collective-permute-start(bf16[1024,256]{1,0:T(8,128)(2,1)S(1)} %get-tuple-element.43.refs_8_.odd_ref.refs_6_), channel_id=1, source_target_pairs={{0,1},{1,0},{2,3},{3,2},{4,5},{5,4},{6,7},{7,6},{8,9},{9,8},{10,11... | collective-permute-start | bytes 1572872 | tf_op jit(solution)/shard_map/ppermute | solution.py:317
  9.1 4.9 %collective-permute-start.12 = (bf16[1024,256]{1,0:T(8,128)(2,1)S(1)}, bf16[1024,256]{1,0:T(8,128)(2,1)S(1)}, u32[]{:S(2)}, u32[]{:S(2)}) collective-permute-start(bf16[1024,256]{1,0:T(8,128)(2,1)S(1)} %get-tuple-element.44.refs_10_.odd_ref.refs_8_), channel_id=1, source_target_pairs={{0,1},{1,0},{2,3},{3,2},{4,5},{5,4},{6,7},{7,6},{8,9},{9,8},{10,11... | collective-permute-start | bytes 1572872 | tf_op jit(solution)/shard_map/ppermute | solution.py:317
  9.4 5.3 %collective-permute-start.2 = (bf16[256,1024]{1,0:T(8,128)(2,1)S(1)}, bf16[256,1024]{1,0:T(8,128)(2,1)S(1)}, u32[]{:S(2)}, u32[]{:S(2)}) collective-permute-start(bf16[256,1024]{1,0:T(8,128)(2,1)S(1)} %get-tuple-element.40), channel_id=1, source_target_pairs={{0,1},{1,0},{2,3},{3,2},{4,5},{5,4},{6,7},{7,6},{8,9},{9,8},{10,11... | collective-permute-start | bytes 1572872 | tf_op jit(solution)/shard_map/ppermute | solution.py:317
  10.3 5.1 %collective-permute-start.9 = (bf16[1024,256]{1,0:T(8,128)(2,1)S(1)}, bf16[1024,256]{1,0:T(8,128)(2,1)S(1)}, u32[]{:S(2)}, u32[]{:S(2)}) collective-permute-start(bf16[1024,256]{1,0:T(8,128)(2,1)S(1)} %get-tuple-element.41.refs_4_.refs_2_), channel_id=1, source_target_pairs={{0,1},{1,0},{2,3},{3,2},{4,5},{5,4},{6,7},{7,6},{8,9},{9,8},{10,11... | collective-permute-start | bytes 1572872 | tf_op jit(solution)/shard_map/ppermute | solution.py:317
  11.1 7.9 %collective-permute-start.15 = (bf16[1024,256]{1,0:T(8,128)(2,1)S(1)}, bf16[1024,256]{1,0:T(8,128)(2,1)S(1)}, u32[]{:S(2)}, u32[]{:S(2)}) collective-permute-start(bf16[1024,256]{1,0:T(8,128)(2,1)S(1)} %get-tuple-element.42.refs_6_.odd_ref.refs_4_), channel_id=1, source_target_pairs={{4,0},{8,4},{12,8},{5,1},{9,5},{13,9},{20,16},{24,20},{28,24},{21,... | collective-permute-start | bytes 1572872 | tf_op jit(solution)/shard_map/ppermute | solution.py:307
  11.8 14.2 %collective-permute-start.3 = (bf16[1024,256]{1,0:T(8,128)(2,1)S(1)}, bf16[1024,256]{1,0:T(8,128)(2,1)S(1)}, u32[]{:S(2)}, u32[]{:S(2)}) collective-permute-start(bf16[1024,256]{1,0:T(8,128)(2,1)S(1)} %get-tuple-element.41.refs_4_.refs_2_), channel_id=1, source_target_pairs={{2,0},{6,4},{10,8},{14,12},{0,2},{4,6},{8,10},{12,14},{3,1},{7,5},... | collective-permute-start | bytes 1572872 | tf_op jit(solution)/shard_map/ppermute | solution.py:307
  14.0 18.8 %collective-permute-start.14 = (bf16[1024,256]{1,0:T(8,128)(2,1)S(1)}, bf16[1024,256]{1,0:T(8,128)(2,1)S(1)}, u32[]{:S(2)}, u32[]{:S(2)}) collective-permute-start(bf16[1024,256]{1,0:T(8,128)(2,1)S(1)} %get-tuple-element.43.refs_8_.odd_ref.refs_6_), channel_id=1, source_target_pairs={{4,0},{8,4},{12,8},{5,1},{9,5},{13,9},{20,16},{24,20},{28,24},{21,... | collective-permute-start | bytes 1572872 | tf_op jit(solution)/shard_map/ppermute | solution.py:307
  14.7 21.6 %collective-permute-start.13 = (bf16[1024,256]{1,0:T(8,128)(2,1)S(1)}, bf16[1024,256]{1,0:T(8,128)(2,1)S(1)}, u32[]{:S(2)}, u32[]{:S(2)}) collective-permute-start(bf16[1024,256]{1,0:T(8,128)(2,1)S(1)} %get-tuple-element.44.refs_10_.odd_ref.refs_8_), channel_id=1, source_target_pairs={{4,0},{8,4},{12,8},{5,1},{9,5},{13,9},{20,16},{24,20},{28,24},{21,... | collective-permute-start | bytes 1572872 | tf_op jit(solution)/shard_map/ppermute | solution.py:307
  15.4 35.1 %collective-permute-start.7 = (bf16[256,1024]{1,0:T(8,128)(2,1)S(1)}, bf16[256,1024]{1,0:T(8,128)(2,1)S(1)}, u32[]{:S(2)}, u32[]{:S(2)}) collective-permute-start(bf16[256,1024]{1,0:T(8,128)(2,1)S(1)} %get-tuple-element.37.refs_0_.refs_1_), channel_id=1, source_target_pairs={{0,4},{2,6},{4,8},{6,10},{8,12},{10,14},{1,5},{3,7},{5,9},{7,11},{... | collective-permute-start | bytes 1572872 | tf_op jit(solution)/shard_map/ppermute | solution.py:307
  19.0 31.6 %collective-permute-start.17 = (bf16[256,1024]{1,0:T(8,128)(2,1)S(1)}, bf16[256,1024]{1,0:T(8,128)(2,1)S(1)}, u32[]{:S(2)}, u32[]{:S(2)}) collective-permute-start(bf16[256,1024]{1,0:T(8,128)(2,1)S(1)} %get-tuple-element.39.refs_2_.refs_3_), channel_id=1, source_target_pairs={{0,4},{2,6},{4,8},{6,10},{8,12},{10,14},{1,5},{3,7},{5,9},{7,11},{... | collective-permute-start | bytes 1572872 | tf_op jit(solution)/shard_map/ppermute | solution.py:307
  26.0 24.7 %collective-permute-start.4 = (bf16[1024,256]{1,0:T(8,128)(2,1)S(1)}, bf16[1024,256]{1,0:T(8,128)(2,1)S(1)}, u32[]{:S(2)}, u32[]{:S(2)}) collective-permute-start(bf16[1024,256]{1,0:T(8,128)(2,1)S(1)} %collective-permute-done.3.even_ref), channel_id=1, source_target_pairs={{6,2},{10,6},{14,10},{7,3},{11,7},{15,11},{22,18},{26,22},{30,26},... | collective-permute-start | bytes 1572872 | tf_op jit(solution)/shard_map/ppermute | solution.py:307
  32.8 20.4 %collective-permute-start.8 = (bf16[256,1024]{1,0:T(8,128)(2,1)S(1)}, bf16[256,1024]{1,0:T(8,128)(2,1)S(1)}, u32[]{:S(2)}, u32[]{:S(2)}) collective-permute-start(bf16[256,1024]{1,0:T(8,128)(2,1)S(1)} %collective-permute-done.1.refs_1_.refs_2_), channel_id=1, source_target_pairs={{0,4},{2,6},{4,8},{6,10},{8,12},{10,14},{1,5},{3,7},{5,9},{7,11},{... | collective-permute-start | bytes 1572872 | tf_op jit(solution)/shard_map/ppermute | solution.py:307
  36.3 26.4 %collective-permute-start.24 = (bf16[1024,256]{1,0:T(8,128)(2,1)S(1)}, bf16[1024,256]{1,0:T(8,128)(2,1)S(1)}, u32[]{:S(2)}, u32[]{:S(2)}) collective-permute-start(bf16[1024,256]{1,0:T(8,128)(2,1)S(1)} %get-tuple-element.52), channel_id=1, source_target_pairs={{2,0},{6,4},{10,8},{14,12},{0,2},{4,6},{8,10},{12,14},{3,1},{7,5},... | collective-permute-start | bytes 1572872 | tf_op jit(solution)/shard_map/ppermute | solution.py:307
  50.5 14.3 %collective-permute-start.22 = (bf16[1024,256]{1,0:T(8,128)(2,1)S(1)}, bf16[1024,256]{1,0:T(8,128)(2,1)S(1)}, u32[]{:S(2)}, u32[]{:S(2)}) collective-permute-start(bf16[1024,256]{1,0:T(8,128)(2,1)S(1)} %collective-permute-done.15.even_ref.refs_5_), channel_id=1, source_target_pairs={{0,1},{1,0},{2,3},{3,2},{4,5},{5,4},{6,7},{7,6},{8,9},{9,8},{10,11... | collective-permute-start | bytes 1572872 | tf_op jit(solution)/shard_map/ppermute | solution.py:317
  50.6 23.4 %collective-permute-start.19 = (bf16[1024,256]{1,0:T(8,128)(2,1)S(1)}, bf16[1024,256]{1,0:T(8,128)(2,1)S(1)}, u32[]{:S(2)}, u32[]{:S(2)}) collective-permute-start(bf16[1024,256]{1,0:T(8,128)(2,1)S(1)} %get-tuple-element.50), channel_id=1, source_target_pairs={{2,0},{6,4},{10,8},{14,12},{0,2},{4,6},{8,10},{12,14},{3,1},{7,5},... | collective-permute-start | bytes 1572872 | tf_op jit(solution)/shard_map/ppermute | solution.py:307
  50.7 23.3 %collective-permute-start.21 = (bf16[1024,256]{1,0:T(8,128)(2,1)S(1)}, bf16[1024,256]{1,0:T(8,128)(2,1)S(1)}, u32[]{:S(2)}, u32[]{:S(2)}) collective-permute-start(bf16[1024,256]{1,0:T(8,128)(2,1)S(1)} %collective-permute-done.14.even_ref.refs_5_), channel_id=1, source_target_pairs={{0,1},{1,0},{2,3},{3,2},{4,5},{5,4},{6,7},{7,6},{8,9},{9,8},{10,11... | collective-permute-start | bytes 1572872 | tf_op jit(solution)/shard_map/ppermute | solution.py:317
  53.2 22.7 %collective-permute-start.23 = (bf16[1024,256]{1,0:T(8,128)(2,1)S(1)}, bf16[1024,256]{1,0:T(8,128)(2,1)S(1)}, u32[]{:S(2)}, u32[]{:S(2)}) collective-permute-start(bf16[1024,256]{1,0:T(8,128)(2,1)S(1)} %get-tuple-element.51.refs_5_.refs_2_), channel_id=1, source_target_pairs={{0,1},{1,0},{2,3},{3,2},{4,5},{5,4},{6,7},{7,6},{8,9},{9,8},{10,11... | collective-permute-start | bytes 1572872 | tf_op jit(solution)/shard_map/ppermute | solution.py:317
  62.8 22.0 %collective-permute-start.30 = (bf16[1024,256]{1,0:T(8,128)(2,1)S(1)}, bf16[1024,256]{1,0:T(8,128)(2,1)S(1)}, u32[]{:S(2)}, u32[]{:S(2)}) collective-permute-start(bf16[1024,256]{1,0:T(8,128)(2,1)S(1)} %get-tuple-element.61), channel_id=1, source_target_pairs={{2,0},{6,4},{10,8},{14,12},{0,2},{4,6},{8,10},{12,14},{3,1},{7,5},... | collective-permute-start | bytes 1572872 | tf_op jit(solution)/shard_map/ppermute | solution.py:307
  64.8 21.8 %collective-permute-start.25 = (bf16[1024,256]{1,0:T(8,128)(2,1)S(1)}, bf16[1024,256]{1,0:T(8,128)(2,1)S(1)}, u32[]{:S(2)}, u32[]{:S(2)}) collective-permute-start(bf16[1024,256]{1,0:T(8,128)(2,1)S(1)} %collective-permute-done.24.refs_5_.refs_4_), channel_id=1, source_target_pairs={{0,1},{1,0},{2,3},{3,2},{4,5},{5,4},{6,7},{7,6},{8,9},{9,8},{10,11... | collective-permute-start | bytes 1572872 | tf_op jit(solution)/shard_map/ppermute | solution.py:317
  74.0 13.2 %collective-permute-start.20 = (bf16[1024,256]{1,0:T(8,128)(2,1)S(1)}, bf16[1024,256]{1,0:T(8,128)(2,1)S(1)}, u32[]{:S(2)}, u32[]{:S(2)}) collective-permute-start(bf16[1024,256]{1,0:T(8,128)(2,1)S(1)} %collective-permute-done.19.refs_5_.refs_4_), channel_id=1, source_target_pairs={{0,1},{1,0},{2,3},{3,2},{4,5},{5,4},{6,7},{7,6},{8,9},{9,8},{10,11... | collective-permute-start | bytes 1572872 | tf_op jit(solution)/shard_map/ppermute | solution.py:317
  74.0 26.1 %collective-permute-start.18 = (bf16[256,1024]{1,0:T(8,128)(2,1)S(1)}, bf16[256,1024]{1,0:T(8,128)(2,1)S(1)}, u32[]{:S(2)}, u32[]{:S(2)}) collective-permute-start(bf16[256,1024]{1,0:T(8,128)(2,1)S(1)} %collective-permute-done.2.refs_3_.refs_4_), channel_id=1, source_target_pairs={{0,4},{2,6},{4,8},{6,10},{8,12},{10,14},{1,5},{3,7},{5,9},{7,11},{... | collective-permute-start | bytes 1572872 | tf_op jit(solution)/shard_map/ppermute | solution.py:307
  75.9 31.0 %collective-permute-start.5 = (bf16[1024,256]{1,0:T(8,128)(2,1)S(1)}, bf16[1024,256]{1,0:T(8,128)(2,1)S(1)}, u32[]{:S(2)}, u32[]{:S(2)}) collective-permute-start(bf16[1024,256]{1,0:T(8,128)(2,1)S(1)} %collective-permute-done.4.odd_ref), channel_id=1, source_target_pairs={{2,0},{6,4},{10,8},{14,12},{3,1},{7,5},{11,9},{15,13},{18,16},{22,... | collective-permute-start | bytes 1572872 | tf_op jit(solution)/shard_map/ppermute | solution.py:307
  84.8 24.1 %collective-permute-start.31 = (bf16[1024,256]{1,0:T(8,128)(2,1)S(1)}, bf16[1024,256]{1,0:T(8,128)(2,1)S(1)}, u32[]{:S(2)}, u32[]{:S(2)}) collective-permute-start(bf16[1024,256]{1,0:T(8,128)(2,1)S(1)} %collective-permute-done.30.refs_4_.refs_5_), channel_id=1, source_target_pairs={{0,1},{1,0},{2,3},{3,2},{4,5},{5,4},{6,7},{7,6},{8,9},{9,8},{10,11... | collective-permute-start | bytes 1572872 | tf_op jit(solution)/shard_map/ppermute | solution.py:317
  86.6 23.6 %collective-permute-start.33 = (bf16[1024,256]{1,0:T(8,128)(2,1)S(1)}, bf16[1024,256]{1,0:T(8,128)(2,1)S(1)}, u32[]{:S(2)}, u32[]{:S(2)}) collective-permute-start(bf16[1024,256]{1,0:T(8,128)(2,1)S(1)} %collective-permute-done.13.even_ref.refs_5_), channel_id=1, source_target_pairs={{0,1},{1,0},{2,3},{3,2},{4,5},{5,4},{6,7},{7,6},{8,9},{9,8},{10,11... | collective-permute-start | bytes 1572872 | tf_op jit(solution)/shard_map/ppermute | solution.py:317
  87.2 25.0 %collective-permute-start.16 = (bf16[256,1024]{1,0:T(8,128)(2,1)S(1)}, bf16[256,1024]{1,0:T(8,128)(2,1)S(1)}, u32[]{:S(2)}, u32[]{:S(2)}) collective-permute-start(bf16[256,1024]{1,0:T(8,128)(2,1)S(1)} %get-tuple-element.49), channel_id=1, source_target_pairs={{6,2},{10,6},{14,10},{7,3},{11,7},{15,11},{22,18},{26,22},{30,26},... | collective-permute-start | bytes 1572872 | tf_op jit(solution)/shard_map/ppermute | solution.py:307
  104.6 11.1 %collective-permute-start.29 = (bf16[512,256]{1,0:T(8,128)(2,1)S(1)}, bf16[512,256]{1,0:T(8,128)(2,1)S(1)}, u32[]{:S(2)}, u32[]{:S(2)}) collective-permute-start(bf16[512,256]{1,0:T(8,128)(2,1)S(1)} %get-tuple-element.60), channel_id=1, source_target_pairs={{4,0},{6,2},{8,4},{10,6},{12,8},{14,10},{5,1},{7,3},{9,5},{11,7},{... | collective-permute-start | bytes 786440 | tf_op jit(solution)/shard_map/ppermute | solution.py:307
  106.9 31.2 %collective-permute-start.26 = (bf16[256,1024]{1,0:T(8,128)(2,1)S(1)}, bf16[256,1024]{1,0:T(8,128)(2,1)S(1)}, u32[]{:S(2)}, u32[]{:S(2)}) collective-permute-start(bf16[256,1024]{1,0:T(8,128)(2,1)S(1)} %get-tuple-element.55), channel_id=1, source_target_pairs={{6,2},{10,6},{14,10},{7,3},{11,7},{15,11},{22,18},{26,22},{30,26},... | collective-permute-start | bytes 1572872 | tf_op jit(solution)/shard_map/ppermute | solution.py:307
  108.9 29.3 %collective-permute-start.6 = (bf16[1024,256]{1,0:T(8,128)(2,1)S(1)}, bf16[1024,256]{1,0:T(8,128)(2,1)S(1)}, u32[]{:S(2)}, u32[]{:S(2)}) collective-permute-start(bf16[1024,256]{1,0:T(8,128)(2,1)S(1)} %collective-permute-done.5.refs_5_), channel_id=1, source_target_pairs={{0,1},{1,0},{2,3},{3,2},{4,5},{5,4},{6,7},{7,6},{8,9},{9,8},{10,11... | collective-permute-start | bytes 1572872 | tf_op jit(solution)/shard_map/ppermute | solution.py:317
  110.2 22.3 %collective-permute-start.28 = (bf16[256,512]{1,0:T(8,128)(2,1)S(1)}, bf16[256,512]{1,0:T(8,128)(2,1)S(1)}, u32[]{:S(2)}, u32[]{:S(2)}) collective-permute-start(bf16[256,512]{1,0:T(8,128)(2,1)S(1)} %get-tuple-element.58), channel_id=1, source_target_pairs={{4,0},{6,2},{8,4},{10,6},{12,8},{14,10},{5,1},{7,3},{9,5},{11,7},{... | collective-permute-start | bytes 786440 | tf_op jit(solution)/shard_map/ppermute | solution.py:307
  112.2 26.0 %collective-permute-start.27 = (bf16[256,512]{1,0:T(8,128)(2,1)S(1)}, bf16[256,512]{1,0:T(8,128)(2,1)S(1)}, u32[]{:S(2)}, u32[]{:S(2)}) collective-permute-start(bf16[256,512]{1,0:T(8,128)(2,1)S(1)} %get-tuple-element.56), channel_id=1, source_target_pairs={{4,0},{6,2},{8,4},{10,6},{12,8},{14,10},{5,1},{7,3},{9,5},{11,7},{... | collective-permute-start | bytes 786440 | tf_op jit(solution)/shard_map/ppermute | solution.py:307
  115.7 27.2 %collective-permute-start.32 = (bf16[512,256]{1,0:T(8,128)(2,1)S(1)}, bf16[512,256]{1,0:T(8,128)(2,1)S(1)}, u32[]{:S(2)}, u32[]{:S(2)}) collective-permute-start(bf16[512,256]{1,0:T(8,128)(2,1)S(1)} %get-tuple-element.63), channel_id=1, source_target_pairs={{4,0},{6,2},{8,4},{10,6},{12,8},{14,10},{5,1},{7,3},{9,5},{11,7},{... | collective-permute-start | bytes 786440 | tf_op jit(solution)/shard_map/ppermute | solution.py:307

commit v3 on v1

v3 whole, which is shorter than its diff:
```python
import functools

import jax
import jax.numpy as jnp
from jax import lax
from jax.experimental import pallas as pl
from jax.experimental.pallas import tpu as pltpu
from jax.sharding import PartitionSpec as P

WIN = 4
QUARTERS = 4
PARTS = 2
BLOCKS = 8
STATS_VMEM = 50
epsilon = 1e-05

SMEM = pl.BlockSpec(memory_space=pltpu.SMEM)
VMEM = pl.BlockSpec(memory_space=pltpu.VMEM)
ANY = pl.BlockSpec(memory_space=pl.ANY)
PARAMS = pltpu.CompilerParams(vmem_limit_bytes=32 * 1024 * 1024)
COST = pl.CostEstimate(flops=1000, bytes_accessed=1000, transcendentals=0)


def stats_kernel(dosage_hbm, observed_hbm, sums_ref, masked_ref, dosage_ref, observed_ref, sems):
    samples, width = dosage_ref.shape
    block = samples // BLOCKS
    copies = []
    for n in range(BLOCKS):
        at = pl.ds(n * block, block)
        pair = [
            pltpu.make_async_copy(observed_hbm.at[at], observed_ref.at[at], sems.at[0, n]),
            pltpu.make_async_copy(dosage_hbm.at[at], dosage_ref.at[at], sems.at[1, n]),
        ]
        for copy in pair:
            copy.start()
        copies.append(pair)

    def fold(terms):
        return jnp.sum(terms.reshape(block // 8, 8, width), axis=0)

    totals = [jnp.zeros((8, width), jnp.float32)] * 3
    for n in range(BLOCKS):
        for copy in copies[n]:
            copy.wait()
        at = slice(n * block, (n + 1) * block)
        values = dosage_ref[at, :].astype(jnp.float32)
        present = observed_ref[at, :] > 0
        kept = jnp.where(present, values, 0.0)
        masked_ref[at, :] = jnp.where(present, values, -1.0).astype(masked_ref.dtype)
        terms = [jnp.where(present, 1.0, 0.0), kept, kept * kept]
        totals = [total + fold(term) for total, term in zip(totals, terms)]
    for n in range(3):
        sums_ref[n : n + 1, :] = jnp.sum(totals[n], axis=0, keepdims=True)
    sums_ref[3:, :] = jnp.zeros((5, width), jnp.float32)


def stats(dosage, observed):
    samples, width = dosage.shape
    return pl.pallas_call(
        stats_kernel,
        in_specs=[pl.BlockSpec(memory_space=pltpu.HBM)] * 2,
        out_specs=[VMEM, VMEM],
        out_shape=[
            jax.ShapeDtypeStruct((8, width), jnp.float32),
            jax.ShapeDtypeStruct((samples, width), jnp.bfloat16),
        ],
        scratch_shapes=[
            pltpu.VMEM(dosage.shape, dosage.dtype),
            pltpu.VMEM(observed.shape, observed.dtype),
            pltpu.SemaphoreType.DMA((2, BLOCKS)),
        ],
        compiler_params=pltpu.CompilerParams(vmem_limit_bytes=STATS_VMEM * 1024 * 1024),
        cost_estimate=COST,
    )(dosage, observed)


def score_kernel(place_ref, masked_ref, sums_ref, sums_other_ref, *outs):
    pieces, whole_ref = outs[:QUARTERS], outs[QUARTERS]
    rows_here, rows_away = outs[QUARTERS + 1 :]
    core = place_ref[1]
    quarter = pieces[0].shape[1]
    per_core = QUARTERS // 2
    for j in range(QUARTERS):
        columns = slice(j * quarter, (j + 1) * quarter)
        totals = [
            sums_ref[n : n + 1, columns] + sums_other_ref[n : n + 1, columns]
            for n in range(3)
        ]
        count = jnp.maximum(totals[0], 1.0)
        center = totals[1] / count
        spread = totals[2] / count - center * center
        factor = lax.rsqrt(spread + epsilon)
        masked = masked_ref[:, columns].astype(jnp.float32)
        scored = jnp.where(masked >= 0.0, (masked - center) * factor, 0.0)
        scored = scored.astype(jnp.bfloat16)
        pieces[j][...] = scored
        whole_ref[:, columns] = scored
        turned = scored.T
        here = core == j // per_core
        at = slice((j % per_core) * quarter, (j % per_core + 1) * quarter)

        @pl.when(here)
        def _():
            rows_here[at, :] = turned

        @pl.when(jnp.logical_not(here))
        def _():
            rows_away[at, :] = turned


def score(place, masked, sums, sums_other):
    samples, width = masked.shape
    quarter = width // QUARTERS
    return pl.pallas_call(
        score_kernel,
        in_specs=[SMEM, VMEM, VMEM, VMEM],
        out_specs=[VMEM] * (QUARTERS + 3),
        out_shape=[jax.ShapeDtypeStruct((samples, quarter), jnp.bfloat16)] * QUARTERS
        + [jax.ShapeDtypeStruct((samples, width), jnp.bfloat16)]
        + [jax.ShapeDtypeStruct((width // 2, samples), jnp.bfloat16)] * 2,
        compiler_params=PARAMS,
        cost_estimate=COST,
    )(place, masked, sums, sums_other)


def stack_kernel(here_ref, arrived_ref, *outs):
    part = outs[0].shape[0] // 2
    for r in range(PARTS):
        outs[r][0:part, :] = here_ref[r * part : (r + 1) * part, :]
        outs[r][part:, :] = arrived_ref[r * part : (r + 1) * part, :]


def stack(here, arrived):
    count, samples = here.shape
    return pl.pallas_call(
        stack_kernel,
        in_specs=[VMEM, VMEM],
        out_specs=[VMEM] * PARTS,
        out_shape=[jax.ShapeDtypeStruct((2 * count // PARTS, samples), here.dtype)] * PARTS,
        compiler_params=PARAMS,
        cost_estimate=COST,
    )(here, arrived)


def blocks(rows, rights, scale):
    part = rows[0].shape[0] // 2
    piece = min(right.shape[1] for right in rights)
    at = 0
    for q in range(len(rights) // 2):
        mine, other = rights[2 * q], rights[2 * q + 1]
        width = mine.shape[1]
        for begin in range(0, width, 256):
            end = min(begin + 256, width)
            for r, row in enumerate(rows):
                total = jnp.dot(
                    row[0:part, :], mine[:, begin:end], preferred_element_type=jnp.float32
                )
                total += jnp.dot(
                    row[part:, :], other[:, begin:end], preferred_element_type=jnp.float32
                )
                yield (
                    slice(r * part, (r + 1) * part),
                    slice(at + begin, at + end),
                    total * scale,
                )
        at += width


def tile_kernel(k, parts, scale, place_ref, *refs):
    out_ref = refs[-1]
    keep = k < place_ref[2]
    for at, columns, block in blocks(refs[:parts], refs[parts:-1], scale):
        out_ref[0, at, columns] = jnp.where(keep, block, 0.0).astype(out_ref.dtype)


def tile(place, buffer, k, column, rows, rights, samples, width, after=()):
    count = rows[0].shape[0] // 2 * len(rows)
    wide = sum(right.shape[1] for right in rights) // 2
    operands = [place, *rows, *rights]
    specs = [SMEM] + [VMEM] * (len(operands) - 1)
    kernel = functools.partial(tile_kernel, k, len(rows), 1.0 / samples)
    aliases = {}
    if buffer is not None:
        aliases = {len(operands): 0}
        operands += [buffer, *after]
        specs += [ANY] * (1 + len(after))
        inner, count_in = kernel, len(operands) - 1 - len(after)

        def kernel(*refs):
            inner(*refs[:count_in], refs[-1])

    return pl.pallas_call(
        kernel,
        grid=(1,),
        in_specs=specs,
        out_specs=pl.BlockSpec((1, count, wide), lambda i: (k, 0, column)),
        out_shape=jax.ShapeDtypeStruct((WIN, count, width), jnp.bfloat16),
        input_output_aliases=aliases,
        compiler_params=PARAMS,
        cost_estimate=COST,
    )(*operands)


def far_kernel(only_odd, scale, parts, pieces, place_ref, *refs):
    out_ref = refs[-2]

    def work():
        for at, columns, block in blocks(refs[:parts], refs[parts : parts + pieces], scale):
            out_ref[at, columns] = block.astype(out_ref.dtype)

    if only_odd:
        pl.when(place_ref[0] == 1)(work)
    else:
        work()


def far(place, buffer, rows, rights, samples, only_odd=False, after=()):
    shape = (
        rows[0].shape[0] // 2 * len(rows),
        sum(right.shape[1] for right in rights) // 2,
    )
    operands = [place, *rows, *rights, *after, buffer]
    return pl.pallas_call(
        functools.partial(far_kernel, only_odd, 1.0 / samples, len(rows), len(rights)),
        in_specs=[SMEM] + [VMEM] * (len(rows) + len(rights)) + [ANY] * (len(after) + 1),
        out_specs=[VMEM, ANY],
        out_shape=[
            jax.ShapeDtypeStruct(shape, jnp.bfloat16),
            jax.ShapeDtypeStruct(buffer.shape, buffer.dtype),
        ],
        input_output_aliases={len(operands) - 1: 1},
        compiler_params=PARAMS,
        cost_estimate=COST,
    )(*operands)


def choose_kernel(place_ref, odd_ref, even_ref, *refs):
    out_ref = refs[-1]

    @pl.when(place_ref[0] == 1)
    def _():
        out_ref[...] = odd_ref[...]

    @pl.when(place_ref[0] == 0)
    def _():
        out_ref[...] = even_ref[...]


def choose(place, if_odd, if_even, *passed):
    operands = [if_even, *passed]
    return pl.pallas_call(
        choose_kernel,
        in_specs=[SMEM, VMEM, VMEM] + [ANY] * len(passed),
        out_specs=[VMEM] + [ANY] * len(passed) + [VMEM],
        out_shape=[jax.ShapeDtypeStruct(x.shape, x.dtype) for x in (*operands, if_odd)],
        input_output_aliases={2 + n: n for n in range(len(operands))},
        compiler_params=PARAMS,
        cost_estimate=COST,
    )(place, if_odd, *operands)


def hold(after, *passed):
    def kernel(*refs):
        pass

    return pl.pallas_call(
        kernel,
        in_specs=[ANY] * (len(after) + len(passed)),
        out_specs=[ANY] * len(passed),
        out_shape=[jax.ShapeDtypeStruct(x.shape, x.dtype) for x in passed],
        input_output_aliases={len(after) + n: n for n in range(len(passed))},
        compiler_params=PARAMS,
        cost_estimate=COST,
    )(*after, *passed)


def last_kernel(place_ref, low_a, low_b, top, bottom, third, fourth, out_ref, two, three, sems):
    keep2, keep3 = 2 < place_ref[2], 3 < place_ref[2]
    part, half = top.shape
    quarter = half // 2

    def kept(keep, ref):
        return jnp.where(keep, ref[...], 0.0).astype(out_ref.dtype)

    three[0:part, 0:half] = kept(keep3, top)
    three[part:, 0:half] = kept(keep3, bottom)
    three[:, half : half + quarter] = kept(keep3, third)
    three[:, half + quarter :] = kept(keep3, fourth)
    copy3 = pltpu.make_async_copy(three, out_ref.at[3], sems.at[0])
    copy3.start()

    @pl.when(place_ref[0] == 1)
    def _():
        two[0:part, :] = kept(keep2, low_a)
        two[part:, :] = kept(keep2, low_b)
        copy2 = pltpu.make_async_copy(two, out_ref.at[2, :, half:], sems.at[1])
        copy2.start()
        copy2.wait()

    copy3.wait()


def last(place, buffer, back2, back3):
    operands = [place, *back2, *back3, buffer]
    count, width = buffer.shape[1:]

    def kernel(*refs):
        n = len(operands)
        last_kernel(*refs[: n - 1], *refs[n:])

    return pl.pallas_call(
        kernel,
        in_specs=[SMEM] + [VMEM] * (len(operands) - 2) + [ANY],
        out_specs=ANY,
        out_shape=jax.ShapeDtypeStruct(buffer.shape, buffer.dtype),
        scratch_shapes=[
            pltpu.VMEM((count, width // 2), buffer.dtype),
            pltpu.VMEM((count, width), buffer.dtype),
            pltpu.SemaphoreType.DMA((2,)),
        ],
        input_output_aliases={len(operands) - 1: 0},
        compiler_params=PARAMS,
        cost_estimate=COST,
    )(*operands)


def per_device(dosage, observed, counts):
    places = lax.axis_size("var")
    samples = dosage.shape[0] * lax.axis_size("samp")
    width = dosage.shape[1]
    place = jnp.stack(
        [
            (lax.axis_index("var") % 2).astype(jnp.int32),
            lax.axis_index("samp").astype(jnp.int32),
            counts[0],
        ]
    )

    def send(shard, pairs):
        return lax.ppermute(shard, "var", pairs)

    up = [(i, i + 2) for i in range(places - 2)]
    down = [(i + 2, i) for i in range(places - 2)]
    down_even = [pair for pair in down if pair[0] % 2 == 0]
    down_odd = [pair for pair in down if pair[0] % 2 == 1]
    to_even = [(i + 1, i) for i in range(0, places - 1, 2)]
    swap = to_even + [(i, i + 1) for i in range(0, places - 1, 2)]

    def mate(shard):
        return lax.ppermute(shard, "samp", [(0, 1), (1, 0)])

    sums, masked = stats(dosage, observed)
    *own, whole, here, away = score(place, masked, sums, mate(sums))
    above = [None] * QUARTERS
    above[0] = send(own[0], down)
    above[1] = send(own[1], down)
    rows = stack(here, mate(away))
    below = [send(rows[0], up), None]
    whole_other = mate(whole)
    next_one, other = [None] * QUARTERS, [None] * QUARTERS
    back2, back3 = [None] * 2, [None] * 4

    buffer = tile(place, None, 0, 0, rows, [whole, whole_other], samples, width)

    above[0], own[2], buffer, swapped = choose(place, own[0], above[0], own[2], buffer)
    next_one[0] = send(swapped, swap)
    above[2] = send(own[2], down_even)

    (buffer,) = hold((next_one[0],), buffer)
    above[1], own[3], buffer, swapped = choose(place, own[1], above[1], own[3], buffer)
    next_one[1] = send(swapped, swap)
    above[3] = send(own[3], down_even)
    row, buffer = hold((below[0],), rows[1], buffer)
    rows = [rows[0], row]
    below[1] = send(rows[1], up)
    own_upper = [own[2], mate(own[2]), own[3], mate(own[3])]
    made, buffer = far(place, buffer, below[:1], own_upper, samples, True)
    back2[0] = send(made, down_odd)
    other[0] = mate(next_one[0])
    buffer = tile(
        place, buffer, 2, 0, rows, [above[0], mate(above[0]), above[1], mate(above[1])],
        samples, width,
    )

    (buffer,) = hold((next_one[1],), buffer)
    above[2], buffer, swapped = choose(place, own[2], above[2], buffer)
    next_one[2] = send(swapped, swap)
    other[1] = mate(next_one[1])
    low = [next_one[0], other[0], next_one[1], other[1]]
    made, buffer = far(place, buffer, below[:1], low, samples)
    back3[0] = send(made, down)
    buffer = tile(place, buffer, 1, 0, rows, low, samples, width, (back2[0],))

    made, buffer = far(place, buffer, below[1:], own_upper, samples, True, (back3[0],))
    back2[1] = send(made, down_odd)

    (buffer,) = hold((next_one[2],), buffer)
    above[3], buffer, swapped = choose(place, own[3], above[3], buffer)
    next_one[3] = send(swapped, swap)
    made, buffer = far(place, buffer, below[1:], low, samples)
    back3[1] = send(made, down)
    other[2] = mate(next_one[2])
    made, buffer = far(
        place, buffer, below, [next_one[2], other[2]], samples, False, (back2[1],)
    )
    back3[2] = send(made, down)

    other[3] = mate(next_one[3])
    made, buffer = far(
        place, buffer, below, [next_one[3], other[3]], samples, False, (back3[1],)
    )
    back3[3] = send(made, down)
    buffer = tile(
        place, buffer, 2, 1, rows, [above[2], mate(above[2]), above[3], mate(above[3])],
        samples, width,
    )
    buffer = tile(
        place, buffer, 1, 1, rows, [next_one[2], other[2], next_one[3], other[3]], samples, width
    )
    buffer = last(place, buffer, back2, back3)
    return buffer[None]


def solution(mesh):
    in_specs = (P("samp", ("region", "var")), P("samp", ("region", "var")), P(("region", "var")))
    out_specs = P(("region", "var"), None, "samp", None)
    return jax.shard_map(
        per_device, mesh=mesh, in_specs=in_specs, out_specs=out_specs, check_vma=False
    )
```

time: 221 us -> 124 us (0.56)
  the two profiles are of different devices: /device:TPU:7 before, /device:TPU:0 now
where the time goes in v3:
time: 124 us; the launch traced here: 123 us
  waiting for transfers between devices  64.3 us (52%)
  Pallas kernels  29.3 us (24%)
  starting transfers between devices  27.9 us (22%)
    ppermute x16, waiting for transfers between devices, send(): return lax.ppermute(shard, 'var', pairs)  60.3 us
    ppermute x16, starting transfers between devices, send(): return lax.ppermute(shard, 'var', pairs)  25.3 us
    pallas_call x5, Pallas kernels, tile(): pl.pallas_call(kernel, grid=(1,), in_specs=specs, out_specs=pl.BlockSpec(...  14.3 us
    pallas_call x6, Pallas kernels, far(): pl.pallas_call(functools.partial(far_kernel, only_odd, 1.0 / samples, len...  6.09 us
    ppermute x13, waiting for transfers between devices, mate(): return lax.ppermute(shard, 'samp', [(0, 1), (1, 0)])  4.02 us
    pallas_call x1, Pallas kernels, stats(): pl.pallas_call(stats_kernel, in_specs=[pl.BlockSpec(memory_space=pltpu.HB...  3.08 us
    ppermute x13, starting transfers between devices, mate(): return lax.ppermute(shard, 'samp', [(0, 1), (1, 0)])  2.62 us
  transfers between devices with their start and end apart: 29, of which 11 were waited for; matrix products, arithmetic and copies ran while one was open for 0% of the time, Pallas kernels for 18%

profile of v3, /device:TPU:0, one launch (start us, length us, event | category | flops | bytes accessed | tf_op | source)
XLA Modules:
  0.0 122.8 jit_solution(16922923347614621017)
XLA Ops:
  0.0 3.1 %shard_map.37 = (f32[8,1024]{1,0:T(8,128)S(1)}, bf16[1024,1024]{1,0:T(8,128)(2,1)S(1)}) custom-call(bf16[1024,1024]{1,0:T(8,128)(2,1)} %dosage_hbm.1, s32[1024,1024]{1,0:T(8,128)} %observed_hbm.1), custom_call_target="tpu_custom_call" | custom-call | flops 1000 | bytes 1000 | tf_op jit(solution)/shard_map/pallas_call | solution.py:59
  3.1 0.5 collective-permute-start
  4.3 0.1 pad_add_fusion.place_ref.refs_0_
  4.3 0.1 collective-permute-done.sums_other_ref
  4.5 1.7 %shard_map.38 = (bf16[1024,256]{1,0:T(8,128)(2,1)S(1)}, bf16[1024,256]{1,0:T(8,128)(2,1)S(1)}, bf16[1024,256]{1,0:T(8,128)(2,1)S(1)}, bf16[1024,256]{1,0:T(8,128...) custom-call(s32[3]{0:T(128)S(1)} %pad_add_fusion.place_ref.refs_0_, ...), custom_call_target="tpu_custom_call" | custom-call | flops 1000 | bytes 1000 | tf_op jit(solution)/shard_map/pallas_call | solution.py:114
  6.2 0.4 collective-permute-start.4
  6.6 0.2 collective-permute-start.1
  6.8 1.3 %collective-permute-start.3 = (bf16[1024,256]{1,0:T(8,128)(2,1)S(1)}, bf16[1024,256]{1,0:T(8,128)(2,1)S(1)}, u32[]{:S(2)}, u32[]{:S(2)}) collective-permute-start(bf16[1024,256]{1,0:T(8,128)(2,1)S(1)} %get-tuple-element.49.odd_ref), channel_id=1, source_target_pairs={{4,0},{6,2},{8,4},{10,6},{12,8},{14,10},{5,1},{7,3},{9,5},{11,7},{... | collective-permute-start | bytes 1572872 | tf_op jit(solution)/shard_map/ppermute | solution.py:340
  8.1 3.9 %collective-permute-done.1.arrived_ref = bf16[512,1024]{1,0:T(8,128)(2,1)S(1)} collective-permute-done((bf16[512,1024]{1,0:T(8,128)(2,1)S(1)}, bf16[512,1024]{1,0:T(8,128)(2,1)S(1)}, u32[]{:S(2)}, u32[]{:S(2)}) %collective-permute-start.1) | collective-permute-done | bytes 1048608 | tf_op jit(solution)/shard_map/ppermute | solution.py:350
  11.9 0.1 shard_map.39
  12.1 4.9 %collective-permute-start.2 = (bf16[512,1024]{1,0:T(8,128)(2,1)S(1)}, bf16[512,1024]{1,0:T(8,128)(2,1)S(1)}, u32[]{:S(2)}, u32[]{:S(2)}) collective-permute-start(bf16[512,1024]{1,0:T(8,128)(2,1)S(1)} %get-tuple-element.48.refs_0_.refs_1_), channel_id=1, source_target_pairs={{0,4},{2,6},{4,8},{6,10},{8,12},{10,14},{1,5},{3,7},{5,9},{7,11},{... | collective-permute-start | bytes 3145736 | tf_op jit(solution)/shard_map/ppermute | solution.py:340
  17.0 3.9 %shard_map.40.refs_1_ = bf16[4,512,1024]{2,1,0:T(8,128)(2,1)} custom-call(s32[3]{0:T(128)S(1)} %pad_add_fusion.place_ref.refs_0_, bf16[512,1024]{1,0:T(8,128)(2,1)S(1)} %get-tuple-element.48.refs_0_.refs_1_, bf16[512,1024]{1,0:T(8,128)(2,1)S(1)} %get-tuple-element.51.refs_1_, bf16[1024,1024]{1,0:T(8,128)(2,1)S(1)} %get-tuple-element.52.refs_2_, ...), custom_call_target="tpu_custom_call" | custom-call | flops 1000 | bytes 1000 | tf_op jit(solution)/shard_map/pallas_call | solution.py:192
  20.9 3.0 %collective-permute-done.3.even_ref = bf16[1024,256]{1,0:T(8,128)(2,1)S(1)} collective-permute-done((bf16[1024,256]{1,0:T(8,128)(2,1)S(1)}, bf16[1024,256]{1,0:T(8,128)(2,1)S(1)}, u32[]{:S(2)}, u32[]{:S(2)}) %collective-permute-start.3) | collective-permute-done | bytes 524320 | tf_op jit(solution)/shard_map/ppermute | solution.py:340
  23.9 0.6 shard_map.41
  24.5 1.7 %collective-permute-start.7 = (bf16[1024,256]{1,0:T(8,128)(2,1)S(1)}, bf16[1024,256]{1,0:T(8,128)(2,1)S(1)}, u32[]{:S(2)}, u32[]{:S(2)}) collective-permute-start(bf16[1024,256]{1,0:T(8,128)(2,1)S(1)} %get-tuple-element.56), channel_id=1, source_target_pairs={{2,0},{6,4},{10,8},{14,12},{0,2},{4,6},{8,10},{12,14},{3,1},{7,5},... | collective-permute-start | bytes 1572872 | tf_op jit(solution)/shard_map/ppermute | solution.py:340
  26.2 1.3 %collective-permute-start.6 = (bf16[1024,256]{1,0:T(8,128)(2,1)S(1)}, bf16[1024,256]{1,0:T(8,128)(2,1)S(1)}, u32[]{:S(2)}, u32[]{:S(2)}) collective-permute-start(bf16[1024,256]{1,0:T(8,128)(2,1)S(1)} %get-tuple-element.54.odd_ref), channel_id=1, source_target_pairs={{4,0},{6,2},{8,4},{10,6},{12,8},{14,10},{5,1},{7,3},{9,5},{11,7},{... | collective-permute-start | bytes 1572872 | tf_op jit(solution)/shard_map/ppermute | solution.py:340
  27.5 0.1 collective-permute-start.5
  27.6 0.5 collective-permute-start.15
  28.1 9.9 %collective-permute-done.7.refs_0_.refs_1_.refs_3_ = bf16[1024,256]{1,0:T(8,128)(2,1)S(1)} collective-permute-done((bf16[1024,256]{1,0:T(8,128)(2,1)S(1)}, bf16[1024,256]{1,0:T(8,128)(2,1)S(1)}, u32[]{:S(2)}, u32[]{:S(2)}) %collective-permute-start.7) | collective-permute-done | bytes 524320 | tf_op jit(solution)/shard_map/ppermute | solution.py:340
  38.0 3.0 %collective-permute-done.6.even_ref = bf16[1024,256]{1,0:T(8,128)(2,1)S(1)} collective-permute-done((bf16[1024,256]{1,0:T(8,128)(2,1)S(1)}, bf16[1024,256]{1,0:T(8,128)(2,1)S(1)}, u32[]{:S(2)}, u32[]{:S(2)}) %collective-permute-start.6) | collective-permute-done | bytes 524320 | tf_op jit(solution)/shard_map/ppermute | solution.py:340
  41.0 0.6 shard_map.43
  41.6 0.1 collective-permute-start.8
  41.6 0.7 collective-permute-start.12
  42.4 0.0 collective-permute-done.2.refs_0_
  42.4 0.2 collective-permute-start.16
  42.5 1.3 %collective-permute-start.14 = (bf16[1024,256]{1,0:T(8,128)(2,1)S(1)}, bf16[1024,256]{1,0:T(8,128)(2,1)S(1)}, u32[]{:S(2)}, u32[]{:S(2)}) collective-permute-start(bf16[1024,256]{1,0:T(8,128)(2,1)S(1)} %get-tuple-element.53.refs_1_.odd_ref), channel_id=1, source_target_pairs={{4,0},{8,4},{12,8},{5,1},{9,5},{13,9},{20,16},{24,20},{28,24},{21,... | collective-permute-start | bytes 1572872 | tf_op jit(solution)/shard_map/ppermute | solution.py:340
  43.8 0.0 collective-permute-done.15.refs_4_
  43.8 4.6 %collective-permute-start.10 = (bf16[512,1024]{1,0:T(8,128)(2,1)S(1)}, bf16[512,1024]{1,0:T(8,128)(2,1)S(1)}, u32[]{:S(2)}, u32[]{:S(2)}) collective-permute-start(bf16[512,1024]{1,0:T(8,128)(2,1)S(1)} %get-tuple-element.62.refs_2_), channel_id=1, source_target_pairs={{0,4},{2,6},{4,8},{6,10},{8,12},{10,14},{1,5},{3,7},{5,9},{7,11},{... | collective-permute-start | bytes 3145736 | tf_op jit(solution)/shard_map/ppermute | solution.py:340
  48.5 0.1 collective-permute-start.11
  48.6 7.4 %collective-permute-done.12.refs_0_.refs_3_.refs_5_ = bf16[1024,256]{1,0:T(8,128)(2,1)S(1)} collective-permute-done((bf16[1024,256]{1,0:T(8,128)(2,1)S(1)}, bf16[1024,256]{1,0:T(8,128)(2,1)S(1)}, u32[]{:S(2)}, u32[]{:S(2)}) %collective-permute-start.12) | collective-permute-done | bytes 524320 | tf_op jit(solution)/shard_map/ppermute | solution.py:340
  56.0 0.0 collective-permute-start.13
  56.0 0.5 shard_map.45
  56.5 0.0 collective-permute-done.16.refs_6_
  56.5 2.6 %shard_map.46.refs_1_ = bf16[4,512,1024]{2,1,0:T(8,128)(2,1)} custom-call(s32[3]{0:T(128)S(1)} %pad_add_fusion.place_ref.refs_0_, bf16[512,1024]{1,0:T(8,128)(2,1)S(1)} %get-tuple-element.48.refs_0_.refs_1_, bf16[512,1024]{1,0:T(8,128)(2,1)S(1)} %get-tuple-element.62.refs_2_, ...), custom_call_target="tpu_custom_call", output_to_operand_aliasing={{}: (7, {})} | custom-call | flops 1000 | bytes 1000 | tf_op jit(solution)/shard_map/pallas_call | solution.py:192
  59.1 0.0 collective-permute-done.14.even_ref
  59.1 0.6 shard_map.48
  59.7 1.4 %collective-permute-start.20 = (bf16[1024,256]{1,0:T(8,128)(2,1)S(1)}, bf16[1024,256]{1,0:T(8,128)(2,1)S(1)}, u32[]{:S(2)}, u32[]{:S(2)}) collective-permute-start(bf16[1024,256]{1,0:T(8,128)(2,1)S(1)} %get-tuple-element.71), channel_id=1, source_target_pairs={{2,0},{6,4},{10,8},{14,12},{0,2},{4,6},{8,10},{12,14},{3,1},{7,5},... | collective-permute-start | bytes 1572872 | tf_op jit(solution)/shard_map/ppermute | solution.py:340
  61.2 1.3 %collective-permute-start.19 = (bf16[1024,256]{1,0:T(8,128)(2,1)S(1)}, bf16[1024,256]{1,0:T(8,128)(2,1)S(1)}, u32[]{:S(2)}, u32[]{:S(2)}) collective-permute-start(bf16[1024,256]{1,0:T(8,128)(2,1)S(1)} %get-tuple-element.58.refs_3_.odd_ref), channel_id=1, source_target_pairs={{4,0},{8,4},{12,8},{5,1},{9,5},{13,9},{20,16},{24,20},{28,24},{21,... | collective-permute-start | bytes 1572872 | tf_op jit(solution)/shard_map/ppermute | solution.py:340
  62.5 0.0 collective-permute-done.11.refs_2_.refs_4_
  62.5 0.7 collective-permute-start.9
  63.2 1.3 %shard_map.49 = (bf16[256,512]{1,0:T(8,128)(2,1)S(1)}, bf16[4,512,1024]{2,1,0:T(8,128)(2,1)}) custom-call(s32[3]{0:T(128)S(1)} %pad_add_fusion.place_ref.refs_0_, bf16[512,1024]{1,0:T(8,128)(2,1)S(1)} %collective-permute-done.2.refs_0_, bf16[1024,256]{1,0:T(8,128)(2,1)S(1)} %collective-permute-done.7.refs_0_.refs_1_.refs_3_, ...), custom_call_target="tpu_custom_call", output_to_operand_aliasing={{1}: (6, {})} | custom-call | flops 1000 | bytes 1000 | tf_op jit(solution)/shard_map/pallas_call | solution.py:223
  64.4 1.3 %collective-permute-start.17 = (bf16[256,512]{1,0:T(8,128)(2,1)S(1)}, bf16[256,512]{1,0:T(8,128)(2,1)S(1)}, u32[]{:S(2)}, u32[]{:S(2)}) collective-permute-start(bf16[256,512]{1,0:T(8,128)(2,1)S(1)} %get-tuple-element.68), channel_id=1, source_target_pairs={{4,0},{6,2},{8,4},{10,6},{12,8},{14,10},{5,1},{7,3},{9,5},{11,7},{... | collective-permute-start | bytes 786440 | tf_op jit(solution)/shard_map/ppermute | solution.py:340
  65.7 2.6 %shard_map.50.refs_6_ = bf16[4,512,1024]{2,1,0:T(8,128)(2,1)} custom-call(s32[3]{0:T(128)S(1)} %pad_add_fusion.place_ref.refs_0_, bf16[512,1024]{1,0:T(8,128)(2,1)S(1)} %get-tuple-element.48.refs_0_.refs_1_, bf16[512,1024]{1,0:T(8,128)(2,1)S(1)} %get-tuple-element.62.refs_2_, ...), custom_call_target="tpu_custom_call", output_to_operand_aliasing={{}: (7, {})} | custom-call | flops 1000 | bytes 1000 | tf_op jit(solution)/shard_map/pallas_call | solution.py:192
  68.3 2.7 %collective-permute-done.10.refs_0_.refs_1_ = bf16[512,1024]{1,0:T(8,128)(2,1)S(1)} collective-permute-done((bf16[512,1024]{1,0:T(8,128)(2,1)S(1)}, bf16[512,1024]{1,0:T(8,128)(2,1)S(1)}, u32[]{:S(2)}, u32[]{:S(2)}) %collective-permute-start.10) | collective-permute-done | bytes 1048608 | tf_op jit(solution)/shard_map/ppermute | solution.py:340
  71.0 11.7 %collective-permute-done.17.refs_5_.refs_3_ = bf16[256,512]{1,0:T(8,128)(2,1)S(1)} collective-permute-done((bf16[256,512]{1,0:T(8,128)(2,1)S(1)}, bf16[256,512]{1,0:T(8,128)(2,1)S(1)}, u32[]{:S(2)}, u32[]{:S(2)}) %collective-permute-start.17) | collective-permute-done | bytes 262176 | tf_op jit(solution)/shard_map/ppermute | solution.py:340
  82.7 0.5 shard_map.51
  83.3 0.6 shard_map.53
  83.9 0.1 collective-permute-start.24
  84.0 0.1 collective-permute-start.22
  84.1 13.2 %collective-permute-done.24.refs_2_.refs_5_ = bf16[1024,256]{1,0:T(8,128)(2,1)S(1)} collective-permute-done((bf16[1024,256]{1,0:T(8,128)(2,1)S(1)}, bf16[1024,256]{1,0:T(8,128)(2,1)S(1)}, u32[]{:S(2)}, u32[]{:S(2)}) %collective-permute-start.24) | collective-permute-done | bytes 524320 | tf_op jit(solution)/shard_map/ppermute | solution.py:340
  97.2 0.5 collective-permute-start.27
  97.8 0.7 collective-permute-start.18
  98.4 1.3 %shard_map.54 = (bf16[256,512]{1,0:T(8,128)(2,1)S(1)}, bf16[4,512,1024]{2,1,0:T(8,128)(2,1)}) custom-call(s32[3]{0:T(128)S(1)} %pad_add_fusion.place_ref.refs_0_, bf16[512,1024]{1,0:T(8,128)(2,1)S(1)} %collective-permute-done.10.refs_0_.refs_1_, ...), custom_call_target="tpu_custom_call", output_to_operand_aliasing={{1}: (6, {})} | custom-call | flops 1000 | bytes 1000 | tf_op jit(solution)/shard_map/pallas_call | solution.py:223
  99.7 1.3 %collective-permute-start.21 = (bf16[256,512]{1,0:T(8,128)(2,1)S(1)}, bf16[256,512]{1,0:T(8,128)(2,1)S(1)}, u32[]{:S(2)}, u32[]{:S(2)}) collective-permute-start(bf16[256,512]{1,0:T(8,128)(2,1)S(1)} %get-tuple-element.74), channel_id=1, source_target_pairs={{4,0},{6,2},{8,4},{10,6},{12,8},{14,10},{5,1},{7,3},{9,5},{11,7},{... | collective-permute-start | bytes 786440 | tf_op jit(solution)/shard_map/ppermute | solution.py:340
  101.0 0.1 collective-permute-start.28
  101.1 1.2 %shard_map.55 = (bf16[512,256]{1,0:T(8,128)(2,1)S(1)}, bf16[4,512,1024]{2,1,0:T(8,128)(2,1)}) custom-call(s32[3]{0:T(128)S(1)} %pad_add_fusion.place_ref.refs_0_, bf16[512,1024]{1,0:T(8,128)(2,1)S(1)} %collective-permute-done.2.refs_0_, bf16[512,1024]{1,0:T(8,128)(2,1)S(1)} %collective-permute-done.10.refs_0_.refs_1_, ...), custom_call_target="tpu_custom_call", output_to_operand_aliasing={{1}: (6, {})} | custom-call | flops 1000 | bytes 1000 | tf_op jit(solution)/shard_map/pallas_call | solution.py:223
  102.3 1.5 %collective-permute-start.23 = (bf16[512,256]{1,0:T(8,128)(2,1)S(1)}, bf16[512,256]{1,0:T(8,128)(2,1)S(1)}, u32[]{:S(2)}, u32[]{:S(2)}) collective-permute-start(bf16[512,256]{1,0:T(8,128)(2,1)S(1)} %get-tuple-element.76), channel_id=1, source_target_pairs={{4,0},{6,2},{8,4},{10,6},{12,8},{14,10},{5,1},{7,3},{9,5},{11,7},{... | collective-permute-start | bytes 786440 | tf_op jit(solution)/shard_map/ppermute | solution.py:340
  103.8 6.9 %collective-permute-done.21.refs_4_ = bf16[256,512]{1,0:T(8,128)(2,1)S(1)} collective-permute-done((bf16[256,512]{1,0:T(8,128)(2,1)S(1)}, bf16[256,512]{1,0:T(8,128)(2,1)S(1)}, u32[]{:S(2)}, u32[]{:S(2)}) %collective-permute-start.21) | collective-permute-done | bytes 262176 | tf_op jit(solution)/shard_map/ppermute | solution.py:340
  110.8 1.2 %shard_map.56 = (bf16[512,256]{1,0:T(8,128)(2,1)S(1)}, bf16[4,512,1024]{2,1,0:T(8,128)(2,1)}) custom-call(s32[3]{0:T(128)S(1)} %pad_add_fusion.place_ref.refs_0_, bf16[512,1024]{1,0:T(8,128)(2,1)S(1)} %collective-permute-done.2.refs_0_, bf16[512,1024]{1,0:T(8,128)(2,1)S(1)} %collective-permute-done.10.refs_0_.refs_1_, ...), custom_call_target="tpu_custom_call", output_to_operand_aliasing={{1}: (6, {})} | custom-call | flops 1000 | bytes 1000 | tf_op jit(solution)/shard_map/pallas_call | solution.py:223
  112.0 1.3 %collective-permute-start.26 = (bf16[512,256]{1,0:T(8,128)(2,1)S(1)}, bf16[512,256]{1,0:T(8,128)(2,1)S(1)}, u32[]{:S(2)}, u32[]{:S(2)}) collective-permute-start(bf16[512,256]{1,0:T(8,128)(2,1)S(1)} %get-tuple-element.79), channel_id=1, source_target_pairs={{4,0},{6,2},{8,4},{10,6},{12,8},{14,10},{5,1},{7,3},{9,5},{11,7},{... | collective-permute-start | bytes 786440 | tf_op jit(solution)/shard_map/ppermute | solution.py:340
  113.3 2.6 %shard_map.57.refs_7_ = bf16[4,512,1024]{2,1,0:T(8,128)(2,1)} custom-call(s32[3]{0:T(128)S(1)} %pad_add_fusion.place_ref.refs_0_, bf16[512,1024]{1,0:T(8,128)(2,1)S(1)} %get-tuple-element.48.refs_0_.refs_1_, bf16[512,1024]{1,0:T(8,128)(2,1)S(1)} %get-tuple-element.62.refs_2_, ...), custom_call_target="tpu_custom_call", output_to_operand_aliasing={{}: (7, {})} | custom-call | flops 1000 | bytes 1000 | tf_op jit(solution)/shard_map/pallas_call | solution.py:192
  115.9 2.6 %shard_map.58.refs_7_ = bf16[4,512,1024]{2,1,0:T(8,128)(2,1)} custom-call(s32[3]{0:T(128)S(1)} %pad_add_fusion.place_ref.refs_0_, bf16[512,1024]{1,0:T(8,128)(2,1)S(1)} %get-tuple-element.48.refs_0_.refs_1_, bf16[512,1024]{1,0:T(8,128)(2,1)S(1)} %get-tuple-element.62.refs_2_, ...), custom_call_target="tpu_custom_call", output_to_operand_aliasing={{}: (7, {})} | custom-call | flops 1000 | bytes 1000 | tf_op jit(solution)/shard_map/pallas_call | solution.py:192
  118.5 2.5 %collective-permute-done.26.refs_6_ = bf16[512,256]{1,0:T(8,128)(2,1)S(1)} collective-permute-done((bf16[512,256]{1,0:T(8,128)(2,1)S(1)}, bf16[512,256]{1,0:T(8,128)(2,1)S(1)}, u32[]{:S(2)}, u32[]{:S(2)}) %collective-permute-start.26) | collective-permute-done | bytes 262176 | tf_op jit(solution)/shard_map/ppermute | solution.py:340
  121.0 1.6 %shard_map.59 = bf16[4,512,1024]{2,1,0:T(8,128)(2,1)} custom-call(s32[3]{0:T(128)S(1)} %pad_add_fusion.place_ref.refs_0_, bf16[256,512]{1,0:T(8,128)(2,1)S(1)} %collective-permute-done.9.refs_8_.refs_1_, bf16[256,512]{1,0:T(8,128)(2,1)S(1)} %collective-permute-done.18.refs_4_.refs_2_, ...), custom_call_target="tpu_custom_call", output_to_operand_aliasing={{}: (7, {})} | custom-call | flops 1000 | bytes 1000 | tf_op jit(solution)/shard_map/pallas_call | solution.py:311
  (18 shorter events, 0.0 us)
Async XLA Ops:
  3.1 1.4 %collective-permute-start = (f32[8,1024]{1,0:T(8,128)S(1)}, f32[8,1024]{1,0:T(8,128)S(1)}, u32[]{:S(2)}, u32[]{:S(2)}) collective-permute-start(f32[8,1024]{1,0:T(8,128)S(1)} %get-tuple-element.45.sums_ref), channel_id=1, source_target_pairs={{0,1},{1,0},{2,3},{3,2},{4,5},{5,4},{6,7},{7,6},{8,9},{9,8},{10,11... | collective-permute-start | bytes 98312 | tf_op jit(solution)/shard_map/ppermute | solution.py:350
  6.2 10.8 %collective-permute-start.4 = (bf16[1024,1024]{1,0:T(8,128)(2,1)S(1)}, bf16[1024,1024]{1,0:T(8,128)(2,1)S(1)}, u32[]{:S(2)}, u32[]{:S(2)}) collective-permute-start(bf16[1024,1024]{1,0:T(8,128)(2,1)S(1)} %get-tuple-element.52.refs_2_), channel_id=1, source_target_pairs={{0,1},{1,0},{2,3},{3,2},{4,5},{5,4},{6,7},{7,6},{8,9},{9,8},{10,11... | collective-permute-start | bytes 6291464 | tf_op jit(solution)/shard_map/ppermute | solution.py:350
  6.6 5.3 %collective-permute-start.1 = (bf16[512,1024]{1,0:T(8,128)(2,1)S(1)}, bf16[512,1024]{1,0:T(8,128)(2,1)S(1)}, u32[]{:S(2)}, u32[]{:S(2)}) collective-permute-start(bf16[512,1024]{1,0:T(8,128)(2,1)S(1)} %get-tuple-element.47), channel_id=1, source_target_pairs={{0,1},{1,0},{2,3},{3,2},{4,5},{5,4},{6,7},{7,6},{8,9},{9,8},{10,11... | collective-permute-start | bytes 3145736 | tf_op jit(solution)/shard_map/ppermute | solution.py:350
  6.8 17.1 %collective-permute-start.3 = (bf16[1024,256]{1,0:T(8,128)(2,1)S(1)}, bf16[1024,256]{1,0:T(8,128)(2,1)S(1)}, u32[]{:S(2)}, u32[]{:S(2)}) collective-permute-start(bf16[1024,256]{1,0:T(8,128)(2,1)S(1)} %get-tuple-element.49.odd_ref), channel_id=1, source_target_pairs={{4,0},{6,2},{8,4},{10,6},{12,8},{14,10},{5,1},{7,3},{9,5},{11,7},{... | collective-permute-start | bytes 1572872 | tf_op jit(solution)/shard_map/ppermute | solution.py:340
  12.1 30.3 %collective-permute-start.2 = (bf16[512,1024]{1,0:T(8,128)(2,1)S(1)}, bf16[512,1024]{1,0:T(8,128)(2,1)S(1)}, u32[]{:S(2)}, u32[]{:S(2)}) collective-permute-start(bf16[512,1024]{1,0:T(8,128)(2,1)S(1)} %get-tuple-element.48.refs_0_.refs_1_), channel_id=1, source_target_pairs={{0,4},{2,6},{4,8},{6,10},{8,12},{10,14},{1,5},{3,7},{5,9},{7,11},{... | collective-permute-start | bytes 3145736 | tf_op jit(solution)/shard_map/ppermute | solution.py:340
  24.5 13.6 %collective-permute-start.7 = (bf16[1024,256]{1,0:T(8,128)(2,1)S(1)}, bf16[1024,256]{1,0:T(8,128)(2,1)S(1)}, u32[]{:S(2)}, u32[]{:S(2)}) collective-permute-start(bf16[1024,256]{1,0:T(8,128)(2,1)S(1)} %get-tuple-element.56), channel_id=1, source_target_pairs={{2,0},{6,4},{10,8},{14,12},{0,2},{4,6},{8,10},{12,14},{3,1},{7,5},... | collective-permute-start | bytes 1572872 | tf_op jit(solution)/shard_map/ppermute | solution.py:340
  26.2 14.8 %collective-permute-start.6 = (bf16[1024,256]{1,0:T(8,128)(2,1)S(1)}, bf16[1024,256]{1,0:T(8,128)(2,1)S(1)}, u32[]{:S(2)}, u32[]{:S(2)}) collective-permute-start(bf16[1024,256]{1,0:T(8,128)(2,1)S(1)} %get-tuple-element.54.odd_ref), channel_id=1, source_target_pairs={{4,0},{6,2},{8,4},{10,6},{12,8},{14,10},{5,1},{7,3},{9,5},{11,7},{... | collective-permute-start | bytes 1572872 | tf_op jit(solution)/shard_map/ppermute | solution.py:340
  27.5 15.1 %collective-permute-start.5 = (bf16[1024,256]{1,0:T(8,128)(2,1)S(1)}, bf16[1024,256]{1,0:T(8,128)(2,1)S(1)}, u32[]{:S(2)}, u32[]{:S(2)}) collective-permute-start(bf16[1024,256]{1,0:T(8,128)(2,1)S(1)} %get-tuple-element.53.refs_1_.odd_ref), channel_id=1, source_target_pairs={{0,1},{1,0},{2,3},{3,2},{4,5},{5,4},{6,7},{7,6},{8,9},{9,8},{10,11... | collective-permute-start | bytes 1572872 | tf_op jit(solution)/shard_map/ppermute | solution.py:350
  27.6 16.3 %collective-permute-start.15 = (bf16[1024,256]{1,0:T(8,128)(2,1)S(1)}, bf16[1024,256]{1,0:T(8,128)(2,1)S(1)}, u32[]{:S(2)}, u32[]{:S(2)}) collective-permute-start(bf16[1024,256]{1,0:T(8,128)(2,1)S(1)} %get-tuple-element.64.refs_3_), channel_id=1, source_target_pairs={{0,1},{1,0},{2,3},{3,2},{4,5},{5,4},{6,7},{7,6},{8,9},{9,8},{10,11... | collective-permute-start | bytes 1572872 | tf_op jit(solution)/shard_map/ppermute | solution.py:350
  41.6 6.9 %collective-permute-start.8 = (bf16[1024,256]{1,0:T(8,128)(2,1)S(1)}, bf16[1024,256]{1,0:T(8,128)(2,1)S(1)}, u32[]{:S(2)}, u32[]{:S(2)}) collective-permute-start(bf16[1024,256]{1,0:T(8,128)(2,1)S(1)} %get-tuple-element.58.refs_3_.odd_ref), channel_id=1, source_target_pairs={{0,1},{1,0},{2,3},{3,2},{4,5},{5,4},{6,7},{7,6},{8,9},{9,8},{10,11... | collective-permute-start | bytes 1572872 | tf_op jit(solution)/shard_map/ppermute | solution.py:350
  41.6 14.3 %collective-permute-start.12 = (bf16[1024,256]{1,0:T(8,128)(2,1)S(1)}, bf16[1024,256]{1,0:T(8,128)(2,1)S(1)}, u32[]{:S(2)}, u32[]{:S(2)}) collective-permute-start(bf16[1024,256]{1,0:T(8,128)(2,1)S(1)} %get-tuple-element.63), channel_id=1, source_target_pairs={{2,0},{6,4},{10,8},{14,12},{0,2},{4,6},{8,10},{12,14},{3,1},{7,5},... | collective-permute-start | bytes 1572872 | tf_op jit(solution)/shard_map/ppermute | solution.py:340
  42.4 14.2 %collective-permute-start.16 = (bf16[1024,256]{1,0:T(8,128)(2,1)S(1)}, bf16[1024,256]{1,0:T(8,128)(2,1)S(1)}, u32[]{:S(2)}, u32[]{:S(2)}) collective-permute-start(bf16[1024,256]{1,0:T(8,128)(2,1)S(1)} %get-tuple-element.65.refs_5_), channel_id=1, source_target_pairs={{0,1},{1,0},{2,3},{3,2},{4,5},{5,4},{6,7},{7,6},{8,9},{9,8},{10,11... | collective-permute-start | bytes 1572872 | tf_op jit(solution)/shard_map/ppermute | solution.py:350
  42.5 16.6 %collective-permute-start.14 = (bf16[1024,256]{1,0:T(8,128)(2,1)S(1)}, bf16[1024,256]{1,0:T(8,128)(2,1)S(1)}, u32[]{:S(2)}, u32[]{:S(2)}) collective-permute-start(bf16[1024,256]{1,0:T(8,128)(2,1)S(1)} %get-tuple-element.53.refs_1_.odd_ref), channel_id=1, source_target_pairs={{4,0},{8,4},{12,8},{5,1},{9,5},{13,9},{20,16},{24,20},{28,24},{21,... | collective-permute-start | bytes 1572872 | tf_op jit(solution)/shard_map/ppermute | solution.py:340
  43.8 27.2 %collective-permute-start.10 = (bf16[512,1024]{1,0:T(8,128)(2,1)S(1)}, bf16[512,1024]{1,0:T(8,128)(2,1)S(1)}, u32[]{:S(2)}, u32[]{:S(2)}) collective-permute-start(bf16[512,1024]{1,0:T(8,128)(2,1)S(1)} %get-tuple-element.62.refs_2_), channel_id=1, source_target_pairs={{0,4},{2,6},{4,8},{6,10},{8,12},{10,14},{1,5},{3,7},{5,9},{7,11},{... | collective-permute-start | bytes 3145736 | tf_op jit(solution)/shard_map/ppermute | solution.py:340
  48.5 14.0 %collective-permute-start.11 = (bf16[1024,256]{1,0:T(8,128)(2,1)S(1)}, bf16[1024,256]{1,0:T(8,128)(2,1)S(1)}, u32[]{:S(2)}, u32[]{:S(2)}) collective-permute-start(bf16[1024,256]{1,0:T(8,128)(2,1)S(1)} %collective-permute-done.7.refs_0_.refs_1_.refs_3_), channel_id=1, source_target_pairs={{0,1},{1,0},{2,3},{3,2},{4,5},{5,4},{6,7},{7,6},{8,9},{9,8},{10,11... | collective-permute-start | bytes 1572872 | tf_op jit(solution)/shard_map/ppermute | solution.py:350
  56.0 7.2 %collective-permute-start.13 = (bf16[1024,256]{1,0:T(8,128)(2,1)S(1)}, bf16[1024,256]{1,0:T(8,128)(2,1)S(1)}, u32[]{:S(2)}, u32[]{:S(2)}) collective-permute-start(bf16[1024,256]{1,0:T(8,128)(2,1)S(1)} %collective-permute-done.12.refs_0_.refs_3_.refs_5_), channel_id=1, source_target_pairs={{0,1},{1,0},{2,3},{3,2},{4,5},{5,4},{6,7},{7,6},{8,9},{9,8},{10,11... | collective-permute-start | bytes 1572872 | tf_op jit(solution)/shard_map/ppermute | solution.py:350
  59.7 23.6 %collective-permute-start.20 = (bf16[1024,256]{1,0:T(8,128)(2,1)S(1)}, bf16[1024,256]{1,0:T(8,128)(2,1)S(1)}, u32[]{:S(2)}, u32[]{:S(2)}) collective-permute-start(bf16[1024,256]{1,0:T(8,128)(2,1)S(1)} %get-tuple-element.71), channel_id=1, source_target_pairs={{2,0},{6,4},{10,8},{14,12},{0,2},{4,6},{8,10},{12,14},{3,1},{7,5},... | collective-permute-start | bytes 1572872 | tf_op jit(solution)/shard_map/ppermute | solution.py:340
  61.2 22.1 %collective-permute-start.19 = (bf16[1024,256]{1,0:T(8,128)(2,1)S(1)}, bf16[1024,256]{1,0:T(8,128)(2,1)S(1)}, u32[]{:S(2)}, u32[]{:S(2)}) collective-permute-start(bf16[1024,256]{1,0:T(8,128)(2,1)S(1)} %get-tuple-element.58.refs_3_.odd_ref), channel_id=1, source_target_pairs={{4,0},{8,4},{12,8},{5,1},{9,5},{13,9},{20,16},{24,20},{28,24},{21,... | collective-permute-start | bytes 1572872 | tf_op jit(solution)/shard_map/ppermute | solution.py:340
  62.5 3.3 %collective-permute-start.9 = (bf16[256,512]{1,0:T(8,128)(2,1)S(1)}, bf16[256,512]{1,0:T(8,128)(2,1)S(1)}, u32[]{:S(2)}, u32[]{:S(2)}) collective-permute-start(bf16[256,512]{1,0:T(8,128)(2,1)S(1)} %get-tuple-element.61), channel_id=1, source_target_pairs={{6,2},{10,6},{14,10},{7,3},{11,7},{15,11},{22,18},{26,22},{30,26},... | collective-permute-start | bytes 786440 | tf_op jit(solution)/shard_map/ppermute | solution.py:340
  64.4 18.3 %collective-permute-start.17 = (bf16[256,512]{1,0:T(8,128)(2,1)S(1)}, bf16[256,512]{1,0:T(8,128)(2,1)S(1)}, u32[]{:S(2)}, u32[]{:S(2)}) collective-permute-start(bf16[256,512]{1,0:T(8,128)(2,1)S(1)} %get-tuple-element.68), channel_id=1, source_target_pairs={{4,0},{6,2},{8,4},{10,6},{12,8},{14,10},{5,1},{7,3},{9,5},{11,7},{... | collective-permute-start | bytes 786440 | tf_op jit(solution)/shard_map/ppermute | solution.py:340
  83.9 13.3 %collective-permute-start.24 = (bf16[1024,256]{1,0:T(8,128)(2,1)S(1)}, bf16[1024,256]{1,0:T(8,128)(2,1)S(1)}, u32[]{:S(2)}, u32[]{:S(2)}) collective-permute-start(bf16[1024,256]{1,0:T(8,128)(2,1)S(1)} %get-tuple-element.77), channel_id=1, source_target_pairs={{2,0},{6,4},{10,8},{14,12},{0,2},{4,6},{8,10},{12,14},{3,1},{7,5},... | collective-permute-start | bytes 1572872 | tf_op jit(solution)/shard_map/ppermute | solution.py:340
  84.0 17.0 %collective-permute-start.22 = (bf16[1024,256]{1,0:T(8,128)(2,1)S(1)}, bf16[1024,256]{1,0:T(8,128)(2,1)S(1)}, u32[]{:S(2)}, u32[]{:S(2)}) collective-permute-start(bf16[1024,256]{1,0:T(8,128)(2,1)S(1)} %collective-permute-done.20.refs_0_.refs_2_.refs_3_), channel_id=1, source_target_pairs={{0,1},{1,0},{2,3},{3,2},{4,5},{5,4},{6,7},{7,6},{8,9},{9,8},{10,11... | collective-permute-start | bytes 1572872 | tf_op jit(solution)/shard_map/ppermute | solution.py:350
  97.2 13.5 %collective-permute-start.25 = (bf16[1024,256]{1,0:T(8,128)(2,1)S(1)}, bf16[1024,256]{1,0:T(8,128)(2,1)S(1)}, u32[]{:S(2)}, u32[]{:S(2)}) collective-permute-start(bf16[1024,256]{1,0:T(8,128)(2,1)S(1)} %collective-permute-done.24.refs_2_.refs_5_), channel_id=1, source_target_pairs={{0,1},{1,0},{2,3},{3,2},{4,5},{5,4},{6,7},{7,6},{8,9},{9,8},{10,11... | collective-permute-start | bytes 1572872 | tf_op jit(solution)/shard_map/ppermute | solution.py:350
  97.2 16.1 %collective-permute-start.27 = (bf16[1024,256]{1,0:T(8,128)(2,1)S(1)}, bf16[1024,256]{1,0:T(8,128)(2,1)S(1)}, u32[]{:S(2)}, u32[]{:S(2)}) collective-permute-start(bf16[1024,256]{1,0:T(8,128)(2,1)S(1)} %get-tuple-element.80.refs_3_), channel_id=1, source_target_pairs={{0,1},{1,0},{2,3},{3,2},{4,5},{5,4},{6,7},{7,6},{8,9},{9,8},{10,11... | collective-permute-start | bytes 1572872 | tf_op jit(solution)/shard_map/ppermute | solution.py:350
  97.8 3.3 %collective-permute-start.18 = (bf16[256,512]{1,0:T(8,128)(2,1)S(1)}, bf16[256,512]{1,0:T(8,128)(2,1)S(1)}, u32[]{:S(2)}, u32[]{:S(2)}) collective-permute-start(bf16[256,512]{1,0:T(8,128)(2,1)S(1)} %get-tuple-element.70), channel_id=1, source_target_pairs={{6,2},{10,6},{14,10},{7,3},{11,7},{15,11},{22,18},{26,22},{30,26},... | collective-permute-start | bytes 786440 | tf_op jit(solution)/shard_map/ppermute | solution.py:340
  99.7 11.1 %collective-permute-start.21 = (bf16[256,512]{1,0:T(8,128)(2,1)S(1)}, bf16[256,512]{1,0:T(8,128)(2,1)S(1)}, u32[]{:S(2)}, u32[]{:S(2)}) collective-permute-start(bf16[256,512]{1,0:T(8,128)(2,1)S(1)} %get-tuple-element.74), channel_id=1, source_target_pairs={{4,0},{6,2},{8,4},{10,6},{12,8},{14,10},{5,1},{7,3},{9,5},{11,7},{... | collective-permute-start | bytes 786440 | tf_op jit(solution)/shard_map/ppermute | solution.py:340
  101.0 12.3 %collective-permute-start.28 = (bf16[1024,256]{1,0:T(8,128)(2,1)S(1)}, bf16[1024,256]{1,0:T(8,128)(2,1)S(1)}, u32[]{:S(2)}, u32[]{:S(2)}) collective-permute-start(bf16[1024,256]{1,0:T(8,128)(2,1)S(1)} %get-tuple-element.81.refs_5_), channel_id=1, source_target_pairs={{0,1},{1,0},{2,3},{3,2},{4,5},{5,4},{6,7},{7,6},{8,9},{9,8},{10,11... | collective-permute-start | bytes 1572872 | tf_op jit(solution)/shard_map/ppermute | solution.py:350
  102.3 16.2 %collective-permute-start.23 = (bf16[512,256]{1,0:T(8,128)(2,1)S(1)}, bf16[512,256]{1,0:T(8,128)(2,1)S(1)}, u32[]{:S(2)}, u32[]{:S(2)}) collective-permute-start(bf16[512,256]{1,0:T(8,128)(2,1)S(1)} %get-tuple-element.76), channel_id=1, source_target_pairs={{4,0},{6,2},{8,4},{10,6},{12,8},{14,10},{5,1},{7,3},{9,5},{11,7},{... | collective-permute-start | bytes 786440 | tf_op jit(solution)/shard_map/ppermute | solution.py:340
  112.0 9.0 %collective-permute-start.26 = (bf16[512,256]{1,0:T(8,128)(2,1)S(1)}, bf16[512,256]{1,0:T(8,128)(2,1)S(1)}, u32[]{:S(2)}, u32[]{:S(2)}) collective-permute-start(bf16[512,256]{1,0:T(8,128)(2,1)S(1)} %get-tuple-element.79), channel_id=1, source_target_pairs={{4,0},{6,2},{8,4},{10,6},{12,8},{14,10},{5,1},{7,3},{9,5},{11,7},{... | collective-permute-start | bytes 786440 | tf_op jit(solution)/shard_map/ppermute | solution.py:340

commit v4 on v3

--- a/solution.py
+++ b/solution.py
@@ -123,33 +123,36 @@
     )(place, masked, sums, sums_other)
 
 
-def stack_kernel(here_ref, arrived_ref, *outs):
+def stack_kernel(here_ref, arrived_ref, whole_ref, *outs):
     part = outs[0].shape[0] // 2
     for r in range(PARTS):
         outs[r][0:part, :] = here_ref[r * part : (r + 1) * part, :]
         outs[r][part:, :] = arrived_ref[r * part : (r + 1) * part, :]
 
 
-def stack(here, arrived):
+def stack(here, arrived, whole):
     count, samples = here.shape
     return pl.pallas_call(
         stack_kernel,
-        in_specs=[VMEM, VMEM],
-        out_specs=[VMEM] * PARTS,
-        out_shape=[jax.ShapeDtypeStruct((2 * count // PARTS, samples), here.dtype)] * PARTS,
-        compiler_params=PARAMS,
-        cost_estimate=COST,
-    )(here, arrived)
-
-
-def blocks(rows, rights, scale):
+        in_specs=[VMEM, VMEM, ANY],
+        out_specs=[VMEM] * PARTS + [ANY],
+        out_shape=[jax.ShapeDtypeStruct((2 * count // PARTS, samples), here.dtype)] * PARTS
+        + [jax.ShapeDtypeStruct(whole.shape, whole.dtype)],
+        input_output_aliases={2: PARTS},
+        compiler_params=PARAMS,
+        cost_estimate=COST,
+    )(here, arrived, whole)
+
+
+def blocks(rows, rights, scale, skip=0):
     part = rows[0].shape[0] // 2
-    piece = min(right.shape[1] for right in rights)
     at = 0
     for q in range(len(rights) // 2):
         mine, other = rights[2 * q], rights[2 * q + 1]
         width = mine.shape[1]
-        for begin in range(0, width, 256):
+        start = skip if q == len(rights) // 2 - 1 else 0
+        at -= start
+        for begin in range(start, width, 256):
             end = min(begin + 256, width)
             for r, row in enumerate(rows):
                 total = jnp.dot(
@@ -201,11 +204,11 @@
     )(*operands)
 
 
-def far_kernel(only_odd, scale, parts, pieces, place_ref, *refs):
+def far_kernel(only_odd, scale, parts, pieces, skip, place_ref, *refs):
     out_ref = refs[-2]
 
     def work():
-        for at, columns, block in blocks(refs[:parts], refs[parts : parts + pieces], scale):
+        for at, columns, block in blocks(refs[:parts], refs[parts : parts + pieces], scale, skip):
             out_ref[at, columns] = block.astype(out_ref.dtype)
 
     if only_odd:
@@ -214,14 +217,14 @@
         work()
 
 
-def far(place, buffer, rows, rights, samples, only_odd=False, after=()):
+def far(place, buffer, rows, rights, samples, only_odd=False, after=(), skip=0):
     shape = (
         rows[0].shape[0] // 2 * len(rows),
-        sum(right.shape[1] for right in rights) // 2,
+        sum(right.shape[1] for right in rights) // 2 - skip,
     )
     operands = [place, *rows, *rights, *after, buffer]
     return pl.pallas_call(
-        functools.partial(far_kernel, only_odd, 1.0 / samples, len(rows), len(rights)),
+        functools.partial(far_kernel, only_odd, 1.0 / samples, len(rows), len(rights), skip),
         in_specs=[SMEM] + [VMEM] * (len(rows) + len(rights)) + [ANY] * (len(after) + 1),
         out_specs=[VMEM, ANY],
         out_shape=[
@@ -274,34 +277,29 @@
     )(*after, *passed)
 
 
-def last_kernel(place_ref, low_a, low_b, top, bottom, third, fourth, out_ref, two, three, sems):
+def last_kernel(place_ref, top2, top3, bottom, side, out_ref, two, three, sems):
     keep2, keep3 = 2 < place_ref[2], 3 < place_ref[2]
-    part, half = top.shape
-    quarter = half // 2
-
-    def kept(keep, ref):
-        return jnp.where(keep, ref[...], 0.0).astype(out_ref.dtype)
-
-    three[0:part, 0:half] = kept(keep3, top)
-    three[part:, 0:half] = kept(keep3, bottom)
-    three[:, half : half + quarter] = kept(keep3, third)
-    three[:, half + quarter :] = kept(keep3, fourth)
-    copy3 = pltpu.make_async_copy(three, out_ref.at[3], sems.at[0])
+    part, half = top2.shape
+    wide = top3.shape[1]
+
+    def kept(keep, block):
+        return jnp.where(keep, block, 0.0).astype(out_ref.dtype)
+
+    two[0:part, :] = kept(keep2, top2[...])
+    two[part:, :] = kept(keep2, bottom[:, wide:])
+    copy2 = pltpu.make_async_copy(two, out_ref.at[2, :, half:], sems.at[0])
+    copy2.start()
+    three[0:part, 0:wide] = kept(keep3, top3[...])
+    three[part:, 0:wide] = kept(keep3, bottom[:, 0:wide])
+    three[:, wide:] = kept(keep3, side[...])
+    copy3 = pltpu.make_async_copy(three, out_ref.at[3], sems.at[1])
     copy3.start()
-
-    @pl.when(place_ref[0] == 1)
-    def _():
-        two[0:part, :] = kept(keep2, low_a)
-        two[part:, :] = kept(keep2, low_b)
-        copy2 = pltpu.make_async_copy(two, out_ref.at[2, :, half:], sems.at[1])
-        copy2.start()
-        copy2.wait()
-
+    copy2.wait()
     copy3.wait()
 
 
-def last(place, buffer, back2, back3):
-    operands = [place, *back2, *back3, buffer]
+def last(place, buffer, *received):
+    operands = [place, *received, buffer]
     count, width = buffer.shape[1:]
 
     def kernel(*refs):
@@ -339,9 +337,9 @@
     def send(shard, pairs):
         return lax.ppermute(shard, "var", pairs)
 
+    before = [(i + 1, i) for i in range(places - 1)]
     up = [(i, i + 2) for i in range(places - 2)]
     down = [(i + 2, i) for i in range(places - 2)]
-    down_even = [pair for pair in down if pair[0] % 2 == 0]
     down_odd = [pair for pair in down if pair[0] % 2 == 1]
     to_even = [(i + 1, i) for i in range(0, places - 1, 2)]
     swap = to_even + [(i, i + 1) for i in range(0, places - 1, 2)]
@@ -352,72 +350,52 @@
     sums, masked = stats(dosage, observed)
     *own, whole, here, away = score(place, masked, sums, mate(sums))
     above = [None] * QUARTERS
+    next_one, other = [None] * QUARTERS, [None] * QUARTERS
+
     above[0] = send(own[0], down)
+    across = send(own[2], swap)
+    *rows, whole = stack(here, mate(away), whole)
+    below = [send(rows[0], up), send(rows[1], up)]
+    whole_other = mate(whole)
+    buffer = tile(place, None, 0, 0, rows, [whole, whole_other], samples, width)
+
+    above[0], own[1], buffer, swapped = choose(place, own[0], above[0], own[1], buffer)
+    next_one[0] = send(swapped, swap)
     above[1] = send(own[1], down)
-    rows = stack(here, mate(away))
-    below = [send(rows[0], up), None]
-    whole_other = mate(whole)
-    next_one, other = [None] * QUARTERS, [None] * QUARTERS
-    back2, back3 = [None] * 2, [None] * 4
-
-    buffer = tile(place, None, 0, 0, rows, [whole, whole_other], samples, width)
-
-    above[0], own[2], buffer, swapped = choose(place, own[0], above[0], own[2], buffer)
-    next_one[0] = send(swapped, swap)
-    above[2] = send(own[2], down_even)
-
-    (buffer,) = hold((next_one[0],), buffer)
+
+    across, buffer = hold((next_one[0], below[0]), across, buffer)
     above[1], own[3], buffer, swapped = choose(place, own[1], above[1], own[3], buffer)
     next_one[1] = send(swapped, swap)
-    above[3] = send(own[3], down_even)
-    row, buffer = hold((below[0],), rows[1], buffer)
-    rows = [rows[0], row]
-    below[1] = send(rows[1], up)
-    own_upper = [own[2], mate(own[2]), own[3], mate(own[3])]
-    made, buffer = far(place, buffer, below[:1], own_upper, samples, True)
-    back2[0] = send(made, down_odd)
-    other[0] = mate(next_one[0])
+    around = send(across, down_odd)
+    next_one[3] = send(own[3], before)
+    made, buffer = far(place, buffer, below[:1], [whole, whole_other], samples, False, (), width // 2)
+    top2 = send(made, down)
+
+    (buffer,) = hold((next_one[1], top2), buffer)
+    across, buffer, next_one[2] = choose(place, around, across, buffer)
+    other[:3] = [mate(piece) for piece in next_one[:3]]
+    low = [next_one[0], other[0], next_one[1], other[1]]
+    high = [next_one[2], other[2]]
+    made, buffer = far(place, buffer, below[:1], low + high, samples)
+    top3 = send(made, down)
+    (buffer,) = hold((below[1],), buffer)
+    made, buffer = far(
+        place, buffer, below[1:], low + high + [whole, whole_other], samples, False, (), width // 2
+    )
+    bottom = send(made, down)
+    (next_one[3],) = hold((made, top3), next_one[3])
+    buffer = tile(place, buffer, 1, 0, rows, low, samples, width)
+    other[3] = mate(next_one[3])
+    made, buffer = far(
+        place, buffer, below, [next_one[3], other[3]], samples
+    )
+    side = send(made, down)
     buffer = tile(
         place, buffer, 2, 0, rows, [above[0], mate(above[0]), above[1], mate(above[1])],
         samples, width,
     )
-
-    (buffer,) = hold((next_one[1],), buffer)
-    above[2], buffer, swapped = choose(place, own[2], above[2], buffer)
-    next_one[2] = send(swapped, swap)
-    other[1] = mate(next_one[1])
-    low = [next_one[0], other[0], next_one[1], other[1]]
-    made, buffer = far(place, buffer, below[:1], low, samples)
-    back3[0] = send(made, down)
-    buffer = tile(place, buffer, 1, 0, rows, low, samples, width, (back2[0],))
-
-    made, buffer = far(place, buffer, below[1:], own_upper, samples, True, (back3[0],))
-    back2[1] = send(made, down_odd)
-
-    (buffer,) = hold((next_one[2],), buffer)
-    above[3], buffer, swapped = choose(place, own[3], above[3], buffer)
-    next_one[3] = send(swapped, swap)
-    made, buffer = far(place, buffer, below[1:], low, samples)
-    back3[1] = send(made, down)
-    other[2] = mate(next_one[2])
-    made, buffer = far(
-        place, buffer, below, [next_one[2], other[2]], samples, False, (back2[1],)
-    )
-    back3[2] = send(made, down)
-
-    other[3] = mate(next_one[3])
-    made, buffer = far(
-        place, buffer, below, [next_one[3], other[3]], samples, False, (back3[1],)
-    )
-    back3[3] = send(made, down)
-    buffer = tile(
-        place, buffer, 2, 1, rows, [above[2], mate(above[2]), above[3], mate(above[3])],
-        samples, width,
-    )
-    buffer = tile(
-        place, buffer, 1, 1, rows, [next_one[2], other[2], next_one[3], other[3]], samples, width
-    )
-    buffer = last(place, buffer, back2, back3)
+    buffer = tile(place, buffer, 1, 1, rows, high + [next_one[3], other[3]], samples, width)
+    buffer = last(place, buffer, top2, top3, bottom, side)
     return buffer[None]
 
 

time: 124 us -> 117 us (0.944); the launches traced: 123 us -> 117 us
  Pallas kernels: 29.3 us -> 26.2 us
    pallas_call x5 -> x4, Pallas kernels: 14.3 us -> 11.6 us  [tile(): pl.pallas_call(kernel, grid=(1,), in_specs=specs, out_specs=pl.BlockSpec(...]
    ppermute x13 -> x9, waiting for transfers between devices: 4.02 us -> 2.68 us  [mate(): return lax.ppermute(shard, 'samp', [(0, 1), (1, 0)])]
    ppermute x16 -> x13, starting transfers between devices: 25.3 us -> 24.1 us  [send(): return lax.ppermute(shard, 'var', pairs)]
    ppermute x16 -> x13, waiting for transfers between devices: 60.3 us -> 60.5 us  [send(): return lax.ppermute(shard, 'var', pairs)]
    ppermute x13 -> x9, starting transfers between devices: 2.62 us -> 2.64 us  [mate(): return lax.ppermute(shard, 'samp', [(0, 1), (1, 0)])]
    pallas_call x6 -> x4, Pallas kernels: 6.09 us -> 6.09 us  [far(): pl.pallas_call(functools.partial(far_kernel, only_odd, 1.0 / samples, len...]
  transfers between devices with their start and end apart: 29 -> 22, of which waited for: 11 -> 14; matrix products, arithmetic and copies ran while one was open for 0% -> 0% of each run, Pallas kernels for 18% -> 16%
where the time goes in v4:
time: 117 us
  waiting for transfers between devices  63.2 us (54%)
  starting transfers between devices  26.8 us (23%)
  Pallas kernels  26.2 us (22%)
    ppermute x13, waiting for transfers between devices, send(): return lax.ppermute(shard, 'var', pairs)  60.5 us
    ppermute x13, starting transfers between devices, send(): return lax.ppermute(shard, 'var', pairs)  24.1 us
    pallas_call x4, Pallas kernels, tile(): pl.pallas_call(kernel, grid=(1,), in_specs=specs, out_specs=pl.BlockSpec(...  11.6 us
    pallas_call x4, Pallas kernels, far(): pl.pallas_call(functools.partial(far_kernel, only_odd, 1.0 / samples, len...  6.09 us
    pallas_call x1, Pallas kernels, stats(): pl.pallas_call(stats_kernel, in_specs=[pl.BlockSpec(memory_space=pltpu.HB...  3.08 us
    ppermute x9, waiting for transfers between devices, mate(): return lax.ppermute(shard, 'samp', [(0, 1), (1, 0)])  2.68 us
    ppermute x9, starting transfers between devices, mate(): return lax.ppermute(shard, 'samp', [(0, 1), (1, 0)])  2.64 us
  transfers between devices with their start and end apart: 22, of which 14 were waited for; matrix products, arithmetic and copies ran while one was open for 0% of the time, Pallas kernels for 16%

profile of v4, /device:TPU:0, one launch (start us, length us, event | category | flops | bytes accessed | tf_op | source)
XLA Modules:
  0.0 117.1 jit_solution(9584637501536117216)
XLA Ops:
  0.0 3.1 %shard_map.37 = (f32[8,1024]{1,0:T(8,128)S(1)}, bf16[1024,1024]{1,0:T(8,128)(2,1)S(1)}) custom-call(bf16[1024,1024]{1,0:T(8,128)(2,1)} %dosage_hbm.1, s32[1024,1024]{1,0:T(8,128)} %observed_hbm.1), custom_call_target="tpu_custom_call" | custom-call | flops 1000 | bytes 1000 | tf_op jit(solution)/shard_map/pallas_call | solution.py:59
  3.1 0.5 collective-permute-start
  4.3 0.1 pad_add_fusion.place_ref.refs_0_
  4.3 0.1 collective-permute-done.sums_other_ref
  4.5 1.7 %shard_map.38 = (bf16[1024,256]{1,0:T(8,128)(2,1)S(1)}, bf16[1024,256]{1,0:T(8,128)(2,1)S(1)}, bf16[1024,256]{1,0:T(8,128)(2,1)S(1)}, bf16[1024,256]{1,0:T(8,128...) custom-call(s32[3]{0:T(128)S(1)} %pad_add_fusion.place_ref.refs_0_, ...), custom_call_target="tpu_custom_call" | custom-call | flops 1000 | bytes 1000 | tf_op jit(solution)/shard_map/pallas_call | solution.py:114
  6.2 0.4 collective-permute-start.1
  6.6 2.3 %collective-permute-done.1.arrived_ref = bf16[512,1024]{1,0:T(8,128)(2,1)S(1)} collective-permute-done((bf16[512,1024]{1,0:T(8,128)(2,1)S(1)}, bf16[512,1024]{1,0:T(8,128)(2,1)S(1)}, u32[]{:S(2)}, u32[]{:S(2)}) %collective-permute-start.1) | collective-permute-done | bytes 1048608 | tf_op jit(solution)/shard_map/ppermute | solution.py:348
  8.9 0.1 shard_map.39
  9.1 0.4 collective-permute-start.3
  9.5 1.3 %collective-permute-start.4 = (bf16[1024,256]{1,0:T(8,128)(2,1)S(1)}, bf16[1024,256]{1,0:T(8,128)(2,1)S(1)}, u32[]{:S(2)}, u32[]{:S(2)}) collective-permute-start(bf16[1024,256]{1,0:T(8,128)(2,1)S(1)} %get-tuple-element.44.odd_ref), channel_id=1, source_target_pairs={{4,0},{6,2},{8,4},{10,6},{12,8},{14,10},{5,1},{7,3},{9,5},{11,7},{... | collective-permute-start | bytes 1572872 | tf_op jit(solution)/shard_map/ppermute | solution.py:338
  10.8 5.3 %collective-permute-start.2 = (bf16[512,1024]{1,0:T(8,128)(2,1)S(1)}, bf16[512,1024]{1,0:T(8,128)(2,1)S(1)}, u32[]{:S(2)}, u32[]{:S(2)}) collective-permute-start(bf16[512,1024]{1,0:T(8,128)(2,1)S(1)} %get-tuple-element.42.refs_0_.refs_1_), channel_id=1, source_target_pairs={{0,4},{2,6},{4,8},{6,10},{8,12},{10,14},{1,5},{3,7},{5,9},{7,11},{... | collective-permute-start | bytes 3145736 | tf_op jit(solution)/shard_map/ppermute | solution.py:338
  16.1 2.0 %collective-permute-start.7 = (bf16[1024,256]{1,0:T(8,128)(2,1)S(1)}, bf16[1024,256]{1,0:T(8,128)(2,1)S(1)}, u32[]{:S(2)}, u32[]{:S(2)}) collective-permute-start(bf16[1024,256]{1,0:T(8,128)(2,1)S(1)} %get-tuple-element.50), channel_id=1, source_target_pairs={{2,0},{6,4},{10,8},{14,12},{0,2},{4,6},{8,10},{12,14},{3,1},{7,5},... | collective-permute-start | bytes 1572872 | tf_op jit(solution)/shard_map/ppermute | solution.py:338
  18.2 0.0 collective-permute-done.3.refs_3_.refs_2_.refs_8_
  18.2 3.8 %shard_map.40.refs_1_ = bf16[4,512,1024]{2,1,0:T(8,128)(2,1)} custom-call(s32[3]{0:T(128)S(1)} %pad_add_fusion.place_ref.refs_0_, bf16[512,1024]{1,0:T(8,128)(2,1)S(1)} %get-tuple-element.42.refs_0_.refs_1_, bf16[512,1024]{1,0:T(8,128)(2,1)S(1)} %get-tuple-element.46.refs_1_.refs_2_, bf16[1024,1024]{1,0:T(8,128)(2,1)S(1)} %get-tuple-element.43.refs_2_.refs_1_.refs_7_, ...), custom_call_target="tpu_custom_call" | custom-call | flops 1000 | bytes 1000 | tf_op jit(solution)/shard_map/pallas_call | solution.py:195
  22.0 4.6 %collective-permute-done.4.even_ref = bf16[1024,256]{1,0:T(8,128)(2,1)S(1)} collective-permute-done((bf16[1024,256]{1,0:T(8,128)(2,1)S(1)}, bf16[1024,256]{1,0:T(8,128)(2,1)S(1)}, u32[]{:S(2)}, u32[]{:S(2)}) %collective-permute-start.4) | collective-permute-done | bytes 524320 | tf_op jit(solution)/shard_map/ppermute | solution.py:338
  26.6 0.6 shard_map.41
  27.2 1.7 %collective-permute-start.6 = (bf16[1024,256]{1,0:T(8,128)(2,1)S(1)}, bf16[1024,256]{1,0:T(8,128)(2,1)S(1)}, u32[]{:S(2)}, u32[]{:S(2)}) collective-permute-start(bf16[1024,256]{1,0:T(8,128)(2,1)S(1)} %get-tuple-element.49), channel_id=1, source_target_pairs={{2,0},{6,4},{10,8},{14,12},{0,2},{4,6},{8,10},{12,14},{3,1},{7,5},... | collective-permute-start | bytes 1572872 | tf_op jit(solution)/shard_map/ppermute | solution.py:338
  28.9 1.3 %collective-permute-start.5 = (bf16[1024,256]{1,0:T(8,128)(2,1)S(1)}, bf16[1024,256]{1,0:T(8,128)(2,1)S(1)}, u32[]{:S(2)}, u32[]{:S(2)}) collective-permute-start(bf16[1024,256]{1,0:T(8,128)(2,1)S(1)} %get-tuple-element.47.odd_ref), channel_id=1, source_target_pairs={{4,0},{6,2},{8,4},{10,6},{12,8},{14,10},{5,1},{7,3},{9,5},{11,7},{... | collective-permute-start | bytes 1572872 | tf_op jit(solution)/shard_map/ppermute | solution.py:338
  30.2 0.3 collective-permute-done.7.refs_2_
  30.4 8.5 %collective-permute-done.2.refs_1_.refs_0_ = bf16[512,1024]{1,0:T(8,128)(2,1)S(1)} collective-permute-done((bf16[512,1024]{1,0:T(8,128)(2,1)S(1)}, bf16[512,1024]{1,0:T(8,128)(2,1)S(1)}, u32[]{:S(2)}, u32[]{:S(2)}) %collective-permute-start.2) | collective-permute-done | bytes 1048608 | tf_op jit(solution)/shard_map/ppermute | solution.py:338
  39.0 2.4 %collective-permute-done.6.refs_0_.refs_1_.refs_3_ = bf16[1024,256]{1,0:T(8,128)(2,1)S(1)} collective-permute-done((bf16[1024,256]{1,0:T(8,128)(2,1)S(1)}, bf16[1024,256]{1,0:T(8,128)(2,1)S(1)}, u32[]{:S(2)}, u32[]{:S(2)}) %collective-permute-start.6) | collective-permute-done | bytes 524320 | tf_op jit(solution)/shard_map/ppermute | solution.py:338
  41.3 2.5 %collective-permute-done.5.even_ref = bf16[1024,256]{1,0:T(8,128)(2,1)S(1)} collective-permute-done((bf16[1024,256]{1,0:T(8,128)(2,1)S(1)}, bf16[1024,256]{1,0:T(8,128)(2,1)S(1)}, u32[]{:S(2)}, u32[]{:S(2)}) %collective-permute-start.5) | collective-permute-done | bytes 524320 | tf_op jit(solution)/shard_map/ppermute | solution.py:338
  43.9 0.6 shard_map.43
  44.5 0.7 collective-permute-start.10
  45.2 0.7 collective-permute-start.12
  45.9 1.2 %shard_map.44 = (bf16[256,512]{1,0:T(8,128)(2,1)S(1)}, bf16[4,512,1024]{2,1,0:T(8,128)(2,1)}) custom-call(s32[3]{0:T(128)S(1)} %pad_add_fusion.place_ref.refs_0_, bf16[512,1024]{1,0:T(8,128)(2,1)S(1)} %collective-permute-done.2.refs_1_.refs_0_, bf16[1024,1024]{1,0:T(8,128)(2,1)S(1)} %get-tuple-element.43.refs_2_.refs_1_.refs_7_, ...), custom_call_target="tpu_custom_call", output_to_operand_aliasing={{1}: (4, {})} | custom-call | flops 1000 | bytes 1000 | tf_op jit(solution)/shard_map/pallas_call | solution.py:226
  47.1 1.3 %collective-permute-start.8 = (bf16[256,512]{1,0:T(8,128)(2,1)S(1)}, bf16[256,512]{1,0:T(8,128)(2,1)S(1)}, u32[]{:S(2)}, u32[]{:S(2)}) collective-permute-start(bf16[256,512]{1,0:T(8,128)(2,1)S(1)} %get-tuple-element.54), channel_id=1, source_target_pairs={{4,0},{6,2},{8,4},{10,6},{12,8},{14,10},{5,1},{7,3},{9,5},{11,7},{... | collective-permute-start | bytes 786440 | tf_op jit(solution)/shard_map/ppermute | solution.py:338
  48.4 4.6 %collective-permute-start.15 = (bf16[512,1024]{1,0:T(8,128)(2,1)S(1)}, bf16[512,1024]{1,0:T(8,128)(2,1)S(1)}, u32[]{:S(2)}, u32[]{:S(2)}) collective-permute-start(bf16[512,1024]{1,0:T(8,128)(2,1)S(1)} %get-tuple-element.46.refs_1_.refs_2_), channel_id=1, source_target_pairs={{0,4},{2,6},{4,8},{6,10},{8,12},{10,14},{1,5},{3,7},{5,9},{7,11},{... | collective-permute-start | bytes 3145736 | tf_op jit(solution)/shard_map/ppermute | solution.py:338
  53.1 0.1 collective-permute-start.9
  53.1 3.6 %collective-permute-done.10.refs_0_.refs_3_.refs_5_ = bf16[1024,256]{1,0:T(8,128)(2,1)S(1)} collective-permute-done((bf16[1024,256]{1,0:T(8,128)(2,1)S(1)}, bf16[1024,256]{1,0:T(8,128)(2,1)S(1)}, u32[]{:S(2)}, u32[]{:S(2)}) %collective-permute-start.10) | collective-permute-done | bytes 524320 | tf_op jit(solution)/shard_map/ppermute | solution.py:338
  56.7 0.0 collective-permute-start.11
  56.7 0.0 collective-permute-done.8.refs_1_
  56.7 0.0 collective-permute-done.12.odd_ref
  56.7 0.6 shard_map.46
  57.3 0.6 collective-permute-start.13
  57.9 1.3 %collective-permute-start.17 = (bf16[1024,256]{1,0:T(8,128)(2,1)S(1)}, bf16[1024,256]{1,0:T(8,128)(2,1)S(1)}, u32[]{:S(2)}, u32[]{:S(2)}) collective-permute-start(bf16[1024,256]{1,0:T(8,128)(2,1)S(1)} %get-tuple-element.63), channel_id=1, source_target_pairs={{2,0},{4,2},{6,4},{8,6},{10,8},{12,10},{14,12},{3,1},{5,3},{7,5},{... | collective-permute-start | bytes 1572872 | tf_op jit(solution)/shard_map/ppermute | solution.py:338
  59.2 0.0 collective-permute-done.9.refs_2_.refs_4_
  59.2 0.0 collective-permute-done.11.refs_4_.refs_6_
  59.2 0.2 collective-permute-done.13.refs_6_.refs_4_
  59.4 1.5 %shard_map.47 = (bf16[256,768]{1,0:T(8,128)(2,1)S(1)}, bf16[4,512,1024]{2,1,0:T(8,128)(2,1)}) custom-call(s32[3]{0:T(128)S(1)} %pad_add_fusion.place_ref.refs_0_, bf16[512,1024]{1,0:T(8,128)(2,1)S(1)} %collective-permute-done.2.refs_1_.refs_0_, bf16[1024,256]{1,0:T(8,128)(2,1)S(1)} %collective-permute-done.6.refs_0_.refs_1_.refs_3_, ...), custom_call_target="tpu_custom_call", output_to_operand_aliasing={{1}: (8, {})} | custom-call | flops 1000 | bytes 1000 | tf_op jit(solution)/shard_map/pallas_call | solution.py:226
  60.9 1.3 %collective-permute-start.14 = (bf16[256,768]{1,0:T(8,128)(2,1)S(1)}, bf16[256,768]{1,0:T(8,128)(2,1)S(1)}, u32[]{:S(2)}, u32[]{:S(2)}) collective-permute-start(bf16[256,768]{1,0:T(8,128)(2,1)S(1)} %get-tuple-element.60), channel_id=1, source_target_pairs={{4,0},{6,2},{8,4},{10,6},{12,8},{14,10},{5,1},{7,3},{9,5},{11,7},{... | collective-permute-start | bytes 1179656 | tf_op jit(solution)/shard_map/ppermute | solution.py:338
  62.2 11.4 %collective-permute-done.15.refs_0_.refs_1_ = bf16[512,1024]{1,0:T(8,128)(2,1)S(1)} collective-permute-done((bf16[512,1024]{1,0:T(8,128)(2,1)S(1)}, bf16[512,1024]{1,0:T(8,128)(2,1)S(1)}, u32[]{:S(2)}, u32[]{:S(2)}) %collective-permute-start.15) | collective-permute-done | bytes 1048608 | tf_op jit(solution)/shard_map/ppermute | solution.py:338
  73.7 2.1 %shard_map.49 = (bf16[256,1280]{1,0:T(8,128)(2,1)S(1)}, bf16[4,512,1024]{2,1,0:T(8,128)(2,1)}) custom-call(s32[3]{0:T(128)S(1)} %pad_add_fusion.place_ref.refs_0_, bf16[512,1024]{1,0:T(8,128)(2,1)S(1)} %collective-permute-done.15.refs_0_.refs_1_, ...), custom_call_target="tpu_custom_call", output_to_operand_aliasing={{1}: (10, {})} | custom-call | flops 1000 | bytes 1000 | tf_op jit(solution)/shard_map/pallas_call | solution.py:226
  75.7 5.3 %collective-permute-done.17.refs_2_ = bf16[1024,256]{1,0:T(8,128)(2,1)S(1)} collective-permute-done((bf16[1024,256]{1,0:T(8,128)(2,1)S(1)}, bf16[1024,256]{1,0:T(8,128)(2,1)S(1)}, u32[]{:S(2)}, u32[]{:S(2)}) %collective-permute-start.17) | collective-permute-done | bytes 524320 | tf_op jit(solution)/shard_map/ppermute | solution.py:338
  81.1 9.6 %collective-permute-done.14.refs_1_.refs_2_ = bf16[256,768]{1,0:T(8,128)(2,1)S(1)} collective-permute-done((bf16[256,768]{1,0:T(8,128)(2,1)S(1)}, bf16[256,768]{1,0:T(8,128)(2,1)S(1)}, u32[]{:S(2)}, u32[]{:S(2)}) %collective-permute-start.14) | collective-permute-done | bytes 393248 | tf_op jit(solution)/shard_map/ppermute | solution.py:338
  90.7 0.0 collective-permute-start.18
  90.7 1.3 %collective-permute-start.16 = (bf16[256,1280]{1,0:T(8,128)(2,1)S(1)}, bf16[256,1280]{1,0:T(8,128)(2,1)S(1)}, u32[]{:S(2)}, u32[]{:S(2)}) collective-permute-start(bf16[256,1280]{1,0:T(8,128)(2,1)S(1)} %get-tuple-element.62.refs_0_), channel_id=1, source_target_pairs={{4,0},{6,2},{8,4},{10,6},{12,8},{14,10},{5,1},{7,3},{9,5},{11,7},{... | collective-permute-start | bytes 1966088 | tf_op jit(solution)/shard_map/ppermute | solution.py:338
  92.0 0.6 collective-permute-start.20
  92.6 0.1 collective-permute-start.21
  92.6 2.6 %shard_map.51.refs_4_ = bf16[4,512,1024]{2,1,0:T(8,128)(2,1)} custom-call(s32[3]{0:T(128)S(1)} %pad_add_fusion.place_ref.refs_0_, bf16[512,1024]{1,0:T(8,128)(2,1)S(1)} %get-tuple-element.42.refs_0_.refs_1_, bf16[512,1024]{1,0:T(8,128)(2,1)S(1)} %get-tuple-element.46.refs_1_.refs_2_, ...), custom_call_target="tpu_custom_call", output_to_operand_aliasing={{}: (7, {})} | custom-call | flops 1000 | bytes 1000 | tf_op jit(solution)/shard_map/pallas_call | solution.py:195
  95.2 0.0 collective-permute-done.18.refs_3_.refs_6_
  95.2 1.2 %shard_map.52 = (bf16[512,256]{1,0:T(8,128)(2,1)S(1)}, bf16[4,512,1024]{2,1,0:T(8,128)(2,1)}) custom-call(s32[3]{0:T(128)S(1)} %pad_add_fusion.place_ref.refs_0_, bf16[512,1024]{1,0:T(8,128)(2,1)S(1)} %collective-permute-done.2.refs_1_.refs_0_, bf16[512,1024]{1,0:T(8,128)(2,1)S(1)} %collective-permute-done.15.refs_0_.refs_1_, ...), custom_call_target="tpu_custom_call", output_to_operand_aliasing={{1}: (5, {})} | custom-call | flops 1000 | bytes 1000 | tf_op jit(solution)/shard_map/pallas_call | solution.py:226
  96.5 1.3 %collective-permute-start.19 = (bf16[512,256]{1,0:T(8,128)(2,1)S(1)}, bf16[512,256]{1,0:T(8,128)(2,1)S(1)}, u32[]{:S(2)}, u32[]{:S(2)}) collective-permute-start(bf16[512,256]{1,0:T(8,128)(2,1)S(1)} %get-tuple-element.65), channel_id=1, source_target_pairs={{4,0},{6,2},{8,4},{10,6},{12,8},{14,10},{5,1},{7,3},{9,5},{11,7},{... | collective-permute-start | bytes 786440 | tf_op jit(solution)/shard_map/ppermute | solution.py:338
  97.8 0.0 collective-permute-done.20.refs_4_
  97.8 0.0 collective-permute-done.21.refs_6_
  97.8 2.6 %shard_map.53.refs_7_ = bf16[4,512,1024]{2,1,0:T(8,128)(2,1)} custom-call(s32[3]{0:T(128)S(1)} %pad_add_fusion.place_ref.refs_0_, bf16[512,1024]{1,0:T(8,128)(2,1)S(1)} %get-tuple-element.42.refs_0_.refs_1_, bf16[512,1024]{1,0:T(8,128)(2,1)S(1)} %get-tuple-element.46.refs_1_.refs_2_, ...), custom_call_target="tpu_custom_call", output_to_operand_aliasing={{}: (7, {})} | custom-call | flops 1000 | bytes 1000 | tf_op jit(solution)/shard_map/pallas_call | solution.py:195
  100.4 2.6 %shard_map.54.refs_5_ = bf16[4,512,1024]{2,1,0:T(8,128)(2,1)} custom-call(s32[3]{0:T(128)S(1)} %pad_add_fusion.place_ref.refs_0_, bf16[512,1024]{1,0:T(8,128)(2,1)S(1)} %get-tuple-element.42.refs_0_.refs_1_, bf16[512,1024]{1,0:T(8,128)(2,1)S(1)} %get-tuple-element.46.refs_1_.refs_2_, ...), custom_call_target="tpu_custom_call", output_to_operand_aliasing={{}: (7, {})} | custom-call | flops 1000 | bytes 1000 | tf_op jit(solution)/shard_map/pallas_call | solution.py:195
  103.0 7.1 %collective-permute-done.16.refs_3_ = bf16[256,1280]{1,0:T(8,128)(2,1)S(1)} collective-permute-done((bf16[256,1280]{1,0:T(8,128)(2,1)S(1)}, bf16[256,1280]{1,0:T(8,128)(2,1)S(1)}, u32[]{:S(2)}, u32[]{:S(2)}) %collective-permute-start.16) | collective-permute-done | bytes 655392 | tf_op jit(solution)/shard_map/ppermute | solution.py:338
  110.1 5.2 %collective-permute-done.19.refs_4_ = bf16[512,256]{1,0:T(8,128)(2,1)S(1)} collective-permute-done((bf16[512,256]{1,0:T(8,128)(2,1)S(1)}, bf16[512,256]{1,0:T(8,128)(2,1)S(1)}, u32[]{:S(2)}, u32[]{:S(2)}) %collective-permute-start.19) | collective-permute-done | bytes 262176 | tf_op jit(solution)/shard_map/ppermute | solution.py:338
  115.3 1.7 %shard_map.55 = bf16[4,512,1024]{2,1,0:T(8,128)(2,1)} custom-call(s32[3]{0:T(128)S(1)} %pad_add_fusion.place_ref.refs_0_, bf16[256,512]{1,0:T(8,128)(2,1)S(1)} %collective-permute-done.8.refs_1_, bf16[256,768]{1,0:T(8,128)(2,1)S(1)} %collective-permute-done.14.refs_1_.refs_2_, ...), custom_call_target="tpu_custom_call", output_to_operand_aliasing={{}: (5, {})} | custom-call | flops 1000 | bytes 1000 | tf_op jit(solution)/shard_map/pallas_call | solution.py:309
  (4 shorter events, 0.0 us)
Async XLA Ops:
  3.1 1.4 %collective-permute-start = (f32[8,1024]{1,0:T(8,128)S(1)}, f32[8,1024]{1,0:T(8,128)S(1)}, u32[]{:S(2)}, u32[]{:S(2)}) collective-permute-start(f32[8,1024]{1,0:T(8,128)S(1)} %get-tuple-element.38.sums_ref), channel_id=1, source_target_pairs={{0,1},{1,0},{2,3},{3,2},{4,5},{5,4},{6,7},{7,6},{8,9},{9,8},{10,11... | collective-permute-start | bytes 98312 | tf_op jit(solution)/shard_map/ppermute | solution.py:348
  6.2 2.7 %collective-permute-start.1 = (bf16[512,1024]{1,0:T(8,128)(2,1)S(1)}, bf16[512,1024]{1,0:T(8,128)(2,1)S(1)}, u32[]{:S(2)}, u32[]{:S(2)}) collective-permute-start(bf16[512,1024]{1,0:T(8,128)(2,1)S(1)} %get-tuple-element.40), channel_id=1, source_target_pairs={{0,1},{1,0},{2,3},{3,2},{4,5},{5,4},{6,7},{7,6},{8,9},{9,8},{10,11... | collective-permute-start | bytes 3145736 | tf_op jit(solution)/shard_map/ppermute | solution.py:348
  9.1 9.1 %collective-permute-start.3 = (bf16[1024,1024]{1,0:T(8,128)(2,1)S(1)}, bf16[1024,1024]{1,0:T(8,128)(2,1)S(1)}, u32[]{:S(2)}, u32[]{:S(2)}) collective-permute-start(bf16[1024,1024]{1,0:T(8,128)(2,1)S(1)} %get-tuple-element.43.refs_2_.refs_1_.refs_7_), channel_id=1, source_target_pairs={{0,1},{1,0},{2,3},{3,2},{4,5},{5,4},{6,7},{7,6},{8,9},{9,8},{10,11... | collective-permute-start | bytes 6291464 | tf_op jit(solution)/shard_map/ppermute | solution.py:348
  9.5 17.1 %collective-permute-start.4 = (bf16[1024,256]{1,0:T(8,128)(2,1)S(1)}, bf16[1024,256]{1,0:T(8,128)(2,1)S(1)}, u32[]{:S(2)}, u32[]{:S(2)}) collective-permute-start(bf16[1024,256]{1,0:T(8,128)(2,1)S(1)} %get-tuple-element.44.odd_ref), channel_id=1, source_target_pairs={{4,0},{6,2},{8,4},{10,6},{12,8},{14,10},{5,1},{7,3},{9,5},{11,7},{... | collective-permute-start | bytes 1572872 | tf_op jit(solution)/shard_map/ppermute | solution.py:338
  10.8 28.2 %collective-permute-start.2 = (bf16[512,1024]{1,0:T(8,128)(2,1)S(1)}, bf16[512,1024]{1,0:T(8,128)(2,1)S(1)}, u32[]{:S(2)}, u32[]{:S(2)}) collective-permute-start(bf16[512,1024]{1,0:T(8,128)(2,1)S(1)} %get-tuple-element.42.refs_0_.refs_1_), channel_id=1, source_target_pairs={{0,4},{2,6},{4,8},{6,10},{8,12},{10,14},{1,5},{3,7},{5,9},{7,11},{... | collective-permute-start | bytes 3145736 | tf_op jit(solution)/shard_map/ppermute | solution.py:338
  16.1 14.3 %collective-permute-start.7 = (bf16[1024,256]{1,0:T(8,128)(2,1)S(1)}, bf16[1024,256]{1,0:T(8,128)(2,1)S(1)}, u32[]{:S(2)}, u32[]{:S(2)}) collective-permute-start(bf16[1024,256]{1,0:T(8,128)(2,1)S(1)} %get-tuple-element.50), channel_id=1, source_target_pairs={{2,0},{6,4},{10,8},{14,12},{0,2},{4,6},{8,10},{12,14},{3,1},{7,5},... | collective-permute-start | bytes 1572872 | tf_op jit(solution)/shard_map/ppermute | solution.py:338
  27.2 14.2 %collective-permute-start.6 = (bf16[1024,256]{1,0:T(8,128)(2,1)S(1)}, bf16[1024,256]{1,0:T(8,128)(2,1)S(1)}, u32[]{:S(2)}, u32[]{:S(2)}) collective-permute-start(bf16[1024,256]{1,0:T(8,128)(2,1)S(1)} %get-tuple-element.49), channel_id=1, source_target_pairs={{2,0},{6,4},{10,8},{14,12},{0,2},{4,6},{8,10},{12,14},{3,1},{7,5},... | collective-permute-start | bytes 1572872 | tf_op jit(solution)/shard_map/ppermute | solution.py:338
  28.9 15.0 %collective-permute-start.5 = (bf16[1024,256]{1,0:T(8,128)(2,1)S(1)}, bf16[1024,256]{1,0:T(8,128)(2,1)S(1)}, u32[]{:S(2)}, u32[]{:S(2)}) collective-permute-start(bf16[1024,256]{1,0:T(8,128)(2,1)S(1)} %get-tuple-element.47.odd_ref), channel_id=1, source_target_pairs={{4,0},{6,2},{8,4},{10,6},{12,8},{14,10},{5,1},{7,3},{9,5},{11,7},{... | collective-permute-start | bytes 1572872 | tf_op jit(solution)/shard_map/ppermute | solution.py:338
  44.5 12.2 %collective-permute-start.10 = (bf16[1024,256]{1,0:T(8,128)(2,1)S(1)}, bf16[1024,256]{1,0:T(8,128)(2,1)S(1)}, u32[]{:S(2)}, u32[]{:S(2)}) collective-permute-start(bf16[1024,256]{1,0:T(8,128)(2,1)S(1)} %get-tuple-element.55), channel_id=1, source_target_pairs={{2,0},{6,4},{10,8},{14,12},{0,2},{4,6},{8,10},{12,14},{3,1},{7,5},... | collective-permute-start | bytes 1572872 | tf_op jit(solution)/shard_map/ppermute | solution.py:338
  45.2 11.5 %collective-permute-start.12 = (bf16[1024,256]{1,0:T(8,128)(2,1)S(1)}, bf16[1024,256]{1,0:T(8,128)(2,1)S(1)}, u32[]{:S(2)}, u32[]{:S(2)}) collective-permute-start(bf16[1024,256]{1,0:T(8,128)(2,1)S(1)} %get-tuple-element.56.even_ref), channel_id=1, source_target_pairs={{6,2},{10,6},{14,10},{7,3},{11,7},{15,11},{22,18},{26,22},{30,26},... | collective-permute-start | bytes 1572872 | tf_op jit(solution)/shard_map/ppermute | solution.py:338
  47.1 9.6 %collective-permute-start.8 = (bf16[256,512]{1,0:T(8,128)(2,1)S(1)}, bf16[256,512]{1,0:T(8,128)(2,1)S(1)}, u32[]{:S(2)}, u32[]{:S(2)}) collective-permute-start(bf16[256,512]{1,0:T(8,128)(2,1)S(1)} %get-tuple-element.54), channel_id=1, source_target_pairs={{4,0},{6,2},{8,4},{10,6},{12,8},{14,10},{5,1},{7,3},{9,5},{11,7},{... | collective-permute-start | bytes 786440 | tf_op jit(solution)/shard_map/ppermute | solution.py:338
  48.4 25.2 %collective-permute-start.15 = (bf16[512,1024]{1,0:T(8,128)(2,1)S(1)}, bf16[512,1024]{1,0:T(8,128)(2,1)S(1)}, u32[]{:S(2)}, u32[]{:S(2)}) collective-permute-start(bf16[512,1024]{1,0:T(8,128)(2,1)S(1)} %get-tuple-element.46.refs_1_.refs_2_), channel_id=1, source_target_pairs={{0,4},{2,6},{4,8},{6,10},{8,12},{10,14},{1,5},{3,7},{5,9},{7,11},{... | collective-permute-start | bytes 3145736 | tf_op jit(solution)/shard_map/ppermute | solution.py:338
  53.1 6.1 %collective-permute-start.9 = (bf16[1024,256]{1,0:T(8,128)(2,1)S(1)}, bf16[1024,256]{1,0:T(8,128)(2,1)S(1)}, u32[]{:S(2)}, u32[]{:S(2)}) collective-permute-start(bf16[1024,256]{1,0:T(8,128)(2,1)S(1)} %collective-permute-done.6.refs_0_.refs_1_.refs_3_), channel_id=1, source_target_pairs={{0,1},{1,0},{2,3},{3,2},{4,5},{5,4},{6,7},{7,6},{8,9},{9,8},{10,11... | collective-permute-start | bytes 1572872 | tf_op jit(solution)/shard_map/ppermute | solution.py:348
  56.7 2.5 %collective-permute-start.11 = (bf16[1024,256]{1,0:T(8,128)(2,1)S(1)}, bf16[1024,256]{1,0:T(8,128)(2,1)S(1)}, u32[]{:S(2)}, u32[]{:S(2)}) collective-permute-start(bf16[1024,256]{1,0:T(8,128)(2,1)S(1)} %collective-permute-done.10.refs_0_.refs_3_.refs_5_), channel_id=1, source_target_pairs={{0,1},{1,0},{2,3},{3,2},{4,5},{5,4},{6,7},{7,6},{8,9},{9,8},{10,11... | collective-permute-start | bytes 1572872 | tf_op jit(solution)/shard_map/ppermute | solution.py:348
  57.3 2.1 %collective-permute-start.13 = (bf16[1024,256]{1,0:T(8,128)(2,1)S(1)}, bf16[1024,256]{1,0:T(8,128)(2,1)S(1)}, u32[]{:S(2)}, u32[]{:S(2)}) collective-permute-start(bf16[1024,256]{1,0:T(8,128)(2,1)S(1)} %get-tuple-element.58.refs_5_.refs_3_), channel_id=1, source_target_pairs={{0,1},{1,0},{2,3},{3,2},{4,5},{5,4},{6,7},{7,6},{8,9},{9,8},{10,11... | collective-permute-start | bytes 1572872 | tf_op jit(solution)/shard_map/ppermute | solution.py:348
  57.9 23.2 %collective-permute-start.17 = (bf16[1024,256]{1,0:T(8,128)(2,1)S(1)}, bf16[1024,256]{1,0:T(8,128)(2,1)S(1)}, u32[]{:S(2)}, u32[]{:S(2)}) collective-permute-start(bf16[1024,256]{1,0:T(8,128)(2,1)S(1)} %get-tuple-element.63), channel_id=1, source_target_pairs={{2,0},{4,2},{6,4},{8,6},{10,8},{12,10},{14,12},{3,1},{5,3},{7,5},{... | collective-permute-start | bytes 1572872 | tf_op jit(solution)/shard_map/ppermute | solution.py:338
  60.9 29.7 %collective-permute-start.14 = (bf16[256,768]{1,0:T(8,128)(2,1)S(1)}, bf16[256,768]{1,0:T(8,128)(2,1)S(1)}, u32[]{:S(2)}, u32[]{:S(2)}) collective-permute-start(bf16[256,768]{1,0:T(8,128)(2,1)S(1)} %get-tuple-element.60), channel_id=1, source_target_pairs={{4,0},{6,2},{8,4},{10,6},{12,8},{14,10},{5,1},{7,3},{9,5},{11,7},{... | collective-permute-start | bytes 1179656 | tf_op jit(solution)/shard_map/ppermute | solution.py:338
  90.7 4.5 %collective-permute-start.18 = (bf16[1024,256]{1,0:T(8,128)(2,1)S(1)}, bf16[1024,256]{1,0:T(8,128)(2,1)S(1)}, u32[]{:S(2)}, u32[]{:S(2)}) collective-permute-start(bf16[1024,256]{1,0:T(8,128)(2,1)S(1)} %shard_map.50.refs_2_.refs_5_), channel_id=1, source_target_pairs={{0,1},{1,0},{2,3},{3,2},{4,5},{5,4},{6,7},{7,6},{8,9},{9,8},{10,11... | collective-permute-start | bytes 1572872 | tf_op jit(solution)/shard_map/ppermute | solution.py:348
  90.7 19.4 %collective-permute-start.16 = (bf16[256,1280]{1,0:T(8,128)(2,1)S(1)}, bf16[256,1280]{1,0:T(8,128)(2,1)S(1)}, u32[]{:S(2)}, u32[]{:S(2)}) collective-permute-start(bf16[256,1280]{1,0:T(8,128)(2,1)S(1)} %get-tuple-element.62.refs_0_), channel_id=1, source_target_pairs={{4,0},{6,2},{8,4},{10,6},{12,8},{14,10},{5,1},{7,3},{9,5},{11,7},{... | collective-permute-start | bytes 1966088 | tf_op jit(solution)/shard_map/ppermute | solution.py:338
  92.0 5.8 %collective-permute-start.20 = (bf16[1024,256]{1,0:T(8,128)(2,1)S(1)}, bf16[1024,256]{1,0:T(8,128)(2,1)S(1)}, u32[]{:S(2)}, u32[]{:S(2)}) collective-permute-start(bf16[1024,256]{1,0:T(8,128)(2,1)S(1)} %get-tuple-element.66.refs_3_), channel_id=1, source_target_pairs={{0,1},{1,0},{2,3},{3,2},{4,5},{5,4},{6,7},{7,6},{8,9},{9,8},{10,11... | collective-permute-start | bytes 1572872 | tf_op jit(solution)/shard_map/ppermute | solution.py:348
  92.6 5.2 %collective-permute-start.21 = (bf16[1024,256]{1,0:T(8,128)(2,1)S(1)}, bf16[1024,256]{1,0:T(8,128)(2,1)S(1)}, u32[]{:S(2)}, u32[]{:S(2)}) collective-permute-start(bf16[1024,256]{1,0:T(8,128)(2,1)S(1)} %get-tuple-element.67.refs_5_), channel_id=1, source_target_pairs={{0,1},{1,0},{2,3},{3,2},{4,5},{5,4},{6,7},{7,6},{8,9},{9,8},{10,11... | collective-permute-start | bytes 1572872 | tf_op jit(solution)/shard_map/ppermute | solution.py:348
  96.5 18.9 %collective-permute-start.19 = (bf16[512,256]{1,0:T(8,128)(2,1)S(1)}, bf16[512,256]{1,0:T(8,128)(2,1)S(1)}, u32[]{:S(2)}, u32[]{:S(2)}) collective-permute-start(bf16[512,256]{1,0:T(8,128)(2,1)S(1)} %get-tuple-element.65), channel_id=1, source_target_pairs={{4,0},{6,2},{8,4},{10,6},{12,8},{14,10},{5,1},{7,3},{9,5},{11,7},{... | collective-permute-start | bytes 786440 | tf_op jit(solution)/shard_map/ppermute | solution.py:338

commit v5 on v4

--- a/solution.py
+++ b/solution.py
@@ -8,7 +8,7 @@
 from jax.sharding import PartitionSpec as P
 
 WIN = 4
-QUARTERS = 4
+PIECES = (2, 2, 4)
 PARTS = 2
 BLOCKS = 8
 STATS_VMEM = 50
@@ -75,13 +75,12 @@
 
 
 def score_kernel(place_ref, masked_ref, sums_ref, sums_other_ref, *outs):
-    pieces, whole_ref = outs[:QUARTERS], outs[QUARTERS]
-    rows_here, rows_away = outs[QUARTERS + 1 :]
+    pieces, whole_ref = outs[: len(PIECES)], outs[len(PIECES)]
+    rows_here, rows_away = outs[len(PIECES) + 1 : -PARTS], outs[-PARTS:]
     core = place_ref[1]
-    quarter = pieces[0].shape[1]
-    per_core = QUARTERS // 2
-    for j in range(QUARTERS):
-        columns = slice(j * quarter, (j + 1) * quarter)
+    part = rows_here[0].shape[0]
+    for step in range(2 * PARTS):
+        columns = slice(step * part, (step + 1) * part)
         totals = [
             sums_ref[n : n + 1, columns] + sums_other_ref[n : n + 1, columns]
             for n in range(3)
@@ -93,55 +92,56 @@
         masked = masked_ref[:, columns].astype(jnp.float32)
         scored = jnp.where(masked >= 0.0, (masked - center) * factor, 0.0)
         scored = scored.astype(jnp.bfloat16)
-        pieces[j][...] = scored
         whole_ref[:, columns] = scored
         turned = scored.T
-        here = core == j // per_core
-        at = slice((j % per_core) * quarter, (j % per_core + 1) * quarter)
+        here = core == step // PARTS
 
         @pl.when(here)
         def _():
-            rows_here[at, :] = turned
+            rows_here[step % PARTS][...] = turned
 
         @pl.when(jnp.logical_not(here))
         def _():
-            rows_away[at, :] = turned
+            rows_away[step % PARTS][...] = turned
+
+    begin = 0
+    for piece in pieces:
+        piece[...] = whole_ref[:, begin : begin + piece.shape[1]]
+        begin += piece.shape[1]
 
 
 def score(place, masked, sums, sums_other):
     samples, width = masked.shape
-    quarter = width // QUARTERS
     return pl.pallas_call(
         score_kernel,
         in_specs=[SMEM, VMEM, VMEM, VMEM],
-        out_specs=[VMEM] * (QUARTERS + 3),
-        out_shape=[jax.ShapeDtypeStruct((samples, quarter), jnp.bfloat16)] * QUARTERS
+        out_specs=[VMEM] * (len(PIECES) + 1 + 2 * PARTS),
+        out_shape=[
+            jax.ShapeDtypeStruct((samples, width * eighths // 8), jnp.bfloat16) for eighths in PIECES
+        ]
         + [jax.ShapeDtypeStruct((samples, width), jnp.bfloat16)]
-        + [jax.ShapeDtypeStruct((width // 2, samples), jnp.bfloat16)] * 2,
+        + [jax.ShapeDtypeStruct((width // 2 // PARTS, samples), jnp.bfloat16)] * (2 * PARTS),
         compiler_params=PARAMS,
         cost_estimate=COST,
     )(place, masked, sums, sums_other)
 
 
-def stack_kernel(here_ref, arrived_ref, whole_ref, *outs):
-    part = outs[0].shape[0] // 2
-    for r in range(PARTS):
-        outs[r][0:part, :] = here_ref[r * part : (r + 1) * part, :]
-        outs[r][part:, :] = arrived_ref[r * part : (r + 1) * part, :]
-
-
-def stack(here, arrived, whole):
+def stack_kernel(here_ref, arrived_ref, out_ref, *rest):
+    part = here_ref.shape[0]
+    out_ref[0:part, :] = here_ref[...]
+    out_ref[part:, :] = arrived_ref[...]
+
+
+def stack(here, arrived, *made):
     count, samples = here.shape
     return pl.pallas_call(
         stack_kernel,
-        in_specs=[VMEM, VMEM, ANY],
-        out_specs=[VMEM] * PARTS + [ANY],
-        out_shape=[jax.ShapeDtypeStruct((2 * count // PARTS, samples), here.dtype)] * PARTS
-        + [jax.ShapeDtypeStruct(whole.shape, whole.dtype)],
-        input_output_aliases={2: PARTS},
-        compiler_params=PARAMS,
-        cost_estimate=COST,
-    )(here, arrived, whole)
+        in_specs=[VMEM, VMEM],
+        out_specs=[VMEM] + [ANY] * len(made),
+        out_shape=[jax.ShapeDtypeStruct((2 * count, samples), here.dtype), *made],
+        compiler_params=PARAMS,
+        cost_estimate=COST,
+    )(here, arrived)
 
 
 def blocks(rows, rights, scale, skip=0):
@@ -169,63 +169,44 @@
         at += width
 
 
-def tile_kernel(k, parts, scale, place_ref, *refs):
+def tile_kernel(k, parts, pieces, scale, place_ref, *refs):
     out_ref = refs[-1]
     keep = k < place_ref[2]
-    for at, columns, block in blocks(refs[:parts], refs[parts:-1], scale):
+    for at, columns, block in blocks(refs[:parts], refs[parts : parts + pieces], scale):
         out_ref[0, at, columns] = jnp.where(keep, block, 0.0).astype(out_ref.dtype)
 
 
-def tile(place, buffer, k, column, rows, rights, samples, width, after=()):
+def tile(place, buffer, k, column, rows, rights, samples, after=()):
     count = rows[0].shape[0] // 2 * len(rows)
     wide = sum(right.shape[1] for right in rights) // 2
-    operands = [place, *rows, *rights]
-    specs = [SMEM] + [VMEM] * (len(operands) - 1)
-    kernel = functools.partial(tile_kernel, k, len(rows), 1.0 / samples)
-    aliases = {}
-    if buffer is not None:
-        aliases = {len(operands): 0}
-        operands += [buffer, *after]
-        specs += [ANY] * (1 + len(after))
-        inner, count_in = kernel, len(operands) - 1 - len(after)
-
-        def kernel(*refs):
-            inner(*refs[:count_in], refs[-1])
-
-    return pl.pallas_call(
-        kernel,
+    operands = [place, *rows, *rights, *after, buffer]
+    return pl.pallas_call(
+        functools.partial(tile_kernel, k, len(rows), len(rights), 1.0 / samples),
         grid=(1,),
-        in_specs=specs,
+        in_specs=[SMEM] + [VMEM] * (len(rows) + len(rights)) + [ANY] * (1 + len(after)),
         out_specs=pl.BlockSpec((1, count, wide), lambda i: (k, 0, column)),
-        out_shape=jax.ShapeDtypeStruct((WIN, count, width), jnp.bfloat16),
-        input_output_aliases=aliases,
+        out_shape=jax.ShapeDtypeStruct(buffer.shape, buffer.dtype),
+        input_output_aliases={len(operands) - 1: 0},
         compiler_params=PARAMS,
         cost_estimate=COST,
     )(*operands)
 
 
-def far_kernel(only_odd, scale, parts, pieces, skip, place_ref, *refs):
+def far_kernel(scale, parts, pieces, skip, place_ref, *refs):
     out_ref = refs[-2]
-
-    def work():
-        for at, columns, block in blocks(refs[:parts], refs[parts : parts + pieces], scale, skip):
-            out_ref[at, columns] = block.astype(out_ref.dtype)
-
-    if only_odd:
-        pl.when(place_ref[0] == 1)(work)
-    else:
-        work()
-
-
-def far(place, buffer, rows, rights, samples, only_odd=False, after=(), skip=0):
+    for at, columns, block in blocks(refs[:parts], refs[parts : parts + pieces], scale, skip):
+        out_ref[at, columns] = block.astype(out_ref.dtype)
+
+
+def far(place, buffer, rows, rights, samples, skip=0):
     shape = (
         rows[0].shape[0] // 2 * len(rows),
         sum(right.shape[1] for right in rights) // 2 - skip,
     )
-    operands = [place, *rows, *rights, *after, buffer]
-    return pl.pallas_call(
-        functools.partial(far_kernel, only_odd, 1.0 / samples, len(rows), len(rights), skip),
-        in_specs=[SMEM] + [VMEM] * (len(rows) + len(rights)) + [ANY] * (len(after) + 1),
+    operands = [place, *rows, *rights, buffer]
+    return pl.pallas_call(
+        functools.partial(far_kernel, 1.0 / samples, len(rows), len(rights), skip),
+        in_specs=[SMEM] + [VMEM] * (len(rows) + len(rights)) + [ANY],
         out_specs=[VMEM, ANY],
         out_shape=[
             jax.ShapeDtypeStruct(shape, jnp.bfloat16),
@@ -277,29 +258,28 @@
     )(*after, *passed)
 
 
-def last_kernel(place_ref, top2, top3, bottom, side, out_ref, two, three, sems):
+def last_kernel(place_ref, top2, bottom2, wide3, side3, out_ref, two, three, sems):
     keep2, keep3 = 2 < place_ref[2], 3 < place_ref[2]
-    part, half = top2.shape
-    wide = top3.shape[1]
-
-    def kept(keep, block):
-        return jnp.where(keep, block, 0.0).astype(out_ref.dtype)
-
-    two[0:part, :] = kept(keep2, top2[...])
-    two[part:, :] = kept(keep2, bottom[:, wide:])
-    copy2 = pltpu.make_async_copy(two, out_ref.at[2, :, half:], sems.at[0])
+    part = top2.shape[0]
+    first = side3.shape[1]
+
+    def kept(keep, ref):
+        return jnp.where(keep, ref[...], 0.0).astype(out_ref.dtype)
+
+    two[0:part, :] = kept(keep2, top2)
+    two[part:, :] = kept(keep2, bottom2)
+    copy2 = pltpu.make_async_copy(two, out_ref.at[2, :, first:], sems.at[0])
     copy2.start()
-    three[0:part, 0:wide] = kept(keep3, top3[...])
-    three[part:, 0:wide] = kept(keep3, bottom[:, 0:wide])
-    three[:, wide:] = kept(keep3, side[...])
+    three[:, first:] = kept(keep3, wide3)
+    three[:, 0:first] = kept(keep3, side3)
     copy3 = pltpu.make_async_copy(three, out_ref.at[3], sems.at[1])
     copy3.start()
     copy2.wait()
     copy3.wait()
 
 
-def last(place, buffer, *received):
-    operands = [place, *received, buffer]
+def last(place, buffer, top2, bottom2, wide3, side3):
+    operands = [place, top2, bottom2, wide3, side3, buffer]
     count, width = buffer.shape[1:]
 
     def kernel(*refs):
@@ -312,7 +292,7 @@
         out_specs=ANY,
         out_shape=jax.ShapeDtypeStruct(buffer.shape, buffer.dtype),
         scratch_shapes=[
-            pltpu.VMEM((count, width // 2), buffer.dtype),
+            pltpu.VMEM((count, top2.shape[1]), buffer.dtype),
             pltpu.VMEM((count, width), buffer.dtype),
             pltpu.SemaphoreType.DMA((2,)),
         ],
@@ -348,54 +328,47 @@
         return lax.ppermute(shard, "samp", [(0, 1), (1, 0)])
 
     sums, masked = stats(dosage, observed)
-    *own, whole, here, away = score(place, masked, sums, mate(sums))
-    above = [None] * QUARTERS
-    next_one, other = [None] * QUARTERS, [None] * QUARTERS
-
-    above[0] = send(own[0], down)
-    across = send(own[2], swap)
-    *rows, whole = stack(here, mate(away), whole)
-    below = [send(rows[0], up), send(rows[1], up)]
-    whole_other = mate(whole)
-    buffer = tile(place, None, 0, 0, rows, [whole, whole_other], samples, width)
-
-    above[0], own[1], buffer, swapped = choose(place, own[0], above[0], own[1], buffer)
-    next_one[0] = send(swapped, swap)
-    above[1] = send(own[1], down)
-
-    across, buffer = hold((next_one[0], below[0]), across, buffer)
-    above[1], own[3], buffer, swapped = choose(place, own[1], above[1], own[3], buffer)
-    next_one[1] = send(swapped, swap)
+    made = score(place, masked, sums, mate(sums))
+    (relayed, detoured, direct), whole = made[:3], made[3]
+    here, away = made[4:-PARTS], made[-PARTS:]
+    first = relayed.shape[1]
+    unset = jax.ShapeDtypeStruct((WIN, width // 2, width), jnp.bfloat16)
+
+    upper, buffer = stack(here[0], mate(away[0]), unset)
+    below0 = send(upper, up)
+    above = send(relayed, down)
+    across = send(detoured, swap)
+    next_direct = send(direct, before)
+    (lower,) = stack(here[1], mate(away[1]))
+    below1 = send(lower, up)
+    rows = [upper, lower]
+    own = [whole, mate(whole)]
+
     around = send(across, down_odd)
-    next_one[3] = send(own[3], before)
-    made, buffer = far(place, buffer, below[:1], [whole, whole_other], samples, False, (), width // 2)
+    buffer = tile(place, buffer, 0, 0, rows, own, samples)
+    across, buffer, next_detoured = choose(place, around, across, buffer)
+    (buffer,) = hold((below0,), buffer)
+    made, buffer = far(place, buffer, [below0], own, samples, first)
     top2 = send(made, down)
-
-    (buffer,) = hold((next_one[1], top2), buffer)
-    across, buffer, next_one[2] = choose(place, around, across, buffer)
-    other[:3] = [mate(piece) for piece in next_one[:3]]
-    low = [next_one[0], other[0], next_one[1], other[1]]
-    high = [next_one[2], other[2]]
-    made, buffer = far(place, buffer, below[:1], low + high, samples)
-    top3 = send(made, down)
-    (buffer,) = hold((below[1],), buffer)
-    made, buffer = far(
-        place, buffer, below[1:], low + high + [whole, whole_other], samples, False, (), width // 2
-    )
-    bottom = send(made, down)
-    (next_one[3],) = hold((made, top3), next_one[3])
-    buffer = tile(place, buffer, 1, 0, rows, low, samples, width)
-    other[3] = mate(next_one[3])
-    made, buffer = far(
-        place, buffer, below, [next_one[3], other[3]], samples
-    )
-    side = send(made, down)
-    buffer = tile(
-        place, buffer, 2, 0, rows, [above[0], mate(above[0]), above[1], mate(above[1])],
-        samples, width,
-    )
-    buffer = tile(place, buffer, 1, 1, rows, high + [next_one[3], other[3]], samples, width)
-    buffer = last(place, buffer, top2, top3, bottom, side)
+    above, buffer, swapped = choose(place, relayed, above, buffer)
+    next_relayed = send(swapped, swap)
+
+    (buffer,) = hold((below1, top2), buffer)
+    made, buffer = far(place, buffer, [below1], own, samples, first)
+    bottom2 = send(made, down)
+    (next_direct,) = hold((made,), next_direct)
+    high = [next_detoured, mate(next_detoured), next_direct, mate(next_direct)]
+    made, buffer = far(place, buffer, [below0, below1], high, samples)
+    wide3 = send(made, down)
+    (next_relayed,) = hold((made, bottom2), next_relayed)
+    low = [next_relayed, mate(next_relayed)]
+    made, buffer = far(place, buffer, [below0, below1], low, samples)
+    side3 = send(made, down)
+    buffer = tile(place, buffer, 1, 1, rows, high[:2], samples)
+    buffer = tile(place, buffer, 1, 1, rows, high[2:], samples)
+    buffer = tile(place, buffer, 1, 0, rows, low, samples)
+    buffer = tile(place, buffer, 2, 0, rows, [above, mate(above)], samples)
+    buffer = last(place, buffer, top2, bottom2, wide3, side3)
     return buffer[None]
 
 

time: 117 us -> 113 us (0.966)
  starting transfers between devices: 26.8 us -> 22.2 us
    ppermute x13 -> x11, starting transfers between devices: 24.1 us -> 19.7 us  [send(): return lax.ppermute(shard, 'var', pairs)]
    ppermute x13 -> x11, waiting for transfers between devices: 60.5 us -> 59.1 us  [send(): return lax.ppermute(shard, 'var', pairs)]
    pallas_call x9 -> x11, Pallas kernels: 17.8 us -> 19 us  [the longest x5 12.3 us: tile(): pl.pallas_call(functools.partial(tile_kernel, k, len(rows), len(rights),...]
    ppermute x9 -> x8, waiting for transfers between devices: 2.68 us -> 3.16 us  [mate(): return lax.ppermute(shard, 'samp', [(0, 1), (1, 0)])]
    ppermute x9 -> x8, starting transfers between devices: 2.64 us -> 2.58 us  [mate(): return lax.ppermute(shard, 'samp', [(0, 1), (1, 0)])]
  transfers between devices with their start and end apart: 22 -> 19, of which waited for: 14 -> 10; matrix products, arithmetic and copies ran while one was open for 0% -> 0% of each run, Pallas kernels for 16% -> 18%
where the time goes in v5:
time: 113 us
  waiting for transfers between devices  62.2 us (55%)
  Pallas kernels  27 us (24%)
  starting transfers between devices  22.2 us (20%)
    ppermute x11, waiting for transfers between devices, send(): return lax.ppermute(shard, 'var', pairs)  59.1 us
    ppermute x11, starting transfers between devices, send(): return lax.ppermute(shard, 'var', pairs)  19.7 us
    pallas_call x5, Pallas kernels, tile(): pl.pallas_call(functools.partial(tile_kernel, k, len(rows), len(rights),...  12.3 us
    pallas_call x4, Pallas kernels, far(): pl.pallas_call(functools.partial(far_kernel, 1.0 / samples, len(rows), le...  6.6 us
    ppermute x8, waiting for transfers between devices, mate(): return lax.ppermute(shard, 'samp', [(0, 1), (1, 0)])  3.16 us
    pallas_call x1, Pallas kernels, stats(): pl.pallas_call(stats_kernel, in_specs=[pl.BlockSpec(memory_space=pltpu.HB...  3.08 us
    ppermute x8, starting transfers between devices, mate(): return lax.ppermute(shard, 'samp', [(0, 1), (1, 0)])  2.58 us
  transfers between devices with their start and end apart: 19, of which 10 were waited for; matrix products, arithmetic and copies ran while one was open for 0% of the time, Pallas kernels for 18%

profile of v5, /device:TPU:0, one launch (start us, length us, event | category | flops | bytes accessed | tf_op | source)
XLA Modules:
  0.0 112.6 jit_solution(11026605862060008387)
XLA Ops:
  0.0 3.1 %shard_map.37 = (f32[8,1024]{1,0:T(8,128)S(1)}, bf16[1024,1024]{1,0:T(8,128)(2,1)S(1)}) custom-call(bf16[1024,1024]{1,0:T(8,128)(2,1)} %dosage_hbm.1, s32[1024,1024]{1,0:T(8,128)} %observed_hbm.1), custom_call_target="tpu_custom_call" | custom-call | flops 1000 | bytes 1000 | tf_op jit(solution)/shard_map/pallas_call | solution.py:59
  3.1 0.5 collective-permute-start
  4.3 0.1 pad_add_fusion.place_ref.refs_0_
  4.3 0.1 collective-permute-done.sums_other_ref
  4.5 1.9 %shard_map.38 = (bf16[1024,256]{1,0:T(8,128)(2,1)S(1)}, bf16[1024,256]{1,0:T(8,128)(2,1)S(1)}, bf16[1024,512]{1,0:T(8,128)(2,1)S(1)}, bf16[1024,1024]{1,0:T(8,12...) custom-call(s32[3]{0:T(128)S(1)} %pad_add_fusion.place_ref.refs_0_, ...), custom_call_target="tpu_custom_call" | custom-call | flops 1000 | bytes 1000 | tf_op jit(solution)/shard_map/pallas_call | solution.py:115
  6.4 0.4 collective-permute-start.3
  6.8 0.2 collective-permute-start.1
  7.0 0.4 collective-permute-start.6
  7.3 2.7 %collective-permute-start.4 = (bf16[1024,256]{1,0:T(8,128)(2,1)S(1)}, bf16[1024,256]{1,0:T(8,128)(2,1)S(1)}, u32[]{:S(2)}, u32[]{:S(2)}) collective-permute-start(bf16[1024,256]{1,0:T(8,128)(2,1)S(1)} %get-tuple-element.36), channel_id=1, source_target_pairs={{2,0},{6,4},{10,8},{14,12},{0,2},{4,6},{8,10},{12,14},{3,1},{7,5},... | collective-permute-start | bytes 1572872 | tf_op jit(solution)/shard_map/ppermute | solution.py:318
  10.0 1.4 %collective-permute-done.1.arrived_ref = bf16[256,1024]{1,0:T(8,128)(2,1)S(1)} collective-permute-done((bf16[256,1024]{1,0:T(8,128)(2,1)S(1)}, bf16[256,1024]{1,0:T(8,128)(2,1)S(1)}, u32[]{:S(2)}, u32[]{:S(2)}) %collective-permute-start.1) | collective-permute-done | bytes 524320 | tf_op jit(solution)/shard_map/ppermute | solution.py:328
  11.3 0.1 shard_map.39
  11.4 4.9 %collective-permute-start.2 = (bf16[512,1024]{1,0:T(8,128)(2,1)S(1)}, bf16[512,1024]{1,0:T(8,128)(2,1)S(1)}, u32[]{:S(2)}, u32[]{:S(2)}) collective-permute-start(bf16[512,1024]{1,0:T(8,128)(2,1)S(1)} %get-tuple-element.34.refs_0_), channel_id=1, source_target_pairs={{0,4},{2,6},{4,8},{6,10},{8,12},{10,14},{1,5},{3,7},{5,9},{7,11},{... | collective-permute-start | bytes 3145736 | tf_op jit(solution)/shard_map/ppermute | solution.py:318
  16.3 0.0 collective-permute-done.6.arrived_ref
  16.3 0.1 shard_map.40.refs_1_
  16.4 3.5 %collective-permute-start.8 = (bf16[512,1024]{1,0:T(8,128)(2,1)S(1)}, bf16[512,1024]{1,0:T(8,128)(2,1)S(1)}, u32[]{:S(2)}, u32[]{:S(2)}) collective-permute-start(bf16[512,1024]{1,0:T(8,128)(2,1)S(1)} %shard_map.40.refs_1_), channel_id=1, source_target_pairs={{0,4},{2,6},{4,8},{6,10},{8,12},{10,14},{1,5},{3,7},{5,9},{7,11},{... | collective-permute-start | bytes 3145736 | tf_op jit(solution)/shard_map/ppermute | solution.py:318
  19.9 1.3 %collective-permute-start.12 = (bf16[1024,512]{1,0:T(8,128)(2,1)S(1)}, bf16[1024,512]{1,0:T(8,128)(2,1)S(1)}, u32[]{:S(2)}, u32[]{:S(2)}) collective-permute-start(bf16[1024,512]{1,0:T(8,128)(2,1)S(1)} %get-tuple-element.47), channel_id=1, source_target_pairs={{2,0},{4,2},{6,4},{8,6},{10,8},{12,10},{14,12},{3,1},{5,3},{7,5},{... | collective-permute-start | bytes 3145736 | tf_op jit(solution)/shard_map/ppermute | solution.py:318
  21.2 1.2 %collective-permute-done.4.even_ref = bf16[1024,256]{1,0:T(8,128)(2,1)S(1)} collective-permute-done((bf16[1024,256]{1,0:T(8,128)(2,1)S(1)}, bf16[1024,256]{1,0:T(8,128)(2,1)S(1)}, u32[]{:S(2)}, u32[]{:S(2)}) %collective-permute-start.4) | collective-permute-done | bytes 524320 | tf_op jit(solution)/shard_map/ppermute | solution.py:318
  22.4 0.7 collective-permute-start.5
  23.1 0.0 collective-permute-done.3.refs_3_.refs_2_
  23.1 1.3 %collective-permute-start.9 = (bf16[1024,256]{1,0:T(8,128)(2,1)S(1)}, bf16[1024,256]{1,0:T(8,128)(2,1)S(1)}, u32[]{:S(2)}, u32[]{:S(2)}) collective-permute-start(bf16[1024,256]{1,0:T(8,128)(2,1)S(1)} %get-tuple-element.42.odd_ref), channel_id=1, source_target_pairs={{4,0},{6,2},{8,4},{10,6},{12,8},{14,10},{5,1},{7,3},{9,5},{11,7},{... | collective-permute-start | bytes 1572872 | tf_op jit(solution)/shard_map/ppermute | solution.py:318
  24.4 3.9 %shard_map.41.refs_0_ = bf16[4,512,1024]{2,1,0:T(8,128)(2,1)} custom-call(s32[3]{0:T(128)S(1)} %pad_add_fusion.place_ref.refs_0_, bf16[512,1024]{1,0:T(8,128)(2,1)S(1)} %get-tuple-element.34.refs_0_, bf16[512,1024]{1,0:T(8,128)(2,1)S(1)} %shard_map.40.refs_1_, ...), custom_call_target="tpu_custom_call", output_to_operand_aliasing={{}: (5, {})} | custom-call | flops 1000 | bytes 1000 | tf_op jit(solution)/shard_map/pallas_call | solution.py:183
  28.3 0.0 collective-permute-done.5.odd_ref
  28.3 0.6 shard_map.42
  28.9 10.9 %collective-permute-done.2.refs_0_ = bf16[512,1024]{1,0:T(8,128)(2,1)S(1)} collective-permute-done((bf16[512,1024]{1,0:T(8,128)(2,1)S(1)}, bf16[512,1024]{1,0:T(8,128)(2,1)S(1)}, u32[]{:S(2)}, u32[]{:S(2)}) %collective-permute-start.2) | collective-permute-done | bytes 1048608 | tf_op jit(solution)/shard_map/ppermute | solution.py:318
  39.8 1.5 %shard_map.44 = (bf16[256,768]{1,0:T(8,128)(2,1)S(1)}, bf16[4,512,1024]{2,1,0:T(8,128)(2,1)}) custom-call(s32[3]{0:T(128)S(1)} %pad_add_fusion.place_ref.refs_0_, bf16[512,1024]{1,0:T(8,128)(2,1)S(1)} %collective-permute-done.2.refs_0_, bf16[1024,1024]{1,0:T(8,128)(2,1)S(1)} %get-tuple-element.35.refs_2_.refs_1_, ...), custom_call_target="tpu_custom_call", output_to_operand_aliasing={{1}: (4, {})} | custom-call | flops 1000 | bytes 1000 | tf_op jit(solution)/shard_map/pallas_call | solution.py:207
  41.3 1.3 %collective-permute-start.7 = (bf16[256,768]{1,0:T(8,128)(2,1)S(1)}, bf16[256,768]{1,0:T(8,128)(2,1)S(1)}, u32[]{:S(2)}, u32[]{:S(2)}) collective-permute-start(bf16[256,768]{1,0:T(8,128)(2,1)S(1)} %get-tuple-element.41), channel_id=1, source_target_pairs={{4,0},{6,2},{8,4},{10,6},{12,8},{14,10},{5,1},{7,3},{9,5},{11,7},{... | collective-permute-start | bytes 1179656 | tf_op jit(solution)/shard_map/ppermute | solution.py:318
  42.6 17.5 %collective-permute-done.9.even_ref = bf16[1024,256]{1,0:T(8,128)(2,1)S(1)} collective-permute-done((bf16[1024,256]{1,0:T(8,128)(2,1)S(1)}, bf16[1024,256]{1,0:T(8,128)(2,1)S(1)}, u32[]{:S(2)}, u32[]{:S(2)}) %collective-permute-start.9) | collective-permute-done | bytes 524320 | tf_op jit(solution)/shard_map/ppermute | solution.py:318
  60.1 0.6 shard_map.45
  60.7 0.8 collective-permute-done.8.refs_0_.refs_1_
  61.5 5.6 %collective-permute-done.7.refs_1_ = bf16[256,768]{1,0:T(8,128)(2,1)S(1)} collective-permute-done((bf16[256,768]{1,0:T(8,128)(2,1)S(1)}, bf16[256,768]{1,0:T(8,128)(2,1)S(1)}, u32[]{:S(2)}, u32[]{:S(2)}) %collective-permute-start.7) | collective-permute-done | bytes 393248 | tf_op jit(solution)/shard_map/ppermute | solution.py:318
  67.1 1.5 %shard_map.47 = (bf16[256,768]{1,0:T(8,128)(2,1)S(1)}, bf16[4,512,1024]{2,1,0:T(8,128)(2,1)}) custom-call(s32[3]{0:T(128)S(1)} %pad_add_fusion.place_ref.refs_0_, bf16[512,1024]{1,0:T(8,128)(2,1)S(1)} %collective-permute-done.8.refs_0_.refs_1_, bf16[1024,1024]{1,0:T(8,128)(2,1)S(1)} %get-tuple-element.35.refs_2_.refs_1_, ...), custom_call_target="tpu_custom_call", output_to_operand_aliasing={{1}: (4, {})} | custom-call | flops 1000 | bytes 1000 | tf_op jit(solution)/shard_map/pallas_call | solution.py:207
  68.6 0.0 collective-permute-done.12.refs_1_
  68.6 0.1 collective-permute-start.13
  68.7 0.5 collective-permute-start.11
  69.2 0.0 collective-permute-start.15
  69.2 1.3 %collective-permute-start.10 = (bf16[256,768]{1,0:T(8,128)(2,1)S(1)}, bf16[256,768]{1,0:T(8,128)(2,1)S(1)}, u32[]{:S(2)}, u32[]{:S(2)}) collective-permute-start(bf16[256,768]{1,0:T(8,128)(2,1)S(1)} %get-tuple-element.45.refs_0_), channel_id=1, source_target_pairs={{4,0},{6,2},{8,4},{10,6},{12,8},{14,10},{5,1},{7,3},{9,5},{11,7},{... | collective-permute-start | bytes 1179656 | tf_op jit(solution)/shard_map/ppermute | solution.py:318
  70.5 1.6 %collective-permute-done.11.refs_3_ = bf16[1024,256]{1,0:T(8,128)(2,1)S(1)} collective-permute-done((bf16[1024,256]{1,0:T(8,128)(2,1)S(1)}, bf16[1024,256]{1,0:T(8,128)(2,1)S(1)}, u32[]{:S(2)}, u32[]{:S(2)}) %collective-permute-start.11) | collective-permute-done | bytes 524320 | tf_op jit(solution)/shard_map/ppermute | solution.py:328
  72.1 0.0 collective-permute-done.13.refs_5_.refs_3_
  72.1 2.3 %shard_map.49 = (bf16[512,768]{1,0:T(8,128)(2,1)S(1)}, bf16[4,512,1024]{2,1,0:T(8,128)(2,1)}) custom-call(s32[3]{0:T(128)S(1)} %pad_add_fusion.place_ref.refs_0_, bf16[512,1024]{1,0:T(8,128)(2,1)S(1)} %collective-permute-done.2.refs_0_, bf16[512,1024]{1,0:T(8,128)(2,1)S(1)} %collective-permute-done.8.refs_0_.refs_1_, ...), custom_call_target="tpu_custom_call", output_to_operand_aliasing={{1}: (7, {})} | custom-call | flops 1000 | bytes 1000 | tf_op jit(solution)/shard_map/pallas_call | solution.py:207
  74.4 8.7 %collective-permute-done.15.refs_2_ = bf16[1024,256]{1,0:T(8,128)(2,1)S(1)} collective-permute-done((bf16[1024,256]{1,0:T(8,128)(2,1)S(1)}, bf16[1024,256]{1,0:T(8,128)(2,1)S(1)}, u32[]{:S(2)}, u32[]{:S(2)}) %collective-permute-start.15) | collective-permute-done | bytes 524320 | tf_op jit(solution)/shard_map/ppermute | solution.py:318
  83.1 0.0 collective-permute-done.10.refs_1_.refs_2_
  83.1 0.0 collective-permute-start.16
  83.1 1.3 %collective-permute-start.14 = (bf16[512,768]{1,0:T(8,128)(2,1)S(1)}, bf16[512,768]{1,0:T(8,128)(2,1)S(1)}, u32[]{:S(2)}, u32[]{:S(2)}) collective-permute-start(bf16[512,768]{1,0:T(8,128)(2,1)S(1)} %get-tuple-element.49.refs_0_), channel_id=1, source_target_pairs={{4,0},{6,2},{8,4},{10,6},{12,8},{14,10},{5,1},{7,3},{9,5},{11,7},{... | collective-permute-start | bytes 2359304 | tf_op jit(solution)/shard_map/ppermute | solution.py:318
  84.4 0.6 collective-permute-start.18
  85.0 0.0 collective-permute-done.16.refs_3_
  85.0 1.2 %shard_map.51 = (bf16[512,256]{1,0:T(8,128)(2,1)S(1)}, bf16[4,512,1024]{2,1,0:T(8,128)(2,1)}) custom-call(s32[3]{0:T(128)S(1)} %pad_add_fusion.place_ref.refs_0_, bf16[512,1024]{1,0:T(8,128)(2,1)S(1)} %collective-permute-done.2.refs_0_, bf16[512,1024]{1,0:T(8,128)(2,1)S(1)} %collective-permute-done.8.refs_0_.refs_1_, ...), custom_call_target="tpu_custom_call", output_to_operand_aliasing={{1}: (5, {})} | custom-call | flops 1000 | bytes 1000 | tf_op jit(solution)/shard_map/pallas_call | solution.py:207
  86.3 1.5 %collective-permute-start.17 = (bf16[512,256]{1,0:T(8,128)(2,1)S(1)}, bf16[512,256]{1,0:T(8,128)(2,1)S(1)}, u32[]{:S(2)}, u32[]{:S(2)}) collective-permute-start(bf16[512,256]{1,0:T(8,128)(2,1)S(1)} %get-tuple-element.52), channel_id=1, source_target_pairs={{4,0},{6,2},{8,4},{10,6},{12,8},{14,10},{5,1},{7,3},{9,5},{11,7},{... | collective-permute-start | bytes 786440 | tf_op jit(solution)/shard_map/ppermute | solution.py:318
  87.8 2.0 %shard_map.52.refs_4_ = bf16[4,512,1024]{2,1,0:T(8,128)(2,1)} custom-call(s32[3]{0:T(128)S(1)} %pad_add_fusion.place_ref.refs_0_, bf16[512,1024]{1,0:T(8,128)(2,1)S(1)} %get-tuple-element.34.refs_0_, bf16[512,1024]{1,0:T(8,128)(2,1)S(1)} %shard_map.40.refs_1_, bf16[1024,256]{1,0:T(8,128)(2,1)S(1)} %get-tuple-element.46.refs_2_, ...), custom_call_target="tpu_custom_call", output_to_operand_aliasing={{}: (5, {})} | custom-call | flops 1000 | bytes 1000 | tf_op jit(solution)/shard_map/pallas_call | solution.py:183
  89.7 2.6 %shard_map.53.refs_4_ = bf16[4,512,1024]{2,1,0:T(8,128)(2,1)} custom-call(s32[3]{0:T(128)S(1)} %pad_add_fusion.place_ref.refs_0_, bf16[512,1024]{1,0:T(8,128)(2,1)S(1)} %get-tuple-element.34.refs_0_, bf16[512,1024]{1,0:T(8,128)(2,1)S(1)} %shard_map.40.refs_1_, bf16[1024,512]{1,0:T(8,128)(2,1)S(1)} %shard_map.48.refs_4_.refs_2_, ...), custom_call_target="tpu_custom_call", output_to_operand_aliasing={{}: (5, {})} | custom-call | flops 1000 | bytes 1000 | tf_op jit(solution)/shard_map/pallas_call | solution.py:183
  92.3 2.0 %shard_map.54.refs_4_ = bf16[4,512,1024]{2,1,0:T(8,128)(2,1)} custom-call(s32[3]{0:T(128)S(1)} %pad_add_fusion.place_ref.refs_0_, bf16[512,1024]{1,0:T(8,128)(2,1)S(1)} %get-tuple-element.34.refs_0_, bf16[512,1024]{1,0:T(8,128)(2,1)S(1)} %shard_map.40.refs_1_, bf16[1024,256]{1,0:T(8,128)(2,1)S(1)} %shard_map.50.refs_2_, ...), custom_call_target="tpu_custom_call", output_to_operand_aliasing={{}: (5, {})} | custom-call | flops 1000 | bytes 1000 | tf_op jit(solution)/shard_map/pallas_call | solution.py:183
  94.3 0.0 collective-permute-done.18.refs_3_
  94.3 2.0 %shard_map.55.refs_5_ = bf16[4,512,1024]{2,1,0:T(8,128)(2,1)} custom-call(s32[3]{0:T(128)S(1)} %pad_add_fusion.place_ref.refs_0_, bf16[512,1024]{1,0:T(8,128)(2,1)S(1)} %get-tuple-element.34.refs_0_, bf16[512,1024]{1,0:T(8,128)(2,1)S(1)} %shard_map.40.refs_1_, bf16[1024,256]{1,0:T(8,128)(2,1)S(1)} %get-tuple-element.53.refs_2_, ...), custom_call_target="tpu_custom_call", output_to_operand_aliasing={{}: (5, {})} | custom-call | flops 1000 | bytes 1000 | tf_op jit(solution)/shard_map/pallas_call | solution.py:183
  96.2 14.4 %collective-permute-done.17.refs_4_ = bf16[512,256]{1,0:T(8,128)(2,1)S(1)} collective-permute-done((bf16[512,256]{1,0:T(8,128)(2,1)S(1)}, bf16[512,256]{1,0:T(8,128)(2,1)S(1)}, u32[]{:S(2)}, u32[]{:S(2)}) %collective-permute-start.17) | collective-permute-done | bytes 262176 | tf_op jit(solution)/shard_map/ppermute | solution.py:318
  110.6 0.0 collective-permute-done.14.refs_3_
  110.6 1.8 %shard_map.56 = bf16[4,512,1024]{2,1,0:T(8,128)(2,1)} custom-call(s32[3]{0:T(128)S(1)} %pad_add_fusion.place_ref.refs_0_, bf16[256,768]{1,0:T(8,128)(2,1)S(1)} %collective-permute-done.7.refs_1_, bf16[256,768]{1,0:T(8,128)(2,1)S(1)} %collective-permute-done.10.refs_1_.refs_2_, ...), custom_call_target="tpu_custom_call", output_to_operand_aliasing={{}: (5, {})} | custom-call | flops 1000 | bytes 1000 | tf_op jit(solution)/shard_map/pallas_call | solution.py:289
  (4 shorter events, 0.0 us)
Async XLA Ops:
  3.1 1.4 %collective-permute-start = (f32[8,1024]{1,0:T(8,128)S(1)}, f32[8,1024]{1,0:T(8,128)S(1)}, u32[]{:S(2)}, u32[]{:S(2)}) collective-permute-start(f32[8,1024]{1,0:T(8,128)S(1)} %get-tuple-element.31.sums_ref), channel_id=1, source_target_pairs={{0,1},{1,0},{2,3},{3,2},{4,5},{5,4},{6,7},{7,6},{8,9},{9,8},{10,11... | collective-permute-start | bytes 98312 | tf_op jit(solution)/shard_map/ppermute | solution.py:328
  6.4 16.7 %collective-permute-start.3 = (bf16[1024,1024]{1,0:T(8,128)(2,1)S(1)}, bf16[1024,1024]{1,0:T(8,128)(2,1)S(1)}, u32[]{:S(2)}, u32[]{:S(2)}) collective-permute-start(bf16[1024,1024]{1,0:T(8,128)(2,1)S(1)} %get-tuple-element.35.refs_2_.refs_1_), channel_id=1, source_target_pairs={{0,1},{1,0},{2,3},{3,2},{4,5},{5,4},{6,7},{7,6},{8,9},{9,8},{10,11... | collective-permute-start | bytes 6291464 | tf_op jit(solution)/shard_map/ppermute | solution.py:328
  6.8 4.6 %collective-permute-start.1 = (bf16[256,1024]{1,0:T(8,128)(2,1)S(1)}, bf16[256,1024]{1,0:T(8,128)(2,1)S(1)}, u32[]{:S(2)}, u32[]{:S(2)}) collective-permute-start(bf16[256,1024]{1,0:T(8,128)(2,1)S(1)} %get-tuple-element.33), channel_id=1, source_target_pairs={{0,1},{1,0},{2,3},{3,2},{4,5},{5,4},{6,7},{7,6},{8,9},{9,8},{10,11... | collective-permute-start | bytes 1572872 | tf_op jit(solution)/shard_map/ppermute | solution.py:328
  7.0 9.4 %collective-permute-start.6 = (bf16[256,1024]{1,0:T(8,128)(2,1)S(1)}, bf16[256,1024]{1,0:T(8,128)(2,1)S(1)}, u32[]{:S(2)}, u32[]{:S(2)}) collective-permute-start(bf16[256,1024]{1,0:T(8,128)(2,1)S(1)} %get-tuple-element.38), channel_id=1, source_target_pairs={{0,1},{1,0},{2,3},{3,2},{4,5},{5,4},{6,7},{7,6},{8,9},{9,8},{10,11... | collective-permute-start | bytes 1572872 | tf_op jit(solution)/shard_map/ppermute | solution.py:328
  7.3 15.1 %collective-permute-start.4 = (bf16[1024,256]{1,0:T(8,128)(2,1)S(1)}, bf16[1024,256]{1,0:T(8,128)(2,1)S(1)}, u32[]{:S(2)}, u32[]{:S(2)}) collective-permute-start(bf16[1024,256]{1,0:T(8,128)(2,1)S(1)} %get-tuple-element.36), channel_id=1, source_target_pairs={{2,0},{6,4},{10,8},{14,12},{0,2},{4,6},{8,10},{12,14},{3,1},{7,5},... | collective-permute-start | bytes 1572872 | tf_op jit(solution)/shard_map/ppermute | solution.py:318
  11.4 28.3 %collective-permute-start.2 = (bf16[512,1024]{1,0:T(8,128)(2,1)S(1)}, bf16[512,1024]{1,0:T(8,128)(2,1)S(1)}, u32[]{:S(2)}, u32[]{:S(2)}) collective-permute-start(bf16[512,1024]{1,0:T(8,128)(2,1)S(1)} %get-tuple-element.34.refs_0_), channel_id=1, source_target_pairs={{0,4},{2,6},{4,8},{6,10},{8,12},{10,14},{1,5},{3,7},{5,9},{7,11},{... | collective-permute-start | bytes 3145736 | tf_op jit(solution)/shard_map/ppermute | solution.py:318
  16.4 45.0 %collective-permute-start.8 = (bf16[512,1024]{1,0:T(8,128)(2,1)S(1)}, bf16[512,1024]{1,0:T(8,128)(2,1)S(1)}, u32[]{:S(2)}, u32[]{:S(2)}) collective-permute-start(bf16[512,1024]{1,0:T(8,128)(2,1)S(1)} %shard_map.40.refs_1_), channel_id=1, source_target_pairs={{0,4},{2,6},{4,8},{6,10},{8,12},{10,14},{1,5},{3,7},{5,9},{7,11},{... | collective-permute-start | bytes 3145736 | tf_op jit(solution)/shard_map/ppermute | solution.py:318
  19.9 48.7 %collective-permute-start.12 = (bf16[1024,512]{1,0:T(8,128)(2,1)S(1)}, bf16[1024,512]{1,0:T(8,128)(2,1)S(1)}, u32[]{:S(2)}, u32[]{:S(2)}) collective-permute-start(bf16[1024,512]{1,0:T(8,128)(2,1)S(1)} %get-tuple-element.47), channel_id=1, source_target_pairs={{2,0},{4,2},{6,4},{8,6},{10,8},{12,10},{14,12},{3,1},{5,3},{7,5},{... | collective-permute-start | bytes 3145736 | tf_op jit(solution)/shard_map/ppermute | solution.py:318
  22.4 5.9 %collective-permute-start.5 = (bf16[1024,256]{1,0:T(8,128)(2,1)S(1)}, bf16[1024,256]{1,0:T(8,128)(2,1)S(1)}, u32[]{:S(2)}, u32[]{:S(2)}) collective-permute-start(bf16[1024,256]{1,0:T(8,128)(2,1)S(1)} %collective-permute-done.4.even_ref), channel_id=1, source_target_pairs={{6,2},{10,6},{14,10},{7,3},{11,7},{15,11},{22,18},{26,22},{30,26},... | collective-permute-start | bytes 1572872 | tf_op jit(solution)/shard_map/ppermute | solution.py:318
  23.1 37.0 %collective-permute-start.9 = (bf16[1024,256]{1,0:T(8,128)(2,1)S(1)}, bf16[1024,256]{1,0:T(8,128)(2,1)S(1)}, u32[]{:S(2)}, u32[]{:S(2)}) collective-permute-start(bf16[1024,256]{1,0:T(8,128)(2,1)S(1)} %get-tuple-element.42.odd_ref), channel_id=1, source_target_pairs={{4,0},{6,2},{8,4},{10,6},{12,8},{14,10},{5,1},{7,3},{9,5},{11,7},{... | collective-permute-start | bytes 1572872 | tf_op jit(solution)/shard_map/ppermute | solution.py:318
  41.3 25.8 %collective-permute-start.7 = (bf16[256,768]{1,0:T(8,128)(2,1)S(1)}, bf16[256,768]{1,0:T(8,128)(2,1)S(1)}, u32[]{:S(2)}, u32[]{:S(2)}) collective-permute-start(bf16[256,768]{1,0:T(8,128)(2,1)S(1)} %get-tuple-element.41), channel_id=1, source_target_pairs={{4,0},{6,2},{8,4},{10,6},{12,8},{14,10},{5,1},{7,3},{9,5},{11,7},{... | collective-permute-start | bytes 1179656 | tf_op jit(solution)/shard_map/ppermute | solution.py:318
  68.6 3.5 %collective-permute-start.13 = (bf16[1024,512]{1,0:T(8,128)(2,1)S(1)}, bf16[1024,512]{1,0:T(8,128)(2,1)S(1)}, u32[]{:S(2)}, u32[]{:S(2)}) collective-permute-start(bf16[1024,512]{1,0:T(8,128)(2,1)S(1)} %shard_map.48.refs_4_.refs_2_), channel_id=1, source_target_pairs={{0,1},{1,0},{2,3},{3,2},{4,5},{5,4},{6,7},{7,6},{8,9},{9,8},{10,11... | collective-permute-start | bytes 3145736 | tf_op jit(solution)/shard_map/ppermute | solution.py:328
  68.7 3.4 %collective-permute-start.11 = (bf16[1024,256]{1,0:T(8,128)(2,1)S(1)}, bf16[1024,256]{1,0:T(8,128)(2,1)S(1)}, u32[]{:S(2)}, u32[]{:S(2)}) collective-permute-start(bf16[1024,256]{1,0:T(8,128)(2,1)S(1)} %get-tuple-element.46.refs_2_), channel_id=1, source_target_pairs={{0,1},{1,0},{2,3},{3,2},{4,5},{5,4},{6,7},{7,6},{8,9},{9,8},{10,11... | collective-permute-start | bytes 1572872 | tf_op jit(solution)/shard_map/ppermute | solution.py:328
  69.2 13.9 %collective-permute-start.15 = (bf16[1024,256]{1,0:T(8,128)(2,1)S(1)}, bf16[1024,256]{1,0:T(8,128)(2,1)S(1)}, u32[]{:S(2)}, u32[]{:S(2)}) collective-permute-start(bf16[1024,256]{1,0:T(8,128)(2,1)S(1)} %get-tuple-element.50), channel_id=1, source_target_pairs={{2,0},{6,4},{10,8},{14,12},{0,2},{4,6},{8,10},{12,14},{3,1},{7,5},... | collective-permute-start | bytes 1572872 | tf_op jit(solution)/shard_map/ppermute | solution.py:318
  69.2 13.9 %collective-permute-start.10 = (bf16[256,768]{1,0:T(8,128)(2,1)S(1)}, bf16[256,768]{1,0:T(8,128)(2,1)S(1)}, u32[]{:S(2)}, u32[]{:S(2)}) collective-permute-start(bf16[256,768]{1,0:T(8,128)(2,1)S(1)} %get-tuple-element.45.refs_0_), channel_id=1, source_target_pairs={{4,0},{6,2},{8,4},{10,6},{12,8},{14,10},{5,1},{7,3},{9,5},{11,7},{... | collective-permute-start | bytes 1179656 | tf_op jit(solution)/shard_map/ppermute | solution.py:318
  83.1 1.9 %collective-permute-start.16 = (bf16[1024,256]{1,0:T(8,128)(2,1)S(1)}, bf16[1024,256]{1,0:T(8,128)(2,1)S(1)}, u32[]{:S(2)}, u32[]{:S(2)}) collective-permute-start(bf16[1024,256]{1,0:T(8,128)(2,1)S(1)} %shard_map.50.refs_2_), channel_id=1, source_target_pairs={{0,1},{1,0},{2,3},{3,2},{4,5},{5,4},{6,7},{7,6},{8,9},{9,8},{10,11... | collective-permute-start | bytes 1572872 | tf_op jit(solution)/shard_map/ppermute | solution.py:328
  83.1 27.5 %collective-permute-start.14 = (bf16[512,768]{1,0:T(8,128)(2,1)S(1)}, bf16[512,768]{1,0:T(8,128)(2,1)S(1)}, u32[]{:S(2)}, u32[]{:S(2)}) collective-permute-start(bf16[512,768]{1,0:T(8,128)(2,1)S(1)} %get-tuple-element.49.refs_0_), channel_id=1, source_target_pairs={{4,0},{6,2},{8,4},{10,6},{12,8},{14,10},{5,1},{7,3},{9,5},{11,7},{... | collective-permute-start | bytes 2359304 | tf_op jit(solution)/shard_map/ppermute | solution.py:318
  84.4 9.8 %collective-permute-start.18 = (bf16[1024,256]{1,0:T(8,128)(2,1)S(1)}, bf16[1024,256]{1,0:T(8,128)(2,1)S(1)}, u32[]{:S(2)}, u32[]{:S(2)}) collective-permute-start(bf16[1024,256]{1,0:T(8,128)(2,1)S(1)} %get-tuple-element.53.refs_2_), channel_id=1, source_target_pairs={{0,1},{1,0},{2,3},{3,2},{4,5},{5,4},{6,7},{7,6},{8,9},{9,8},{10,11... | collective-permute-start | bytes 1572872 | tf_op jit(solution)/shard_map/ppermute | solution.py:328
  86.3 24.3 %collective-permute-start.17 = (bf16[512,256]{1,0:T(8,128)(2,1)S(1)}, bf16[512,256]{1,0:T(8,128)(2,1)S(1)}, u32[]{:S(2)}, u32[]{:S(2)}) collective-permute-start(bf16[512,256]{1,0:T(8,128)(2,1)S(1)} %get-tuple-element.52), channel_id=1, source_target_pairs={{4,0},{6,2},{8,4},{10,6},{12,8},{14,10},{5,1},{7,3},{9,5},{11,7},{... | collective-permute-start | bytes 786440 | tf_op jit(solution)/shard_map/ppermute | solution.py:318

commit v6 on v5

--- a/solution.py
+++ b/solution.py
@@ -126,22 +126,24 @@
     )(place, masked, sums, sums_other)
 
 
-def stack_kernel(here_ref, arrived_ref, out_ref, *rest):
-    part = here_ref.shape[0]
-    out_ref[0:part, :] = here_ref[...]
-    out_ref[part:, :] = arrived_ref[...]
-
-
-def stack(here, arrived, *made):
+def stack(here, arrived, passed=(), unset=()):
     count, samples = here.shape
-    return pl.pallas_call(
-        stack_kernel,
-        in_specs=[VMEM, VMEM],
-        out_specs=[VMEM] + [ANY] * len(made),
-        out_shape=[jax.ShapeDtypeStruct((2 * count, samples), here.dtype), *made],
-        compiler_params=PARAMS,
-        cost_estimate=COST,
-    )(here, arrived)
+
+    def kernel(here_ref, arrived_ref, *refs):
+        out_ref = refs[len(passed)]
+        out_ref[0:count, :] = here_ref[...]
+        out_ref[count:, :] = arrived_ref[...]
+
+    return pl.pallas_call(
+        kernel,
+        in_specs=[VMEM, VMEM] + [ANY] * len(passed),
+        out_specs=[VMEM] + [ANY] * (len(passed) + len(unset)),
+        out_shape=[jax.ShapeDtypeStruct((2 * count, samples), here.dtype)]
+        + [jax.ShapeDtypeStruct(x.shape, x.dtype) for x in (*passed, *unset)],
+        input_output_aliases={2 + n: 1 + n for n in range(len(passed))},
+        compiler_params=PARAMS,
+        cost_estimate=COST,
+    )(here, arrived, *passed)
 
 
 def blocks(rows, rights, scale, skip=0):
@@ -258,28 +260,49 @@
     )(*after, *passed)
 
 
-def last_kernel(place_ref, top2, bottom2, wide3, side3, out_ref, two, three, sems):
+def split_kernel(count, whole_ref, *refs):
+    outs = refs[-count:]
+    begin = 0
+    for out in outs:
+        out[...] = whole_ref[:, begin : begin + out.shape[1]]
+        begin += out.shape[1]
+
+
+def split(piece, after, count):
+    samples, width = piece.shape
+    return pl.pallas_call(
+        functools.partial(split_kernel, count),
+        in_specs=[VMEM] + [ANY] * len(after),
+        out_specs=[VMEM] * count,
+        out_shape=[jax.ShapeDtypeStruct((samples, width // count), piece.dtype)] * count,
+        compiler_params=PARAMS,
+        cost_estimate=COST,
+    )(piece, *after)
+
+
+def last_kernel(place_ref, top2, top3, bottom, side, out_ref, two, three, sems):
     keep2, keep3 = 2 < place_ref[2], 3 < place_ref[2]
-    part = top2.shape[0]
-    first = side3.shape[1]
-
-    def kept(keep, ref):
-        return jnp.where(keep, ref[...], 0.0).astype(out_ref.dtype)
-
-    two[0:part, :] = kept(keep2, top2)
-    two[part:, :] = kept(keep2, bottom2)
+    part, wide = top2.shape
+    first = side.shape[1]
+
+    def kept(keep, block):
+        return jnp.where(keep, block, 0.0).astype(out_ref.dtype)
+
+    two[0:part, :] = kept(keep2, top2[...])
+    two[part:, :] = kept(keep2, bottom[:, wide:])
     copy2 = pltpu.make_async_copy(two, out_ref.at[2, :, first:], sems.at[0])
     copy2.start()
-    three[:, first:] = kept(keep3, wide3)
-    three[:, 0:first] = kept(keep3, side3)
+    three[0:part, first:] = kept(keep3, top3[...])
+    three[part:, first:] = kept(keep3, bottom[:, 0:wide])
+    three[:, 0:first] = kept(keep3, side[...])
     copy3 = pltpu.make_async_copy(three, out_ref.at[3], sems.at[1])
     copy3.start()
     copy2.wait()
     copy3.wait()
 
 
-def last(place, buffer, top2, bottom2, wide3, side3):
-    operands = [place, top2, bottom2, wide3, side3, buffer]
+def last(place, buffer, top2, top3, bottom, side):
+    operands = [place, top2, top3, bottom, side, buffer]
     count, width = buffer.shape[1:]
 
     def kernel(*refs):
@@ -334,7 +357,7 @@
     first = relayed.shape[1]
     unset = jax.ShapeDtypeStruct((WIN, width // 2, width), jnp.bfloat16)
 
-    upper, buffer = stack(here[0], mate(away[0]), unset)
+    upper, whole, buffer = stack(here[0], mate(away[0]), (whole,), (unset,))
     below0 = send(upper, up)
     above = send(relayed, down)
     across = send(detoured, swap)
@@ -343,32 +366,36 @@
     below1 = send(lower, up)
     rows = [upper, lower]
     own = [whole, mate(whole)]
-
     around = send(across, down_odd)
+
     buffer = tile(place, buffer, 0, 0, rows, own, samples)
-    across, buffer, next_detoured = choose(place, around, across, buffer)
     (buffer,) = hold((below0,), buffer)
     made, buffer = far(place, buffer, [below0], own, samples, first)
     top2 = send(made, down)
+    across, buffer, next_detoured = choose(place, around, across, buffer)
+    high = [next_detoured, mate(next_detoured)]
+    for piece in split(next_direct, (made,), 2):
+        high += [piece, mate(piece)]
+    (buffer,) = hold((top2,), buffer)
+    made, buffer = far(place, buffer, [below0], high, samples)
+    top3 = send(made, down)
+
+    (buffer,) = hold((below1,), buffer)
+    made, buffer = far(place, buffer, [below1], high + own, samples, first)
+    bottom = send(made, down)
+    (buffer,) = hold((top3,), buffer)
     above, buffer, swapped = choose(place, relayed, above, buffer)
     next_relayed = send(swapped, swap)
-
-    (buffer,) = hold((below1, top2), buffer)
-    made, buffer = far(place, buffer, [below1], own, samples, first)
-    bottom2 = send(made, down)
-    (next_direct,) = hold((made,), next_direct)
-    high = [next_detoured, mate(next_detoured), next_direct, mate(next_direct)]
-    made, buffer = far(place, buffer, [below0, below1], high, samples)
-    wide3 = send(made, down)
-    (next_relayed,) = hold((made, bottom2), next_relayed)
-    low = [next_relayed, mate(next_relayed)]
+    low = []
+    for piece in split(next_relayed, (), 2):
+        low += [piece, mate(piece)]
     made, buffer = far(place, buffer, [below0, below1], low, samples)
-    side3 = send(made, down)
+    side = send(made, down)
     buffer = tile(place, buffer, 1, 1, rows, high[:2], samples)
     buffer = tile(place, buffer, 1, 1, rows, high[2:], samples)
     buffer = tile(place, buffer, 1, 0, rows, low, samples)
     buffer = tile(place, buffer, 2, 0, rows, [above, mate(above)], samples)
-    buffer = last(place, buffer, top2, bottom2, wide3, side3)
+    buffer = last(place, buffer, top2, top3, bottom, side)
     return buffer[None]
 
 

time: 113 us -> 133 us (1.18)
  waiting for transfers between devices: 62.2 us -> 74.7 us
  starting transfers between devices: 22.2 us -> 28.9 us
    ppermute x11, waiting for transfers between devices: 59.1 us -> 71.7 us  [send(): return lax.ppermute(shard, 'var', pairs)]
    ppermute x11, starting transfers between devices: 19.7 us -> 26.1 us  [send(): return lax.ppermute(shard, 'var', pairs)]
    ppermute x8 -> x10, starting transfers between devices: 2.58 us -> 2.77 us  [mate(): return lax.ppermute(shard, 'samp', [(0, 1), (1, 0)])]
    ppermute x8 -> x10, waiting for transfers between devices: 3.16 us -> 3.02 us  [mate(): return lax.ppermute(shard, 'samp', [(0, 1), (1, 0)])]
  transfers between devices with their start and end apart: 19 -> 21, of which waited for: 10 -> 9; matrix products, arithmetic and copies ran while one was open for 0% -> 0% of each run, Pallas kernels for 18% -> 16%
where the time goes in v6:
time: 133 us
  waiting for transfers between devices  74.7 us (56%)
  starting transfers between devices  28.9 us (22%)
  Pallas kernels  28.3 us (21%)
    ppermute x11, waiting for transfers between devices, send(): return lax.ppermute(shard, 'var', pairs)  71.7 us
    ppermute x11, starting transfers between devices, send(): return lax.ppermute(shard, 'var', pairs)  26.1 us
    pallas_call x5, Pallas kernels, tile(): pl.pallas_call(functools.partial(tile_kernel, k, len(rows), len(rights),...  12.8 us
    pallas_call x4, Pallas kernels, far(): pl.pallas_call(functools.partial(far_kernel, 1.0 / samples, len(rows), le...  7.17 us
    pallas_call x1, Pallas kernels, stats(): pl.pallas_call(stats_kernel, in_specs=[pl.BlockSpec(memory_space=pltpu.HB...  3.08 us
    ppermute x10, waiting for transfers between devices, mate(): return lax.ppermute(shard, 'samp', [(0, 1), (1, 0)])  3.02 us
    ppermute x10, starting transfers between devices, mate(): return lax.ppermute(shard, 'samp', [(0, 1), (1, 0)])  2.77 us
  transfers between devices with their start and end apart: 21, of which 9 were waited for; matrix products, arithmetic and copies ran while one was open for 0% of the time, Pallas kernels for 16%

profile of v6, /device:TPU:0, one launch (start us, length us, event | category | flops | bytes accessed | tf_op | source)
XLA Modules:
  0.0 133.1 jit_solution(17571181231297925870)
XLA Ops:
  0.0 3.1 %shard_map.37 = (f32[8,1024]{1,0:T(8,128)S(1)}, bf16[1024,1024]{1,0:T(8,128)(2,1)S(1)}) custom-call(bf16[1024,1024]{1,0:T(8,128)(2,1)} %dosage_hbm.1, s32[1024,1024]{1,0:T(8,128)} %observed_hbm.1), custom_call_target="tpu_custom_call" | custom-call | flops 1000 | bytes 1000 | tf_op jit(solution)/shard_map/pallas_call | solution.py:59
  3.1 0.5 collective-permute-start
  4.3 0.1 pad_add_fusion.place_ref.refs_0_
  4.3 0.1 collective-permute-done.sums_other_ref
  4.5 1.9 %shard_map.38 = (bf16[1024,256]{1,0:T(8,128)(2,1)S(1)}, bf16[1024,256]{1,0:T(8,128)(2,1)S(1)}, bf16[1024,512]{1,0:T(8,128)(2,1)S(1)}, bf16[1024,1024]{1,0:T(8,12...) custom-call(s32[3]{0:T(128)S(1)} %pad_add_fusion.place_ref.refs_0_, ...), custom_call_target="tpu_custom_call" | custom-call | flops 1000 | bytes 1000 | tf_op jit(solution)/shard_map/pallas_call | solution.py:115
  6.4 0.4 collective-permute-start.1
  6.8 1.6 %collective-permute-done.1.arrived_ref = bf16[256,1024]{1,0:T(8,128)(2,1)S(1)} collective-permute-done((bf16[256,1024]{1,0:T(8,128)(2,1)S(1)}, bf16[256,1024]{1,0:T(8,128)(2,1)S(1)}, u32[]{:S(2)}, u32[]{:S(2)}) %collective-permute-start.1) | collective-permute-done | bytes 524320 | tf_op jit(solution)/shard_map/ppermute | solution.py:351
  8.4 0.1 shard_map.39
  8.4 0.4 collective-permute-start.3
  8.8 4.7 %collective-permute-start.2 = (bf16[512,1024]{1,0:T(8,128)(2,1)S(1)}, bf16[512,1024]{1,0:T(8,128)(2,1)S(1)}, u32[]{:S(2)}, u32[]{:S(2)}) collective-permute-start(bf16[512,1024]{1,0:T(8,128)(2,1)S(1)} %get-tuple-element.40.refs_0_), channel_id=1, source_target_pairs={{0,4},{2,6},{4,8},{6,10},{8,12},{10,14},{1,5},{3,7},{5,9},{7,11},{... | collective-permute-start | bytes 3145736 | tf_op jit(solution)/shard_map/ppermute | solution.py:341
  13.5 1.6 %collective-permute-start.6 = (bf16[1024,256]{1,0:T(8,128)(2,1)S(1)}, bf16[1024,256]{1,0:T(8,128)(2,1)S(1)}, u32[]{:S(2)}, u32[]{:S(2)}) collective-permute-start(bf16[1024,256]{1,0:T(8,128)(2,1)S(1)} %get-tuple-element.46), channel_id=1, source_target_pairs={{2,0},{6,4},{10,8},{14,12},{0,2},{4,6},{8,10},{12,14},{3,1},{7,5},... | collective-permute-start | bytes 1572872 | tf_op jit(solution)/shard_map/ppermute | solution.py:341
  15.1 1.3 collective-permute-start.9
  16.4 0.1 collective-permute-start.4
  16.5 32.5 %collective-permute-done.6.even_ref = bf16[1024,256]{1,0:T(8,128)(2,1)S(1)} collective-permute-done((bf16[1024,256]{1,0:T(8,128)(2,1)S(1)}, bf16[1024,256]{1,0:T(8,128)(2,1)S(1)}, u32[]{:S(2)}, u32[]{:S(2)}) %collective-permute-start.6) | collective-permute-done | bytes 524320 | tf_op jit(solution)/shard_map/ppermute | solution.py:341
  49.0 0.7 collective-permute-start.7
  49.7 0.0 collective-permute-done.4.arrived_ref
  49.7 0.1 shard_map.40.refs_1_
  49.8 3.5 %collective-permute-start.13 = (bf16[512,1024]{1,0:T(8,128)(2,1)S(1)}, bf16[512,1024]{1,0:T(8,128)(2,1)S(1)}, u32[]{:S(2)}, u32[]{:S(2)}) collective-permute-start(bf16[512,1024]{1,0:T(8,128)(2,1)S(1)} %shard_map.40.refs_1_), channel_id=1, source_target_pairs={{0,4},{2,6},{4,8},{6,10},{8,12},{10,14},{1,5},{3,7},{5,9},{7,11},{... | collective-permute-start | bytes 3145736 | tf_op jit(solution)/shard_map/ppermute | solution.py:341
  53.3 0.0 collective-permute-done.3.refs_3_.refs_2_.refs_8_
  53.3 3.9 %shard_map.41.refs_1_ = bf16[4,512,1024]{2,1,0:T(8,128)(2,1)} custom-call(s32[3]{0:T(128)S(1)} %pad_add_fusion.place_ref.refs_0_, bf16[512,1024]{1,0:T(8,128)(2,1)S(1)} %get-tuple-element.40.refs_0_, bf16[512,1024]{1,0:T(8,128)(2,1)S(1)} %shard_map.40.refs_1_, ...), custom_call_target="tpu_custom_call", output_to_operand_aliasing={{}: (5, {})} | custom-call | flops 1000 | bytes 1000 | tf_op jit(solution)/shard_map/pallas_call | solution.py:185
  57.1 0.0 collective-permute-done.2.refs_0_
  57.1 1.5 %shard_map.43 = (bf16[256,768]{1,0:T(8,128)(2,1)S(1)}, bf16[4,512,1024]{2,1,0:T(8,128)(2,1)}) custom-call(s32[3]{0:T(128)S(1)} %pad_add_fusion.place_ref.refs_0_, bf16[512,1024]{1,0:T(8,128)(2,1)S(1)} %collective-permute-done.2.refs_0_, bf16[1024,1024]{1,0:T(8,128)(2,1)S(1)} %get-tuple-element.41.refs_2_.refs_1_.refs_7_, ...), custom_call_target="tpu_custom_call", output_to_operand_aliasing={{1}: (4, {})} | custom-call | flops 1000 | bytes 1000 | tf_op jit(solution)/shard_map/pallas_call | solution.py:209
  58.7 0.0 collective-permute-done.7.odd_ref
  58.7 0.6 shard_map.44
  59.3 0.1 collective-permute-start.8
  59.4 0.0 collective-permute-done.9.whole_ref
  59.4 0.1 shard_map.45
  59.5 0.5 collective-permute-start.10
  60.0 0.1 collective-permute-start.11
  60.1 1.3 collective-permute-start.5
  61.4 12.1 %collective-permute-done.5.refs_0_.refs_1_ = bf16[256,768]{1,0:T(8,128)(2,1)S(1)} collective-permute-done((bf16[256,768]{1,0:T(8,128)(2,1)S(1)}, bf16[256,768]{1,0:T(8,128)(2,1)S(1)}, u32[]{:S(2)}, u32[]{:S(2)}) %collective-permute-start.5) | collective-permute-done | bytes 393248 | tf_op jit(solution)/shard_map/ppermute | solution.py:341
  73.4 1.3 collective-permute-start.15
  74.7 0.0 collective-permute-done.8.refs_2_.refs_3_
  74.7 0.0 collective-permute-done.10.refs_4_.refs_3_
  74.8 0.0 collective-permute-done.11.refs_6_.refs_5_
  74.8 1.5 %shard_map.47 = (bf16[256,768]{1,0:T(8,128)(2,1)S(1)}, bf16[4,512,1024]{2,1,0:T(8,128)(2,1)}) custom-call(s32[3]{0:T(128)S(1)} %pad_add_fusion.place_ref.refs_0_, bf16[512,1024]{1,0:T(8,128)(2,1)S(1)} %collective-permute-done.2.refs_0_, bf16[1024,256]{1,0:T(8,128)(2,1)S(1)} %get-tuple-element.48.refs_1_.refs_2_, ...), custom_call_target="tpu_custom_call", output_to_operand_aliasing={{1}: (8, {})} | custom-call | flops 1000 | bytes 1000 | tf_op jit(solution)/shard_map/pallas_call | solution.py:209
  76.3 1.3 collective-permute-start.12
  77.6 0.0 collective-permute-done.13.refs_0_.refs_1_
  77.6 2.3 %shard_map.49 = (bf16[256,1536]{1,0:T(8,128)(2,1)S(1)}, bf16[4,512,1024]{2,1,0:T(8,128)(2,1)}) custom-call(s32[3]{0:T(128)S(1)} %pad_add_fusion.place_ref.refs_0_, bf16[512,1024]{1,0:T(8,128)(2,1)S(1)} %collective-permute-done.13.refs_0_.refs_1_, bf16[1024,256]{1,0:T(8,128)(2,1)S(1)} %get-tuple-element.48.refs_1_.refs_2_, ...), custom_call_target="tpu_custom_call", output_to_operand_aliasing={{1}: (10, {})} | custom-call | flops 1000 | bytes 1000 | tf_op jit(solution)/shard_map/pallas_call | solution.py:209
  80.0 17.3 %collective-permute-done.12.refs_0_.refs_2_ = bf16[256,768]{1,0:T(8,128)(2,1)S(1)} collective-permute-done((bf16[256,768]{1,0:T(8,128)(2,1)S(1)}, bf16[256,768]{1,0:T(8,128)(2,1)S(1)}, u32[]{:S(2)}, u32[]{:S(2)}) %collective-permute-start.12) | collective-permute-done | bytes 393248 | tf_op jit(solution)/shard_map/ppermute | solution.py:341
  97.2 0.0 collective-permute-done.15.even_ref
  97.2 0.6 shard_map.51
  97.8 7.8 %collective-permute-start.16 = (bf16[1024,256]{1,0:T(8,128)(2,1)S(1)}, bf16[1024,256]{1,0:T(8,128)(2,1)S(1)}, u32[]{:S(2)}, u32[]{:S(2)}) collective-permute-start(bf16[1024,256]{1,0:T(8,128)(2,1)S(1)} %get-tuple-element.58), channel_id=1, source_target_pairs={{2,0},{6,4},{10,8},{14,12},{0,2},{4,6},{8,10},{12,14},{3,1},{7,5},... | collective-permute-start | bytes 1572872 | tf_op jit(solution)/shard_map/ppermute | solution.py:341
  105.6 1.3 collective-permute-start.14
  106.9 9.6 %collective-permute-done.16.whole_ref = bf16[1024,256]{1,0:T(8,128)(2,1)S(1)} collective-permute-done((bf16[1024,256]{1,0:T(8,128)(2,1)S(1)}, bf16[1024,256]{1,0:T(8,128)(2,1)S(1)}, u32[]{:S(2)}, u32[]{:S(2)}) %collective-permute-start.16) | collective-permute-done | bytes 524320 | tf_op jit(solution)/shard_map/ppermute | solution.py:341
  116.5 0.1 shard_map.52
  116.6 0.1 collective-permute-start.17
  116.6 0.5 collective-permute-start.18
  117.1 0.1 collective-permute-start.20
  117.2 0.9 collective-permute-done.17.refs_3_
  118.2 0.4 collective-permute-done.18.refs_5_
  118.5 1.8 %shard_map.53 = (bf16[512,256]{1,0:T(8,128)(2,1)S(1)}, bf16[4,512,1024]{2,1,0:T(8,128)(2,1)}) custom-call(s32[3]{0:T(128)S(1)} %pad_add_fusion.place_ref.refs_0_, bf16[512,1024]{1,0:T(8,128)(2,1)S(1)} %collective-permute-done.2.refs_0_, bf16[512,1024]{1,0:T(8,128)(2,1)S(1)} %collective-permute-done.13.refs_0_.refs_1_, ...), custom_call_target="tpu_custom_call", output_to_operand_aliasing={{1}: (7, {})} | custom-call | flops 1000 | bytes 1000 | tf_op jit(solution)/shard_map/pallas_call | solution.py:209
  120.3 1.5 %collective-permute-start.19 = (bf16[512,256]{1,0:T(8,128)(2,1)S(1)}, bf16[512,256]{1,0:T(8,128)(2,1)S(1)}, u32[]{:S(2)}, u32[]{:S(2)}) collective-permute-start(bf16[512,256]{1,0:T(8,128)(2,1)S(1)} %get-tuple-element.62), channel_id=1, source_target_pairs={{4,0},{6,2},{8,4},{10,6},{12,8},{14,10},{5,1},{7,3},{9,5},{11,7},{... | collective-permute-start | bytes 786440 | tf_op jit(solution)/shard_map/ppermute | solution.py:341
  121.8 2.0 %shard_map.54.refs_6_ = bf16[4,512,1024]{2,1,0:T(8,128)(2,1)} custom-call(s32[3]{0:T(128)S(1)} %pad_add_fusion.place_ref.refs_0_, bf16[512,1024]{1,0:T(8,128)(2,1)S(1)} %get-tuple-element.40.refs_0_, bf16[512,1024]{1,0:T(8,128)(2,1)S(1)} %shard_map.40.refs_1_, ...), custom_call_target="tpu_custom_call", output_to_operand_aliasing={{}: (5, {})} | custom-call | flops 1000 | bytes 1000 | tf_op jit(solution)/shard_map/pallas_call | solution.py:185
  123.8 2.6 %shard_map.55.refs_6_ = bf16[4,512,1024]{2,1,0:T(8,128)(2,1)} custom-call(s32[3]{0:T(128)S(1)} %pad_add_fusion.place_ref.refs_0_, bf16[512,1024]{1,0:T(8,128)(2,1)S(1)} %get-tuple-element.40.refs_0_, bf16[512,1024]{1,0:T(8,128)(2,1)S(1)} %shard_map.40.refs_1_, ...), custom_call_target="tpu_custom_call", output_to_operand_aliasing={{}: (7, {})} | custom-call | flops 1000 | bytes 1000 | tf_op jit(solution)/shard_map/pallas_call | solution.py:185
  126.4 2.5 %shard_map.56.refs_4_ = bf16[4,512,1024]{2,1,0:T(8,128)(2,1)} custom-call(s32[3]{0:T(128)S(1)} %pad_add_fusion.place_ref.refs_0_, bf16[512,1024]{1,0:T(8,128)(2,1)S(1)} %get-tuple-element.40.refs_0_, bf16[512,1024]{1,0:T(8,128)(2,1)S(1)} %shard_map.40.refs_1_, bf16[1024,128]{1,0:T(8,128)(2,1)S(1)} %get-tuple-element.59.refs_2_, ...), custom_call_target="tpu_custom_call", output_to_operand_aliasing={{}: (7, {})} | custom-call | flops 1000 | bytes 1000 | tf_op jit(solution)/shard_map/pallas_call | solution.py:185
  128.9 0.0 collective-permute-done.20.refs_3_
  128.9 2.0 %shard_map.57.refs_5_ = bf16[4,512,1024]{2,1,0:T(8,128)(2,1)} custom-call(s32[3]{0:T(128)S(1)} %pad_add_fusion.place_ref.refs_0_, bf16[512,1024]{1,0:T(8,128)(2,1)S(1)} %get-tuple-element.40.refs_0_, bf16[512,1024]{1,0:T(8,128)(2,1)S(1)} %shard_map.40.refs_1_, bf16[1024,256]{1,0:T(8,128)(2,1)S(1)} %get-tuple-element.63.refs_2_, ...), custom_call_target="tpu_custom_call", output_to_operand_aliasing={{}: (5, {})} | custom-call | flops 1000 | bytes 1000 | tf_op jit(solution)/shard_map/pallas_call | solution.py:185
  130.8 0.0 collective-permute-done.14.refs_3_
  130.8 0.2 collective-permute-done.19.refs_4_
  131.1 1.8 %shard_map.58 = bf16[4,512,1024]{2,1,0:T(8,128)(2,1)} custom-call(s32[3]{0:T(128)S(1)} %pad_add_fusion.place_ref.refs_0_, bf16[256,768]{1,0:T(8,128)(2,1)S(1)} %collective-permute-done.5.refs_0_.refs_1_, bf16[256,768]{1,0:T(8,128)(2,1)S(1)} %collective-permute-done.12.refs_0_.refs_2_, ...), custom_call_target="tpu_custom_call", output_to_operand_aliasing={{}: (5, {})} | custom-call | flops 1000 | bytes 1000 | tf_op jit(solution)/shard_map/pallas_call | solution.py:312
  (4 shorter events, 0.0 us)
Async XLA Ops:
  3.1 1.4 %collective-permute-start = (f32[8,1024]{1,0:T(8,128)S(1)}, f32[8,1024]{1,0:T(8,128)S(1)}, u32[]{:S(2)}, u32[]{:S(2)}) collective-permute-start(f32[8,1024]{1,0:T(8,128)S(1)} %get-tuple-element.36.sums_ref), channel_id=1, source_target_pairs={{0,1},{1,0},{2,3},{3,2},{4,5},{5,4},{6,7},{7,6},{8,9},{9,8},{10,11... | collective-permute-start | bytes 98312 | tf_op jit(solution)/shard_map/ppermute | solution.py:351
  6.4 2.0 %collective-permute-start.1 = (bf16[256,1024]{1,0:T(8,128)(2,1)S(1)}, bf16[256,1024]{1,0:T(8,128)(2,1)S(1)}, u32[]{:S(2)}, u32[]{:S(2)}) collective-permute-start(bf16[256,1024]{1,0:T(8,128)(2,1)S(1)} %get-tuple-element.38), channel_id=1, source_target_pairs={{0,1},{1,0},{2,3},{3,2},{4,5},{5,4},{6,7},{7,6},{8,9},{9,8},{10,11... | collective-permute-start | bytes 1572872 | tf_op jit(solution)/shard_map/ppermute | solution.py:351
  8.4 44.9 %collective-permute-start.3 = (bf16[1024,1024]{1,0:T(8,128)(2,1)S(1)}, bf16[1024,1024]{1,0:T(8,128)(2,1)S(1)}, u32[]{:S(2)}, u32[]{:S(2)}) collective-permute-start(bf16[1024,1024]{1,0:T(8,128)(2,1)S(1)} %get-tuple-element.41.refs_2_.refs_1_.refs_7_), channel_id=1, source_target_pairs={{0,1},{1,0},{2,3},{3,2},{4,5},{5,4},{6,7},{7,6},{8,9},{9,8},{10,11... | collective-permute-start | bytes 6291464 | tf_op jit(solution)/shard_map/ppermute | solution.py:351
  8.8 48.3 %collective-permute-start.2 = (bf16[512,1024]{1,0:T(8,128)(2,1)S(1)}, bf16[512,1024]{1,0:T(8,128)(2,1)S(1)}, u32[]{:S(2)}, u32[]{:S(2)}) collective-permute-start(bf16[512,1024]{1,0:T(8,128)(2,1)S(1)} %get-tuple-element.40.refs_0_), channel_id=1, source_target_pairs={{0,4},{2,6},{4,8},{6,10},{8,12},{10,14},{1,5},{3,7},{5,9},{7,11},{... | collective-permute-start | bytes 3145736 | tf_op jit(solution)/shard_map/ppermute | solution.py:341
  13.5 35.5 %collective-permute-start.6 = (bf16[1024,256]{1,0:T(8,128)(2,1)S(1)}, bf16[1024,256]{1,0:T(8,128)(2,1)S(1)}, u32[]{:S(2)}, u32[]{:S(2)}) collective-permute-start(bf16[1024,256]{1,0:T(8,128)(2,1)S(1)} %get-tuple-element.46), channel_id=1, source_target_pairs={{2,0},{6,4},{10,8},{14,12},{0,2},{4,6},{8,10},{12,14},{3,1},{7,5},... | collective-permute-start | bytes 1572872 | tf_op jit(solution)/shard_map/ppermute | solution.py:341
  15.1 44.2 %collective-permute-start.9 = (bf16[1024,512]{1,0:T(8,128)(2,1)S(1)}, bf16[1024,512]{1,0:T(8,128)(2,1)S(1)}, u32[]{:S(2)}, u32[]{:S(2)}) collective-permute-start(bf16[1024,512]{1,0:T(8,128)(2,1)S(1)} %get-tuple-element.49), channel_id=1, source_target_pairs={{2,0},{4,2},{6,4},{8,6},{10,8},{12,10},{14,12},{3,1},{5,3},{7,5},{... | collective-permute-start | bytes 3145736 | tf_op jit(solution)/shard_map/ppermute | solution.py:341
  16.4 33.3 %collective-permute-start.4 = (bf16[256,1024]{1,0:T(8,128)(2,1)S(1)}, bf16[256,1024]{1,0:T(8,128)(2,1)S(1)}, u32[]{:S(2)}, u32[]{:S(2)}) collective-permute-start(bf16[256,1024]{1,0:T(8,128)(2,1)S(1)} %get-tuple-element.43), channel_id=1, source_target_pairs={{0,1},{1,0},{2,3},{3,2},{4,5},{5,4},{6,7},{7,6},{8,9},{9,8},{10,11... | collective-permute-start | bytes 1572872 | tf_op jit(solution)/shard_map/ppermute | solution.py:351
  49.0 9.7 %collective-permute-start.7 = (bf16[1024,256]{1,0:T(8,128)(2,1)S(1)}, bf16[1024,256]{1,0:T(8,128)(2,1)S(1)}, u32[]{:S(2)}, u32[]{:S(2)}) collective-permute-start(bf16[1024,256]{1,0:T(8,128)(2,1)S(1)} %collective-permute-done.6.even_ref), channel_id=1, source_target_pairs={{6,2},{10,6},{14,10},{7,3},{11,7},{15,11},{22,18},{26,22},{30,26},... | collective-permute-start | bytes 1572872 | tf_op jit(solution)/shard_map/ppermute | solution.py:341
  49.8 27.8 %collective-permute-start.13 = (bf16[512,1024]{1,0:T(8,128)(2,1)S(1)}, bf16[512,1024]{1,0:T(8,128)(2,1)S(1)}, u32[]{:S(2)}, u32[]{:S(2)}) collective-permute-start(bf16[512,1024]{1,0:T(8,128)(2,1)S(1)} %shard_map.40.refs_1_), channel_id=1, source_target_pairs={{0,4},{2,6},{4,8},{6,10},{8,12},{10,14},{1,5},{3,7},{5,9},{7,11},{... | collective-permute-start | bytes 3145736 | tf_op jit(solution)/shard_map/ppermute | solution.py:341
  59.3 15.4 %collective-permute-start.8 = (bf16[1024,256]{1,0:T(8,128)(2,1)S(1)}, bf16[1024,256]{1,0:T(8,128)(2,1)S(1)}, u32[]{:S(2)}, u32[]{:S(2)}) collective-permute-start(bf16[1024,256]{1,0:T(8,128)(2,1)S(1)} %get-tuple-element.48.refs_1_.refs_2_), channel_id=1, source_target_pairs={{0,1},{1,0},{2,3},{3,2},{4,5},{5,4},{6,7},{7,6},{8,9},{9,8},{10,11... | collective-permute-start | bytes 1572872 | tf_op jit(solution)/shard_map/ppermute | solution.py:351
  59.5 15.3 %collective-permute-start.10 = (bf16[1024,256]{1,0:T(8,128)(2,1)S(1)}, bf16[1024,256]{1,0:T(8,128)(2,1)S(1)}, u32[]{:S(2)}, u32[]{:S(2)}) collective-permute-start(bf16[1024,256]{1,0:T(8,128)(2,1)S(1)} %get-tuple-element.50.refs_3_.refs_2_), channel_id=1, source_target_pairs={{0,1},{1,0},{2,3},{3,2},{4,5},{5,4},{6,7},{7,6},{8,9},{9,8},{10,11... | collective-permute-start | bytes 1572872 | tf_op jit(solution)/shard_map/ppermute | solution.py:351
  60.0 14.8 %collective-permute-start.11 = (bf16[1024,256]{1,0:T(8,128)(2,1)S(1)}, bf16[1024,256]{1,0:T(8,128)(2,1)S(1)}, u32[]{:S(2)}, u32[]{:S(2)}) collective-permute-start(bf16[1024,256]{1,0:T(8,128)(2,1)S(1)} %get-tuple-element.51.refs_5_.refs_4_), channel_id=1, source_target_pairs={{0,1},{1,0},{2,3},{3,2},{4,5},{5,4},{6,7},{7,6},{8,9},{9,8},{10,11... | collective-permute-start | bytes 1572872 | tf_op jit(solution)/shard_map/ppermute | solution.py:351
  60.1 13.3 %collective-permute-start.5 = (bf16[256,768]{1,0:T(8,128)(2,1)S(1)}, bf16[256,768]{1,0:T(8,128)(2,1)S(1)}, u32[]{:S(2)}, u32[]{:S(2)}) collective-permute-start(bf16[256,768]{1,0:T(8,128)(2,1)S(1)} %get-tuple-element.45.refs_0_), channel_id=1, source_target_pairs={{4,0},{6,2},{8,4},{10,6},{12,8},{14,10},{5,1},{7,3},{9,5},{11,7},{... | collective-permute-start | bytes 1179656 | tf_op jit(solution)/shard_map/ppermute | solution.py:341
  73.4 23.8 %collective-permute-start.15 = (bf16[1024,256]{1,0:T(8,128)(2,1)S(1)}, bf16[1024,256]{1,0:T(8,128)(2,1)S(1)}, u32[]{:S(2)}, u32[]{:S(2)}) collective-permute-start(bf16[1024,256]{1,0:T(8,128)(2,1)S(1)} %get-tuple-element.56.odd_ref), channel_id=1, source_target_pairs={{4,0},{6,2},{8,4},{10,6},{12,8},{14,10},{5,1},{7,3},{9,5},{11,7},{... | collective-permute-start | bytes 1572872 | tf_op jit(solution)/shard_map/ppermute | solution.py:341
  76.3 20.9 %collective-permute-start.12 = (bf16[256,768]{1,0:T(8,128)(2,1)S(1)}, bf16[256,768]{1,0:T(8,128)(2,1)S(1)}, u32[]{:S(2)}, u32[]{:S(2)}) collective-permute-start(bf16[256,768]{1,0:T(8,128)(2,1)S(1)} %get-tuple-element.53), channel_id=1, source_target_pairs={{4,0},{6,2},{8,4},{10,6},{12,8},{14,10},{5,1},{7,3},{9,5},{11,7},{... | collective-permute-start | bytes 1179656 | tf_op jit(solution)/shard_map/ppermute | solution.py:341
  97.8 18.6 %collective-permute-start.16 = (bf16[1024,256]{1,0:T(8,128)(2,1)S(1)}, bf16[1024,256]{1,0:T(8,128)(2,1)S(1)}, u32[]{:S(2)}, u32[]{:S(2)}) collective-permute-start(bf16[1024,256]{1,0:T(8,128)(2,1)S(1)} %get-tuple-element.58), channel_id=1, source_target_pairs={{2,0},{6,4},{10,8},{14,12},{0,2},{4,6},{8,10},{12,14},{3,1},{7,5},... | collective-permute-start | bytes 1572872 | tf_op jit(solution)/shard_map/ppermute | solution.py:341
  105.6 25.2 %collective-permute-start.14 = (bf16[256,1536]{1,0:T(8,128)(2,1)S(1)}, bf16[256,1536]{1,0:T(8,128)(2,1)S(1)}, u32[]{:S(2)}, u32[]{:S(2)}) collective-permute-start(bf16[256,1536]{1,0:T(8,128)(2,1)S(1)} %get-tuple-element.55), channel_id=1, source_target_pairs={{4,0},{6,2},{8,4},{10,6},{12,8},{14,10},{5,1},{7,3},{9,5},{11,7},{... | collective-permute-start | bytes 2359304 | tf_op jit(solution)/shard_map/ppermute | solution.py:341
  116.6 1.6 %collective-permute-start.17 = (bf16[1024,128]{1,0:T(8,128)(2,1)S(1)}, bf16[1024,128]{1,0:T(8,128)(2,1)S(1)}, u32[]{:S(2)}, u32[]{:S(2)}) collective-permute-start(bf16[1024,128]{1,0:T(8,128)(2,1)S(1)} %get-tuple-element.59.refs_2_), channel_id=1, source_target_pairs={{0,1},{1,0},{2,3},{3,2},{4,5},{5,4},{6,7},{7,6},{8,9},{9,8},{10,11... | collective-permute-start | bytes 786440 | tf_op jit(solution)/shard_map/ppermute | solution.py:351
  116.6 1.9 %collective-permute-start.18 = (bf16[1024,128]{1,0:T(8,128)(2,1)S(1)}, bf16[1024,128]{1,0:T(8,128)(2,1)S(1)}, u32[]{:S(2)}, u32[]{:S(2)}) collective-permute-start(bf16[1024,128]{1,0:T(8,128)(2,1)S(1)} %get-tuple-element.60.refs_4_), channel_id=1, source_target_pairs={{0,1},{1,0},{2,3},{3,2},{4,5},{5,4},{6,7},{7,6},{8,9},{9,8},{10,11... | collective-permute-start | bytes 786440 | tf_op jit(solution)/shard_map/ppermute | solution.py:351
  117.1 11.7 %collective-permute-start.20 = (bf16[1024,256]{1,0:T(8,128)(2,1)S(1)}, bf16[1024,256]{1,0:T(8,128)(2,1)S(1)}, u32[]{:S(2)}, u32[]{:S(2)}) collective-permute-start(bf16[1024,256]{1,0:T(8,128)(2,1)S(1)} %get-tuple-element.63.refs_2_), channel_id=1, source_target_pairs={{0,1},{1,0},{2,3},{3,2},{4,5},{5,4},{6,7},{7,6},{8,9},{9,8},{10,11... | collective-permute-start | bytes 1572872 | tf_op jit(solution)/shard_map/ppermute | solution.py:351
  120.3 10.7 %collective-permute-start.19 = (bf16[512,256]{1,0:T(8,128)(2,1)S(1)}, bf16[512,256]{1,0:T(8,128)(2,1)S(1)}, u32[]{:S(2)}, u32[]{:S(2)}) collective-permute-start(bf16[512,256]{1,0:T(8,128)(2,1)S(1)} %get-tuple-element.62), channel_id=1, source_target_pairs={{4,0},{6,2},{8,4},{10,6},{12,8},{14,10},{5,1},{7,3},{9,5},{11,7},{... | collective-permute-start | bytes 786440 | tf_op jit(solution)/shard_map/ppermute | solution.py:341

commit v7 on v6

--- a/solution.py
+++ b/solution.py
@@ -361,6 +361,7 @@
     below0 = send(upper, up)
     above = send(relayed, down)
     across = send(detoured, swap)
+    (direct,) = hold((across, above), direct)
     next_direct = send(direct, before)
     (lower,) = stack(here[1], mate(away[1]))
     below1 = send(lower, up)
@@ -373,6 +374,8 @@
     made, buffer = far(place, buffer, [below0], own, samples, first)
     top2 = send(made, down)
     across, buffer, next_detoured = choose(place, around, across, buffer)
+    above, buffer, swapped = choose(place, relayed, above, buffer)
+    next_relayed = send(swapped, swap)
     high = [next_detoured, mate(next_detoured)]
     for piece in split(next_direct, (made,), 2):
         high += [piece, mate(piece)]
@@ -383,11 +386,8 @@
     (buffer,) = hold((below1,), buffer)
     made, buffer = far(place, buffer, [below1], high + own, samples, first)
     bottom = send(made, down)
-    (buffer,) = hold((top3,), buffer)
-    above, buffer, swapped = choose(place, relayed, above, buffer)
-    next_relayed = send(swapped, swap)
     low = []
-    for piece in split(next_relayed, (), 2):
+    for piece in split(next_relayed, (made, top3), 2):
         low += [piece, mate(piece)]
     made, buffer = far(place, buffer, [below0, below1], low, samples)
     side = send(made, down)

time: 133 us -> 107 us (0.80)
  waiting for transfers between devices: 74.7 us -> 52.6 us
  starting transfers between devices: 28.9 us -> 24.6 us
    ppermute x11, waiting for transfers between devices: 71.7 us -> 48.4 us  [send(): return lax.ppermute(shard, 'var', pairs)]
    ppermute x11, starting transfers between devices: 26.1 us -> 21.8 us  [send(): return lax.ppermute(shard, 'var', pairs)]
  transfers between devices with their start and end apart: 21 -> 21, of which waited for: 9 -> 14; matrix products, arithmetic and copies ran while one was open for 0% -> 0% of each run, Pallas kernels for 16% -> 20%
where the time goes in v7:
time: 107 us
  waiting for transfers between devices  52.6 us (49%)
  Pallas kernels  28.3 us (26%)
  starting transfers between devices  24.6 us (23%)
    ppermute x11, waiting for transfers between devices, send(): return lax.ppermute(shard, 'var', pairs)  48.4 us
    ppermute x11, starting transfers between devices, send(): return lax.ppermute(shard, 'var', pairs)  21.8 us
    pallas_call x5, Pallas kernels, tile(): pl.pallas_call(functools.partial(tile_kernel, k, len(rows), len(rights),...  12.8 us
    pallas_call x4, Pallas kernels, far(): pl.pallas_call(functools.partial(far_kernel, 1.0 / samples, len(rows), le...  7.16 us
    ppermute x10, waiting for transfers between devices, mate(): return lax.ppermute(shard, 'samp', [(0, 1), (1, 0)])  4.21 us
    pallas_call x1, Pallas kernels, stats(): pl.pallas_call(stats_kernel, in_specs=[pl.BlockSpec(memory_space=pltpu.HB...  3.08 us
    ppermute x10, starting transfers between devices, mate(): return lax.ppermute(shard, 'samp', [(0, 1), (1, 0)])  2.71 us
  transfers between devices with their start and end apart: 21, of which 14 were waited for; matrix products, arithmetic and copies ran while one was open for 0% of the time, Pallas kernels for 20%

profile of v7, /device:TPU:0, one launch (start us, length us, event | category | flops | bytes accessed | tf_op | source)
XLA Modules:
  0.0 106.5 jit_solution(1010367296593774703)
XLA Ops:
  0.0 3.1 %shard_map.37 = (f32[8,1024]{1,0:T(8,128)S(1)}, bf16[1024,1024]{1,0:T(8,128)(2,1)S(1)}) custom-call(bf16[1024,1024]{1,0:T(8,128)(2,1)} %dosage_hbm.1, s32[1024,1024]{1,0:T(8,128)} %observed_hbm.1), custom_call_target="tpu_custom_call" | custom-call | flops 1000 | bytes 1000 | tf_op jit(solution)/shard_map/pallas_call | solution.py:59
  3.1 0.5 collective-permute-start
  4.3 0.1 pad_add_fusion.place_ref.refs_0_
  4.3 0.1 collective-permute-done.sums_other_ref
  4.5 1.9 %shard_map.38 = (bf16[1024,256]{1,0:T(8,128)(2,1)S(1)}, bf16[1024,256]{1,0:T(8,128)(2,1)S(1)}, bf16[1024,512]{1,0:T(8,128)(2,1)S(1)}, bf16[1024,1024]{1,0:T(8,12...) custom-call(s32[3]{0:T(128)S(1)} %pad_add_fusion.place_ref.refs_0_, ...), custom_call_target="tpu_custom_call" | custom-call | flops 1000 | bytes 1000 | tf_op jit(solution)/shard_map/pallas_call | solution.py:115
  6.4 0.4 collective-permute-start.1
  6.8 1.6 %collective-permute-done.1.arrived_ref = bf16[256,1024]{1,0:T(8,128)(2,1)S(1)} collective-permute-done((bf16[256,1024]{1,0:T(8,128)(2,1)S(1)}, bf16[256,1024]{1,0:T(8,128)(2,1)S(1)}, u32[]{:S(2)}, u32[]{:S(2)}) %collective-permute-start.1) | collective-permute-done | bytes 524320 | tf_op jit(solution)/shard_map/ppermute | solution.py:351
  8.4 0.1 shard_map.39
  8.4 0.4 collective-permute-start.3
  8.8 2.7 %collective-permute-start.6 = (bf16[1024,256]{1,0:T(8,128)(2,1)S(1)}, bf16[1024,256]{1,0:T(8,128)(2,1)S(1)}, u32[]{:S(2)}, u32[]{:S(2)}) collective-permute-start(bf16[1024,256]{1,0:T(8,128)(2,1)S(1)} %get-tuple-element.46), channel_id=1, source_target_pairs={{2,0},{6,4},{10,8},{14,12},{0,2},{4,6},{8,10},{12,14},{3,1},{7,5},... | collective-permute-start | bytes 1572872 | tf_op jit(solution)/shard_map/ppermute | solution.py:341
  11.5 1.3 %collective-permute-start.9 = (bf16[1024,256]{1,0:T(8,128)(2,1)S(1)}, bf16[1024,256]{1,0:T(8,128)(2,1)S(1)}, u32[]{:S(2)}, u32[]{:S(2)}) collective-permute-start(bf16[1024,256]{1,0:T(8,128)(2,1)S(1)} %get-tuple-element.49.odd_ref), channel_id=1, source_target_pairs={{4,0},{6,2},{8,4},{10,6},{12,8},{14,10},{5,1},{7,3},{9,5},{11,7},{... | collective-permute-start | bytes 1572872 | tf_op jit(solution)/shard_map/ppermute | solution.py:341
  12.8 4.6 %collective-permute-start.2 = (bf16[512,1024]{1,0:T(8,128)(2,1)S(1)}, bf16[512,1024]{1,0:T(8,128)(2,1)S(1)}, u32[]{:S(2)}, u32[]{:S(2)}) collective-permute-start(bf16[512,1024]{1,0:T(8,128)(2,1)S(1)} %get-tuple-element.40.refs_0_), channel_id=1, source_target_pairs={{0,4},{2,6},{4,8},{6,10},{8,12},{10,14},{1,5},{3,7},{5,9},{7,11},{... | collective-permute-start | bytes 3145736 | tf_op jit(solution)/shard_map/ppermute | solution.py:341
  17.4 6.5 %collective-permute-done.6.even_ref.refs_0_ = bf16[1024,256]{1,0:T(8,128)(2,1)S(1)} collective-permute-done((bf16[1024,256]{1,0:T(8,128)(2,1)S(1)}, bf16[1024,256]{1,0:T(8,128)(2,1)S(1)}, u32[]{:S(2)}, u32[]{:S(2)}) %collective-permute-start.6) | collective-permute-done | bytes 524320 | tf_op jit(solution)/shard_map/ppermute | solution.py:341
  23.9 3.3 %collective-permute-done.9.refs_1_.even_ref = bf16[1024,256]{1,0:T(8,128)(2,1)S(1)} collective-permute-done((bf16[1024,256]{1,0:T(8,128)(2,1)S(1)}, bf16[1024,256]{1,0:T(8,128)(2,1)S(1)}, u32[]{:S(2)}, u32[]{:S(2)}) %collective-permute-start.9) | collective-permute-done | bytes 524320 | tf_op jit(solution)/shard_map/ppermute | solution.py:341
  27.3 1.3 %collective-permute-start.10 = (bf16[1024,512]{1,0:T(8,128)(2,1)S(1)}, bf16[1024,512]{1,0:T(8,128)(2,1)S(1)}, u32[]{:S(2)}, u32[]{:S(2)}) collective-permute-start(bf16[1024,512]{1,0:T(8,128)(2,1)S(1)} %shard_map.45), channel_id=1, source_target_pairs={{2,0},{4,2},{6,4},{8,6},{10,8},{12,10},{14,12},{3,1},{5,3},{7,5},{... | collective-permute-start | bytes 3145736 | tf_op jit(solution)/shard_map/ppermute | solution.py:341
  28.6 0.1 collective-permute-start.4
  28.7 0.7 collective-permute-start.7
  29.4 1.2 %collective-permute-done.4.arrived_ref = bf16[256,1024]{1,0:T(8,128)(2,1)S(1)} collective-permute-done((bf16[256,1024]{1,0:T(8,128)(2,1)S(1)}, bf16[256,1024]{1,0:T(8,128)(2,1)S(1)}, u32[]{:S(2)}, u32[]{:S(2)}) %collective-permute-start.4) | collective-permute-done | bytes 524320 | tf_op jit(solution)/shard_map/ppermute | solution.py:351
  30.6 0.1 shard_map.40.refs_1_
  30.6 4.4 %collective-permute-start.14 = (bf16[512,1024]{1,0:T(8,128)(2,1)S(1)}, bf16[512,1024]{1,0:T(8,128)(2,1)S(1)}, u32[]{:S(2)}, u32[]{:S(2)}) collective-permute-start(bf16[512,1024]{1,0:T(8,128)(2,1)S(1)} %shard_map.40.refs_1_), channel_id=1, source_target_pairs={{0,4},{2,6},{4,8},{6,10},{8,12},{10,14},{1,5},{3,7},{5,9},{7,11},{... | collective-permute-start | bytes 3145736 | tf_op jit(solution)/shard_map/ppermute | solution.py:341
  35.0 0.0 collective-permute-done.3.refs_3_.refs_2_.refs_8_
  35.0 3.8 %shard_map.41.refs_1_ = bf16[4,512,1024]{2,1,0:T(8,128)(2,1)} custom-call(s32[3]{0:T(128)S(1)} %pad_add_fusion.place_ref.refs_0_, bf16[512,1024]{1,0:T(8,128)(2,1)S(1)} %get-tuple-element.40.refs_0_, bf16[512,1024]{1,0:T(8,128)(2,1)S(1)} %shard_map.40.refs_1_, ...), custom_call_target="tpu_custom_call", output_to_operand_aliasing={{}: (5, {})} | custom-call | flops 1000 | bytes 1000 | tf_op jit(solution)/shard_map/pallas_call | solution.py:185
  38.9 2.0 %collective-permute-done.2.refs_0_ = bf16[512,1024]{1,0:T(8,128)(2,1)S(1)} collective-permute-done((bf16[512,1024]{1,0:T(8,128)(2,1)S(1)}, bf16[512,1024]{1,0:T(8,128)(2,1)S(1)}, u32[]{:S(2)}, u32[]{:S(2)}) %collective-permute-start.2) | collective-permute-done | bytes 1048608 | tf_op jit(solution)/shard_map/ppermute | solution.py:341
  40.9 1.5 %shard_map.43 = (bf16[256,768]{1,0:T(8,128)(2,1)S(1)}, bf16[4,512,1024]{2,1,0:T(8,128)(2,1)}) custom-call(s32[3]{0:T(128)S(1)} %pad_add_fusion.place_ref.refs_0_, bf16[512,1024]{1,0:T(8,128)(2,1)S(1)} %collective-permute-done.2.refs_0_, bf16[1024,1024]{1,0:T(8,128)(2,1)S(1)} %get-tuple-element.41.refs_2_.refs_1_.refs_7_, ...), custom_call_target="tpu_custom_call", output_to_operand_aliasing={{1}: (4, {})} | custom-call | flops 1000 | bytes 1000 | tf_op jit(solution)/shard_map/pallas_call | solution.py:209
  42.4 0.0 collective-permute-done.7.odd_ref
  42.5 0.6 shard_map.44
  43.1 0.1 collective-permute-start.8
  43.1 10.3 %collective-permute-done.10.whole_ref = bf16[1024,512]{1,0:T(8,128)(2,1)S(1)} collective-permute-done((bf16[1024,512]{1,0:T(8,128)(2,1)S(1)}, bf16[1024,512]{1,0:T(8,128)(2,1)S(1)}, u32[]{:S(2)}, u32[]{:S(2)}) %collective-permute-start.10) | collective-permute-done | bytes 1048608 | tf_op jit(solution)/shard_map/ppermute | solution.py:341
  53.5 0.1 shard_map.46
  53.5 0.1 collective-permute-start.11
  53.6 0.5 collective-permute-start.12
  54.1 1.3 %collective-permute-start.5 = (bf16[256,768]{1,0:T(8,128)(2,1)S(1)}, bf16[256,768]{1,0:T(8,128)(2,1)S(1)}, u32[]{:S(2)}, u32[]{:S(2)}) collective-permute-start(bf16[256,768]{1,0:T(8,128)(2,1)S(1)} %get-tuple-element.45.refs_0_), channel_id=1, source_target_pairs={{4,0},{6,2},{8,4},{10,6},{12,8},{14,10},{5,1},{7,3},{9,5},{11,7},{... | collective-permute-start | bytes 1179656 | tf_op jit(solution)/shard_map/ppermute | solution.py:341
  55.4 0.6 shard_map.47
  56.0 11.1 %collective-permute-done.5.refs_0_.refs_1_ = bf16[256,768]{1,0:T(8,128)(2,1)S(1)} collective-permute-done((bf16[256,768]{1,0:T(8,128)(2,1)S(1)}, bf16[256,768]{1,0:T(8,128)(2,1)S(1)}, u32[]{:S(2)}, u32[]{:S(2)}) %collective-permute-start.5) | collective-permute-done | bytes 393248 | tf_op jit(solution)/shard_map/ppermute | solution.py:341
  67.1 1.6 %collective-permute-start.16 = (bf16[1024,256]{1,0:T(8,128)(2,1)S(1)}, bf16[1024,256]{1,0:T(8,128)(2,1)S(1)}, u32[]{:S(2)}, u32[]{:S(2)}) collective-permute-start(bf16[1024,256]{1,0:T(8,128)(2,1)S(1)} %get-tuple-element.58), channel_id=1, source_target_pairs={{2,0},{6,4},{10,8},{14,12},{0,2},{4,6},{8,10},{12,14},{3,1},{7,5},... | collective-permute-start | bytes 1572872 | tf_op jit(solution)/shard_map/ppermute | solution.py:341
  68.7 0.0 collective-permute-done.8.refs_2_.refs_3_
  68.7 0.0 collective-permute-done.11.refs_4_.refs_3_
  68.7 0.0 collective-permute-done.12.refs_6_.refs_5_
  68.7 1.5 %shard_map.49 = (bf16[256,768]{1,0:T(8,128)(2,1)S(1)}, bf16[4,512,1024]{2,1,0:T(8,128)(2,1)}) custom-call(s32[3]{0:T(128)S(1)} %pad_add_fusion.place_ref.refs_0_, bf16[512,1024]{1,0:T(8,128)(2,1)S(1)} %collective-permute-done.2.refs_0_, bf16[1024,256]{1,0:T(8,128)(2,1)S(1)} %get-tuple-element.48.refs_1_.refs_2_, ...), custom_call_target="tpu_custom_call", output_to_operand_aliasing={{1}: (8, {})} | custom-call | flops 1000 | bytes 1000 | tf_op jit(solution)/shard_map/pallas_call | solution.py:209
  70.2 1.3 %collective-permute-start.13 = (bf16[256,768]{1,0:T(8,128)(2,1)S(1)}, bf16[256,768]{1,0:T(8,128)(2,1)S(1)}, u32[]{:S(2)}, u32[]{:S(2)}) collective-permute-start(bf16[256,768]{1,0:T(8,128)(2,1)S(1)} %get-tuple-element.55), channel_id=1, source_target_pairs={{4,0},{6,2},{8,4},{10,6},{12,8},{14,10},{5,1},{7,3},{9,5},{11,7},{... | collective-permute-start | bytes 1179656 | tf_op jit(solution)/shard_map/ppermute | solution.py:341
  71.5 0.0 collective-permute-done.14.refs_0_.refs_1_
  71.5 2.3 %shard_map.51 = (bf16[256,1536]{1,0:T(8,128)(2,1)S(1)}, bf16[4,512,1024]{2,1,0:T(8,128)(2,1)}) custom-call(s32[3]{0:T(128)S(1)} %pad_add_fusion.place_ref.refs_0_, bf16[512,1024]{1,0:T(8,128)(2,1)S(1)} %collective-permute-done.14.refs_0_.refs_1_, bf16[1024,256]{1,0:T(8,128)(2,1)S(1)} %get-tuple-element.48.refs_1_.refs_2_, ...), custom_call_target="tpu_custom_call", output_to_operand_aliasing={{1}: (10, {})} | custom-call | flops 1000 | bytes 1000 | tf_op jit(solution)/shard_map/pallas_call | solution.py:209
  73.9 1.3 %collective-permute-start.15 = (bf16[256,1536]{1,0:T(8,128)(2,1)S(1)}, bf16[256,1536]{1,0:T(8,128)(2,1)S(1)}, u32[]{:S(2)}, u32[]{:S(2)}) collective-permute-start(bf16[256,1536]{1,0:T(8,128)(2,1)S(1)} %get-tuple-element.57.refs_0_), channel_id=1, source_target_pairs={{4,0},{6,2},{8,4},{10,6},{12,8},{14,10},{5,1},{7,3},{9,5},{11,7},{... | collective-permute-start | bytes 2359304 | tf_op jit(solution)/shard_map/ppermute | solution.py:341
  75.2 5.0 %collective-permute-done.16.whole_ref = bf16[1024,256]{1,0:T(8,128)(2,1)S(1)} collective-permute-done((bf16[1024,256]{1,0:T(8,128)(2,1)S(1)}, bf16[1024,256]{1,0:T(8,128)(2,1)S(1)}, u32[]{:S(2)}, u32[]{:S(2)}) %collective-permute-start.16) | collective-permute-done | bytes 524320 | tf_op jit(solution)/shard_map/ppermute | solution.py:341
  80.2 4.0 %collective-permute-done.13.refs_1_.refs_2_ = bf16[256,768]{1,0:T(8,128)(2,1)S(1)} collective-permute-done((bf16[256,768]{1,0:T(8,128)(2,1)S(1)}, bf16[256,768]{1,0:T(8,128)(2,1)S(1)}, u32[]{:S(2)}, u32[]{:S(2)}) %collective-permute-start.13) | collective-permute-done | bytes 393248 | tf_op jit(solution)/shard_map/ppermute | solution.py:341
  84.1 0.1 shard_map.52
  84.2 0.1 collective-permute-start.17
  84.3 0.5 collective-permute-start.18
  84.8 0.1 collective-permute-start.20
  84.9 0.9 collective-permute-done.17.refs_3_
  85.8 0.4 collective-permute-done.18.refs_5_
  86.2 1.8 %shard_map.53 = (bf16[512,256]{1,0:T(8,128)(2,1)S(1)}, bf16[4,512,1024]{2,1,0:T(8,128)(2,1)}) custom-call(s32[3]{0:T(128)S(1)} %pad_add_fusion.place_ref.refs_0_, bf16[512,1024]{1,0:T(8,128)(2,1)S(1)} %collective-permute-done.2.refs_0_, bf16[512,1024]{1,0:T(8,128)(2,1)S(1)} %collective-permute-done.14.refs_0_.refs_1_, ...), custom_call_target="tpu_custom_call", output_to_operand_aliasing={{1}: (7, {})} | custom-call | flops 1000 | bytes 1000 | tf_op jit(solution)/shard_map/pallas_call | solution.py:209
  88.0 1.5 %collective-permute-start.19 = (bf16[512,256]{1,0:T(8,128)(2,1)S(1)}, bf16[512,256]{1,0:T(8,128)(2,1)S(1)}, u32[]{:S(2)}, u32[]{:S(2)}) collective-permute-start(bf16[512,256]{1,0:T(8,128)(2,1)S(1)} %get-tuple-element.62), channel_id=1, source_target_pairs={{4,0},{6,2},{8,4},{10,6},{12,8},{14,10},{5,1},{7,3},{9,5},{11,7},{... | collective-permute-start | bytes 786440 | tf_op jit(solution)/shard_map/ppermute | solution.py:341
  89.5 2.0 %shard_map.54.refs_6_ = bf16[4,512,1024]{2,1,0:T(8,128)(2,1)} custom-call(s32[3]{0:T(128)S(1)} %pad_add_fusion.place_ref.refs_0_, bf16[512,1024]{1,0:T(8,128)(2,1)S(1)} %get-tuple-element.40.refs_0_, bf16[512,1024]{1,0:T(8,128)(2,1)S(1)} %shard_map.40.refs_1_, ...), custom_call_target="tpu_custom_call", output_to_operand_aliasing={{}: (5, {})} | custom-call | flops 1000 | bytes 1000 | tf_op jit(solution)/shard_map/pallas_call | solution.py:185
  91.4 2.6 %shard_map.55.refs_6_ = bf16[4,512,1024]{2,1,0:T(8,128)(2,1)} custom-call(s32[3]{0:T(128)S(1)} %pad_add_fusion.place_ref.refs_0_, bf16[512,1024]{1,0:T(8,128)(2,1)S(1)} %get-tuple-element.40.refs_0_, bf16[512,1024]{1,0:T(8,128)(2,1)S(1)} %shard_map.40.refs_1_, ...), custom_call_target="tpu_custom_call", output_to_operand_aliasing={{}: (7, {})} | custom-call | flops 1000 | bytes 1000 | tf_op jit(solution)/shard_map/pallas_call | solution.py:185
  94.0 2.5 %shard_map.56.refs_4_ = bf16[4,512,1024]{2,1,0:T(8,128)(2,1)} custom-call(s32[3]{0:T(128)S(1)} %pad_add_fusion.place_ref.refs_0_, bf16[512,1024]{1,0:T(8,128)(2,1)S(1)} %get-tuple-element.40.refs_0_, bf16[512,1024]{1,0:T(8,128)(2,1)S(1)} %shard_map.40.refs_1_, bf16[1024,128]{1,0:T(8,128)(2,1)S(1)} %get-tuple-element.59.refs_2_, ...), custom_call_target="tpu_custom_call", output_to_operand_aliasing={{}: (7, {})} | custom-call | flops 1000 | bytes 1000 | tf_op jit(solution)/shard_map/pallas_call | solution.py:185
  96.5 0.0 collective-permute-done.20.refs_3_
  96.5 2.0 %shard_map.57.refs_5_ = bf16[4,512,1024]{2,1,0:T(8,128)(2,1)} custom-call(s32[3]{0:T(128)S(1)} %pad_add_fusion.place_ref.refs_0_, bf16[512,1024]{1,0:T(8,128)(2,1)S(1)} %get-tuple-element.40.refs_0_, bf16[512,1024]{1,0:T(8,128)(2,1)S(1)} %shard_map.40.refs_1_, bf16[1024,256]{1,0:T(8,128)(2,1)S(1)} %get-tuple-element.63.refs_2_, ...), custom_call_target="tpu_custom_call", output_to_operand_aliasing={{}: (5, {})} | custom-call | flops 1000 | bytes 1000 | tf_op jit(solution)/shard_map/pallas_call | solution.py:185
  98.5 2.5 %collective-permute-done.15.refs_3_ = bf16[256,1536]{1,0:T(8,128)(2,1)S(1)} collective-permute-done((bf16[256,1536]{1,0:T(8,128)(2,1)S(1)}, bf16[256,1536]{1,0:T(8,128)(2,1)S(1)}, u32[]{:S(2)}, u32[]{:S(2)}) %collective-permute-start.15) | collective-permute-done | bytes 786464 | tf_op jit(solution)/shard_map/ppermute | solution.py:341
  101.0 3.5 %collective-permute-done.19.refs_4_ = bf16[512,256]{1,0:T(8,128)(2,1)S(1)} collective-permute-done((bf16[512,256]{1,0:T(8,128)(2,1)S(1)}, bf16[512,256]{1,0:T(8,128)(2,1)S(1)}, u32[]{:S(2)}, u32[]{:S(2)}) %collective-permute-start.19) | collective-permute-done | bytes 262176 | tf_op jit(solution)/shard_map/ppermute | solution.py:341
  104.5 1.8 %shard_map.58 = bf16[4,512,1024]{2,1,0:T(8,128)(2,1)} custom-call(s32[3]{0:T(128)S(1)} %pad_add_fusion.place_ref.refs_0_, bf16[256,768]{1,0:T(8,128)(2,1)S(1)} %collective-permute-done.5.refs_0_.refs_1_, bf16[256,768]{1,0:T(8,128)(2,1)S(1)} %collective-permute-done.13.refs_1_.refs_2_, ...), custom_call_target="tpu_custom_call", output_to_operand_aliasing={{}: (5, {})} | custom-call | flops 1000 | bytes 1000 | tf_op jit(solution)/shard_map/pallas_call | solution.py:312
  (4 shorter events, 0.0 us)
Async XLA Ops:
  3.1 1.4 %collective-permute-start = (f32[8,1024]{1,0:T(8,128)S(1)}, f32[8,1024]{1,0:T(8,128)S(1)}, u32[]{:S(2)}, u32[]{:S(2)}) collective-permute-start(f32[8,1024]{1,0:T(8,128)S(1)} %get-tuple-element.36.sums_ref), channel_id=1, source_target_pairs={{0,1},{1,0},{2,3},{3,2},{4,5},{5,4},{6,7},{7,6},{8,9},{9,8},{10,11... | collective-permute-start | bytes 98312 | tf_op jit(solution)/shard_map/ppermute | solution.py:351
  6.4 2.0 %collective-permute-start.1 = (bf16[256,1024]{1,0:T(8,128)(2,1)S(1)}, bf16[256,1024]{1,0:T(8,128)(2,1)S(1)}, u32[]{:S(2)}, u32[]{:S(2)}) collective-permute-start(bf16[256,1024]{1,0:T(8,128)(2,1)S(1)} %get-tuple-element.38), channel_id=1, source_target_pairs={{0,1},{1,0},{2,3},{3,2},{4,5},{5,4},{6,7},{7,6},{8,9},{9,8},{10,11... | collective-permute-start | bytes 1572872 | tf_op jit(solution)/shard_map/ppermute | solution.py:351
  8.4 26.6 %collective-permute-start.3 = (bf16[1024,1024]{1,0:T(8,128)(2,1)S(1)}, bf16[1024,1024]{1,0:T(8,128)(2,1)S(1)}, u32[]{:S(2)}, u32[]{:S(2)}) collective-permute-start(bf16[1024,1024]{1,0:T(8,128)(2,1)S(1)} %get-tuple-element.41.refs_2_.refs_1_.refs_7_), channel_id=1, source_target_pairs={{0,1},{1,0},{2,3},{3,2},{4,5},{5,4},{6,7},{7,6},{8,9},{9,8},{10,11... | collective-permute-start | bytes 6291464 | tf_op jit(solution)/shard_map/ppermute | solution.py:351
  8.8 15.1 %collective-permute-start.6 = (bf16[1024,256]{1,0:T(8,128)(2,1)S(1)}, bf16[1024,256]{1,0:T(8,128)(2,1)S(1)}, u32[]{:S(2)}, u32[]{:S(2)}) collective-permute-start(bf16[1024,256]{1,0:T(8,128)(2,1)S(1)} %get-tuple-element.46), channel_id=1, source_target_pairs={{2,0},{6,4},{10,8},{14,12},{0,2},{4,6},{8,10},{12,14},{3,1},{7,5},... | collective-permute-start | bytes 1572872 | tf_op jit(solution)/shard_map/ppermute | solution.py:341
  11.5 15.8 %collective-permute-start.9 = (bf16[1024,256]{1,0:T(8,128)(2,1)S(1)}, bf16[1024,256]{1,0:T(8,128)(2,1)S(1)}, u32[]{:S(2)}, u32[]{:S(2)}) collective-permute-start(bf16[1024,256]{1,0:T(8,128)(2,1)S(1)} %get-tuple-element.49.odd_ref), channel_id=1, source_target_pairs={{4,0},{6,2},{8,4},{10,6},{12,8},{14,10},{5,1},{7,3},{9,5},{11,7},{... | collective-permute-start | bytes 1572872 | tf_op jit(solution)/shard_map/ppermute | solution.py:341
  12.8 28.1 %collective-permute-start.2 = (bf16[512,1024]{1,0:T(8,128)(2,1)S(1)}, bf16[512,1024]{1,0:T(8,128)(2,1)S(1)}, u32[]{:S(2)}, u32[]{:S(2)}) collective-permute-start(bf16[512,1024]{1,0:T(8,128)(2,1)S(1)} %get-tuple-element.40.refs_0_), channel_id=1, source_target_pairs={{0,4},{2,6},{4,8},{6,10},{8,12},{10,14},{1,5},{3,7},{5,9},{7,11},{... | collective-permute-start | bytes 3145736 | tf_op jit(solution)/shard_map/ppermute | solution.py:341
  27.3 26.2 %collective-permute-start.10 = (bf16[1024,512]{1,0:T(8,128)(2,1)S(1)}, bf16[1024,512]{1,0:T(8,128)(2,1)S(1)}, u32[]{:S(2)}, u32[]{:S(2)}) collective-permute-start(bf16[1024,512]{1,0:T(8,128)(2,1)S(1)} %shard_map.45), channel_id=1, source_target_pairs={{2,0},{4,2},{6,4},{8,6},{10,8},{12,10},{14,12},{3,1},{5,3},{7,5},{... | collective-permute-start | bytes 3145736 | tf_op jit(solution)/shard_map/ppermute | solution.py:341
  28.6 2.0 %collective-permute-start.4 = (bf16[256,1024]{1,0:T(8,128)(2,1)S(1)}, bf16[256,1024]{1,0:T(8,128)(2,1)S(1)}, u32[]{:S(2)}, u32[]{:S(2)}) collective-permute-start(bf16[256,1024]{1,0:T(8,128)(2,1)S(1)} %get-tuple-element.43), channel_id=1, source_target_pairs={{0,1},{1,0},{2,3},{3,2},{4,5},{5,4},{6,7},{7,6},{8,9},{9,8},{10,11... | collective-permute-start | bytes 1572872 | tf_op jit(solution)/shard_map/ppermute | solution.py:351
  28.7 13.8 %collective-permute-start.7 = (bf16[1024,256]{1,0:T(8,128)(2,1)S(1)}, bf16[1024,256]{1,0:T(8,128)(2,1)S(1)}, u32[]{:S(2)}, u32[]{:S(2)}) collective-permute-start(bf16[1024,256]{1,0:T(8,128)(2,1)S(1)} %collective-permute-done.6.even_ref.refs_0_), channel_id=1, source_target_pairs={{6,2},{10,6},{14,10},{7,3},{11,7},{15,11},{22,18},{26,22},{30,26},... | collective-permute-start | bytes 1572872 | tf_op jit(solution)/shard_map/ppermute | solution.py:341
  30.6 40.9 %collective-permute-start.14 = (bf16[512,1024]{1,0:T(8,128)(2,1)S(1)}, bf16[512,1024]{1,0:T(8,128)(2,1)S(1)}, u32[]{:S(2)}, u32[]{:S(2)}) collective-permute-start(bf16[512,1024]{1,0:T(8,128)(2,1)S(1)} %shard_map.40.refs_1_), channel_id=1, source_target_pairs={{0,4},{2,6},{4,8},{6,10},{8,12},{10,14},{1,5},{3,7},{5,9},{7,11},{... | collective-permute-start | bytes 3145736 | tf_op jit(solution)/shard_map/ppermute | solution.py:341
  43.1 25.6 %collective-permute-start.8 = (bf16[1024,256]{1,0:T(8,128)(2,1)S(1)}, bf16[1024,256]{1,0:T(8,128)(2,1)S(1)}, u32[]{:S(2)}, u32[]{:S(2)}) collective-permute-start(bf16[1024,256]{1,0:T(8,128)(2,1)S(1)} %get-tuple-element.48.refs_1_.refs_2_), channel_id=1, source_target_pairs={{0,1},{1,0},{2,3},{3,2},{4,5},{5,4},{6,7},{7,6},{8,9},{9,8},{10,11... | collective-permute-start | bytes 1572872 | tf_op jit(solution)/shard_map/ppermute | solution.py:351
  53.5 15.1 %collective-permute-start.11 = (bf16[1024,256]{1,0:T(8,128)(2,1)S(1)}, bf16[1024,256]{1,0:T(8,128)(2,1)S(1)}, u32[]{:S(2)}, u32[]{:S(2)}) collective-permute-start(bf16[1024,256]{1,0:T(8,128)(2,1)S(1)} %get-tuple-element.51.refs_3_.refs_2_), channel_id=1, source_target_pairs={{0,1},{1,0},{2,3},{3,2},{4,5},{5,4},{6,7},{7,6},{8,9},{9,8},{10,11... | collective-permute-start | bytes 1572872 | tf_op jit(solution)/shard_map/ppermute | solution.py:351
  53.6 15.1 %collective-permute-start.12 = (bf16[1024,256]{1,0:T(8,128)(2,1)S(1)}, bf16[1024,256]{1,0:T(8,128)(2,1)S(1)}, u32[]{:S(2)}, u32[]{:S(2)}) collective-permute-start(bf16[1024,256]{1,0:T(8,128)(2,1)S(1)} %get-tuple-element.52.refs_5_.refs_4_), channel_id=1, source_target_pairs={{0,1},{1,0},{2,3},{3,2},{4,5},{5,4},{6,7},{7,6},{8,9},{9,8},{10,11... | collective-permute-start | bytes 1572872 | tf_op jit(solution)/shard_map/ppermute | solution.py:351
  54.1 13.0 %collective-permute-start.5 = (bf16[256,768]{1,0:T(8,128)(2,1)S(1)}, bf16[256,768]{1,0:T(8,128)(2,1)S(1)}, u32[]{:S(2)}, u32[]{:S(2)}) collective-permute-start(bf16[256,768]{1,0:T(8,128)(2,1)S(1)} %get-tuple-element.45.refs_0_), channel_id=1, source_target_pairs={{4,0},{6,2},{8,4},{10,6},{12,8},{14,10},{5,1},{7,3},{9,5},{11,7},{... | collective-permute-start | bytes 1179656 | tf_op jit(solution)/shard_map/ppermute | solution.py:341
  67.1 13.1 %collective-permute-start.16 = (bf16[1024,256]{1,0:T(8,128)(2,1)S(1)}, bf16[1024,256]{1,0:T(8,128)(2,1)S(1)}, u32[]{:S(2)}, u32[]{:S(2)}) collective-permute-start(bf16[1024,256]{1,0:T(8,128)(2,1)S(1)} %get-tuple-element.58), channel_id=1, source_target_pairs={{2,0},{6,4},{10,8},{14,12},{0,2},{4,6},{8,10},{12,14},{3,1},{7,5},... | collective-permute-start | bytes 1572872 | tf_op jit(solution)/shard_map/ppermute | solution.py:341
  70.2 13.9 %collective-permute-start.13 = (bf16[256,768]{1,0:T(8,128)(2,1)S(1)}, bf16[256,768]{1,0:T(8,128)(2,1)S(1)}, u32[]{:S(2)}, u32[]{:S(2)}) collective-permute-start(bf16[256,768]{1,0:T(8,128)(2,1)S(1)} %get-tuple-element.55), channel_id=1, source_target_pairs={{4,0},{6,2},{8,4},{10,6},{12,8},{14,10},{5,1},{7,3},{9,5},{11,7},{... | collective-permute-start | bytes 1179656 | tf_op jit(solution)/shard_map/ppermute | solution.py:341
  73.9 27.1 %collective-permute-start.15 = (bf16[256,1536]{1,0:T(8,128)(2,1)S(1)}, bf16[256,1536]{1,0:T(8,128)(2,1)S(1)}, u32[]{:S(2)}, u32[]{:S(2)}) collective-permute-start(bf16[256,1536]{1,0:T(8,128)(2,1)S(1)} %get-tuple-element.57.refs_0_), channel_id=1, source_target_pairs={{4,0},{6,2},{8,4},{10,6},{12,8},{14,10},{5,1},{7,3},{9,5},{11,7},{... | collective-permute-start | bytes 2359304 | tf_op jit(solution)/shard_map/ppermute | solution.py:341
  84.2 1.6 %collective-permute-start.17 = (bf16[1024,128]{1,0:T(8,128)(2,1)S(1)}, bf16[1024,128]{1,0:T(8,128)(2,1)S(1)}, u32[]{:S(2)}, u32[]{:S(2)}) collective-permute-start(bf16[1024,128]{1,0:T(8,128)(2,1)S(1)} %get-tuple-element.59.refs_2_), channel_id=1, source_target_pairs={{0,1},{1,0},{2,3},{3,2},{4,5},{5,4},{6,7},{7,6},{8,9},{9,8},{10,11... | collective-permute-start | bytes 786440 | tf_op jit(solution)/shard_map/ppermute | solution.py:351
  84.3 1.9 %collective-permute-start.18 = (bf16[1024,128]{1,0:T(8,128)(2,1)S(1)}, bf16[1024,128]{1,0:T(8,128)(2,1)S(1)}, u32[]{:S(2)}, u32[]{:S(2)}) collective-permute-start(bf16[1024,128]{1,0:T(8,128)(2,1)S(1)} %get-tuple-element.60.refs_4_), channel_id=1, source_target_pairs={{0,1},{1,0},{2,3},{3,2},{4,5},{5,4},{6,7},{7,6},{8,9},{9,8},{10,11... | collective-permute-start | bytes 786440 | tf_op jit(solution)/shard_map/ppermute | solution.py:351
  84.8 11.7 %collective-permute-start.20 = (bf16[1024,256]{1,0:T(8,128)(2,1)S(1)}, bf16[1024,256]{1,0:T(8,128)(2,1)S(1)}, u32[]{:S(2)}, u32[]{:S(2)}) collective-permute-start(bf16[1024,256]{1,0:T(8,128)(2,1)S(1)} %get-tuple-element.63.refs_2_), channel_id=1, source_target_pairs={{0,1},{1,0},{2,3},{3,2},{4,5},{5,4},{6,7},{7,6},{8,9},{9,8},{10,11... | collective-permute-start | bytes 1572872 | tf_op jit(solution)/shard_map/ppermute | solution.py:351
  88.0 16.5 %collective-permute-start.19 = (bf16[512,256]{1,0:T(8,128)(2,1)S(1)}, bf16[512,256]{1,0:T(8,128)(2,1)S(1)}, u32[]{:S(2)}, u32[]{:S(2)}) collective-permute-start(bf16[512,256]{1,0:T(8,128)(2,1)S(1)} %get-tuple-element.62), channel_id=1, source_target_pairs={{4,0},{6,2},{8,4},{10,6},{12,8},{14,10},{5,1},{7,3},{9,5},{11,7},{... | collective-permute-start | bytes 786440 | tf_op jit(solution)/shard_map/ppermute | solution.py:341

commit v8 on v7

--- a/solution.py
+++ b/solution.py
@@ -361,12 +361,13 @@
     below0 = send(upper, up)
     above = send(relayed, down)
     across = send(detoured, swap)
-    (direct,) = hold((across, above), direct)
+    (direct,) = hold((across,), direct)
     next_direct = send(direct, before)
     (lower,) = stack(here[1], mate(away[1]))
     below1 = send(lower, up)
     rows = [upper, lower]
     own = [whole, mate(whole)]
+    (across,) = hold((above,), across)
     around = send(across, down_odd)
 
     buffer = tile(place, buffer, 0, 0, rows, own, samples)
@@ -379,11 +380,10 @@
     high = [next_detoured, mate(next_detoured)]
     for piece in split(next_direct, (made,), 2):
         high += [piece, mate(piece)]
-    (buffer,) = hold((top2,), buffer)
     made, buffer = far(place, buffer, [below0], high, samples)
     top3 = send(made, down)
 
-    (buffer,) = hold((below1,), buffer)
+    (buffer,) = hold((below1, top2), buffer)
     made, buffer = far(place, buffer, [below1], high + own, samples, first)
     bottom = send(made, down)
     low = []

time: 107 us -> 98.4 us (0.920)
  waiting for transfers between devices: 52.6 us -> 43.2 us
    ppermute x11, waiting for transfers between devices: 48.4 us -> 40.1 us  [send(): return lax.ppermute(shard, 'var', pairs)]
    ppermute x10, waiting for transfers between devices: 4.21 us -> 3.02 us  [mate(): return lax.ppermute(shard, 'samp', [(0, 1), (1, 0)])]
  transfers between devices with their start and end apart: 21 -> 21, of which waited for: 14 -> 13; matrix products, arithmetic and copies ran while one was open for 0% -> 0% of each run, Pallas kernels for 20% -> 22%
where the time goes in v8:
time: 98.4 us; the launch traced here: 97.4 us
  waiting for transfers between devices  43.2 us (44%)
  Pallas kernels  28.3 us (29%)
  starting transfers between devices  24.8 us (25%)
  between operations  1.04 us (1%)
    ppermute x11, waiting for transfers between devices, send(): return lax.ppermute(shard, 'var', pairs)  40.1 us
    ppermute x11, starting transfers between devices, send(): return lax.ppermute(shard, 'var', pairs)  22.1 us
    pallas_call x5, Pallas kernels, tile(): pl.pallas_call(functools.partial(tile_kernel, k, len(rows), len(rights),...  12.8 us
    pallas_call x4, Pallas kernels, far(): pl.pallas_call(functools.partial(far_kernel, 1.0 / samples, len(rows), le...  7.15 us
    pallas_call x1, Pallas kernels, stats(): pl.pallas_call(stats_kernel, in_specs=[pl.BlockSpec(memory_space=pltpu.HB...  3.08 us
    ppermute x10, waiting for transfers between devices, mate(): return lax.ppermute(shard, 'samp', [(0, 1), (1, 0)])  3.02 us
    ppermute x10, starting transfers between devices, mate(): return lax.ppermute(shard, 'samp', [(0, 1), (1, 0)])  2.71 us
  transfers between devices with their start and end apart: 21, of which 13 were waited for; matrix products, arithmetic and copies ran while one was open for 0% of the time, Pallas kernels for 22%

profile of v8, /device:TPU:0, one launch (start us, length us, event | category | flops | bytes accessed | tf_op | source)
XLA Modules:
  0.0 97.4 jit_solution(311245101422908927)
XLA Ops:
  0.0 3.1 %shard_map.37 = (f32[8,1024]{1,0:T(8,128)S(1)}, bf16[1024,1024]{1,0:T(8,128)(2,1)S(1)}) custom-call(bf16[1024,1024]{1,0:T(8,128)(2,1)} %dosage_hbm.1, s32[1024,1024]{1,0:T(8,128)} %observed_hbm.1), custom_call_target="tpu_custom_call" | custom-call | flops 1000 | bytes 1000 | tf_op jit(solution)/shard_map/pallas_call | solution.py:59
  3.1 0.5 collective-permute-start
  4.3 0.1 pad_add_fusion.place_ref.refs_0_
  4.3 0.1 collective-permute-done.sums_other_ref
  4.5 1.9 %shard_map.38 = (bf16[1024,256]{1,0:T(8,128)(2,1)S(1)}, bf16[1024,256]{1,0:T(8,128)(2,1)S(1)}, bf16[1024,512]{1,0:T(8,128)(2,1)S(1)}, bf16[1024,1024]{1,0:T(8,12...) custom-call(s32[3]{0:T(128)S(1)} %pad_add_fusion.place_ref.refs_0_, ...), custom_call_target="tpu_custom_call" | custom-call | flops 1000 | bytes 1000 | tf_op jit(solution)/shard_map/pallas_call | solution.py:115
  6.4 0.4 collective-permute-start.1
  6.8 1.6 %collective-permute-done.1.arrived_ref = bf16[256,1024]{1,0:T(8,128)(2,1)S(1)} collective-permute-done((bf16[256,1024]{1,0:T(8,128)(2,1)S(1)}, bf16[256,1024]{1,0:T(8,128)(2,1)S(1)}, u32[]{:S(2)}, u32[]{:S(2)}) %collective-permute-start.1) | collective-permute-done | bytes 524320 | tf_op jit(solution)/shard_map/ppermute | solution.py:351
  8.4 0.1 shard_map.39
  8.4 0.4 collective-permute-start.3
  8.8 2.7 %collective-permute-start.7 = (bf16[1024,256]{1,0:T(8,128)(2,1)S(1)}, bf16[1024,256]{1,0:T(8,128)(2,1)S(1)}, u32[]{:S(2)}, u32[]{:S(2)}) collective-permute-start(bf16[1024,256]{1,0:T(8,128)(2,1)S(1)} %get-tuple-element.47), channel_id=1, source_target_pairs={{2,0},{6,4},{10,8},{14,12},{0,2},{4,6},{8,10},{12,14},{3,1},{7,5},... | collective-permute-start | bytes 1572872 | tf_op jit(solution)/shard_map/ppermute | solution.py:341
  11.5 3.5 %collective-permute-start.2 = (bf16[512,1024]{1,0:T(8,128)(2,1)S(1)}, bf16[512,1024]{1,0:T(8,128)(2,1)S(1)}, u32[]{:S(2)}, u32[]{:S(2)}) collective-permute-start(bf16[512,1024]{1,0:T(8,128)(2,1)S(1)} %get-tuple-element.40.refs_0_), channel_id=1, source_target_pairs={{0,4},{2,6},{4,8},{6,10},{8,12},{10,14},{1,5},{3,7},{5,9},{7,11},{... | collective-permute-start | bytes 3145736 | tf_op jit(solution)/shard_map/ppermute | solution.py:341
  15.1 1.3 %collective-permute-start.6 = (bf16[1024,256]{1,0:T(8,128)(2,1)S(1)}, bf16[1024,256]{1,0:T(8,128)(2,1)S(1)}, u32[]{:S(2)}, u32[]{:S(2)}) collective-permute-start(bf16[1024,256]{1,0:T(8,128)(2,1)S(1)} %get-tuple-element.46.odd_ref), channel_id=1, source_target_pairs={{4,0},{6,2},{8,4},{10,6},{12,8},{14,10},{5,1},{7,3},{9,5},{11,7},{... | collective-permute-start | bytes 1572872 | tf_op jit(solution)/shard_map/ppermute | solution.py:341
  16.4 7.6 %collective-permute-done.7.refs_1_.refs_0_ = bf16[1024,256]{1,0:T(8,128)(2,1)S(1)} collective-permute-done((bf16[1024,256]{1,0:T(8,128)(2,1)S(1)}, bf16[1024,256]{1,0:T(8,128)(2,1)S(1)}, u32[]{:S(2)}, u32[]{:S(2)}) %collective-permute-start.7) | collective-permute-done | bytes 524320 | tf_op jit(solution)/shard_map/ppermute | solution.py:341
  23.9 1.3 %collective-permute-start.10 = (bf16[1024,512]{1,0:T(8,128)(2,1)S(1)}, bf16[1024,512]{1,0:T(8,128)(2,1)S(1)}, u32[]{:S(2)}, u32[]{:S(2)}) collective-permute-start(bf16[1024,512]{1,0:T(8,128)(2,1)S(1)} %shard_map.46), channel_id=1, source_target_pairs={{2,0},{4,2},{6,4},{8,6},{10,8},{12,10},{14,12},{3,1},{5,3},{7,5},{... | collective-permute-start | bytes 3145736 | tf_op jit(solution)/shard_map/ppermute | solution.py:341
  25.2 0.1 collective-permute-start.4
  25.3 6.5 %collective-permute-done.6.refs_0_.even_ref = bf16[1024,256]{1,0:T(8,128)(2,1)S(1)} collective-permute-done((bf16[1024,256]{1,0:T(8,128)(2,1)S(1)}, bf16[1024,256]{1,0:T(8,128)(2,1)S(1)}, u32[]{:S(2)}, u32[]{:S(2)}) %collective-permute-start.6) | collective-permute-done | bytes 524320 | tf_op jit(solution)/shard_map/ppermute | solution.py:341
  31.8 0.7 collective-permute-start.8
  32.5 0.0 collective-permute-done.4.arrived_ref
  32.5 0.1 shard_map.40.refs_1_
  32.6 3.5 %collective-permute-start.14 = (bf16[512,1024]{1,0:T(8,128)(2,1)S(1)}, bf16[512,1024]{1,0:T(8,128)(2,1)S(1)}, u32[]{:S(2)}, u32[]{:S(2)}) collective-permute-start(bf16[512,1024]{1,0:T(8,128)(2,1)S(1)} %shard_map.40.refs_1_), channel_id=1, source_target_pairs={{0,4},{2,6},{4,8},{6,10},{8,12},{10,14},{1,5},{3,7},{5,9},{7,11},{... | collective-permute-start | bytes 3145736 | tf_op jit(solution)/shard_map/ppermute | solution.py:341
  36.0 0.0 collective-permute-done.3.refs_3_.refs_2_.refs_8_
  36.1 3.8 %shard_map.41.refs_1_ = bf16[4,512,1024]{2,1,0:T(8,128)(2,1)} custom-call(s32[3]{0:T(128)S(1)} %pad_add_fusion.place_ref.refs_0_, bf16[512,1024]{1,0:T(8,128)(2,1)S(1)} %get-tuple-element.40.refs_0_, bf16[512,1024]{1,0:T(8,128)(2,1)S(1)} %shard_map.40.refs_1_, ...), custom_call_target="tpu_custom_call", output_to_operand_aliasing={{}: (5, {})} | custom-call | flops 1000 | bytes 1000 | tf_op jit(solution)/shard_map/pallas_call | solution.py:185
  39.9 0.0 collective-permute-done.2.refs_0_
  39.9 1.5 %shard_map.43 = (bf16[256,768]{1,0:T(8,128)(2,1)S(1)}, bf16[4,512,1024]{2,1,0:T(8,128)(2,1)}) custom-call(s32[3]{0:T(128)S(1)} %pad_add_fusion.place_ref.refs_0_, bf16[512,1024]{1,0:T(8,128)(2,1)S(1)} %collective-permute-done.2.refs_0_, bf16[1024,1024]{1,0:T(8,128)(2,1)S(1)} %get-tuple-element.41.refs_2_.refs_1_.refs_7_, ...), custom_call_target="tpu_custom_call", output_to_operand_aliasing={{1}: (4, {})} | custom-call | flops 1000 | bytes 1000 | tf_op jit(solution)/shard_map/pallas_call | solution.py:209
  41.4 0.0 collective-permute-done.8.odd_ref
  41.5 0.6 shard_map.45
  42.1 0.1 collective-permute-start.9
  42.1 8.6 %collective-permute-done.10.whole_ref = bf16[1024,512]{1,0:T(8,128)(2,1)S(1)} collective-permute-done((bf16[1024,512]{1,0:T(8,128)(2,1)S(1)}, bf16[1024,512]{1,0:T(8,128)(2,1)S(1)}, u32[]{:S(2)}, u32[]{:S(2)}) %collective-permute-start.10) | collective-permute-done | bytes 1048608 | tf_op jit(solution)/shard_map/ppermute | solution.py:341
  50.8 0.1 shard_map.47
  50.8 0.1 collective-permute-start.11
  50.9 0.5 collective-permute-start.12
  51.4 1.3 %collective-permute-start.5 = (bf16[256,768]{1,0:T(8,128)(2,1)S(1)}, bf16[256,768]{1,0:T(8,128)(2,1)S(1)}, u32[]{:S(2)}, u32[]{:S(2)}) collective-permute-start(bf16[256,768]{1,0:T(8,128)(2,1)S(1)} %get-tuple-element.45.refs_0_), channel_id=1, source_target_pairs={{4,0},{6,2},{8,4},{10,6},{12,8},{14,10},{5,1},{7,3},{9,5},{11,7},{... | collective-permute-start | bytes 1179656 | tf_op jit(solution)/shard_map/ppermute | solution.py:341
  52.7 0.6 shard_map.48
  53.3 0.0 collective-permute-done.9.refs_2_.refs_3_
  53.3 3.8 %collective-permute-start.16 = (bf16[1024,256]{1,0:T(8,128)(2,1)S(1)}, bf16[1024,256]{1,0:T(8,128)(2,1)S(1)}, u32[]{:S(2)}, u32[]{:S(2)}) collective-permute-start(bf16[1024,256]{1,0:T(8,128)(2,1)S(1)} %get-tuple-element.58), channel_id=1, source_target_pairs={{2,0},{6,4},{10,8},{14,12},{0,2},{4,6},{8,10},{12,14},{3,1},{7,5},... | collective-permute-start | bytes 1572872 | tf_op jit(solution)/shard_map/ppermute | solution.py:341
  57.1 0.0 collective-permute-done.11.refs_4_.refs_3_
  57.1 0.0 collective-permute-done.12.refs_6_.refs_5_
  57.1 1.5 %shard_map.49 = (bf16[256,768]{1,0:T(8,128)(2,1)S(1)}, bf16[4,512,1024]{2,1,0:T(8,128)(2,1)}) custom-call(s32[3]{0:T(128)S(1)} %pad_add_fusion.place_ref.refs_0_, bf16[512,1024]{1,0:T(8,128)(2,1)S(1)} %collective-permute-done.2.refs_0_, bf16[1024,256]{1,0:T(8,128)(2,1)S(1)} %get-tuple-element.49.refs_1_.refs_2_, ...), custom_call_target="tpu_custom_call", output_to_operand_aliasing={{1}: (8, {})} | custom-call | flops 1000 | bytes 1000 | tf_op jit(solution)/shard_map/pallas_call | solution.py:209
  58.6 1.3 %collective-permute-start.13 = (bf16[256,768]{1,0:T(8,128)(2,1)S(1)}, bf16[256,768]{1,0:T(8,128)(2,1)S(1)}, u32[]{:S(2)}, u32[]{:S(2)}) collective-permute-start(bf16[256,768]{1,0:T(8,128)(2,1)S(1)} %get-tuple-element.55), channel_id=1, source_target_pairs={{4,0},{6,2},{8,4},{10,6},{12,8},{14,10},{5,1},{7,3},{9,5},{11,7},{... | collective-permute-start | bytes 1179656 | tf_op jit(solution)/shard_map/ppermute | solution.py:341
  59.9 0.1 collective-permute-done.14.refs_0_.refs_1_
  60.1 5.1 %collective-permute-done.5.refs_1_ = bf16[256,768]{1,0:T(8,128)(2,1)S(1)} collective-permute-done((bf16[256,768]{1,0:T(8,128)(2,1)S(1)}, bf16[256,768]{1,0:T(8,128)(2,1)S(1)}, u32[]{:S(2)}, u32[]{:S(2)}) %collective-permute-start.5) | collective-permute-done | bytes 393248 | tf_op jit(solution)/shard_map/ppermute | solution.py:341
  65.2 2.3 %shard_map.51 = (bf16[256,1536]{1,0:T(8,128)(2,1)S(1)}, bf16[4,512,1024]{2,1,0:T(8,128)(2,1)}) custom-call(s32[3]{0:T(128)S(1)} %pad_add_fusion.place_ref.refs_0_, bf16[512,1024]{1,0:T(8,128)(2,1)S(1)} %collective-permute-done.14.refs_0_.refs_1_, bf16[1024,256]{1,0:T(8,128)(2,1)S(1)} %get-tuple-element.49.refs_1_.refs_2_, ...), custom_call_target="tpu_custom_call", output_to_operand_aliasing={{1}: (10, {})} | custom-call | flops 1000 | bytes 1000 | tf_op jit(solution)/shard_map/pallas_call | solution.py:209
  67.6 1.3 %collective-permute-start.15 = (bf16[256,1536]{1,0:T(8,128)(2,1)S(1)}, bf16[256,1536]{1,0:T(8,128)(2,1)S(1)}, u32[]{:S(2)}, u32[]{:S(2)}) collective-permute-start(bf16[256,1536]{1,0:T(8,128)(2,1)S(1)} %get-tuple-element.57.refs_0_), channel_id=1, source_target_pairs={{4,0},{6,2},{8,4},{10,6},{12,8},{14,10},{5,1},{7,3},{9,5},{11,7},{... | collective-permute-start | bytes 2359304 | tf_op jit(solution)/shard_map/ppermute | solution.py:341
  68.9 0.4 collective-permute-done.16.whole_ref
  69.3 4.4 %collective-permute-done.13.refs_1_.refs_2_ = bf16[256,768]{1,0:T(8,128)(2,1)S(1)} collective-permute-done((bf16[256,768]{1,0:T(8,128)(2,1)S(1)}, bf16[256,768]{1,0:T(8,128)(2,1)S(1)}, u32[]{:S(2)}, u32[]{:S(2)}) %collective-permute-start.13) | collective-permute-done | bytes 393248 | tf_op jit(solution)/shard_map/ppermute | solution.py:341
  73.7 0.1 shard_map.52
  73.8 0.1 collective-permute-start.17
  73.8 0.5 collective-permute-start.18
  74.3 0.1 collective-permute-start.20
  74.4 0.9 collective-permute-done.17.refs_3_
  75.4 0.4 collective-permute-done.18.refs_5_
  75.7 1.8 %shard_map.53 = (bf16[512,256]{1,0:T(8,128)(2,1)S(1)}, bf16[4,512,1024]{2,1,0:T(8,128)(2,1)}) custom-call(s32[3]{0:T(128)S(1)} %pad_add_fusion.place_ref.refs_0_, bf16[512,1024]{1,0:T(8,128)(2,1)S(1)} %collective-permute-done.2.refs_0_, bf16[512,1024]{1,0:T(8,128)(2,1)S(1)} %collective-permute-done.14.refs_0_.refs_1_, ...), custom_call_target="tpu_custom_call", output_to_operand_aliasing={{1}: (7, {})} | custom-call | flops 1000 | bytes 1000 | tf_op jit(solution)/shard_map/pallas_call | solution.py:209
  77.5 1.5 %collective-permute-start.19 = (bf16[512,256]{1,0:T(8,128)(2,1)S(1)}, bf16[512,256]{1,0:T(8,128)(2,1)S(1)}, u32[]{:S(2)}, u32[]{:S(2)}) collective-permute-start(bf16[512,256]{1,0:T(8,128)(2,1)S(1)} %get-tuple-element.62), channel_id=1, source_target_pairs={{4,0},{6,2},{8,4},{10,6},{12,8},{14,10},{5,1},{7,3},{9,5},{11,7},{... | collective-permute-start | bytes 786440 | tf_op jit(solution)/shard_map/ppermute | solution.py:341
  79.0 2.0 %shard_map.54.refs_6_ = bf16[4,512,1024]{2,1,0:T(8,128)(2,1)} custom-call(s32[3]{0:T(128)S(1)} %pad_add_fusion.place_ref.refs_0_, bf16[512,1024]{1,0:T(8,128)(2,1)S(1)} %get-tuple-element.40.refs_0_, bf16[512,1024]{1,0:T(8,128)(2,1)S(1)} %shard_map.40.refs_1_, ...), custom_call_target="tpu_custom_call", output_to_operand_aliasing={{}: (5, {})} | custom-call | flops 1000 | bytes 1000 | tf_op jit(solution)/shard_map/pallas_call | solution.py:185
  81.0 2.6 %shard_map.55.refs_6_ = bf16[4,512,1024]{2,1,0:T(8,128)(2,1)} custom-call(s32[3]{0:T(128)S(1)} %pad_add_fusion.place_ref.refs_0_, bf16[512,1024]{1,0:T(8,128)(2,1)S(1)} %get-tuple-element.40.refs_0_, bf16[512,1024]{1,0:T(8,128)(2,1)S(1)} %shard_map.40.refs_1_, ...), custom_call_target="tpu_custom_call", output_to_operand_aliasing={{}: (7, {})} | custom-call | flops 1000 | bytes 1000 | tf_op jit(solution)/shard_map/pallas_call | solution.py:185
  83.5 2.5 %shard_map.56.refs_4_ = bf16[4,512,1024]{2,1,0:T(8,128)(2,1)} custom-call(s32[3]{0:T(128)S(1)} %pad_add_fusion.place_ref.refs_0_, bf16[512,1024]{1,0:T(8,128)(2,1)S(1)} %get-tuple-element.40.refs_0_, bf16[512,1024]{1,0:T(8,128)(2,1)S(1)} %shard_map.40.refs_1_, bf16[1024,128]{1,0:T(8,128)(2,1)S(1)} %get-tuple-element.59.refs_2_, ...), custom_call_target="tpu_custom_call", output_to_operand_aliasing={{}: (7, {})} | custom-call | flops 1000 | bytes 1000 | tf_op jit(solution)/shard_map/pallas_call | solution.py:185
  86.0 0.0 collective-permute-done.20.refs_3_
  86.0 2.0 %shard_map.57.refs_5_ = bf16[4,512,1024]{2,1,0:T(8,128)(2,1)} custom-call(s32[3]{0:T(128)S(1)} %pad_add_fusion.place_ref.refs_0_, bf16[512,1024]{1,0:T(8,128)(2,1)S(1)} %get-tuple-element.40.refs_0_, bf16[512,1024]{1,0:T(8,128)(2,1)S(1)} %shard_map.40.refs_1_, bf16[1024,256]{1,0:T(8,128)(2,1)S(1)} %get-tuple-element.63.refs_2_, ...), custom_call_target="tpu_custom_call", output_to_operand_aliasing={{}: (5, {})} | custom-call | flops 1000 | bytes 1000 | tf_op jit(solution)/shard_map/pallas_call | solution.py:185
  88.0 2.5 %collective-permute-done.15.refs_3_ = bf16[256,1536]{1,0:T(8,128)(2,1)S(1)} collective-permute-done((bf16[256,1536]{1,0:T(8,128)(2,1)S(1)}, bf16[256,1536]{1,0:T(8,128)(2,1)S(1)}, u32[]{:S(2)}, u32[]{:S(2)}) %collective-permute-start.15) | collective-permute-done | bytes 786464 | tf_op jit(solution)/shard_map/ppermute | solution.py:341
  90.5 4.9 %collective-permute-done.19.refs_4_ = bf16[512,256]{1,0:T(8,128)(2,1)S(1)} collective-permute-done((bf16[512,256]{1,0:T(8,128)(2,1)S(1)}, bf16[512,256]{1,0:T(8,128)(2,1)S(1)}, u32[]{:S(2)}, u32[]{:S(2)}) %collective-permute-start.19) | collective-permute-done | bytes 262176 | tf_op jit(solution)/shard_map/ppermute | solution.py:341
  95.4 1.8 %shard_map.58 = bf16[4,512,1024]{2,1,0:T(8,128)(2,1)} custom-call(s32[3]{0:T(128)S(1)} %pad_add_fusion.place_ref.refs_0_, bf16[256,768]{1,0:T(8,128)(2,1)S(1)} %collective-permute-done.5.refs_1_, bf16[256,768]{1,0:T(8,128)(2,1)S(1)} %collective-permute-done.13.refs_1_.refs_2_, ...), custom_call_target="tpu_custom_call", output_to_operand_aliasing={{}: (5, {})} | custom-call | flops 1000 | bytes 1000 | tf_op jit(solution)/shard_map/pallas_call | solution.py:312
  (4 shorter events, 0.0 us)
Async XLA Ops:
  3.1 1.4 %collective-permute-start = (f32[8,1024]{1,0:T(8,128)S(1)}, f32[8,1024]{1,0:T(8,128)S(1)}, u32[]{:S(2)}, u32[]{:S(2)}) collective-permute-start(f32[8,1024]{1,0:T(8,128)S(1)} %get-tuple-element.36.sums_ref), channel_id=1, source_target_pairs={{0,1},{1,0},{2,3},{3,2},{4,5},{5,4},{6,7},{7,6},{8,9},{9,8},{10,11... | collective-permute-start | bytes 98312 | tf_op jit(solution)/shard_map/ppermute | solution.py:351
  6.4 2.0 %collective-permute-start.1 = (bf16[256,1024]{1,0:T(8,128)(2,1)S(1)}, bf16[256,1024]{1,0:T(8,128)(2,1)S(1)}, u32[]{:S(2)}, u32[]{:S(2)}) collective-permute-start(bf16[256,1024]{1,0:T(8,128)(2,1)S(1)} %get-tuple-element.38), channel_id=1, source_target_pairs={{0,1},{1,0},{2,3},{3,2},{4,5},{5,4},{6,7},{7,6},{8,9},{9,8},{10,11... | collective-permute-start | bytes 1572872 | tf_op jit(solution)/shard_map/ppermute | solution.py:351
  8.4 27.6 %collective-permute-start.3 = (bf16[1024,1024]{1,0:T(8,128)(2,1)S(1)}, bf16[1024,1024]{1,0:T(8,128)(2,1)S(1)}, u32[]{:S(2)}, u32[]{:S(2)}) collective-permute-start(bf16[1024,1024]{1,0:T(8,128)(2,1)S(1)} %get-tuple-element.41.refs_2_.refs_1_.refs_7_), channel_id=1, source_target_pairs={{0,1},{1,0},{2,3},{3,2},{4,5},{5,4},{6,7},{7,6},{8,9},{9,8},{10,11... | collective-permute-start | bytes 6291464 | tf_op jit(solution)/shard_map/ppermute | solution.py:351
  8.8 15.1 %collective-permute-start.7 = (bf16[1024,256]{1,0:T(8,128)(2,1)S(1)}, bf16[1024,256]{1,0:T(8,128)(2,1)S(1)}, u32[]{:S(2)}, u32[]{:S(2)}) collective-permute-start(bf16[1024,256]{1,0:T(8,128)(2,1)S(1)} %get-tuple-element.47), channel_id=1, source_target_pairs={{2,0},{6,4},{10,8},{14,12},{0,2},{4,6},{8,10},{12,14},{3,1},{7,5},... | collective-permute-start | bytes 1572872 | tf_op jit(solution)/shard_map/ppermute | solution.py:341
  11.5 28.4 %collective-permute-start.2 = (bf16[512,1024]{1,0:T(8,128)(2,1)S(1)}, bf16[512,1024]{1,0:T(8,128)(2,1)S(1)}, u32[]{:S(2)}, u32[]{:S(2)}) collective-permute-start(bf16[512,1024]{1,0:T(8,128)(2,1)S(1)} %get-tuple-element.40.refs_0_), channel_id=1, source_target_pairs={{0,4},{2,6},{4,8},{6,10},{8,12},{10,14},{1,5},{3,7},{5,9},{7,11},{... | collective-permute-start | bytes 3145736 | tf_op jit(solution)/shard_map/ppermute | solution.py:341
  15.1 16.7 %collective-permute-start.6 = (bf16[1024,256]{1,0:T(8,128)(2,1)S(1)}, bf16[1024,256]{1,0:T(8,128)(2,1)S(1)}, u32[]{:S(2)}, u32[]{:S(2)}) collective-permute-start(bf16[1024,256]{1,0:T(8,128)(2,1)S(1)} %get-tuple-element.46.odd_ref), channel_id=1, source_target_pairs={{4,0},{6,2},{8,4},{10,6},{12,8},{14,10},{5,1},{7,3},{9,5},{11,7},{... | collective-permute-start | bytes 1572872 | tf_op jit(solution)/shard_map/ppermute | solution.py:341
  23.9 26.8 %collective-permute-start.10 = (bf16[1024,512]{1,0:T(8,128)(2,1)S(1)}, bf16[1024,512]{1,0:T(8,128)(2,1)S(1)}, u32[]{:S(2)}, u32[]{:S(2)}) collective-permute-start(bf16[1024,512]{1,0:T(8,128)(2,1)S(1)} %shard_map.46), channel_id=1, source_target_pairs={{2,0},{4,2},{6,4},{8,6},{10,8},{12,10},{14,12},{3,1},{5,3},{7,5},{... | collective-permute-start | bytes 3145736 | tf_op jit(solution)/shard_map/ppermute | solution.py:341
  25.2 7.2 %collective-permute-start.4 = (bf16[256,1024]{1,0:T(8,128)(2,1)S(1)}, bf16[256,1024]{1,0:T(8,128)(2,1)S(1)}, u32[]{:S(2)}, u32[]{:S(2)}) collective-permute-start(bf16[256,1024]{1,0:T(8,128)(2,1)S(1)} %get-tuple-element.43), channel_id=1, source_target_pairs={{0,1},{1,0},{2,3},{3,2},{4,5},{5,4},{6,7},{7,6},{8,9},{9,8},{10,11... | collective-permute-start | bytes 1572872 | tf_op jit(solution)/shard_map/ppermute | solution.py:351
  31.8 9.7 %collective-permute-start.8 = (bf16[1024,256]{1,0:T(8,128)(2,1)S(1)}, bf16[1024,256]{1,0:T(8,128)(2,1)S(1)}, u32[]{:S(2)}, u32[]{:S(2)}) collective-permute-start(bf16[1024,256]{1,0:T(8,128)(2,1)S(1)} %shard_map.44.even_ref), channel_id=1, source_target_pairs={{6,2},{10,6},{14,10},{7,3},{11,7},{15,11},{22,18},{26,22},{30,26},... | collective-permute-start | bytes 1572872 | tf_op jit(solution)/shard_map/ppermute | solution.py:341
  32.6 27.5 %collective-permute-start.14 = (bf16[512,1024]{1,0:T(8,128)(2,1)S(1)}, bf16[512,1024]{1,0:T(8,128)(2,1)S(1)}, u32[]{:S(2)}, u32[]{:S(2)}) collective-permute-start(bf16[512,1024]{1,0:T(8,128)(2,1)S(1)} %shard_map.40.refs_1_), channel_id=1, source_target_pairs={{0,4},{2,6},{4,8},{6,10},{8,12},{10,14},{1,5},{3,7},{5,9},{7,11},{... | collective-permute-start | bytes 3145736 | tf_op jit(solution)/shard_map/ppermute | solution.py:341
  42.1 11.2 %collective-permute-start.9 = (bf16[1024,256]{1,0:T(8,128)(2,1)S(1)}, bf16[1024,256]{1,0:T(8,128)(2,1)S(1)}, u32[]{:S(2)}, u32[]{:S(2)}) collective-permute-start(bf16[1024,256]{1,0:T(8,128)(2,1)S(1)} %get-tuple-element.49.refs_1_.refs_2_), channel_id=1, source_target_pairs={{0,1},{1,0},{2,3},{3,2},{4,5},{5,4},{6,7},{7,6},{8,9},{9,8},{10,11... | collective-permute-start | bytes 1572872 | tf_op jit(solution)/shard_map/ppermute | solution.py:351
  50.8 6.3 %collective-permute-start.11 = (bf16[1024,256]{1,0:T(8,128)(2,1)S(1)}, bf16[1024,256]{1,0:T(8,128)(2,1)S(1)}, u32[]{:S(2)}, u32[]{:S(2)}) collective-permute-start(bf16[1024,256]{1,0:T(8,128)(2,1)S(1)} %get-tuple-element.51.refs_3_.refs_2_), channel_id=1, source_target_pairs={{0,1},{1,0},{2,3},{3,2},{4,5},{5,4},{6,7},{7,6},{8,9},{9,8},{10,11... | collective-permute-start | bytes 1572872 | tf_op jit(solution)/shard_map/ppermute | solution.py:351
  50.9 6.2 %collective-permute-start.12 = (bf16[1024,256]{1,0:T(8,128)(2,1)S(1)}, bf16[1024,256]{1,0:T(8,128)(2,1)S(1)}, u32[]{:S(2)}, u32[]{:S(2)}) collective-permute-start(bf16[1024,256]{1,0:T(8,128)(2,1)S(1)} %get-tuple-element.52.refs_5_.refs_4_), channel_id=1, source_target_pairs={{0,1},{1,0},{2,3},{3,2},{4,5},{5,4},{6,7},{7,6},{8,9},{9,8},{10,11... | collective-permute-start | bytes 1572872 | tf_op jit(solution)/shard_map/ppermute | solution.py:351
  51.4 13.8 %collective-permute-start.5 = (bf16[256,768]{1,0:T(8,128)(2,1)S(1)}, bf16[256,768]{1,0:T(8,128)(2,1)S(1)}, u32[]{:S(2)}, u32[]{:S(2)}) collective-permute-start(bf16[256,768]{1,0:T(8,128)(2,1)S(1)} %get-tuple-element.45.refs_0_), channel_id=1, source_target_pairs={{4,0},{6,2},{8,4},{10,6},{12,8},{14,10},{5,1},{7,3},{9,5},{11,7},{... | collective-permute-start | bytes 1179656 | tf_op jit(solution)/shard_map/ppermute | solution.py:341
  53.3 16.0 %collective-permute-start.16 = (bf16[1024,256]{1,0:T(8,128)(2,1)S(1)}, bf16[1024,256]{1,0:T(8,128)(2,1)S(1)}, u32[]{:S(2)}, u32[]{:S(2)}) collective-permute-start(bf16[1024,256]{1,0:T(8,128)(2,1)S(1)} %get-tuple-element.58), channel_id=1, source_target_pairs={{2,0},{6,4},{10,8},{14,12},{0,2},{4,6},{8,10},{12,14},{3,1},{7,5},... | collective-permute-start | bytes 1572872 | tf_op jit(solution)/shard_map/ppermute | solution.py:341
  58.6 15.0 %collective-permute-start.13 = (bf16[256,768]{1,0:T(8,128)(2,1)S(1)}, bf16[256,768]{1,0:T(8,128)(2,1)S(1)}, u32[]{:S(2)}, u32[]{:S(2)}) collective-permute-start(bf16[256,768]{1,0:T(8,128)(2,1)S(1)} %get-tuple-element.55), channel_id=1, source_target_pairs={{4,0},{6,2},{8,4},{10,6},{12,8},{14,10},{5,1},{7,3},{9,5},{11,7},{... | collective-permute-start | bytes 1179656 | tf_op jit(solution)/shard_map/ppermute | solution.py:341
  67.6 22.9 %collective-permute-start.15 = (bf16[256,1536]{1,0:T(8,128)(2,1)S(1)}, bf16[256,1536]{1,0:T(8,128)(2,1)S(1)}, u32[]{:S(2)}, u32[]{:S(2)}) collective-permute-start(bf16[256,1536]{1,0:T(8,128)(2,1)S(1)} %get-tuple-element.57.refs_0_), channel_id=1, source_target_pairs={{4,0},{6,2},{8,4},{10,6},{12,8},{14,10},{5,1},{7,3},{9,5},{11,7},{... | collective-permute-start | bytes 2359304 | tf_op jit(solution)/shard_map/ppermute | solution.py:341
  73.8 1.6 %collective-permute-start.17 = (bf16[1024,128]{1,0:T(8,128)(2,1)S(1)}, bf16[1024,128]{1,0:T(8,128)(2,1)S(1)}, u32[]{:S(2)}, u32[]{:S(2)}) collective-permute-start(bf16[1024,128]{1,0:T(8,128)(2,1)S(1)} %get-tuple-element.59.refs_2_), channel_id=1, source_target_pairs={{0,1},{1,0},{2,3},{3,2},{4,5},{5,4},{6,7},{7,6},{8,9},{9,8},{10,11... | collective-permute-start | bytes 786440 | tf_op jit(solution)/shard_map/ppermute | solution.py:351
  73.8 1.9 %collective-permute-start.18 = (bf16[1024,128]{1,0:T(8,128)(2,1)S(1)}, bf16[1024,128]{1,0:T(8,128)(2,1)S(1)}, u32[]{:S(2)}, u32[]{:S(2)}) collective-permute-start(bf16[1024,128]{1,0:T(8,128)(2,1)S(1)} %get-tuple-element.60.refs_4_), channel_id=1, source_target_pairs={{0,1},{1,0},{2,3},{3,2},{4,5},{5,4},{6,7},{7,6},{8,9},{9,8},{10,11... | collective-permute-start | bytes 786440 | tf_op jit(solution)/shard_map/ppermute | solution.py:351
  74.3 11.7 %collective-permute-start.20 = (bf16[1024,256]{1,0:T(8,128)(2,1)S(1)}, bf16[1024,256]{1,0:T(8,128)(2,1)S(1)}, u32[]{:S(2)}, u32[]{:S(2)}) collective-permute-start(bf16[1024,256]{1,0:T(8,128)(2,1)S(1)} %get-tuple-element.63.refs_2_), channel_id=1, source_target_pairs={{0,1},{1,0},{2,3},{3,2},{4,5},{5,4},{6,7},{7,6},{8,9},{9,8},{10,11... | collective-permute-start | bytes 1572872 | tf_op jit(solution)/shard_map/ppermute | solution.py:351
  77.5 17.8 %collective-permute-start.19 = (bf16[512,256]{1,0:T(8,128)(2,1)S(1)}, bf16[512,256]{1,0:T(8,128)(2,1)S(1)}, u32[]{:S(2)}, u32[]{:S(2)}) collective-permute-start(bf16[512,256]{1,0:T(8,128)(2,1)S(1)} %get-tuple-element.62), channel_id=1, source_target_pairs={{4,0},{6,2},{8,4},{10,6},{12,8},{14,10},{5,1},{7,3},{9,5},{11,7},{... | collective-permute-start | bytes 786440 | tf_op jit(solution)/shard_map/ppermute | solution.py:341

commit v9 on v8

--- a/solution.py
+++ b/solution.py
@@ -8,7 +8,8 @@
 from jax.sharding import PartitionSpec as P
 
 WIN = 4
-PIECES = (2, 2, 4)
+PIECES = (4, 2, 2)
+ROWS = (4, 4)
 PARTS = 2
 BLOCKS = 8
 STATS_VMEM = 50
@@ -75,12 +76,13 @@
 
 
 def score_kernel(place_ref, masked_ref, sums_ref, sums_other_ref, *outs):
-    pieces, whole_ref = outs[: len(PIECES)], outs[len(PIECES)]
-    rows_here, rows_away = outs[len(PIECES) + 1 : -PARTS], outs[-PARTS:]
+    pieces = outs[: len(PIECES)]
+    rows_here, rows_away = outs[len(PIECES) : -PARTS], outs[-PARTS:]
     core = place_ref[1]
-    part = rows_here[0].shape[0]
-    for step in range(2 * PARTS):
-        columns = slice(step * part, (step + 1) * part)
+    half = masked_ref.shape[1] // 2
+    size = half // 2
+    for step in range(4):
+        columns = slice(step * size, (step + 1) * size)
         totals = [
             sums_ref[n : n + 1, columns] + sums_other_ref[n : n + 1, columns]
             for n in range(3)
@@ -92,22 +94,25 @@
         masked = masked_ref[:, columns].astype(jnp.float32)
         scored = jnp.where(masked >= 0.0, (masked - center) * factor, 0.0)
         scored = scored.astype(jnp.bfloat16)
-        whole_ref[:, columns] = scored
+        at = 0
+        for piece in pieces:
+            low, high = max(step * size, at), min(step * size + size, at + piece.shape[1])
+            if low < high:
+                piece[:, low - at : high - at] = scored[:, low - step * size : high - step * size]
+            at += piece.shape[1]
         turned = scored.T
-        here = core == step // PARTS
-
-        @pl.when(here)
-        def _():
-            rows_here[step % PARTS][...] = turned
-
-        @pl.when(jnp.logical_not(here))
-        def _():
-            rows_away[step % PARTS][...] = turned
-
-    begin = 0
-    for piece in pieces:
-        piece[...] = whole_ref[:, begin : begin + piece.shape[1]]
-        begin += piece.shape[1]
+
+        def put(parts, turned=turned, begin=step % 2 * size):
+            at = 0
+            for part in parts:
+                low, high = max(begin, at), min(begin + size, at + part.shape[0])
+                if low < high:
+                    part[low - at : high - at, :] = turned[low - begin : high - begin, :]
+                at += part.shape[0]
+
+        here = core == step // 2
+        pl.when(here)(functools.partial(put, rows_here))
+        pl.when(jnp.logical_not(here))(functools.partial(put, rows_away))
 
 
 def score(place, masked, sums, sums_other):
@@ -115,12 +120,14 @@
     return pl.pallas_call(
         score_kernel,
         in_specs=[SMEM, VMEM, VMEM, VMEM],
-        out_specs=[VMEM] * (len(PIECES) + 1 + 2 * PARTS),
+        out_specs=[VMEM] * (len(PIECES) + 2 * PARTS),
         out_shape=[
             jax.ShapeDtypeStruct((samples, width * eighths // 8), jnp.bfloat16) for eighths in PIECES
         ]
-        + [jax.ShapeDtypeStruct((samples, width), jnp.bfloat16)]
-        + [jax.ShapeDtypeStruct((width // 2 // PARTS, samples), jnp.bfloat16)] * (2 * PARTS),
+        + [
+            jax.ShapeDtypeStruct((width // 2 * eighths // 8, samples), jnp.bfloat16)
+            for eighths in ROWS + ROWS
+        ],
         compiler_params=PARAMS,
         cost_estimate=COST,
     )(place, masked, sums, sums_other)
@@ -146,29 +153,27 @@
     )(here, arrived, *passed)
 
 
-def blocks(rows, rights, scale, skip=0):
-    part = rows[0].shape[0] // 2
-    at = 0
+def blocks(rows, rights, scale, stop=None):
+    left = 0
     for q in range(len(rights) // 2):
         mine, other = rights[2 * q], rights[2 * q + 1]
         width = mine.shape[1]
-        start = skip if q == len(rights) // 2 - 1 else 0
-        at -= start
-        for begin in range(start, width, 256):
+        if stop is not None and q == len(rights) // 2 - 1:
+            width = stop
+        for begin in range(0, width, 256):
             end = min(begin + 256, width)
-            for r, row in enumerate(rows):
+            top = 0
+            for row in rows:
+                part = row.shape[0] // 2
                 total = jnp.dot(
                     row[0:part, :], mine[:, begin:end], preferred_element_type=jnp.float32
                 )
                 total += jnp.dot(
                     row[part:, :], other[:, begin:end], preferred_element_type=jnp.float32
                 )
-                yield (
-                    slice(r * part, (r + 1) * part),
-                    slice(at + begin, at + end),
-                    total * scale,
-                )
-        at += width
+                yield slice(top, top + part), slice(left + begin, left + end), total * scale
+                top += part
+        left += width
 
 
 def tile_kernel(k, parts, pieces, scale, place_ref, *refs):
@@ -179,7 +184,7 @@
 
 
 def tile(place, buffer, k, column, rows, rights, samples, after=()):
-    count = rows[0].shape[0] // 2 * len(rows)
+    count = sum(row.shape[0] for row in rows) // 2
     wide = sum(right.shape[1] for right in rights) // 2
     operands = [place, *rows, *rights, *after, buffer]
     return pl.pallas_call(
@@ -194,20 +199,20 @@
     )(*operands)
 
 
-def far_kernel(scale, parts, pieces, skip, place_ref, *refs):
+def far_kernel(scale, parts, pieces, stop, place_ref, *refs):
     out_ref = refs[-2]
-    for at, columns, block in blocks(refs[:parts], refs[parts : parts + pieces], scale, skip):
+    for at, columns, block in blocks(refs[:parts], refs[parts : parts + pieces], scale, stop):
         out_ref[at, columns] = block.astype(out_ref.dtype)
 
 
-def far(place, buffer, rows, rights, samples, skip=0):
-    shape = (
-        rows[0].shape[0] // 2 * len(rows),
-        sum(right.shape[1] for right in rights) // 2 - skip,
-    )
+def far(place, buffer, rows, rights, samples, stop=None):
+    wide = sum(right.shape[1] for right in rights) // 2
+    if stop is not None:
+        wide += stop - rights[-1].shape[1]
+    shape = (sum(row.shape[0] for row in rows) // 2, wide)
     operands = [place, *rows, *rights, buffer]
     return pl.pallas_call(
-        functools.partial(far_kernel, 1.0 / samples, len(rows), len(rights), skip),
+        functools.partial(far_kernel, 1.0 / samples, len(rows), len(rights), stop),
         in_specs=[SMEM] + [VMEM] * (len(rows) + len(rights)) + [ANY],
         out_specs=[VMEM, ANY],
         out_shape=[
@@ -232,17 +237,17 @@
         out_ref[...] = even_ref[...]
 
 
-def choose(place, if_odd, if_even, *passed):
+def choose(place, if_odd, if_even, passed=(), after=()):
     operands = [if_even, *passed]
     return pl.pallas_call(
         choose_kernel,
-        in_specs=[SMEM, VMEM, VMEM] + [ANY] * len(passed),
+        in_specs=[SMEM, VMEM, VMEM] + [ANY] * (len(passed) + len(after)),
         out_specs=[VMEM] + [ANY] * len(passed) + [VMEM],
         out_shape=[jax.ShapeDtypeStruct(x.shape, x.dtype) for x in (*operands, if_odd)],
         input_output_aliases={2 + n: n for n in range(len(operands))},
         compiler_params=PARAMS,
         cost_estimate=COST,
-    )(place, if_odd, *operands)
+    )(place, if_odd, *operands, *after)
 
 
 def hold(after, *passed):
@@ -283,22 +288,28 @@
 def last_kernel(place_ref, top2, top3, bottom, side, out_ref, two, three, sems):
     keep2, keep3 = 2 < place_ref[2], 3 < place_ref[2]
     part, wide = top2.shape
-    first = side.shape[1]
+    first, after = wide - wide * PIECES[2] // (PIECES[0] + PIECES[2]), side.shape[1]
 
     def kept(keep, block):
         return jnp.where(keep, block, 0.0).astype(out_ref.dtype)
 
-    two[0:part, :] = kept(keep2, top2[...])
-    two[part:, :] = kept(keep2, bottom[:, wide:])
-    copy2 = pltpu.make_async_copy(two, out_ref.at[2, :, first:], sems.at[0])
-    copy2.start()
-    three[0:part, first:] = kept(keep3, top3[...])
-    three[part:, first:] = kept(keep3, bottom[:, 0:wide])
-    three[:, 0:first] = kept(keep3, side[...])
-    copy3 = pltpu.make_async_copy(three, out_ref.at[3], sems.at[1])
-    copy3.start()
-    copy2.wait()
-    copy3.wait()
+    two[0:part, 0:wide] = kept(keep2, top2[...])
+    two[part:, 0:wide] = kept(keep2, bottom[:, wide:])
+    copies = [
+        pltpu.make_async_copy(two.at[:, 0:first], out_ref.at[2, :, 0:first], sems.at[0]),
+        pltpu.make_async_copy(two.at[:, first:], out_ref.at[2, :, first + after :], sems.at[1]),
+        pltpu.make_async_copy(three, out_ref.at[3], sems.at[2]),
+    ]
+    copies[0].start()
+    copies[1].start()
+    for at, columns in ((0, slice(0, first)), (first, slice(first + after, None))):
+        received = slice(at, first if at == 0 else wide)
+        three[0:part, columns] = kept(keep3, top3[:, received])
+        three[part:, columns] = kept(keep3, bottom[:, received])
+    three[:, first : first + after] = kept(keep3, side[...])
+    copies[2].start()
+    for copy in copies:
+        copy.wait()
 
 
 def last(place, buffer, top2, top3, bottom, side):
@@ -317,7 +328,7 @@
         scratch_shapes=[
             pltpu.VMEM((count, top2.shape[1]), buffer.dtype),
             pltpu.VMEM((count, width), buffer.dtype),
-            pltpu.SemaphoreType.DMA((2,)),
+            pltpu.SemaphoreType.DMA((3,)),
         ],
         input_output_aliases={len(operands) - 1: 0},
         compiler_params=PARAMS,
@@ -352,12 +363,11 @@
 
     sums, masked = stats(dosage, observed)
     made = score(place, masked, sums, mate(sums))
-    (relayed, detoured, direct), whole = made[:3], made[3]
-    here, away = made[4:-PARTS], made[-PARTS:]
-    first = relayed.shape[1]
+    direct, relayed, detoured = made[:3]
+    here, away = made[3:-PARTS], made[-PARTS:]
     unset = jax.ShapeDtypeStruct((WIN, width // 2, width), jnp.bfloat16)
 
-    upper, whole, buffer = stack(here[0], mate(away[0]), (whole,), (unset,))
+    upper, buffer = stack(here[0], mate(away[0]), (), (unset,))
     below0 = send(upper, up)
     above = send(relayed, down)
     across = send(detoured, swap)
@@ -366,35 +376,38 @@
     (lower,) = stack(here[1], mate(away[1]))
     below1 = send(lower, up)
     rows = [upper, lower]
-    own = [whole, mate(whole)]
+    own = [direct, mate(direct), detoured, mate(detoured)]
     (across,) = hold((above,), across)
     around = send(across, down_odd)
 
-    buffer = tile(place, buffer, 0, 0, rows, own, samples)
     (buffer,) = hold((below0,), buffer)
-    made, buffer = far(place, buffer, [below0], own, samples, first)
+    made, buffer = far(place, buffer, [below0], own, samples)
     top2 = send(made, down)
-    across, buffer, next_detoured = choose(place, around, across, buffer)
-    above, buffer, swapped = choose(place, relayed, above, buffer)
+    across, buffer, next_detoured = choose(place, around, across, (buffer,))
+    above, buffer, swapped = choose(place, relayed, above, (buffer,))
     next_relayed = send(swapped, swap)
-    high = [next_detoured, mate(next_detoured)]
+    high = []
     for piece in split(next_direct, (made,), 2):
         high += [piece, mate(piece)]
+    high += [next_detoured, mate(next_detoured)]
     made, buffer = far(place, buffer, [below0], high, samples)
     top3 = send(made, down)
+    buffer = tile(place, buffer, 0, 0, rows, own[:2], samples)
+    buffer = tile(place, buffer, 0, 3, rows, own[2:], samples)
+    buffer = tile(place, buffer, 0, 2, rows, [relayed, mate(relayed)], samples)
 
     (buffer,) = hold((below1, top2), buffer)
-    made, buffer = far(place, buffer, [below1], high + own, samples, first)
+    made, buffer = far(place, buffer, [below1], high + own, samples)
     bottom = send(made, down)
     low = []
     for piece in split(next_relayed, (made, top3), 2):
         low += [piece, mate(piece)]
     made, buffer = far(place, buffer, [below0, below1], low, samples)
     side = send(made, down)
-    buffer = tile(place, buffer, 1, 1, rows, high[:2], samples)
-    buffer = tile(place, buffer, 1, 1, rows, high[2:], samples)
-    buffer = tile(place, buffer, 1, 0, rows, low, samples)
-    buffer = tile(place, buffer, 2, 0, rows, [above, mate(above)], samples)
+    buffer = tile(place, buffer, 1, 0, rows, high[:-2], samples)
+    buffer = tile(place, buffer, 1, 3, rows, high[-2:], samples)
+    buffer = tile(place, buffer, 1, 2, rows, low, samples)
+    buffer = tile(place, buffer, 2, 2, rows, [above, mate(above)], samples)
     buffer = last(place, buffer, top2, top3, bottom, side)
     return buffer[None]
 

time: 98.4 us -> 97.8 us (level)
  waiting for transfers between devices: 43.2 us -> 39.7 us
  Pallas kernels: 28.3 us -> 30.8 us
  starting transfers between devices: 24.8 us -> 25.9 us
    pallas_call x5 -> x7, Pallas kernels: 12.8 us -> 15.5 us  [tile(): pl.pallas_call(functools.partial(tile_kernel, k, len(rows), len(rights),...]
    ppermute x11, waiting for transfers between devices: 40.1 us -> 38.2 us  [send(): return lax.ppermute(shard, 'var', pairs)]
    ppermute x10 -> x12, waiting for transfers between devices: 3.02 us -> 1.47 us  [mate(): return lax.ppermute(shard, 'samp', [(0, 1), (1, 0)])]
    ppermute x10 -> x12, starting transfers between devices: 2.71 us -> 2.81 us  [mate(): return lax.ppermute(shard, 'samp', [(0, 1), (1, 0)])]
  transfers between devices with their start and end apart: 21 -> 23, of which waited for: 13 -> 10; matrix products, arithmetic and copies ran while one was open for 0% -> 0% of each run, Pallas kernels for 22% -> 25%
where the time goes in v9:
time: 97.8 us; the launch traced here: 97.5 us
  waiting for transfers between devices  39.7 us (41%)
  Pallas kernels  30.8 us (31%)
  starting transfers between devices  25.9 us (26%)
  between operations  1.05 us (1%)
    ppermute x11, waiting for transfers between devices, send(): return lax.ppermute(shard, 'var', pairs)  38.2 us
    ppermute x11, starting transfers between devices, send(): return lax.ppermute(shard, 'var', pairs)  23 us
    pallas_call x7, Pallas kernels, tile(): pl.pallas_call(functools.partial(tile_kernel, k, len(rows), len(rights),...  15.5 us
    pallas_call x4, Pallas kernels, far(): pl.pallas_call(functools.partial(far_kernel, 1.0 / samples, len(rows), le...  7.15 us
    pallas_call x1, Pallas kernels, stats(): pl.pallas_call(stats_kernel, in_specs=[pl.BlockSpec(memory_space=pltpu.HB...  3.08 us
    ppermute x12, starting transfers between devices, mate(): return lax.ppermute(shard, 'samp', [(0, 1), (1, 0)])  2.81 us
  transfers between devices with their start and end apart: 23, of which 10 were waited for; matrix products, arithmetic and copies ran while one was open for 0% of the time, Pallas kernels for 25%

profile of v9, /device:TPU:0, one launch (start us, length us, event | category | flops | bytes accessed | tf_op | source)
XLA Modules:
  0.0 97.5 jit_solution(15859332871906645941)
XLA Ops:
  0.0 3.1 %shard_map.37 = (f32[8,1024]{1,0:T(8,128)S(1)}, bf16[1024,1024]{1,0:T(8,128)(2,1)S(1)}) custom-call(bf16[1024,1024]{1,0:T(8,128)(2,1)} %dosage_hbm.1, s32[1024,1024]{1,0:T(8,128)} %observed_hbm.1), custom_call_target="tpu_custom_call" | custom-call | flops 1000 | bytes 1000 | tf_op jit(solution)/shard_map/pallas_call | solution.py:60
  3.1 0.5 collective-permute-start
  4.3 0.1 pad_add_fusion.place_ref.refs_0_
  4.3 0.1 collective-permute-done.sums_other_ref
  4.5 1.7 %shard_map.38 = (bf16[1024,512]{1,0:T(8,128)(2,1)S(1)}, bf16[1024,256]{1,0:T(8,128)(2,1)S(1)}, bf16[1024,256]{1,0:T(8,128)(2,1)S(1)}, bf16[256,1024]{1,0:T(8,128...) custom-call(s32[3]{0:T(128)S(1)} %pad_add_fusion.place_ref.refs_0_, ...), custom_call_target="tpu_custom_call" | custom-call | flops 1000 | bytes 1000 | tf_op jit(solution)/shard_map/pallas_call | solution.py:120
  6.2 0.4 collective-permute-start.1
  6.6 2.7 %collective-permute-start.3 = (bf16[1024,256]{1,0:T(8,128)(2,1)S(1)}, bf16[1024,256]{1,0:T(8,128)(2,1)S(1)}, u32[]{:S(2)}, u32[]{:S(2)}) collective-permute-start(bf16[1024,256]{1,0:T(8,128)(2,1)S(1)} %get-tuple-element.38.refs_3_.refs_2_.refs_9_), channel_id=1, source_target_pairs={{2,0},{6,4},{10,8},{14,12},{0,2},{4,6},{8,10},{12,14},{3,1},{7,5},... | collective-permute-start | bytes 1572872 | tf_op jit(solution)/shard_map/ppermute | solution.py:352
  9.3 0.0 collective-permute-done.1.arrived_ref
  9.3 0.1 shard_map.39
  9.4 3.8 %collective-permute-start.2 = (bf16[512,1024]{1,0:T(8,128)(2,1)S(1)}, bf16[512,1024]{1,0:T(8,128)(2,1)S(1)}, u32[]{:S(2)}, u32[]{:S(2)}) collective-permute-start(bf16[512,1024]{1,0:T(8,128)(2,1)S(1)} %get-tuple-element.37.refs_0_), channel_id=1, source_target_pairs={{0,4},{2,6},{4,8},{6,10},{8,12},{10,14},{1,5},{3,7},{5,9},{7,11},{... | collective-permute-start | bytes 3145736 | tf_op jit(solution)/shard_map/ppermute | solution.py:352
  13.2 1.3 %collective-permute-start.10 = (bf16[1024,256]{1,0:T(8,128)(2,1)S(1)}, bf16[1024,256]{1,0:T(8,128)(2,1)S(1)}, u32[]{:S(2)}, u32[]{:S(2)}) collective-permute-start(bf16[1024,256]{1,0:T(8,128)(2,1)S(1)} %get-tuple-element.44.odd_ref.refs_2_), channel_id=1, source_target_pairs={{4,0},{6,2},{8,4},{10,6},{12,8},{14,10},{5,1},{7,3},{9,5},{11,7},{... | collective-permute-start | bytes 1572872 | tf_op jit(solution)/shard_map/ppermute | solution.py:352
  14.5 7.3 %collective-permute-done.3.refs_0_.refs_1_ = bf16[1024,256]{1,0:T(8,128)(2,1)S(1)} collective-permute-done((bf16[1024,256]{1,0:T(8,128)(2,1)S(1)}, bf16[1024,256]{1,0:T(8,128)(2,1)S(1)}, u32[]{:S(2)}, u32[]{:S(2)}) %collective-permute-start.3) | collective-permute-done | bytes 524320 | tf_op jit(solution)/shard_map/ppermute | solution.py:352
  21.7 0.0 collective-permute-start.4
  21.7 0.5 collective-permute-start.14
  22.3 1.3 %collective-permute-start.7 = (bf16[1024,512]{1,0:T(8,128)(2,1)S(1)}, bf16[1024,512]{1,0:T(8,128)(2,1)S(1)}, u32[]{:S(2)}, u32[]{:S(2)}) collective-permute-start(bf16[1024,512]{1,0:T(8,128)(2,1)S(1)} %shard_map.40.refs_1_.refs_2_.refs_7_), channel_id=1, source_target_pairs={{2,0},{4,2},{6,4},{8,6},{10,8},{12,10},{14,12},{3,1},{5,3},{7,5},{... | collective-permute-start | bytes 3145736 | tf_op jit(solution)/shard_map/ppermute | solution.py:352
  23.5 6.0 %collective-permute-done.10.refs_0_.even_ref = bf16[1024,256]{1,0:T(8,128)(2,1)S(1)} collective-permute-done((bf16[1024,256]{1,0:T(8,128)(2,1)S(1)}, bf16[1024,256]{1,0:T(8,128)(2,1)S(1)}, u32[]{:S(2)}, u32[]{:S(2)}) %collective-permute-start.10) | collective-permute-done | bytes 524320 | tf_op jit(solution)/shard_map/ppermute | solution.py:352
  29.6 0.0 collective-permute-start.5
  29.6 0.0 collective-permute-done.14.arrived_ref
  29.6 0.7 collective-permute-start.11
  30.3 0.1 shard_map.48.refs_1_
  30.3 5.5 %collective-permute-done.2.refs_0_ = bf16[512,1024]{1,0:T(8,128)(2,1)S(1)} collective-permute-done((bf16[512,1024]{1,0:T(8,128)(2,1)S(1)}, bf16[512,1024]{1,0:T(8,128)(2,1)S(1)}, u32[]{:S(2)}, u32[]{:S(2)}) %collective-permute-start.2) | collective-permute-done | bytes 1048608 | tf_op jit(solution)/shard_map/ppermute | solution.py:352
  35.8 4.4 %collective-permute-start.15 = (bf16[512,1024]{1,0:T(8,128)(2,1)S(1)}, bf16[512,1024]{1,0:T(8,128)(2,1)S(1)}, u32[]{:S(2)}, u32[]{:S(2)}) collective-permute-start(bf16[512,1024]{1,0:T(8,128)(2,1)S(1)} %shard_map.48.refs_1_), channel_id=1, source_target_pairs={{0,4},{2,6},{4,8},{6,10},{8,12},{10,14},{1,5},{3,7},{5,9},{7,11},{... | collective-permute-start | bytes 3145736 | tf_op jit(solution)/shard_map/ppermute | solution.py:352
  40.3 0.0 collective-permute-done.5.refs_4_.refs_3_.refs_10_
  40.3 0.0 collective-permute-done.4.refs_2_.refs_3_.refs_8_
  40.3 1.5 %shard_map.42 = (bf16[256,768]{1,0:T(8,128)(2,1)S(1)}, bf16[4,512,1024]{2,1,0:T(8,128)(2,1)}) custom-call(s32[3]{0:T(128)S(1)} %pad_add_fusion.place_ref.refs_0_, bf16[512,1024]{1,0:T(8,128)(2,1)S(1)} %collective-permute-done.2.refs_0_, bf16[1024,512]{1,0:T(8,128)(2,1)S(1)} %shard_map.40.refs_1_.refs_2_.refs_7_, ...), custom_call_target="tpu_custom_call", output_to_operand_aliasing={{1}: (6, {})} | custom-call | flops 1000 | bytes 1000 | tf_op jit(solution)/shard_map/pallas_call | solution.py:214
  41.8 0.0 collective-permute-done.11.odd_ref
  41.9 0.6 shard_map.45
  42.5 0.1 collective-permute-start.12
  42.5 6.7 %collective-permute-done.7.whole_ref = bf16[1024,512]{1,0:T(8,128)(2,1)S(1)} collective-permute-done((bf16[1024,512]{1,0:T(8,128)(2,1)S(1)}, bf16[1024,512]{1,0:T(8,128)(2,1)S(1)}, u32[]{:S(2)}, u32[]{:S(2)}) %collective-permute-start.7) | collective-permute-done | bytes 1048608 | tf_op jit(solution)/shard_map/ppermute | solution.py:352
  49.2 0.1 shard_map.43
  49.3 0.1 collective-permute-start.8
  49.4 0.5 collective-permute-start.9
  49.9 0.1 collective-permute-start.16
  49.9 0.0 collective-permute-done.12.refs_6_.refs_3_
  49.9 1.3 %collective-permute-start.6 = (bf16[256,768]{1,0:T(8,128)(2,1)S(1)}, bf16[256,768]{1,0:T(8,128)(2,1)S(1)}, u32[]{:S(2)}, u32[]{:S(2)}) collective-permute-start(bf16[256,768]{1,0:T(8,128)(2,1)S(1)} %get-tuple-element.41.refs_0_), channel_id=1, source_target_pairs={{4,0},{6,2},{8,4},{10,6},{12,8},{14,10},{5,1},{7,3},{9,5},{11,7},{... | collective-permute-start | bytes 1179656 | tf_op jit(solution)/shard_map/ppermute | solution.py:352
  51.2 0.6 shard_map.46
  51.8 0.0 collective-permute-done.8.refs_2_.refs_3_
  51.8 3.6 %collective-permute-start.18 = (bf16[1024,256]{1,0:T(8,128)(2,1)S(1)}, bf16[1024,256]{1,0:T(8,128)(2,1)S(1)}, u32[]{:S(2)}, u32[]{:S(2)}) collective-permute-start(bf16[1024,256]{1,0:T(8,128)(2,1)S(1)} %get-tuple-element.54), channel_id=1, source_target_pairs={{2,0},{6,4},{10,8},{14,12},{0,2},{4,6},{8,10},{12,14},{3,1},{7,5},... | collective-permute-start | bytes 1572872 | tf_op jit(solution)/shard_map/ppermute | solution.py:352
  55.4 0.0 collective-permute-done.9.refs_4_.refs_5_
  55.4 1.5 %shard_map.47 = (bf16[256,768]{1,0:T(8,128)(2,1)S(1)}, bf16[4,512,1024]{2,1,0:T(8,128)(2,1)}) custom-call(s32[3]{0:T(128)S(1)} %pad_add_fusion.place_ref.refs_0_, bf16[512,1024]{1,0:T(8,128)(2,1)S(1)} %collective-permute-done.2.refs_0_, bf16[1024,256]{1,0:T(8,128)(2,1)S(1)} %get-tuple-element.42.refs_1_.refs_2_, ...), custom_call_target="tpu_custom_call", output_to_operand_aliasing={{1}: (8, {})} | custom-call | flops 1000 | bytes 1000 | tf_op jit(solution)/shard_map/pallas_call | solution.py:214
  56.9 1.3 %collective-permute-start.13 = (bf16[256,768]{1,0:T(8,128)(2,1)S(1)}, bf16[256,768]{1,0:T(8,128)(2,1)S(1)}, u32[]{:S(2)}, u32[]{:S(2)}) collective-permute-start(bf16[256,768]{1,0:T(8,128)(2,1)S(1)} %get-tuple-element.49), channel_id=1, source_target_pairs={{4,0},{6,2},{8,4},{10,6},{12,8},{14,10},{5,1},{7,3},{9,5},{11,7},{... | collective-permute-start | bytes 1179656 | tf_op jit(solution)/shard_map/ppermute | solution.py:352
  58.2 2.6 %shard_map.49.refs_4_ = bf16[4,512,1024]{2,1,0:T(8,128)(2,1)} custom-call(s32[3]{0:T(128)S(1)} %pad_add_fusion.place_ref.refs_0_, bf16[512,1024]{1,0:T(8,128)(2,1)S(1)} %get-tuple-element.37.refs_0_, bf16[512,1024]{1,0:T(8,128)(2,1)S(1)} %shard_map.48.refs_1_, ...), custom_call_target="tpu_custom_call", output_to_operand_aliasing={{}: (5, {})} | custom-call | flops 1000 | bytes 1000 | tf_op jit(solution)/shard_map/pallas_call | solution.py:190
  60.8 2.0 %shard_map.50.refs_4_ = bf16[4,512,1024]{2,1,0:T(8,128)(2,1)} custom-call(s32[3]{0:T(128)S(1)} %pad_add_fusion.place_ref.refs_0_, bf16[512,1024]{1,0:T(8,128)(2,1)S(1)} %get-tuple-element.37.refs_0_, bf16[512,1024]{1,0:T(8,128)(2,1)S(1)} %shard_map.48.refs_1_, ...), custom_call_target="tpu_custom_call", output_to_operand_aliasing={{}: (5, {})} | custom-call | flops 1000 | bytes 1000 | tf_op jit(solution)/shard_map/pallas_call | solution.py:190
  62.8 2.0 %shard_map.51.refs_2_ = bf16[4,512,1024]{2,1,0:T(8,128)(2,1)} custom-call(s32[3]{0:T(128)S(1)} %pad_add_fusion.place_ref.refs_0_, bf16[512,1024]{1,0:T(8,128)(2,1)S(1)} %get-tuple-element.37.refs_0_, bf16[512,1024]{1,0:T(8,128)(2,1)S(1)} %shard_map.48.refs_1_, ...), custom_call_target="tpu_custom_call", output_to_operand_aliasing={{}: (5, {})} | custom-call | flops 1000 | bytes 1000 | tf_op jit(solution)/shard_map/pallas_call | solution.py:190
  64.7 0.0 collective-permute-done.15.refs_0_.refs_1_
  64.7 0.0 collective-permute-done.6.refs_1_
  64.7 2.3 %shard_map.53 = (bf16[256,1536]{1,0:T(8,128)(2,1)S(1)}, bf16[4,512,1024]{2,1,0:T(8,128)(2,1)}) custom-call(s32[3]{0:T(128)S(1)} %pad_add_fusion.place_ref.refs_0_, bf16[512,1024]{1,0:T(8,128)(2,1)S(1)} %collective-permute-done.15.refs_0_.refs_1_, bf16[1024,256]{1,0:T(8,128)(2,1)S(1)} %get-tuple-element.42.refs_1_.refs_2_, ...), custom_call_target="tpu_custom_call", output_to_operand_aliasing={{1}: (12, {})} | custom-call | flops 1000 | bytes 1000 | tf_op jit(solution)/shard_map/pallas_call | solution.py:214
  67.1 1.3 %collective-permute-start.17 = (bf16[256,1536]{1,0:T(8,128)(2,1)S(1)}, bf16[256,1536]{1,0:T(8,128)(2,1)S(1)}, u32[]{:S(2)}, u32[]{:S(2)}) collective-permute-start(bf16[256,1536]{1,0:T(8,128)(2,1)S(1)} %get-tuple-element.53.refs_0_), channel_id=1, source_target_pairs={{4,0},{6,2},{8,4},{10,6},{12,8},{14,10},{5,1},{7,3},{9,5},{11,7},{... | collective-permute-start | bytes 2359304 | tf_op jit(solution)/shard_map/ppermute | solution.py:352
  68.4 3.4 %collective-permute-done.13.refs_1_.refs_2_ = bf16[256,768]{1,0:T(8,128)(2,1)S(1)} collective-permute-done((bf16[256,768]{1,0:T(8,128)(2,1)S(1)}, bf16[256,768]{1,0:T(8,128)(2,1)S(1)}, u32[]{:S(2)}, u32[]{:S(2)}) %collective-permute-start.13) | collective-permute-done | bytes 393248 | tf_op jit(solution)/shard_map/ppermute | solution.py:352
  71.8 0.1 shard_map.54
  71.9 0.1 collective-permute-start.19
  71.9 0.5 collective-permute-start.20
  72.4 0.1 collective-permute-start.22
  72.5 0.9 collective-permute-done.19.refs_3_
  73.5 0.4 collective-permute-done.20.refs_5_
  73.8 1.8 %shard_map.55 = (bf16[512,256]{1,0:T(8,128)(2,1)S(1)}, bf16[4,512,1024]{2,1,0:T(8,128)(2,1)}) custom-call(s32[3]{0:T(128)S(1)} %pad_add_fusion.place_ref.refs_0_, bf16[512,1024]{1,0:T(8,128)(2,1)S(1)} %collective-permute-done.2.refs_0_, bf16[512,1024]{1,0:T(8,128)(2,1)S(1)} %collective-permute-done.15.refs_0_.refs_1_, ...), custom_call_target="tpu_custom_call", output_to_operand_aliasing={{1}: (7, {})} | custom-call | flops 1000 | bytes 1000 | tf_op jit(solution)/shard_map/pallas_call | solution.py:214
  75.6 1.5 %collective-permute-start.21 = (bf16[512,256]{1,0:T(8,128)(2,1)S(1)}, bf16[512,256]{1,0:T(8,128)(2,1)S(1)}, u32[]{:S(2)}, u32[]{:S(2)}) collective-permute-start(bf16[512,256]{1,0:T(8,128)(2,1)S(1)} %get-tuple-element.58), channel_id=1, source_target_pairs={{4,0},{6,2},{8,4},{10,6},{12,8},{14,10},{5,1},{7,3},{9,5},{11,7},{... | collective-permute-start | bytes 786440 | tf_op jit(solution)/shard_map/ppermute | solution.py:352
  77.1 2.6 %shard_map.56.refs_4_ = bf16[4,512,1024]{2,1,0:T(8,128)(2,1)} custom-call(s32[3]{0:T(128)S(1)} %pad_add_fusion.place_ref.refs_0_, bf16[512,1024]{1,0:T(8,128)(2,1)S(1)} %get-tuple-element.37.refs_0_, bf16[512,1024]{1,0:T(8,128)(2,1)S(1)} %shard_map.48.refs_1_, ...), custom_call_target="tpu_custom_call", output_to_operand_aliasing={{}: (7, {})} | custom-call | flops 1000 | bytes 1000 | tf_op jit(solution)/shard_map/pallas_call | solution.py:190
  79.7 2.0 %shard_map.57.refs_6_ = bf16[4,512,1024]{2,1,0:T(8,128)(2,1)} custom-call(s32[3]{0:T(128)S(1)} %pad_add_fusion.place_ref.refs_0_, bf16[512,1024]{1,0:T(8,128)(2,1)S(1)} %get-tuple-element.37.refs_0_, bf16[512,1024]{1,0:T(8,128)(2,1)S(1)} %shard_map.48.refs_1_, ...), custom_call_target="tpu_custom_call", output_to_operand_aliasing={{}: (5, {})} | custom-call | flops 1000 | bytes 1000 | tf_op jit(solution)/shard_map/pallas_call | solution.py:190
  81.6 2.5 %shard_map.58.refs_4_ = bf16[4,512,1024]{2,1,0:T(8,128)(2,1)} custom-call(s32[3]{0:T(128)S(1)} %pad_add_fusion.place_ref.refs_0_, bf16[512,1024]{1,0:T(8,128)(2,1)S(1)} %get-tuple-element.37.refs_0_, bf16[512,1024]{1,0:T(8,128)(2,1)S(1)} %shard_map.48.refs_1_, bf16[1024,128]{1,0:T(8,128)(2,1)S(1)} %get-tuple-element.55.refs_2_, ...), custom_call_target="tpu_custom_call", output_to_operand_aliasing={{}: (7, {})} | custom-call | flops 1000 | bytes 1000 | tf_op jit(solution)/shard_map/pallas_call | solution.py:190
  84.1 2.0 %shard_map.59.refs_5_ = bf16[4,512,1024]{2,1,0:T(8,128)(2,1)} custom-call(s32[3]{0:T(128)S(1)} %pad_add_fusion.place_ref.refs_0_, bf16[512,1024]{1,0:T(8,128)(2,1)S(1)} %get-tuple-element.37.refs_0_, bf16[512,1024]{1,0:T(8,128)(2,1)S(1)} %shard_map.48.refs_1_, bf16[1024,256]{1,0:T(8,128)(2,1)S(1)} %get-tuple-element.59.refs_2_, ...), custom_call_target="tpu_custom_call", output_to_operand_aliasing={{}: (5, {})} | custom-call | flops 1000 | bytes 1000 | tf_op jit(solution)/shard_map/pallas_call | solution.py:190
  86.1 4.5 %collective-permute-done.17.refs_3_ = bf16[256,1536]{1,0:T(8,128)(2,1)S(1)} collective-permute-done((bf16[256,1536]{1,0:T(8,128)(2,1)S(1)}, bf16[256,1536]{1,0:T(8,128)(2,1)S(1)}, u32[]{:S(2)}, u32[]{:S(2)}) %collective-permute-start.17) | collective-permute-done | bytes 786464 | tf_op jit(solution)/shard_map/ppermute | solution.py:352
  90.6 4.8 %collective-permute-done.21.refs_4_ = bf16[512,256]{1,0:T(8,128)(2,1)S(1)} collective-permute-done((bf16[512,256]{1,0:T(8,128)(2,1)S(1)}, bf16[512,256]{1,0:T(8,128)(2,1)S(1)}, u32[]{:S(2)}, u32[]{:S(2)}) %collective-permute-start.21) | collective-permute-done | bytes 262176 | tf_op jit(solution)/shard_map/ppermute | solution.py:352
  95.5 1.8 %shard_map.60 = bf16[4,512,1024]{2,1,0:T(8,128)(2,1)} custom-call(s32[3]{0:T(128)S(1)} %pad_add_fusion.place_ref.refs_0_, bf16[256,768]{1,0:T(8,128)(2,1)S(1)} %collective-permute-done.6.refs_1_, bf16[256,768]{1,0:T(8,128)(2,1)S(1)} %collective-permute-done.13.refs_1_.refs_2_, ...), custom_call_target="tpu_custom_call", output_to_operand_aliasing={{}: (5, {})} | custom-call | flops 1000 | bytes 1000 | tf_op jit(solution)/shard_map/pallas_call | solution.py:323
  (7 shorter events, 0.0 us)
Async XLA Ops:
  3.1 1.4 %collective-permute-start = (f32[8,1024]{1,0:T(8,128)S(1)}, f32[8,1024]{1,0:T(8,128)S(1)}, u32[]{:S(2)}, u32[]{:S(2)}) collective-permute-start(f32[8,1024]{1,0:T(8,128)S(1)} %get-tuple-element.34.sums_ref), channel_id=1, source_target_pairs={{0,1},{1,0},{2,3},{3,2},{4,5},{5,4},{6,7},{7,6},{8,9},{9,8},{10,11... | collective-permute-start | bytes 98312 | tf_op jit(solution)/shard_map/ppermute | solution.py:362
  6.2 3.1 %collective-permute-start.1 = (bf16[256,1024]{1,0:T(8,128)(2,1)S(1)}, bf16[256,1024]{1,0:T(8,128)(2,1)S(1)}, u32[]{:S(2)}, u32[]{:S(2)}) collective-permute-start(bf16[256,1024]{1,0:T(8,128)(2,1)S(1)} %get-tuple-element.36), channel_id=1, source_target_pairs={{0,1},{1,0},{2,3},{3,2},{4,5},{5,4},{6,7},{7,6},{8,9},{9,8},{10,11... | collective-permute-start | bytes 1572872 | tf_op jit(solution)/shard_map/ppermute | solution.py:362
  6.6 15.1 %collective-permute-start.3 = (bf16[1024,256]{1,0:T(8,128)(2,1)S(1)}, bf16[1024,256]{1,0:T(8,128)(2,1)S(1)}, u32[]{:S(2)}, u32[]{:S(2)}) collective-permute-start(bf16[1024,256]{1,0:T(8,128)(2,1)S(1)} %get-tuple-element.38.refs_3_.refs_2_.refs_9_), channel_id=1, source_target_pairs={{2,0},{6,4},{10,8},{14,12},{0,2},{4,6},{8,10},{12,14},{3,1},{7,5},... | collective-permute-start | bytes 1572872 | tf_op jit(solution)/shard_map/ppermute | solution.py:352
  9.4 26.4 %collective-permute-start.2 = (bf16[512,1024]{1,0:T(8,128)(2,1)S(1)}, bf16[512,1024]{1,0:T(8,128)(2,1)S(1)}, u32[]{:S(2)}, u32[]{:S(2)}) collective-permute-start(bf16[512,1024]{1,0:T(8,128)(2,1)S(1)} %get-tuple-element.37.refs_0_), channel_id=1, source_target_pairs={{0,4},{2,6},{4,8},{6,10},{8,12},{10,14},{1,5},{3,7},{5,9},{7,11},{... | collective-permute-start | bytes 3145736 | tf_op jit(solution)/shard_map/ppermute | solution.py:352
  13.2 16.4 %collective-permute-start.10 = (bf16[1024,256]{1,0:T(8,128)(2,1)S(1)}, bf16[1024,256]{1,0:T(8,128)(2,1)S(1)}, u32[]{:S(2)}, u32[]{:S(2)}) collective-permute-start(bf16[1024,256]{1,0:T(8,128)(2,1)S(1)} %get-tuple-element.44.odd_ref.refs_2_), channel_id=1, source_target_pairs={{4,0},{6,2},{8,4},{10,6},{12,8},{14,10},{5,1},{7,3},{9,5},{11,7},{... | collective-permute-start | bytes 1572872 | tf_op jit(solution)/shard_map/ppermute | solution.py:352
  21.7 18.6 %collective-permute-start.4 = (bf16[1024,512]{1,0:T(8,128)(2,1)S(1)}, bf16[1024,512]{1,0:T(8,128)(2,1)S(1)}, u32[]{:S(2)}, u32[]{:S(2)}) collective-permute-start(bf16[1024,512]{1,0:T(8,128)(2,1)S(1)} %shard_map.40.refs_1_.refs_2_.refs_7_), channel_id=1, source_target_pairs={{0,1},{1,0},{2,3},{3,2},{4,5},{5,4},{6,7},{7,6},{8,9},{9,8},{10,11... | collective-permute-start | bytes 3145736 | tf_op jit(solution)/shard_map/ppermute | solution.py:362
  21.7 7.8 %collective-permute-start.14 = (bf16[256,1024]{1,0:T(8,128)(2,1)S(1)}, bf16[256,1024]{1,0:T(8,128)(2,1)S(1)}, u32[]{:S(2)}, u32[]{:S(2)}) collective-permute-start(bf16[256,1024]{1,0:T(8,128)(2,1)S(1)} %get-tuple-element.51), channel_id=1, source_target_pairs={{0,1},{1,0},{2,3},{3,2},{4,5},{5,4},{6,7},{7,6},{8,9},{9,8},{10,11... | collective-permute-start | bytes 1572872 | tf_op jit(solution)/shard_map/ppermute | solution.py:362
  22.3 27.0 %collective-permute-start.7 = (bf16[1024,512]{1,0:T(8,128)(2,1)S(1)}, bf16[1024,512]{1,0:T(8,128)(2,1)S(1)}, u32[]{:S(2)}, u32[]{:S(2)}) collective-permute-start(bf16[1024,512]{1,0:T(8,128)(2,1)S(1)} %shard_map.40.refs_1_.refs_2_.refs_7_), channel_id=1, source_target_pairs={{2,0},{4,2},{6,4},{8,6},{10,8},{12,10},{14,12},{3,1},{5,3},{7,5},{... | collective-permute-start | bytes 3145736 | tf_op jit(solution)/shard_map/ppermute | solution.py:352
  29.6 10.7 %collective-permute-start.5 = (bf16[1024,256]{1,0:T(8,128)(2,1)S(1)}, bf16[1024,256]{1,0:T(8,128)(2,1)S(1)}, u32[]{:S(2)}, u32[]{:S(2)}) collective-permute-start(bf16[1024,256]{1,0:T(8,128)(2,1)S(1)} %get-tuple-element.38.refs_3_.refs_2_.refs_9_), channel_id=1, source_target_pairs={{0,1},{1,0},{2,3},{3,2},{4,5},{5,4},{6,7},{7,6},{8,9},{9,8},{10,11... | collective-permute-start | bytes 1572872 | tf_op jit(solution)/shard_map/ppermute | solution.py:362
  29.6 12.3 %collective-permute-start.11 = (bf16[1024,256]{1,0:T(8,128)(2,1)S(1)}, bf16[1024,256]{1,0:T(8,128)(2,1)S(1)}, u32[]{:S(2)}, u32[]{:S(2)}) collective-permute-start(bf16[1024,256]{1,0:T(8,128)(2,1)S(1)} %shard_map.44.even_ref), channel_id=1, source_target_pairs={{6,2},{10,6},{14,10},{7,3},{11,7},{15,11},{22,18},{26,22},{30,26},... | collective-permute-start | bytes 1572872 | tf_op jit(solution)/shard_map/ppermute | solution.py:352
  35.8 28.9 %collective-permute-start.15 = (bf16[512,1024]{1,0:T(8,128)(2,1)S(1)}, bf16[512,1024]{1,0:T(8,128)(2,1)S(1)}, u32[]{:S(2)}, u32[]{:S(2)}) collective-permute-start(bf16[512,1024]{1,0:T(8,128)(2,1)S(1)} %shard_map.48.refs_1_), channel_id=1, source_target_pairs={{0,4},{2,6},{4,8},{6,10},{8,12},{10,14},{1,5},{3,7},{5,9},{7,11},{... | collective-permute-start | bytes 3145736 | tf_op jit(solution)/shard_map/ppermute | solution.py:352
  42.5 7.5 %collective-permute-start.12 = (bf16[1024,256]{1,0:T(8,128)(2,1)S(1)}, bf16[1024,256]{1,0:T(8,128)(2,1)S(1)}, u32[]{:S(2)}, u32[]{:S(2)}) collective-permute-start(bf16[1024,256]{1,0:T(8,128)(2,1)S(1)} %get-tuple-element.46.refs_5_.refs_2_), channel_id=1, source_target_pairs={{0,1},{1,0},{2,3},{3,2},{4,5},{5,4},{6,7},{7,6},{8,9},{9,8},{10,11... | collective-permute-start | bytes 1572872 | tf_op jit(solution)/shard_map/ppermute | solution.py:362
  49.3 2.5 %collective-permute-start.8 = (bf16[1024,256]{1,0:T(8,128)(2,1)S(1)}, bf16[1024,256]{1,0:T(8,128)(2,1)S(1)}, u32[]{:S(2)}, u32[]{:S(2)}) collective-permute-start(bf16[1024,256]{1,0:T(8,128)(2,1)S(1)} %get-tuple-element.42.refs_1_.refs_2_), channel_id=1, source_target_pairs={{0,1},{1,0},{2,3},{3,2},{4,5},{5,4},{6,7},{7,6},{8,9},{9,8},{10,11... | collective-permute-start | bytes 1572872 | tf_op jit(solution)/shard_map/ppermute | solution.py:362
  49.4 6.0 %collective-permute-start.9 = (bf16[1024,256]{1,0:T(8,128)(2,1)S(1)}, bf16[1024,256]{1,0:T(8,128)(2,1)S(1)}, u32[]{:S(2)}, u32[]{:S(2)}) collective-permute-start(bf16[1024,256]{1,0:T(8,128)(2,1)S(1)} %get-tuple-element.43.refs_3_.refs_4_), channel_id=1, source_target_pairs={{0,1},{1,0},{2,3},{3,2},{4,5},{5,4},{6,7},{7,6},{8,9},{9,8},{10,11... | collective-permute-start | bytes 1572872 | tf_op jit(solution)/shard_map/ppermute | solution.py:362
  49.9 12.9 %collective-permute-start.16 = (bf16[1024,256]{1,0:T(8,128)(2,1)S(1)}, bf16[1024,256]{1,0:T(8,128)(2,1)S(1)}, u32[]{:S(2)}, u32[]{:S(2)}) collective-permute-start(bf16[1024,256]{1,0:T(8,128)(2,1)S(1)} %get-tuple-element.44.odd_ref.refs_2_), channel_id=1, source_target_pairs={{0,1},{1,0},{2,3},{3,2},{4,5},{5,4},{6,7},{7,6},{8,9},{9,8},{10,11... | collective-permute-start | bytes 1572872 | tf_op jit(solution)/shard_map/ppermute | solution.py:362
  49.9 14.8 %collective-permute-start.6 = (bf16[256,768]{1,0:T(8,128)(2,1)S(1)}, bf16[256,768]{1,0:T(8,128)(2,1)S(1)}, u32[]{:S(2)}, u32[]{:S(2)}) collective-permute-start(bf16[256,768]{1,0:T(8,128)(2,1)S(1)} %get-tuple-element.41.refs_0_), channel_id=1, source_target_pairs={{4,0},{6,2},{8,4},{10,6},{12,8},{14,10},{5,1},{7,3},{9,5},{11,7},{... | collective-permute-start | bytes 1179656 | tf_op jit(solution)/shard_map/ppermute | solution.py:352
  51.8 16.5 %collective-permute-start.18 = (bf16[1024,256]{1,0:T(8,128)(2,1)S(1)}, bf16[1024,256]{1,0:T(8,128)(2,1)S(1)}, u32[]{:S(2)}, u32[]{:S(2)}) collective-permute-start(bf16[1024,256]{1,0:T(8,128)(2,1)S(1)} %get-tuple-element.54), channel_id=1, source_target_pairs={{2,0},{6,4},{10,8},{14,12},{0,2},{4,6},{8,10},{12,14},{3,1},{7,5},... | collective-permute-start | bytes 1572872 | tf_op jit(solution)/shard_map/ppermute | solution.py:352
  56.9 14.8 %collective-permute-start.13 = (bf16[256,768]{1,0:T(8,128)(2,1)S(1)}, bf16[256,768]{1,0:T(8,128)(2,1)S(1)}, u32[]{:S(2)}, u32[]{:S(2)}) collective-permute-start(bf16[256,768]{1,0:T(8,128)(2,1)S(1)} %get-tuple-element.49), channel_id=1, source_target_pairs={{4,0},{6,2},{8,4},{10,6},{12,8},{14,10},{5,1},{7,3},{9,5},{11,7},{... | collective-permute-start | bytes 1179656 | tf_op jit(solution)/shard_map/ppermute | solution.py:352
  67.1 23.5 %collective-permute-start.17 = (bf16[256,1536]{1,0:T(8,128)(2,1)S(1)}, bf16[256,1536]{1,0:T(8,128)(2,1)S(1)}, u32[]{:S(2)}, u32[]{:S(2)}) collective-permute-start(bf16[256,1536]{1,0:T(8,128)(2,1)S(1)} %get-tuple-element.53.refs_0_), channel_id=1, source_target_pairs={{4,0},{6,2},{8,4},{10,6},{12,8},{14,10},{5,1},{7,3},{9,5},{11,7},{... | collective-permute-start | bytes 2359304 | tf_op jit(solution)/shard_map/ppermute | solution.py:352
  71.9 1.6 %collective-permute-start.19 = (bf16[1024,128]{1,0:T(8,128)(2,1)S(1)}, bf16[1024,128]{1,0:T(8,128)(2,1)S(1)}, u32[]{:S(2)}, u32[]{:S(2)}) collective-permute-start(bf16[1024,128]{1,0:T(8,128)(2,1)S(1)} %get-tuple-element.55.refs_2_), channel_id=1, source_target_pairs={{0,1},{1,0},{2,3},{3,2},{4,5},{5,4},{6,7},{7,6},{8,9},{9,8},{10,11... | collective-permute-start | bytes 786440 | tf_op jit(solution)/shard_map/ppermute | solution.py:362
  71.9 1.9 %collective-permute-start.20 = (bf16[1024,128]{1,0:T(8,128)(2,1)S(1)}, bf16[1024,128]{1,0:T(8,128)(2,1)S(1)}, u32[]{:S(2)}, u32[]{:S(2)}) collective-permute-start(bf16[1024,128]{1,0:T(8,128)(2,1)S(1)} %get-tuple-element.56.refs_4_), channel_id=1, source_target_pairs={{0,1},{1,0},{2,3},{3,2},{4,5},{5,4},{6,7},{7,6},{8,9},{9,8},{10,11... | collective-permute-start | bytes 786440 | tf_op jit(solution)/shard_map/ppermute | solution.py:362
  72.4 11.7 %collective-permute-start.22 = (bf16[1024,256]{1,0:T(8,128)(2,1)S(1)}, bf16[1024,256]{1,0:T(8,128)(2,1)S(1)}, u32[]{:S(2)}, u32[]{:S(2)}) collective-permute-start(bf16[1024,256]{1,0:T(8,128)(2,1)S(1)} %get-tuple-element.59.refs_2_), channel_id=1, source_target_pairs={{0,1},{1,0},{2,3},{3,2},{4,5},{5,4},{6,7},{7,6},{8,9},{9,8},{10,11... | collective-permute-start | bytes 1572872 | tf_op jit(solution)/shard_map/ppermute | solution.py:362
  75.6 19.8 %collective-permute-start.21 = (bf16[512,256]{1,0:T(8,128)(2,1)S(1)}, bf16[512,256]{1,0:T(8,128)(2,1)S(1)}, u32[]{:S(2)}, u32[]{:S(2)}) collective-permute-start(bf16[512,256]{1,0:T(8,128)(2,1)S(1)} %get-tuple-element.58), channel_id=1, source_target_pairs={{4,0},{6,2},{8,4},{10,6},{12,8},{14,10},{5,1},{7,3},{9,5},{11,7},{... | collective-permute-start | bytes 786440 | tf_op jit(solution)/shard_map/ppermute | solution.py:352

commit v10 on v9

--- a/solution.py
+++ b/solution.py
@@ -9,7 +9,7 @@
 
 WIN = 4
 PIECES = (4, 2, 2)
-ROWS = (4, 4)
+ROWS = (1, 1)
 PARTS = 2
 BLOCKS = 8
 STATS_VMEM = 50
@@ -76,11 +76,11 @@
 
 
 def score_kernel(place_ref, masked_ref, sums_ref, sums_other_ref, *outs):
-    pieces = outs[: len(PIECES)]
-    rows_here, rows_away = outs[len(PIECES) : -PARTS], outs[-PARTS:]
+    pieces, again_ref = outs[: len(PIECES)], outs[len(PIECES)]
+    rows_here, rows_away = outs[len(PIECES) + 1 : -PARTS], outs[-PARTS:]
     core = place_ref[1]
-    half = masked_ref.shape[1] // 2
-    size = half // 2
+    size = masked_ref.shape[1] // 4
+    starts = [sum(piece.shape[1] for piece in pieces[:n]) for n in range(len(pieces))]
     for step in range(4):
         columns = slice(step * size, (step + 1) * size)
         totals = [
@@ -94,12 +94,10 @@
         masked = masked_ref[:, columns].astype(jnp.float32)
         scored = jnp.where(masked >= 0.0, (masked - center) * factor, 0.0)
         scored = scored.astype(jnp.bfloat16)
-        at = 0
-        for piece in pieces:
+        for at, piece in zip((*starts, 0), (*pieces, again_ref)):
             low, high = max(step * size, at), min(step * size + size, at + piece.shape[1])
             if low < high:
                 piece[:, low - at : high - at] = scored[:, low - step * size : high - step * size]
-            at += piece.shape[1]
         turned = scored.T
 
         def put(parts, turned=turned, begin=step % 2 * size):
@@ -120,13 +118,13 @@
     return pl.pallas_call(
         score_kernel,
         in_specs=[SMEM, VMEM, VMEM, VMEM],
-        out_specs=[VMEM] * (len(PIECES) + 2 * PARTS),
+        out_specs=[VMEM] * (len(PIECES) + 1 + 2 * PARTS),
         out_shape=[
-            jax.ShapeDtypeStruct((samples, width * eighths // 8), jnp.bfloat16) for eighths in PIECES
+            jax.ShapeDtypeStruct((samples, width * eighths // 8), jnp.bfloat16) for eighths in (*PIECES, PIECES[0])
         ]
         + [
-            jax.ShapeDtypeStruct((width // 2 * eighths // 8, samples), jnp.bfloat16)
-            for eighths in ROWS + ROWS
+            jax.ShapeDtypeStruct((width // 2 * share // sum(ROWS), samples), jnp.bfloat16)
+            for share in ROWS + ROWS
         ],
         compiler_params=PARAMS,
         cost_estimate=COST,
@@ -153,26 +151,30 @@
     )(here, arrived, *passed)
 
 
-def blocks(rows, rights, scale, stop=None):
+def chunks(rights):
+    pairs = list(zip(rights[::2], rights[1::2]))
+    while pairs:
+        group = [pairs.pop(0)]
+        while pairs and sum(mine.shape[1] for mine, _ in group) + pairs[0][0].shape[1] <= 256:
+            group.append(pairs.pop(0))
+        if len(group) > 1:
+            yield tuple(jnp.concatenate([ref[...] for ref in side], axis=1) for side in zip(*group))
+            continue
+        mine, other = group[0]
+        for begin in range(0, mine.shape[1], 256):
+            yield mine[:, begin : begin + 256], other[:, begin : begin + 256]
+
+
+def blocks(rows, rights, scale):
     left = 0
-    for q in range(len(rights) // 2):
-        mine, other = rights[2 * q], rights[2 * q + 1]
-        width = mine.shape[1]
-        if stop is not None and q == len(rights) // 2 - 1:
-            width = stop
-        for begin in range(0, width, 256):
-            end = min(begin + 256, width)
-            top = 0
-            for row in rows:
-                part = row.shape[0] // 2
-                total = jnp.dot(
-                    row[0:part, :], mine[:, begin:end], preferred_element_type=jnp.float32
-                )
-                total += jnp.dot(
-                    row[part:, :], other[:, begin:end], preferred_element_type=jnp.float32
-                )
-                yield slice(top, top + part), slice(left + begin, left + end), total * scale
-                top += part
+    for mine, other in chunks(rights):
+        width, top = mine.shape[1], 0
+        for row in rows:
+            part = row.shape[0] // 2
+            total = jnp.dot(row[0:part, :], mine, preferred_element_type=jnp.float32)
+            total += jnp.dot(row[part:, :], other, preferred_element_type=jnp.float32)
+            yield slice(top, top + part), slice(left, left + width), total * scale
+            top += part
         left += width
 
 
@@ -199,20 +201,17 @@
     )(*operands)
 
 
-def far_kernel(scale, parts, pieces, stop, place_ref, *refs):
+def far_kernel(scale, parts, pieces, place_ref, *refs):
     out_ref = refs[-2]
-    for at, columns, block in blocks(refs[:parts], refs[parts : parts + pieces], scale, stop):
+    for at, columns, block in blocks(refs[:parts], refs[parts : parts + pieces], scale):
         out_ref[at, columns] = block.astype(out_ref.dtype)
 
 
-def far(place, buffer, rows, rights, samples, stop=None):
-    wide = sum(right.shape[1] for right in rights) // 2
-    if stop is not None:
-        wide += stop - rights[-1].shape[1]
-    shape = (sum(row.shape[0] for row in rows) // 2, wide)
+def far(place, buffer, rows, rights, samples):
+    shape = (sum(row.shape[0] for row in rows) // 2, sum(right.shape[1] for right in rights) // 2)
     operands = [place, *rows, *rights, buffer]
     return pl.pallas_call(
-        functools.partial(far_kernel, 1.0 / samples, len(rows), len(rights), stop),
+        functools.partial(far_kernel, 1.0 / samples, len(rows), len(rights)),
         in_specs=[SMEM] + [VMEM] * (len(rows) + len(rights)) + [ANY],
         out_specs=[VMEM, ANY],
         out_shape=[
@@ -363,16 +362,16 @@
 
     sums, masked = stats(dosage, observed)
     made = score(place, masked, sums, mate(sums))
-    direct, relayed, detoured = made[:3]
-    here, away = made[3:-PARTS], made[-PARTS:]
+    direct, relayed, detoured, sent = made[:4]
+    here, away = made[4:-PARTS], made[-PARTS:]
     unset = jax.ShapeDtypeStruct((WIN, width // 2, width), jnp.bfloat16)
 
     upper, buffer = stack(here[0], mate(away[0]), (), (unset,))
     below0 = send(upper, up)
     above = send(relayed, down)
     across = send(detoured, swap)
-    (direct,) = hold((across,), direct)
-    next_direct = send(direct, before)
+    (sent,) = hold((across,), sent)
+    next_direct = send(sent, before)
     (lower,) = stack(here[1], mate(away[1]))
     below1 = send(lower, up)
     rows = [upper, lower]
@@ -380,6 +379,8 @@
     (across,) = hold((above,), across)
     around = send(across, down_odd)
 
+    buffer = tile(place, buffer, 0, 0, rows, own[:2], samples)
+    buffer = tile(place, buffer, 0, 3, rows, own[2:], samples)
     (buffer,) = hold((below0,), buffer)
     made, buffer = far(place, buffer, [below0], own, samples)
     top2 = send(made, down)
@@ -392,9 +393,6 @@
     high += [next_detoured, mate(next_detoured)]
     made, buffer = far(place, buffer, [below0], high, samples)
     top3 = send(made, down)
-    buffer = tile(place, buffer, 0, 0, rows, own[:2], samples)
-    buffer = tile(place, buffer, 0, 3, rows, own[2:], samples)
-    buffer = tile(place, buffer, 0, 2, rows, [relayed, mate(relayed)], samples)
 
     (buffer,) = hold((below1, top2), buffer)
     made, buffer = far(place, buffer, [below1], high + own, samples)
@@ -406,6 +404,7 @@
     side = send(made, down)
     buffer = tile(place, buffer, 1, 0, rows, high[:-2], samples)
     buffer = tile(place, buffer, 1, 3, rows, high[-2:], samples)
+    buffer = tile(place, buffer, 0, 2, rows, [relayed, mate(relayed)], samples)
     buffer = tile(place, buffer, 1, 2, rows, low, samples)
     buffer = tile(place, buffer, 2, 2, rows, [above, mate(above)], samples)
     buffer = last(place, buffer, top2, top3, bottom, side)

time: 97.8 us -> 96.5 us (0.987)
  Pallas kernels: 30.8 us -> 29.7 us
  transfers between devices with their start and end apart: 23 -> 23, of which waited for: 10 -> 12; matrix products, arithmetic and copies ran while one was open for 0% -> 0% of each run, Pallas kernels for 25% -> 24%
where the time goes in v10:
time: 96.5 us; the launch traced here: 96.2 us
  waiting for transfers between devices  39.4 us (41%)
  Pallas kernels  29.7 us (31%)
  starting transfers between devices  26 us (27%)
  between operations  1.05 us (1%)
    ppermute x11, waiting for transfers between devices, send(): return lax.ppermute(shard, 'var', pairs)  37.9 us
    ppermute x11, starting transfers between devices, send(): return lax.ppermute(shard, 'var', pairs)  23.5 us
    pallas_call x7, Pallas kernels, tile(): pl.pallas_call(functools.partial(tile_kernel, k, len(rows), len(rights),...  14.9 us
    pallas_call x4, Pallas kernels, far(): pl.pallas_call(functools.partial(far_kernel, 1.0 / samples, len(rows), le...  6.6 us
    pallas_call x1, Pallas kernels, stats(): pl.pallas_call(stats_kernel, in_specs=[pl.BlockSpec(memory_space=pltpu.HB...  3.08 us
    ppermute x12, starting transfers between devices, mate(): return lax.ppermute(shard, 'samp', [(0, 1), (1, 0)])  2.5 us
  transfers between devices with their start and end apart: 23, of which 12 were waited for; matrix products, arithmetic and copies ran while one was open for 0% of the time, Pallas kernels for 24%

profile of v10, /device:TPU:0, one launch (start us, length us, event | category | flops | bytes accessed | tf_op | source)
XLA Modules:
  0.0 96.2 jit_solution(8020527090355636489)
XLA Ops:
  0.0 3.1 %shard_map.37 = (f32[8,1024]{1,0:T(8,128)S(1)}, bf16[1024,1024]{1,0:T(8,128)(2,1)S(1)}) custom-call(bf16[1024,1024]{1,0:T(8,128)(2,1)} %dosage_hbm.1, s32[1024,1024]{1,0:T(8,128)} %observed_hbm.1), custom_call_target="tpu_custom_call" | custom-call | flops 1000 | bytes 1000 | tf_op jit(solution)/shard_map/pallas_call | solution.py:60
  3.1 0.5 collective-permute-start
  4.3 0.1 pad_add_fusion.place_ref.refs_0_
  4.3 0.1 collective-permute-done.sums_other_ref
  4.5 1.7 %shard_map.38 = (bf16[1024,512]{1,0:T(8,128)(2,1)S(1)}, bf16[1024,256]{1,0:T(8,128)(2,1)S(1)}, bf16[1024,256]{1,0:T(8,128)(2,1)S(1)}, bf16[1024,512]{1,0:T(8,128...) custom-call(s32[3]{0:T(128)S(1)} %pad_add_fusion.place_ref.refs_0_, ...), custom_call_target="tpu_custom_call" | custom-call | flops 1000 | bytes 1000 | tf_op jit(solution)/shard_map/pallas_call | solution.py:118
  6.2 0.4 collective-permute-start.1
  6.6 2.7 %collective-permute-start.7 = (bf16[1024,256]{1,0:T(8,128)(2,1)S(1)}, bf16[1024,256]{1,0:T(8,128)(2,1)S(1)}, u32[]{:S(2)}, u32[]{:S(2)}) collective-permute-start(bf16[1024,256]{1,0:T(8,128)(2,1)S(1)} %get-tuple-element.40.refs_2_.refs_3_.refs_9_), channel_id=1, source_target_pairs={{2,0},{6,4},{10,8},{14,12},{0,2},{4,6},{8,10},{12,14},{3,1},{7,5},... | collective-permute-start | bytes 1572872 | tf_op jit(solution)/shard_map/ppermute | solution.py:351
  9.3 0.1 collective-permute-start.3
  9.4 1.3 %collective-permute-start.11 = (bf16[1024,256]{1,0:T(8,128)(2,1)S(1)}, bf16[1024,256]{1,0:T(8,128)(2,1)S(1)}, u32[]{:S(2)}, u32[]{:S(2)}) collective-permute-start(bf16[1024,256]{1,0:T(8,128)(2,1)S(1)} %get-tuple-element.48.odd_ref.refs_2_), channel_id=1, source_target_pairs={{4,0},{6,2},{8,4},{10,6},{12,8},{14,10},{5,1},{7,3},{9,5},{11,7},{... | collective-permute-start | bytes 1572872 | tf_op jit(solution)/shard_map/ppermute | solution.py:351
  10.7 0.0 collective-permute-done.1.arrived_ref
  10.7 0.1 shard_map.39
  10.8 4.6 %collective-permute-start.2 = (bf16[512,1024]{1,0:T(8,128)(2,1)S(1)}, bf16[512,1024]{1,0:T(8,128)(2,1)S(1)}, u32[]{:S(2)}, u32[]{:S(2)}) collective-permute-start(bf16[512,1024]{1,0:T(8,128)(2,1)S(1)} %get-tuple-element.38.refs_0_), channel_id=1, source_target_pairs={{0,4},{2,6},{4,8},{6,10},{8,12},{10,14},{1,5},{3,7},{5,9},{7,11},{... | collective-permute-start | bytes 3145736 | tf_op jit(solution)/shard_map/ppermute | solution.py:351
  15.4 6.4 %collective-permute-done.7.refs_0_.refs_1_ = bf16[1024,256]{1,0:T(8,128)(2,1)S(1)} collective-permute-done((bf16[1024,256]{1,0:T(8,128)(2,1)S(1)}, bf16[1024,256]{1,0:T(8,128)(2,1)S(1)}, u32[]{:S(2)}, u32[]{:S(2)}) %collective-permute-start.7) | collective-permute-done | bytes 524320 | tf_op jit(solution)/shard_map/ppermute | solution.py:351
  21.7 1.3 %collective-permute-start.8 = (bf16[1024,512]{1,0:T(8,128)(2,1)S(1)}, bf16[1024,512]{1,0:T(8,128)(2,1)S(1)}, u32[]{:S(2)}, u32[]{:S(2)}) collective-permute-start(bf16[1024,512]{1,0:T(8,128)(2,1)S(1)} %shard_map.45), channel_id=1, source_target_pairs={{2,0},{4,2},{6,4},{8,6},{10,8},{12,10},{14,12},{3,1},{5,3},{7,5},{... | collective-permute-start | bytes 3145736 | tf_op jit(solution)/shard_map/ppermute | solution.py:351
  23.0 0.1 collective-permute-start.5
  23.1 2.4 %collective-permute-done.11.refs_0_.even_ref = bf16[1024,256]{1,0:T(8,128)(2,1)S(1)} collective-permute-done((bf16[1024,256]{1,0:T(8,128)(2,1)S(1)}, bf16[1024,256]{1,0:T(8,128)(2,1)S(1)}, u32[]{:S(2)}, u32[]{:S(2)}) %collective-permute-start.11) | collective-permute-done | bytes 524320 | tf_op jit(solution)/shard_map/ppermute | solution.py:351
  25.5 0.0 collective-permute-done.5.arrived_ref
  25.5 0.7 collective-permute-start.12
  26.2 0.1 shard_map.40.refs_1_
  26.3 0.0 collective-permute-done.3.refs_3_.refs_2_.refs_8_
  26.3 5.3 %collective-permute-start.15 = (bf16[512,1024]{1,0:T(8,128)(2,1)S(1)}, bf16[512,1024]{1,0:T(8,128)(2,1)S(1)}, u32[]{:S(2)}, u32[]{:S(2)}) collective-permute-start(bf16[512,1024]{1,0:T(8,128)(2,1)S(1)} %shard_map.40.refs_1_), channel_id=1, source_target_pairs={{0,4},{2,6},{4,8},{6,10},{8,12},{10,14},{1,5},{3,7},{5,9},{7,11},{... | collective-permute-start | bytes 3145736 | tf_op jit(solution)/shard_map/ppermute | solution.py:351
  31.6 2.6 %shard_map.41.refs_4_ = bf16[4,512,1024]{2,1,0:T(8,128)(2,1)} custom-call(s32[3]{0:T(128)S(1)} %pad_add_fusion.place_ref.refs_0_, bf16[512,1024]{1,0:T(8,128)(2,1)S(1)} %get-tuple-element.38.refs_0_, bf16[512,1024]{1,0:T(8,128)(2,1)S(1)} %shard_map.40.refs_1_, ...), custom_call_target="tpu_custom_call", output_to_operand_aliasing={{}: (5, {})} | custom-call | flops 1000 | bytes 1000 | tf_op jit(solution)/shard_map/pallas_call | solution.py:192
  34.2 0.0 collective-permute-done.4.refs_3_.refs_4_.refs_10_
  34.2 2.0 %shard_map.42.refs_1_ = bf16[4,512,1024]{2,1,0:T(8,128)(2,1)} custom-call(s32[3]{0:T(128)S(1)} %pad_add_fusion.place_ref.refs_0_, bf16[512,1024]{1,0:T(8,128)(2,1)S(1)} %get-tuple-element.38.refs_0_, bf16[512,1024]{1,0:T(8,128)(2,1)S(1)} %shard_map.40.refs_1_, ...), custom_call_target="tpu_custom_call", output_to_operand_aliasing={{}: (5, {})} | custom-call | flops 1000 | bytes 1000 | tf_op jit(solution)/shard_map/pallas_call | solution.py:192
  36.1 2.7 %collective-permute-done.2.refs_0_ = bf16[512,1024]{1,0:T(8,128)(2,1)S(1)} collective-permute-done((bf16[512,1024]{1,0:T(8,128)(2,1)S(1)}, bf16[512,1024]{1,0:T(8,128)(2,1)S(1)}, u32[]{:S(2)}, u32[]{:S(2)}) %collective-permute-start.2) | collective-permute-done | bytes 1048608 | tf_op jit(solution)/shard_map/ppermute | solution.py:351
  38.8 1.5 %shard_map.44 = (bf16[256,768]{1,0:T(8,128)(2,1)S(1)}, bf16[4,512,1024]{2,1,0:T(8,128)(2,1)}) custom-call(s32[3]{0:T(128)S(1)} %pad_add_fusion.place_ref.refs_0_, bf16[512,1024]{1,0:T(8,128)(2,1)S(1)} %collective-permute-done.2.refs_0_, bf16[1024,512]{1,0:T(8,128)(2,1)S(1)} %get-tuple-element.39.refs_2_.refs_1_.refs_7_, ...), custom_call_target="tpu_custom_call", output_to_operand_aliasing={{1}: (6, {})} | custom-call | flops 1000 | bytes 1000 | tf_op jit(solution)/shard_map/pallas_call | solution.py:213
  40.3 8.2 %collective-permute-done.8.whole_ref = bf16[1024,512]{1,0:T(8,128)(2,1)S(1)} collective-permute-done((bf16[1024,512]{1,0:T(8,128)(2,1)S(1)}, bf16[1024,512]{1,0:T(8,128)(2,1)S(1)}, u32[]{:S(2)}, u32[]{:S(2)}) %collective-permute-start.8) | collective-permute-done | bytes 1048608 | tf_op jit(solution)/shard_map/ppermute | solution.py:351
  48.6 0.1 shard_map.46
  48.6 0.1 collective-permute-start.9
  48.7 0.5 collective-permute-start.10
  49.2 0.0 collective-permute-done.12.odd_ref
  49.2 0.6 shard_map.48
  49.8 0.1 collective-permute-start.13
  49.9 1.3 %collective-permute-start.6 = (bf16[256,768]{1,0:T(8,128)(2,1)S(1)}, bf16[256,768]{1,0:T(8,128)(2,1)S(1)}, u32[]{:S(2)}, u32[]{:S(2)}) collective-permute-start(bf16[256,768]{1,0:T(8,128)(2,1)S(1)} %get-tuple-element.44.refs_0_), channel_id=1, source_target_pairs={{4,0},{6,2},{8,4},{10,6},{12,8},{14,10},{5,1},{7,3},{9,5},{11,7},{... | collective-permute-start | bytes 1179656 | tf_op jit(solution)/shard_map/ppermute | solution.py:351
  51.2 0.6 shard_map.49
  51.8 0.0 collective-permute-done.9.refs_2_.refs_3_
  51.8 2.4 %collective-permute-start.17 = (bf16[1024,256]{1,0:T(8,128)(2,1)S(1)}, bf16[1024,256]{1,0:T(8,128)(2,1)S(1)}, u32[]{:S(2)}, u32[]{:S(2)}) collective-permute-start(bf16[1024,256]{1,0:T(8,128)(2,1)S(1)} %get-tuple-element.56), channel_id=1, source_target_pairs={{2,0},{6,4},{10,8},{14,12},{0,2},{4,6},{8,10},{12,14},{3,1},{7,5},... | collective-permute-start | bytes 1572872 | tf_op jit(solution)/shard_map/ppermute | solution.py:351
  54.2 0.0 collective-permute-done.10.refs_4_.refs_5_
  54.2 1.5 %shard_map.50 = (bf16[256,768]{1,0:T(8,128)(2,1)S(1)}, bf16[4,512,1024]{2,1,0:T(8,128)(2,1)}) custom-call(s32[3]{0:T(128)S(1)} %pad_add_fusion.place_ref.refs_0_, bf16[512,1024]{1,0:T(8,128)(2,1)S(1)} %collective-permute-done.2.refs_0_, bf16[1024,256]{1,0:T(8,128)(2,1)S(1)} %get-tuple-element.46.refs_1_.refs_2_, ...), custom_call_target="tpu_custom_call", output_to_operand_aliasing={{1}: (8, {})} | custom-call | flops 1000 | bytes 1000 | tf_op jit(solution)/shard_map/pallas_call | solution.py:213
  55.8 1.3 %collective-permute-start.14 = (bf16[256,768]{1,0:T(8,128)(2,1)S(1)}, bf16[256,768]{1,0:T(8,128)(2,1)S(1)}, u32[]{:S(2)}, u32[]{:S(2)}) collective-permute-start(bf16[256,768]{1,0:T(8,128)(2,1)S(1)} %get-tuple-element.53), channel_id=1, source_target_pairs={{4,0},{6,2},{8,4},{10,6},{12,8},{14,10},{5,1},{7,3},{9,5},{11,7},{... | collective-permute-start | bytes 1179656 | tf_op jit(solution)/shard_map/ppermute | solution.py:351
  57.1 3.5 %collective-permute-done.15.refs_0_.refs_1_ = bf16[512,1024]{1,0:T(8,128)(2,1)S(1)} collective-permute-done((bf16[512,1024]{1,0:T(8,128)(2,1)S(1)}, bf16[512,1024]{1,0:T(8,128)(2,1)S(1)}, u32[]{:S(2)}, u32[]{:S(2)}) %collective-permute-start.15) | collective-permute-done | bytes 1048608 | tf_op jit(solution)/shard_map/ppermute | solution.py:351
  60.5 3.2 %collective-permute-done.6.refs_1_ = bf16[256,768]{1,0:T(8,128)(2,1)S(1)} collective-permute-done((bf16[256,768]{1,0:T(8,128)(2,1)S(1)}, bf16[256,768]{1,0:T(8,128)(2,1)S(1)}, u32[]{:S(2)}, u32[]{:S(2)}) %collective-permute-start.6) | collective-permute-done | bytes 393248 | tf_op jit(solution)/shard_map/ppermute | solution.py:351
  63.7 2.3 %shard_map.52 = (bf16[256,1536]{1,0:T(8,128)(2,1)S(1)}, bf16[4,512,1024]{2,1,0:T(8,128)(2,1)}) custom-call(s32[3]{0:T(128)S(1)} %pad_add_fusion.place_ref.refs_0_, bf16[512,1024]{1,0:T(8,128)(2,1)S(1)} %collective-permute-done.15.refs_0_.refs_1_, bf16[1024,256]{1,0:T(8,128)(2,1)S(1)} %get-tuple-element.46.refs_1_.refs_2_, ...), custom_call_target="tpu_custom_call", output_to_operand_aliasing={{1}: (12, {})} | custom-call | flops 1000 | bytes 1000 | tf_op jit(solution)/shard_map/pallas_call | solution.py:213
  66.1 1.3 %collective-permute-start.16 = (bf16[256,1536]{1,0:T(8,128)(2,1)S(1)}, bf16[256,1536]{1,0:T(8,128)(2,1)S(1)}, u32[]{:S(2)}, u32[]{:S(2)}) collective-permute-start(bf16[256,1536]{1,0:T(8,128)(2,1)S(1)} %get-tuple-element.55.refs_0_), channel_id=1, source_target_pairs={{4,0},{6,2},{8,4},{10,6},{12,8},{14,10},{5,1},{7,3},{9,5},{11,7},{... | collective-permute-start | bytes 2359304 | tf_op jit(solution)/shard_map/ppermute | solution.py:351
  67.4 0.1 collective-permute-start.22
  67.5 0.0 collective-permute-done.17.whole_ref
  67.5 4.7 %collective-permute-done.14.refs_1_.refs_2_ = bf16[256,768]{1,0:T(8,128)(2,1)S(1)} collective-permute-done((bf16[256,768]{1,0:T(8,128)(2,1)S(1)}, bf16[256,768]{1,0:T(8,128)(2,1)S(1)}, u32[]{:S(2)}, u32[]{:S(2)}) %collective-permute-start.14) | collective-permute-done | bytes 393248 | tf_op jit(solution)/shard_map/ppermute | solution.py:351
  72.2 0.1 shard_map.53
  72.3 0.1 collective-permute-start.18
  72.3 0.5 collective-permute-start.19
  72.8 0.1 collective-permute-start.21
  72.9 0.9 collective-permute-done.18.refs_3_
  73.9 0.4 collective-permute-done.19.refs_5_
  74.2 1.2 %shard_map.54 = (bf16[512,256]{1,0:T(8,128)(2,1)S(1)}, bf16[4,512,1024]{2,1,0:T(8,128)(2,1)}) custom-call(s32[3]{0:T(128)S(1)} %pad_add_fusion.place_ref.refs_0_, bf16[512,1024]{1,0:T(8,128)(2,1)S(1)} %collective-permute-done.2.refs_0_, bf16[512,1024]{1,0:T(8,128)(2,1)S(1)} %collective-permute-done.15.refs_0_.refs_1_, ...), custom_call_target="tpu_custom_call", output_to_operand_aliasing={{1}: (7, {})} | custom-call | flops 1000 | bytes 1000 | tf_op jit(solution)/shard_map/pallas_call | solution.py:213
  75.5 1.5 %collective-permute-start.20 = (bf16[512,256]{1,0:T(8,128)(2,1)S(1)}, bf16[512,256]{1,0:T(8,128)(2,1)S(1)}, u32[]{:S(2)}, u32[]{:S(2)}) collective-permute-start(bf16[512,256]{1,0:T(8,128)(2,1)S(1)} %get-tuple-element.60), channel_id=1, source_target_pairs={{4,0},{6,2},{8,4},{10,6},{12,8},{14,10},{5,1},{7,3},{9,5},{11,7},{... | collective-permute-start | bytes 786440 | tf_op jit(solution)/shard_map/ppermute | solution.py:351
  77.0 2.6 %shard_map.55.refs_4_ = bf16[4,512,1024]{2,1,0:T(8,128)(2,1)} custom-call(s32[3]{0:T(128)S(1)} %pad_add_fusion.place_ref.refs_0_, bf16[512,1024]{1,0:T(8,128)(2,1)S(1)} %get-tuple-element.38.refs_0_, bf16[512,1024]{1,0:T(8,128)(2,1)S(1)} %shard_map.40.refs_1_, ...), custom_call_target="tpu_custom_call", output_to_operand_aliasing={{}: (7, {})} | custom-call | flops 1000 | bytes 1000 | tf_op jit(solution)/shard_map/pallas_call | solution.py:192
  79.6 2.0 %shard_map.56.refs_4_ = bf16[4,512,1024]{2,1,0:T(8,128)(2,1)} custom-call(s32[3]{0:T(128)S(1)} %pad_add_fusion.place_ref.refs_0_, bf16[512,1024]{1,0:T(8,128)(2,1)S(1)} %get-tuple-element.38.refs_0_, bf16[512,1024]{1,0:T(8,128)(2,1)S(1)} %shard_map.40.refs_1_, ...), custom_call_target="tpu_custom_call", output_to_operand_aliasing={{}: (5, {})} | custom-call | flops 1000 | bytes 1000 | tf_op jit(solution)/shard_map/pallas_call | solution.py:192
  81.5 0.0 collective-permute-done.22.refs_3_
  81.5 2.0 %shard_map.57.refs_6_ = bf16[4,512,1024]{2,1,0:T(8,128)(2,1)} custom-call(s32[3]{0:T(128)S(1)} %pad_add_fusion.place_ref.refs_0_, bf16[512,1024]{1,0:T(8,128)(2,1)S(1)} %get-tuple-element.38.refs_0_, bf16[512,1024]{1,0:T(8,128)(2,1)S(1)} %shard_map.40.refs_1_, ...), custom_call_target="tpu_custom_call", output_to_operand_aliasing={{}: (5, {})} | custom-call | flops 1000 | bytes 1000 | tf_op jit(solution)/shard_map/pallas_call | solution.py:192
  83.5 2.0 %shard_map.58.refs_4_ = bf16[4,512,1024]{2,1,0:T(8,128)(2,1)} custom-call(s32[3]{0:T(128)S(1)} %pad_add_fusion.place_ref.refs_0_, bf16[512,1024]{1,0:T(8,128)(2,1)S(1)} %get-tuple-element.38.refs_0_, bf16[512,1024]{1,0:T(8,128)(2,1)S(1)} %shard_map.40.refs_1_, bf16[1024,128]{1,0:T(8,128)(2,1)S(1)} %get-tuple-element.57.refs_2_, ...), custom_call_target="tpu_custom_call", output_to_operand_aliasing={{}: (7, {})} | custom-call | flops 1000 | bytes 1000 | tf_op jit(solution)/shard_map/pallas_call | solution.py:192
  85.4 2.0 %shard_map.59.refs_5_ = bf16[4,512,1024]{2,1,0:T(8,128)(2,1)} custom-call(s32[3]{0:T(128)S(1)} %pad_add_fusion.place_ref.refs_0_, bf16[512,1024]{1,0:T(8,128)(2,1)S(1)} %get-tuple-element.38.refs_0_, bf16[512,1024]{1,0:T(8,128)(2,1)S(1)} %shard_map.40.refs_1_, bf16[1024,256]{1,0:T(8,128)(2,1)S(1)} %get-tuple-element.61.refs_2_, ...), custom_call_target="tpu_custom_call", output_to_operand_aliasing={{}: (5, {})} | custom-call | flops 1000 | bytes 1000 | tf_op jit(solution)/shard_map/pallas_call | solution.py:192
  87.4 1.6 %collective-permute-done.16.refs_3_ = bf16[256,1536]{1,0:T(8,128)(2,1)S(1)} collective-permute-done((bf16[256,1536]{1,0:T(8,128)(2,1)S(1)}, bf16[256,1536]{1,0:T(8,128)(2,1)S(1)}, u32[]{:S(2)}, u32[]{:S(2)}) %collective-permute-start.16) | collective-permute-done | bytes 786464 | tf_op jit(solution)/shard_map/ppermute | solution.py:351
  89.0 5.2 %collective-permute-done.20.refs_4_ = bf16[512,256]{1,0:T(8,128)(2,1)S(1)} collective-permute-done((bf16[512,256]{1,0:T(8,128)(2,1)S(1)}, bf16[512,256]{1,0:T(8,128)(2,1)S(1)}, u32[]{:S(2)}, u32[]{:S(2)}) %collective-permute-start.20) | collective-permute-done | bytes 262176 | tf_op jit(solution)/shard_map/ppermute | solution.py:351
  94.2 1.8 %shard_map.60 = bf16[4,512,1024]{2,1,0:T(8,128)(2,1)} custom-call(s32[3]{0:T(128)S(1)} %pad_add_fusion.place_ref.refs_0_, bf16[256,768]{1,0:T(8,128)(2,1)S(1)} %collective-permute-done.6.refs_1_, bf16[256,768]{1,0:T(8,128)(2,1)S(1)} %collective-permute-done.14.refs_1_.refs_2_, ...), custom_call_target="tpu_custom_call", output_to_operand_aliasing={{}: (5, {})} | custom-call | flops 1000 | bytes 1000 | tf_op jit(solution)/shard_map/pallas_call | solution.py:322
  (7 shorter events, 0.0 us)
Async XLA Ops:
  3.1 1.4 %collective-permute-start = (f32[8,1024]{1,0:T(8,128)S(1)}, f32[8,1024]{1,0:T(8,128)S(1)}, u32[]{:S(2)}, u32[]{:S(2)}) collective-permute-start(f32[8,1024]{1,0:T(8,128)S(1)} %get-tuple-element.35.sums_ref), channel_id=1, source_target_pairs={{0,1},{1,0},{2,3},{3,2},{4,5},{5,4},{6,7},{7,6},{8,9},{9,8},{10,11... | collective-permute-start | bytes 98312 | tf_op jit(solution)/shard_map/ppermute | solution.py:361
  6.2 4.4 %collective-permute-start.1 = (bf16[256,1024]{1,0:T(8,128)(2,1)S(1)}, bf16[256,1024]{1,0:T(8,128)(2,1)S(1)}, u32[]{:S(2)}, u32[]{:S(2)}) collective-permute-start(bf16[256,1024]{1,0:T(8,128)(2,1)S(1)} %get-tuple-element.37), channel_id=1, source_target_pairs={{0,1},{1,0},{2,3},{3,2},{4,5},{5,4},{6,7},{7,6},{8,9},{9,8},{10,11... | collective-permute-start | bytes 1572872 | tf_op jit(solution)/shard_map/ppermute | solution.py:361
  6.6 15.1 %collective-permute-start.7 = (bf16[1024,256]{1,0:T(8,128)(2,1)S(1)}, bf16[1024,256]{1,0:T(8,128)(2,1)S(1)}, u32[]{:S(2)}, u32[]{:S(2)}) collective-permute-start(bf16[1024,256]{1,0:T(8,128)(2,1)S(1)} %get-tuple-element.40.refs_2_.refs_3_.refs_9_), channel_id=1, source_target_pairs={{2,0},{6,4},{10,8},{14,12},{0,2},{4,6},{8,10},{12,14},{3,1},{7,5},... | collective-permute-start | bytes 1572872 | tf_op jit(solution)/shard_map/ppermute | solution.py:351
  9.3 17.0 %collective-permute-start.3 = (bf16[1024,512]{1,0:T(8,128)(2,1)S(1)}, bf16[1024,512]{1,0:T(8,128)(2,1)S(1)}, u32[]{:S(2)}, u32[]{:S(2)}) collective-permute-start(bf16[1024,512]{1,0:T(8,128)(2,1)S(1)} %get-tuple-element.39.refs_2_.refs_1_.refs_7_), channel_id=1, source_target_pairs={{0,1},{1,0},{2,3},{3,2},{4,5},{5,4},{6,7},{7,6},{8,9},{9,8},{10,11... | collective-permute-start | bytes 3145736 | tf_op jit(solution)/shard_map/ppermute | solution.py:361
  9.4 16.2 %collective-permute-start.11 = (bf16[1024,256]{1,0:T(8,128)(2,1)S(1)}, bf16[1024,256]{1,0:T(8,128)(2,1)S(1)}, u32[]{:S(2)}, u32[]{:S(2)}) collective-permute-start(bf16[1024,256]{1,0:T(8,128)(2,1)S(1)} %get-tuple-element.48.odd_ref.refs_2_), channel_id=1, source_target_pairs={{4,0},{6,2},{8,4},{10,6},{12,8},{14,10},{5,1},{7,3},{9,5},{11,7},{... | collective-permute-start | bytes 1572872 | tf_op jit(solution)/shard_map/ppermute | solution.py:351
  10.8 28.1 %collective-permute-start.2 = (bf16[512,1024]{1,0:T(8,128)(2,1)S(1)}, bf16[512,1024]{1,0:T(8,128)(2,1)S(1)}, u32[]{:S(2)}, u32[]{:S(2)}) collective-permute-start(bf16[512,1024]{1,0:T(8,128)(2,1)S(1)} %get-tuple-element.38.refs_0_), channel_id=1, source_target_pairs={{0,4},{2,6},{4,8},{6,10},{8,12},{10,14},{1,5},{3,7},{5,9},{7,11},{... | collective-permute-start | bytes 3145736 | tf_op jit(solution)/shard_map/ppermute | solution.py:351
  21.7 26.8 %collective-permute-start.8 = (bf16[1024,512]{1,0:T(8,128)(2,1)S(1)}, bf16[1024,512]{1,0:T(8,128)(2,1)S(1)}, u32[]{:S(2)}, u32[]{:S(2)}) collective-permute-start(bf16[1024,512]{1,0:T(8,128)(2,1)S(1)} %shard_map.45), channel_id=1, source_target_pairs={{2,0},{4,2},{6,4},{8,6},{10,8},{12,10},{14,12},{3,1},{5,3},{7,5},{... | collective-permute-start | bytes 3145736 | tf_op jit(solution)/shard_map/ppermute | solution.py:351
  23.0 2.5 %collective-permute-start.5 = (bf16[256,1024]{1,0:T(8,128)(2,1)S(1)}, bf16[256,1024]{1,0:T(8,128)(2,1)S(1)}, u32[]{:S(2)}, u32[]{:S(2)}) collective-permute-start(bf16[256,1024]{1,0:T(8,128)(2,1)S(1)} %get-tuple-element.42), channel_id=1, source_target_pairs={{0,1},{1,0},{2,3},{3,2},{4,5},{5,4},{6,7},{7,6},{8,9},{9,8},{10,11... | collective-permute-start | bytes 1572872 | tf_op jit(solution)/shard_map/ppermute | solution.py:361
  25.5 8.6 %collective-permute-start.4 = (bf16[1024,256]{1,0:T(8,128)(2,1)S(1)}, bf16[1024,256]{1,0:T(8,128)(2,1)S(1)}, u32[]{:S(2)}, u32[]{:S(2)}) collective-permute-start(bf16[1024,256]{1,0:T(8,128)(2,1)S(1)} %get-tuple-element.40.refs_2_.refs_3_.refs_9_), channel_id=1, source_target_pairs={{0,1},{1,0},{2,3},{3,2},{4,5},{5,4},{6,7},{7,6},{8,9},{9,8},{10,11... | collective-permute-start | bytes 1572872 | tf_op jit(solution)/shard_map/ppermute | solution.py:361
  25.5 23.7 %collective-permute-start.12 = (bf16[1024,256]{1,0:T(8,128)(2,1)S(1)}, bf16[1024,256]{1,0:T(8,128)(2,1)S(1)}, u32[]{:S(2)}, u32[]{:S(2)}) collective-permute-start(bf16[1024,256]{1,0:T(8,128)(2,1)S(1)} %shard_map.47.even_ref), channel_id=1, source_target_pairs={{6,2},{10,6},{14,10},{7,3},{11,7},{15,11},{22,18},{26,22},{30,26},... | collective-permute-start | bytes 1572872 | tf_op jit(solution)/shard_map/ppermute | solution.py:351
  26.3 34.2 %collective-permute-start.15 = (bf16[512,1024]{1,0:T(8,128)(2,1)S(1)}, bf16[512,1024]{1,0:T(8,128)(2,1)S(1)}, u32[]{:S(2)}, u32[]{:S(2)}) collective-permute-start(bf16[512,1024]{1,0:T(8,128)(2,1)S(1)} %shard_map.40.refs_1_), channel_id=1, source_target_pairs={{0,4},{2,6},{4,8},{6,10},{8,12},{10,14},{1,5},{3,7},{5,9},{7,11},{... | collective-permute-start | bytes 3145736 | tf_op jit(solution)/shard_map/ppermute | solution.py:351
  48.6 3.2 %collective-permute-start.9 = (bf16[1024,256]{1,0:T(8,128)(2,1)S(1)}, bf16[1024,256]{1,0:T(8,128)(2,1)S(1)}, u32[]{:S(2)}, u32[]{:S(2)}) collective-permute-start(bf16[1024,256]{1,0:T(8,128)(2,1)S(1)} %get-tuple-element.46.refs_1_.refs_2_), channel_id=1, source_target_pairs={{0,1},{1,0},{2,3},{3,2},{4,5},{5,4},{6,7},{7,6},{8,9},{9,8},{10,11... | collective-permute-start | bytes 1572872 | tf_op jit(solution)/shard_map/ppermute | solution.py:361
  48.7 5.5 %collective-permute-start.10 = (bf16[1024,256]{1,0:T(8,128)(2,1)S(1)}, bf16[1024,256]{1,0:T(8,128)(2,1)S(1)}, u32[]{:S(2)}, u32[]{:S(2)}) collective-permute-start(bf16[1024,256]{1,0:T(8,128)(2,1)S(1)} %get-tuple-element.47.refs_3_.refs_4_), channel_id=1, source_target_pairs={{0,1},{1,0},{2,3},{3,2},{4,5},{5,4},{6,7},{7,6},{8,9},{9,8},{10,11... | collective-permute-start | bytes 1572872 | tf_op jit(solution)/shard_map/ppermute | solution.py:361
  49.8 4.4 %collective-permute-start.13 = (bf16[1024,256]{1,0:T(8,128)(2,1)S(1)}, bf16[1024,256]{1,0:T(8,128)(2,1)S(1)}, u32[]{:S(2)}, u32[]{:S(2)}) collective-permute-start(bf16[1024,256]{1,0:T(8,128)(2,1)S(1)} %get-tuple-element.50.refs_5_.refs_2_), channel_id=1, source_target_pairs={{0,1},{1,0},{2,3},{3,2},{4,5},{5,4},{6,7},{7,6},{8,9},{9,8},{10,11... | collective-permute-start | bytes 1572872 | tf_op jit(solution)/shard_map/ppermute | solution.py:361
  49.9 13.8 %collective-permute-start.6 = (bf16[256,768]{1,0:T(8,128)(2,1)S(1)}, bf16[256,768]{1,0:T(8,128)(2,1)S(1)}, u32[]{:S(2)}, u32[]{:S(2)}) collective-permute-start(bf16[256,768]{1,0:T(8,128)(2,1)S(1)} %get-tuple-element.44.refs_0_), channel_id=1, source_target_pairs={{4,0},{6,2},{8,4},{10,6},{12,8},{14,10},{5,1},{7,3},{9,5},{11,7},{... | collective-permute-start | bytes 1179656 | tf_op jit(solution)/shard_map/ppermute | solution.py:351
  51.8 15.6 %collective-permute-start.17 = (bf16[1024,256]{1,0:T(8,128)(2,1)S(1)}, bf16[1024,256]{1,0:T(8,128)(2,1)S(1)}, u32[]{:S(2)}, u32[]{:S(2)}) collective-permute-start(bf16[1024,256]{1,0:T(8,128)(2,1)S(1)} %get-tuple-element.56), channel_id=1, source_target_pairs={{2,0},{6,4},{10,8},{14,12},{0,2},{4,6},{8,10},{12,14},{3,1},{7,5},... | collective-permute-start | bytes 1572872 | tf_op jit(solution)/shard_map/ppermute | solution.py:351
  55.8 16.4 %collective-permute-start.14 = (bf16[256,768]{1,0:T(8,128)(2,1)S(1)}, bf16[256,768]{1,0:T(8,128)(2,1)S(1)}, u32[]{:S(2)}, u32[]{:S(2)}) collective-permute-start(bf16[256,768]{1,0:T(8,128)(2,1)S(1)} %get-tuple-element.53), channel_id=1, source_target_pairs={{4,0},{6,2},{8,4},{10,6},{12,8},{14,10},{5,1},{7,3},{9,5},{11,7},{... | collective-permute-start | bytes 1179656 | tf_op jit(solution)/shard_map/ppermute | solution.py:351
  66.1 22.9 %collective-permute-start.16 = (bf16[256,1536]{1,0:T(8,128)(2,1)S(1)}, bf16[256,1536]{1,0:T(8,128)(2,1)S(1)}, u32[]{:S(2)}, u32[]{:S(2)}) collective-permute-start(bf16[256,1536]{1,0:T(8,128)(2,1)S(1)} %get-tuple-element.55.refs_0_), channel_id=1, source_target_pairs={{4,0},{6,2},{8,4},{10,6},{12,8},{14,10},{5,1},{7,3},{9,5},{11,7},{... | collective-permute-start | bytes 2359304 | tf_op jit(solution)/shard_map/ppermute | solution.py:351
  67.4 14.1 %collective-permute-start.22 = (bf16[1024,256]{1,0:T(8,128)(2,1)S(1)}, bf16[1024,256]{1,0:T(8,128)(2,1)S(1)}, u32[]{:S(2)}, u32[]{:S(2)}) collective-permute-start(bf16[1024,256]{1,0:T(8,128)(2,1)S(1)} %get-tuple-element.48.odd_ref.refs_2_), channel_id=1, source_target_pairs={{0,1},{1,0},{2,3},{3,2},{4,5},{5,4},{6,7},{7,6},{8,9},{9,8},{10,11... | collective-permute-start | bytes 1572872 | tf_op jit(solution)/shard_map/ppermute | solution.py:361
  72.3 1.6 %collective-permute-start.18 = (bf16[1024,128]{1,0:T(8,128)(2,1)S(1)}, bf16[1024,128]{1,0:T(8,128)(2,1)S(1)}, u32[]{:S(2)}, u32[]{:S(2)}) collective-permute-start(bf16[1024,128]{1,0:T(8,128)(2,1)S(1)} %get-tuple-element.57.refs_2_), channel_id=1, source_target_pairs={{0,1},{1,0},{2,3},{3,2},{4,5},{5,4},{6,7},{7,6},{8,9},{9,8},{10,11... | collective-permute-start | bytes 786440 | tf_op jit(solution)/shard_map/ppermute | solution.py:361
  72.3 1.9 %collective-permute-start.19 = (bf16[1024,128]{1,0:T(8,128)(2,1)S(1)}, bf16[1024,128]{1,0:T(8,128)(2,1)S(1)}, u32[]{:S(2)}, u32[]{:S(2)}) collective-permute-start(bf16[1024,128]{1,0:T(8,128)(2,1)S(1)} %get-tuple-element.58.refs_4_), channel_id=1, source_target_pairs={{0,1},{1,0},{2,3},{3,2},{4,5},{5,4},{6,7},{7,6},{8,9},{9,8},{10,11... | collective-permute-start | bytes 786440 | tf_op jit(solution)/shard_map/ppermute | solution.py:361
  72.8 12.6 %collective-permute-start.21 = (bf16[1024,256]{1,0:T(8,128)(2,1)S(1)}, bf16[1024,256]{1,0:T(8,128)(2,1)S(1)}, u32[]{:S(2)}, u32[]{:S(2)}) collective-permute-start(bf16[1024,256]{1,0:T(8,128)(2,1)S(1)} %get-tuple-element.61.refs_2_), channel_id=1, source_target_pairs={{0,1},{1,0},{2,3},{3,2},{4,5},{5,4},{6,7},{7,6},{8,9},{9,8},{10,11... | collective-permute-start | bytes 1572872 | tf_op jit(solution)/shard_map/ppermute | solution.py:361
  75.5 18.7 %collective-permute-start.20 = (bf16[512,256]{1,0:T(8,128)(2,1)S(1)}, bf16[512,256]{1,0:T(8,128)(2,1)S(1)}, u32[]{:S(2)}, u32[]{:S(2)}) collective-permute-start(bf16[512,256]{1,0:T(8,128)(2,1)S(1)} %get-tuple-element.60), channel_id=1, source_target_pairs={{4,0},{6,2},{8,4},{10,6},{12,8},{14,10},{5,1},{7,3},{9,5},{11,7},{... | collective-permute-start | bytes 786440 | tf_op jit(solution)/shard_map/ppermute | solution.py:351

commit v11 on v10

--- a/solution.py
+++ b/solution.py
@@ -370,7 +370,6 @@
     below0 = send(upper, up)
     above = send(relayed, down)
     across = send(detoured, swap)
-    (sent,) = hold((across,), sent)
     next_direct = send(sent, before)
     (lower,) = stack(here[1], mate(away[1]))
     below1 = send(lower, up)

time: 96.5 us -> 109 us (1.13); the launches traced: 96.2 us -> 107 us
  starting transfers between devices: 26 us -> 50.2 us
  waiting for transfers between devices: 39.4 us -> 26.1 us
    ppermute x11, starting transfers between devices: 23.5 us -> 46.9 us  [send(): return lax.ppermute(shard, 'var', pairs)]
    ppermute x11, waiting for transfers between devices: 37.9 us -> 23.2 us  [send(): return lax.ppermute(shard, 'var', pairs)]
    ppermute x12, waiting for transfers between devices: 1.47 us -> 2.86 us  [mate(): return lax.ppermute(shard, 'samp', [(0, 1), (1, 0)])]
  transfers between devices with their start and end apart: 23 -> 23, of which waited for: 12 -> 10; matrix products, arithmetic and copies ran while one was open for 0% -> 0% of each run, Pallas kernels for 24% -> 22%
where the time goes in v11:
time: 109 us; the launch traced here: 107 us
  starting transfers between devices  50.2 us (46%)
  Pallas kernels  29.7 us (27%)
  waiting for transfers between devices  26.1 us (24%)
    ppermute x11, starting transfers between devices, send(): return lax.ppermute(shard, 'var', pairs)  46.9 us
    ppermute x11, waiting for transfers between devices, send(): return lax.ppermute(shard, 'var', pairs)  23.2 us
    pallas_call x7, Pallas kernels, tile(): pl.pallas_call(functools.partial(tile_kernel, k, len(rows), len(rights),...  14.9 us
    pallas_call x4, Pallas kernels, far(): pl.pallas_call(functools.partial(far_kernel, 1.0 / samples, len(rows), le...  6.61 us
    ppermute x12, starting transfers between devices, mate(): return lax.ppermute(shard, 'samp', [(0, 1), (1, 0)])  3.26 us
    pallas_call x1, Pallas kernels, stats(): pl.pallas_call(stats_kernel, in_specs=[pl.BlockSpec(memory_space=pltpu.HB...  3.08 us
    ppermute x12, waiting for transfers between devices, mate(): return lax.ppermute(shard, 'samp', [(0, 1), (1, 0)])  2.86 us
  transfers between devices with their start and end apart: 23, of which 10 were waited for; matrix products, arithmetic and copies ran while one was open for 0% of the time, Pallas kernels for 22%

profile of v11, /device:TPU:0, one launch (start us, length us, event | category | flops | bytes accessed | tf_op | source)
XLA Modules:
  0.0 107.0 jit_solution(4353267240124285582)
XLA Ops:
  0.0 3.1 %shard_map.37 = (f32[8,1024]{1,0:T(8,128)S(1)}, bf16[1024,1024]{1,0:T(8,128)(2,1)S(1)}) custom-call(bf16[1024,1024]{1,0:T(8,128)(2,1)} %dosage_hbm.1, s32[1024,1024]{1,0:T(8,128)} %observed_hbm.1), custom_call_target="tpu_custom_call" | custom-call | flops 1000 | bytes 1000 | tf_op jit(solution)/shard_map/pallas_call | solution.py:60
  3.1 0.5 collective-permute-start
  4.3 0.1 pad_add_fusion.place_ref.refs_0_
  4.3 0.1 collective-permute-done.sums_other_ref
  4.5 1.7 %shard_map.38 = (bf16[1024,512]{1,0:T(8,128)(2,1)S(1)}, bf16[1024,256]{1,0:T(8,128)(2,1)S(1)}, bf16[1024,256]{1,0:T(8,128)(2,1)S(1)}, bf16[1024,512]{1,0:T(8,128...) custom-call(s32[3]{0:T(128)S(1)} %pad_add_fusion.place_ref.refs_0_, ...), custom_call_target="tpu_custom_call" | custom-call | flops 1000 | bytes 1000 | tf_op jit(solution)/shard_map/pallas_call | solution.py:118
  6.2 0.4 collective-permute-start.1
  6.6 1.3 %collective-permute-start.10 = (bf16[1024,256]{1,0:T(8,128)(2,1)S(1)}, bf16[1024,256]{1,0:T(8,128)(2,1)S(1)}, u32[]{:S(2)}, u32[]{:S(2)}) collective-permute-start(bf16[1024,256]{1,0:T(8,128)(2,1)S(1)} %get-tuple-element.48.odd_ref.refs_2_), channel_id=1, source_target_pairs={{4,0},{6,2},{8,4},{10,6},{12,8},{14,10},{5,1},{7,3},{9,5},{11,7},{... | collective-permute-start | bytes 1572872 | tf_op jit(solution)/shard_map/ppermute | solution.py:351
  7.9 0.2 collective-permute-start.3
  8.2 2.9 %collective-permute-start.11 = (bf16[1024,256]{1,0:T(8,128)(2,1)S(1)}, bf16[1024,256]{1,0:T(8,128)(2,1)S(1)}, u32[]{:S(2)}, u32[]{:S(2)}) collective-permute-start(bf16[1024,256]{1,0:T(8,128)(2,1)S(1)} %get-tuple-element.40.refs_2_.refs_3_.refs_9_), channel_id=1, source_target_pairs={{2,0},{6,4},{10,8},{14,12},{0,2},{4,6},{8,10},{12,14},{3,1},{7,5},... | collective-permute-start | bytes 1572872 | tf_op jit(solution)/shard_map/ppermute | solution.py:351
  11.0 0.0 collective-permute-done.1.arrived_ref
  11.0 0.1 shard_map.39
  11.1 4.3 %collective-permute-start.2 = (bf16[512,1024]{1,0:T(8,128)(2,1)S(1)}, bf16[512,1024]{1,0:T(8,128)(2,1)S(1)}, u32[]{:S(2)}, u32[]{:S(2)}) collective-permute-start(bf16[512,1024]{1,0:T(8,128)(2,1)S(1)} %get-tuple-element.38.refs_0_), channel_id=1, source_target_pairs={{0,4},{2,6},{4,8},{6,10},{8,12},{10,14},{1,5},{3,7},{5,9},{7,11},{... | collective-permute-start | bytes 3145736 | tf_op jit(solution)/shard_map/ppermute | solution.py:351
  15.4 1.3 %collective-permute-start.7 = (bf16[1024,512]{1,0:T(8,128)(2,1)S(1)}, bf16[1024,512]{1,0:T(8,128)(2,1)S(1)}, u32[]{:S(2)}, u32[]{:S(2)}) collective-permute-start(bf16[1024,512]{1,0:T(8,128)(2,1)S(1)} %get-tuple-element.45), channel_id=1, source_target_pairs={{2,0},{4,2},{6,4},{8,6},{10,8},{12,10},{14,12},{3,1},{5,3},{7,5},{... | collective-permute-start | bytes 3145736 | tf_op jit(solution)/shard_map/ppermute | solution.py:351
  16.7 7.2 %collective-permute-done.10.refs_0_.even_ref = bf16[1024,256]{1,0:T(8,128)(2,1)S(1)} collective-permute-done((bf16[1024,256]{1,0:T(8,128)(2,1)S(1)}, bf16[1024,256]{1,0:T(8,128)(2,1)S(1)}, u32[]{:S(2)}, u32[]{:S(2)}) %collective-permute-start.10) | collective-permute-done | bytes 524320 | tf_op jit(solution)/shard_map/ppermute | solution.py:351
  23.9 0.0 collective-permute-start.5
  23.9 0.0 collective-permute-done.11.refs_1_
  24.0 0.5 collective-permute-start.4
  24.5 1.4 %collective-permute-done.5.arrived_ref = bf16[256,1024]{1,0:T(8,128)(2,1)S(1)} collective-permute-done((bf16[256,1024]{1,0:T(8,128)(2,1)S(1)}, bf16[256,1024]{1,0:T(8,128)(2,1)S(1)}, u32[]{:S(2)}, u32[]{:S(2)}) %collective-permute-start.5) | collective-permute-done | bytes 524320 | tf_op jit(solution)/shard_map/ppermute | solution.py:361
  25.9 0.7 collective-permute-start.12
  26.5 0.1 shard_map.40.refs_1_
  26.6 0.0 collective-permute-done.3.refs_3_.refs_2_.refs_8_
  26.6 23.8 %collective-permute-start.15 = (bf16[512,1024]{1,0:T(8,128)(2,1)S(1)}, bf16[512,1024]{1,0:T(8,128)(2,1)S(1)}, u32[]{:S(2)}, u32[]{:S(2)}) collective-permute-start(bf16[512,1024]{1,0:T(8,128)(2,1)S(1)} %shard_map.40.refs_1_), channel_id=1, source_target_pairs={{0,4},{2,6},{4,8},{6,10},{8,12},{10,14},{1,5},{3,7},{5,9},{7,11},{... | collective-permute-start | bytes 3145736 | tf_op jit(solution)/shard_map/ppermute | solution.py:351
  50.4 2.6 %shard_map.41.refs_4_ = bf16[4,512,1024]{2,1,0:T(8,128)(2,1)} custom-call(s32[3]{0:T(128)S(1)} %pad_add_fusion.place_ref.refs_0_, bf16[512,1024]{1,0:T(8,128)(2,1)S(1)} %get-tuple-element.38.refs_0_, bf16[512,1024]{1,0:T(8,128)(2,1)S(1)} %shard_map.40.refs_1_, ...), custom_call_target="tpu_custom_call", output_to_operand_aliasing={{}: (5, {})} | custom-call | flops 1000 | bytes 1000 | tf_op jit(solution)/shard_map/pallas_call | solution.py:192
  53.0 0.0 collective-permute-done.4.refs_3_.refs_4_.refs_10_
  53.0 2.0 %shard_map.42.refs_1_ = bf16[4,512,1024]{2,1,0:T(8,128)(2,1)} custom-call(s32[3]{0:T(128)S(1)} %pad_add_fusion.place_ref.refs_0_, bf16[512,1024]{1,0:T(8,128)(2,1)S(1)} %get-tuple-element.38.refs_0_, bf16[512,1024]{1,0:T(8,128)(2,1)S(1)} %shard_map.40.refs_1_, ...), custom_call_target="tpu_custom_call", output_to_operand_aliasing={{}: (5, {})} | custom-call | flops 1000 | bytes 1000 | tf_op jit(solution)/shard_map/pallas_call | solution.py:192
  55.0 0.0 collective-permute-done.2.refs_0_
  55.0 1.5 %shard_map.44 = (bf16[256,768]{1,0:T(8,128)(2,1)S(1)}, bf16[4,512,1024]{2,1,0:T(8,128)(2,1)}) custom-call(s32[3]{0:T(128)S(1)} %pad_add_fusion.place_ref.refs_0_, bf16[512,1024]{1,0:T(8,128)(2,1)S(1)} %collective-permute-done.2.refs_0_, bf16[1024,512]{1,0:T(8,128)(2,1)S(1)} %get-tuple-element.39.refs_2_.refs_1_.refs_7_, ...), custom_call_target="tpu_custom_call", output_to_operand_aliasing={{1}: (6, {})} | custom-call | flops 1000 | bytes 1000 | tf_op jit(solution)/shard_map/pallas_call | solution.py:213
  56.5 0.0 collective-permute-done.7.whole_ref
  56.5 0.1 shard_map.45
  56.6 0.3 collective-permute-start.8
  56.9 0.3 collective-permute-start.9
  57.2 0.0 collective-permute-done.12.odd_ref
  57.2 0.6 shard_map.47
  57.8 0.3 collective-permute-start.13
  58.1 1.3 %collective-permute-start.6 = (bf16[256,768]{1,0:T(8,128)(2,1)S(1)}, bf16[256,768]{1,0:T(8,128)(2,1)S(1)}, u32[]{:S(2)}, u32[]{:S(2)}) collective-permute-start(bf16[256,768]{1,0:T(8,128)(2,1)S(1)} %get-tuple-element.44.refs_0_), channel_id=1, source_target_pairs={{4,0},{6,2},{8,4},{10,6},{12,8},{14,10},{5,1},{7,3},{9,5},{11,7},{... | collective-permute-start | bytes 1179656 | tf_op jit(solution)/shard_map/ppermute | solution.py:351
  59.3 0.6 shard_map.48
  59.9 0.0 collective-permute-done.8.refs_2_.refs_3_
  59.9 7.3 %collective-permute-start.17 = (bf16[1024,256]{1,0:T(8,128)(2,1)S(1)}, bf16[1024,256]{1,0:T(8,128)(2,1)S(1)}, u32[]{:S(2)}, u32[]{:S(2)}) collective-permute-start(bf16[1024,256]{1,0:T(8,128)(2,1)S(1)} %get-tuple-element.56), channel_id=1, source_target_pairs={{2,0},{6,4},{10,8},{14,12},{0,2},{4,6},{8,10},{12,14},{3,1},{7,5},... | collective-permute-start | bytes 1572872 | tf_op jit(solution)/shard_map/ppermute | solution.py:351
  67.3 0.0 collective-permute-done.9.refs_4_.refs_5_
  67.3 1.5 %shard_map.49 = (bf16[256,768]{1,0:T(8,128)(2,1)S(1)}, bf16[4,512,1024]{2,1,0:T(8,128)(2,1)}) custom-call(s32[3]{0:T(128)S(1)} %pad_add_fusion.place_ref.refs_0_, bf16[512,1024]{1,0:T(8,128)(2,1)S(1)} %collective-permute-done.2.refs_0_, bf16[1024,256]{1,0:T(8,128)(2,1)S(1)} %get-tuple-element.46.refs_1_.refs_2_, ...), custom_call_target="tpu_custom_call", output_to_operand_aliasing={{1}: (8, {})} | custom-call | flops 1000 | bytes 1000 | tf_op jit(solution)/shard_map/pallas_call | solution.py:213
  68.8 1.3 %collective-permute-start.14 = (bf16[256,768]{1,0:T(8,128)(2,1)S(1)}, bf16[256,768]{1,0:T(8,128)(2,1)S(1)}, u32[]{:S(2)}, u32[]{:S(2)}) collective-permute-start(bf16[256,768]{1,0:T(8,128)(2,1)S(1)} %get-tuple-element.53), channel_id=1, source_target_pairs={{4,0},{6,2},{8,4},{10,6},{12,8},{14,10},{5,1},{7,3},{9,5},{11,7},{... | collective-permute-start | bytes 1179656 | tf_op jit(solution)/shard_map/ppermute | solution.py:351
  70.1 3.3 %collective-permute-done.15.refs_0_.refs_1_ = bf16[512,1024]{1,0:T(8,128)(2,1)S(1)} collective-permute-done((bf16[512,1024]{1,0:T(8,128)(2,1)S(1)}, bf16[512,1024]{1,0:T(8,128)(2,1)S(1)}, u32[]{:S(2)}, u32[]{:S(2)}) %collective-permute-start.15) | collective-permute-done | bytes 1048608 | tf_op jit(solution)/shard_map/ppermute | solution.py:351
  73.4 2.3 %shard_map.51 = (bf16[256,1536]{1,0:T(8,128)(2,1)S(1)}, bf16[4,512,1024]{2,1,0:T(8,128)(2,1)}) custom-call(s32[3]{0:T(128)S(1)} %pad_add_fusion.place_ref.refs_0_, bf16[512,1024]{1,0:T(8,128)(2,1)S(1)} %collective-permute-done.15.refs_0_.refs_1_, bf16[1024,256]{1,0:T(8,128)(2,1)S(1)} %get-tuple-element.46.refs_1_.refs_2_, ...), custom_call_target="tpu_custom_call", output_to_operand_aliasing={{1}: (12, {})} | custom-call | flops 1000 | bytes 1000 | tf_op jit(solution)/shard_map/pallas_call | solution.py:213
  75.8 1.3 %collective-permute-start.16 = (bf16[256,1536]{1,0:T(8,128)(2,1)S(1)}, bf16[256,1536]{1,0:T(8,128)(2,1)S(1)}, u32[]{:S(2)}, u32[]{:S(2)}) collective-permute-start(bf16[256,1536]{1,0:T(8,128)(2,1)S(1)} %get-tuple-element.55.refs_0_), channel_id=1, source_target_pairs={{4,0},{6,2},{8,4},{10,6},{12,8},{14,10},{5,1},{7,3},{9,5},{11,7},{... | collective-permute-start | bytes 2359304 | tf_op jit(solution)/shard_map/ppermute | solution.py:351
  77.1 0.1 collective-permute-start.22
  77.1 2.7 %collective-permute-done.17.whole_ref = bf16[1024,256]{1,0:T(8,128)(2,1)S(1)} collective-permute-done((bf16[1024,256]{1,0:T(8,128)(2,1)S(1)}, bf16[1024,256]{1,0:T(8,128)(2,1)S(1)}, u32[]{:S(2)}, u32[]{:S(2)}) %collective-permute-start.17) | collective-permute-done | bytes 524320 | tf_op jit(solution)/shard_map/ppermute | solution.py:351
  79.8 3.4 %collective-permute-done.14.refs_1_.refs_2_ = bf16[256,768]{1,0:T(8,128)(2,1)S(1)} collective-permute-done((bf16[256,768]{1,0:T(8,128)(2,1)S(1)}, bf16[256,768]{1,0:T(8,128)(2,1)S(1)}, u32[]{:S(2)}, u32[]{:S(2)}) %collective-permute-start.14) | collective-permute-done | bytes 393248 | tf_op jit(solution)/shard_map/ppermute | solution.py:351
  83.3 0.1 shard_map.52
  83.4 0.1 collective-permute-start.18
  83.5 0.5 collective-permute-start.19
  84.0 0.1 collective-permute-start.21
  84.0 0.9 collective-permute-done.18.refs_3_
  85.0 0.4 collective-permute-done.19.refs_5_
  85.4 1.2 %shard_map.53 = (bf16[512,256]{1,0:T(8,128)(2,1)S(1)}, bf16[4,512,1024]{2,1,0:T(8,128)(2,1)}) custom-call(s32[3]{0:T(128)S(1)} %pad_add_fusion.place_ref.refs_0_, bf16[512,1024]{1,0:T(8,128)(2,1)S(1)} %collective-permute-done.2.refs_0_, bf16[512,1024]{1,0:T(8,128)(2,1)S(1)} %collective-permute-done.15.refs_0_.refs_1_, ...), custom_call_target="tpu_custom_call", output_to_operand_aliasing={{1}: (7, {})} | custom-call | flops 1000 | bytes 1000 | tf_op jit(solution)/shard_map/pallas_call | solution.py:213
  86.6 1.5 %collective-permute-start.20 = (bf16[512,256]{1,0:T(8,128)(2,1)S(1)}, bf16[512,256]{1,0:T(8,128)(2,1)S(1)}, u32[]{:S(2)}, u32[]{:S(2)}) collective-permute-start(bf16[512,256]{1,0:T(8,128)(2,1)S(1)} %get-tuple-element.60), channel_id=1, source_target_pairs={{4,0},{6,2},{8,4},{10,6},{12,8},{14,10},{5,1},{7,3},{9,5},{11,7},{... | collective-permute-start | bytes 786440 | tf_op jit(solution)/shard_map/ppermute | solution.py:351
  88.1 2.6 %shard_map.54.refs_4_ = bf16[4,512,1024]{2,1,0:T(8,128)(2,1)} custom-call(s32[3]{0:T(128)S(1)} %pad_add_fusion.place_ref.refs_0_, bf16[512,1024]{1,0:T(8,128)(2,1)S(1)} %get-tuple-element.38.refs_0_, bf16[512,1024]{1,0:T(8,128)(2,1)S(1)} %shard_map.40.refs_1_, ...), custom_call_target="tpu_custom_call", output_to_operand_aliasing={{}: (7, {})} | custom-call | flops 1000 | bytes 1000 | tf_op jit(solution)/shard_map/pallas_call | solution.py:192
  90.7 2.0 %shard_map.55.refs_4_ = bf16[4,512,1024]{2,1,0:T(8,128)(2,1)} custom-call(s32[3]{0:T(128)S(1)} %pad_add_fusion.place_ref.refs_0_, bf16[512,1024]{1,0:T(8,128)(2,1)S(1)} %get-tuple-element.38.refs_0_, bf16[512,1024]{1,0:T(8,128)(2,1)S(1)} %shard_map.40.refs_1_, ...), custom_call_target="tpu_custom_call", output_to_operand_aliasing={{}: (5, {})} | custom-call | flops 1000 | bytes 1000 | tf_op jit(solution)/shard_map/pallas_call | solution.py:192
  92.6 2.0 %shard_map.56.refs_6_ = bf16[4,512,1024]{2,1,0:T(8,128)(2,1)} custom-call(s32[3]{0:T(128)S(1)} %pad_add_fusion.place_ref.refs_0_, bf16[512,1024]{1,0:T(8,128)(2,1)S(1)} %get-tuple-element.38.refs_0_, bf16[512,1024]{1,0:T(8,128)(2,1)S(1)} %shard_map.40.refs_1_, ...), custom_call_target="tpu_custom_call", output_to_operand_aliasing={{}: (5, {})} | custom-call | flops 1000 | bytes 1000 | tf_op jit(solution)/shard_map/pallas_call | solution.py:192
  94.6 2.0 %shard_map.57.refs_4_ = bf16[4,512,1024]{2,1,0:T(8,128)(2,1)} custom-call(s32[3]{0:T(128)S(1)} %pad_add_fusion.place_ref.refs_0_, bf16[512,1024]{1,0:T(8,128)(2,1)S(1)} %get-tuple-element.38.refs_0_, bf16[512,1024]{1,0:T(8,128)(2,1)S(1)} %shard_map.40.refs_1_, bf16[1024,128]{1,0:T(8,128)(2,1)S(1)} %get-tuple-element.57.refs_2_, ...), custom_call_target="tpu_custom_call", output_to_operand_aliasing={{}: (7, {})} | custom-call | flops 1000 | bytes 1000 | tf_op jit(solution)/shard_map/pallas_call | solution.py:192
  96.5 0.0 collective-permute-done.21.refs_3_
  96.5 2.0 %shard_map.58.refs_5_ = bf16[4,512,1024]{2,1,0:T(8,128)(2,1)} custom-call(s32[3]{0:T(128)S(1)} %pad_add_fusion.place_ref.refs_0_, bf16[512,1024]{1,0:T(8,128)(2,1)S(1)} %get-tuple-element.38.refs_0_, bf16[512,1024]{1,0:T(8,128)(2,1)S(1)} %shard_map.40.refs_1_, bf16[1024,256]{1,0:T(8,128)(2,1)S(1)} %get-tuple-element.61.refs_2_, ...), custom_call_target="tpu_custom_call", output_to_operand_aliasing={{}: (5, {})} | custom-call | flops 1000 | bytes 1000 | tf_op jit(solution)/shard_map/pallas_call | solution.py:192
  98.5 1.6 %collective-permute-done.16.refs_3_ = bf16[256,1536]{1,0:T(8,128)(2,1)S(1)} collective-permute-done((bf16[256,1536]{1,0:T(8,128)(2,1)S(1)}, bf16[256,1536]{1,0:T(8,128)(2,1)S(1)}, u32[]{:S(2)}, u32[]{:S(2)}) %collective-permute-start.16) | collective-permute-done | bytes 786464 | tf_op jit(solution)/shard_map/ppermute | solution.py:351
  100.1 4.9 %collective-permute-done.20.refs_4_ = bf16[512,256]{1,0:T(8,128)(2,1)S(1)} collective-permute-done((bf16[512,256]{1,0:T(8,128)(2,1)S(1)}, bf16[512,256]{1,0:T(8,128)(2,1)S(1)}, u32[]{:S(2)}, u32[]{:S(2)}) %collective-permute-start.20) | collective-permute-done | bytes 262176 | tf_op jit(solution)/shard_map/ppermute | solution.py:351
  105.0 1.8 %shard_map.59 = bf16[4,512,1024]{2,1,0:T(8,128)(2,1)} custom-call(s32[3]{0:T(128)S(1)} %pad_add_fusion.place_ref.refs_0_, bf16[256,768]{1,0:T(8,128)(2,1)S(1)} %collective-permute-done.6.refs_1_, bf16[256,768]{1,0:T(8,128)(2,1)S(1)} %collective-permute-done.14.refs_1_.refs_2_, ...), custom_call_target="tpu_custom_call", output_to_operand_aliasing={{}: (5, {})} | custom-call | flops 1000 | bytes 1000 | tf_op jit(solution)/shard_map/pallas_call | solution.py:322
  (6 shorter events, 0.0 us)
Async XLA Ops:
  3.1 1.4 %collective-permute-start = (f32[8,1024]{1,0:T(8,128)S(1)}, f32[8,1024]{1,0:T(8,128)S(1)}, u32[]{:S(2)}, u32[]{:S(2)}) collective-permute-start(f32[8,1024]{1,0:T(8,128)S(1)} %get-tuple-element.35.sums_ref), channel_id=1, source_target_pairs={{0,1},{1,0},{2,3},{3,2},{4,5},{5,4},{6,7},{7,6},{8,9},{9,8},{10,11... | collective-permute-start | bytes 98312 | tf_op jit(solution)/shard_map/ppermute | solution.py:361
  6.2 4.8 %collective-permute-start.1 = (bf16[256,1024]{1,0:T(8,128)(2,1)S(1)}, bf16[256,1024]{1,0:T(8,128)(2,1)S(1)}, u32[]{:S(2)}, u32[]{:S(2)}) collective-permute-start(bf16[256,1024]{1,0:T(8,128)(2,1)S(1)} %get-tuple-element.37), channel_id=1, source_target_pairs={{0,1},{1,0},{2,3},{3,2},{4,5},{5,4},{6,7},{7,6},{8,9},{9,8},{10,11... | collective-permute-start | bytes 1572872 | tf_op jit(solution)/shard_map/ppermute | solution.py:361
  6.6 17.3 %collective-permute-start.10 = (bf16[1024,256]{1,0:T(8,128)(2,1)S(1)}, bf16[1024,256]{1,0:T(8,128)(2,1)S(1)}, u32[]{:S(2)}, u32[]{:S(2)}) collective-permute-start(bf16[1024,256]{1,0:T(8,128)(2,1)S(1)} %get-tuple-element.48.odd_ref.refs_2_), channel_id=1, source_target_pairs={{4,0},{6,2},{8,4},{10,6},{12,8},{14,10},{5,1},{7,3},{9,5},{11,7},{... | collective-permute-start | bytes 1572872 | tf_op jit(solution)/shard_map/ppermute | solution.py:351
  7.9 18.7 %collective-permute-start.3 = (bf16[1024,512]{1,0:T(8,128)(2,1)S(1)}, bf16[1024,512]{1,0:T(8,128)(2,1)S(1)}, u32[]{:S(2)}, u32[]{:S(2)}) collective-permute-start(bf16[1024,512]{1,0:T(8,128)(2,1)S(1)} %get-tuple-element.39.refs_2_.refs_1_.refs_7_), channel_id=1, source_target_pairs={{0,1},{1,0},{2,3},{3,2},{4,5},{5,4},{6,7},{7,6},{8,9},{9,8},{10,11... | collective-permute-start | bytes 3145736 | tf_op jit(solution)/shard_map/ppermute | solution.py:361
  8.2 15.8 %collective-permute-start.11 = (bf16[1024,256]{1,0:T(8,128)(2,1)S(1)}, bf16[1024,256]{1,0:T(8,128)(2,1)S(1)}, u32[]{:S(2)}, u32[]{:S(2)}) collective-permute-start(bf16[1024,256]{1,0:T(8,128)(2,1)S(1)} %get-tuple-element.40.refs_2_.refs_3_.refs_9_), channel_id=1, source_target_pairs={{2,0},{6,4},{10,8},{14,12},{0,2},{4,6},{8,10},{12,14},{3,1},{7,5},... | collective-permute-start | bytes 1572872 | tf_op jit(solution)/shard_map/ppermute | solution.py:351
  11.1 43.9 %collective-permute-start.2 = (bf16[512,1024]{1,0:T(8,128)(2,1)S(1)}, bf16[512,1024]{1,0:T(8,128)(2,1)S(1)}, u32[]{:S(2)}, u32[]{:S(2)}) collective-permute-start(bf16[512,1024]{1,0:T(8,128)(2,1)S(1)} %get-tuple-element.38.refs_0_), channel_id=1, source_target_pairs={{0,4},{2,6},{4,8},{6,10},{8,12},{10,14},{1,5},{3,7},{5,9},{7,11},{... | collective-permute-start | bytes 3145736 | tf_op jit(solution)/shard_map/ppermute | solution.py:351
  15.4 41.1 %collective-permute-start.7 = (bf16[1024,512]{1,0:T(8,128)(2,1)S(1)}, bf16[1024,512]{1,0:T(8,128)(2,1)S(1)}, u32[]{:S(2)}, u32[]{:S(2)}) collective-permute-start(bf16[1024,512]{1,0:T(8,128)(2,1)S(1)} %get-tuple-element.45), channel_id=1, source_target_pairs={{2,0},{4,2},{6,4},{8,6},{10,8},{12,10},{14,12},{3,1},{5,3},{7,5},{... | collective-permute-start | bytes 3145736 | tf_op jit(solution)/shard_map/ppermute | solution.py:351
  23.9 1.9 %collective-permute-start.5 = (bf16[256,1024]{1,0:T(8,128)(2,1)S(1)}, bf16[256,1024]{1,0:T(8,128)(2,1)S(1)}, u32[]{:S(2)}, u32[]{:S(2)}) collective-permute-start(bf16[256,1024]{1,0:T(8,128)(2,1)S(1)} %get-tuple-element.42), channel_id=1, source_target_pairs={{0,1},{1,0},{2,3},{3,2},{4,5},{5,4},{6,7},{7,6},{8,9},{9,8},{10,11... | collective-permute-start | bytes 1572872 | tf_op jit(solution)/shard_map/ppermute | solution.py:361
  24.0 29.1 %collective-permute-start.4 = (bf16[1024,256]{1,0:T(8,128)(2,1)S(1)}, bf16[1024,256]{1,0:T(8,128)(2,1)S(1)}, u32[]{:S(2)}, u32[]{:S(2)}) collective-permute-start(bf16[1024,256]{1,0:T(8,128)(2,1)S(1)} %get-tuple-element.40.refs_2_.refs_3_.refs_9_), channel_id=1, source_target_pairs={{0,1},{1,0},{2,3},{3,2},{4,5},{5,4},{6,7},{7,6},{8,9},{9,8},{10,11... | collective-permute-start | bytes 1572872 | tf_op jit(solution)/shard_map/ppermute | solution.py:361
  25.9 31.3 %collective-permute-start.12 = (bf16[1024,256]{1,0:T(8,128)(2,1)S(1)}, bf16[1024,256]{1,0:T(8,128)(2,1)S(1)}, u32[]{:S(2)}, u32[]{:S(2)}) collective-permute-start(bf16[1024,256]{1,0:T(8,128)(2,1)S(1)} %shard_map.46.even_ref), channel_id=1, source_target_pairs={{6,2},{10,6},{14,10},{7,3},{11,7},{15,11},{22,18},{26,22},{30,26},... | collective-permute-start | bytes 1572872 | tf_op jit(solution)/shard_map/ppermute | solution.py:351
  26.6 46.8 %collective-permute-start.15 = (bf16[512,1024]{1,0:T(8,128)(2,1)S(1)}, bf16[512,1024]{1,0:T(8,128)(2,1)S(1)}, u32[]{:S(2)}, u32[]{:S(2)}) collective-permute-start(bf16[512,1024]{1,0:T(8,128)(2,1)S(1)} %shard_map.40.refs_1_), channel_id=1, source_target_pairs={{0,4},{2,6},{4,8},{6,10},{8,12},{10,14},{1,5},{3,7},{5,9},{7,11},{... | collective-permute-start | bytes 3145736 | tf_op jit(solution)/shard_map/ppermute | solution.py:351
  56.6 3.4 %collective-permute-start.8 = (bf16[1024,256]{1,0:T(8,128)(2,1)S(1)}, bf16[1024,256]{1,0:T(8,128)(2,1)S(1)}, u32[]{:S(2)}, u32[]{:S(2)}) collective-permute-start(bf16[1024,256]{1,0:T(8,128)(2,1)S(1)} %get-tuple-element.46.refs_1_.refs_2_), channel_id=1, source_target_pairs={{0,1},{1,0},{2,3},{3,2},{4,5},{5,4},{6,7},{7,6},{8,9},{9,8},{10,11... | collective-permute-start | bytes 1572872 | tf_op jit(solution)/shard_map/ppermute | solution.py:361
  56.9 10.4 %collective-permute-start.9 = (bf16[1024,256]{1,0:T(8,128)(2,1)S(1)}, bf16[1024,256]{1,0:T(8,128)(2,1)S(1)}, u32[]{:S(2)}, u32[]{:S(2)}) collective-permute-start(bf16[1024,256]{1,0:T(8,128)(2,1)S(1)} %get-tuple-element.47.refs_3_.refs_4_), channel_id=1, source_target_pairs={{0,1},{1,0},{2,3},{3,2},{4,5},{5,4},{6,7},{7,6},{8,9},{9,8},{10,11... | collective-permute-start | bytes 1572872 | tf_op jit(solution)/shard_map/ppermute | solution.py:361
  57.8 9.5 %collective-permute-start.13 = (bf16[1024,256]{1,0:T(8,128)(2,1)S(1)}, bf16[1024,256]{1,0:T(8,128)(2,1)S(1)}, u32[]{:S(2)}, u32[]{:S(2)}) collective-permute-start(bf16[1024,256]{1,0:T(8,128)(2,1)S(1)} %get-tuple-element.50.refs_5_.refs_2_), channel_id=1, source_target_pairs={{0,1},{1,0},{2,3},{3,2},{4,5},{5,4},{6,7},{7,6},{8,9},{9,8},{10,11... | collective-permute-start | bytes 1572872 | tf_op jit(solution)/shard_map/ppermute | solution.py:361
  58.1 15.4 %collective-permute-start.6 = (bf16[256,768]{1,0:T(8,128)(2,1)S(1)}, bf16[256,768]{1,0:T(8,128)(2,1)S(1)}, u32[]{:S(2)}, u32[]{:S(2)}) collective-permute-start(bf16[256,768]{1,0:T(8,128)(2,1)S(1)} %get-tuple-element.44.refs_0_), channel_id=1, source_target_pairs={{4,0},{6,2},{8,4},{10,6},{12,8},{14,10},{5,1},{7,3},{9,5},{11,7},{... | collective-permute-start | bytes 1179656 | tf_op jit(solution)/shard_map/ppermute | solution.py:351
  59.9 19.9 %collective-permute-start.17 = (bf16[1024,256]{1,0:T(8,128)(2,1)S(1)}, bf16[1024,256]{1,0:T(8,128)(2,1)S(1)}, u32[]{:S(2)}, u32[]{:S(2)}) collective-permute-start(bf16[1024,256]{1,0:T(8,128)(2,1)S(1)} %get-tuple-element.56), channel_id=1, source_target_pairs={{2,0},{6,4},{10,8},{14,12},{0,2},{4,6},{8,10},{12,14},{3,1},{7,5},... | collective-permute-start | bytes 1572872 | tf_op jit(solution)/shard_map/ppermute | solution.py:351
  68.8 14.5 %collective-permute-start.14 = (bf16[256,768]{1,0:T(8,128)(2,1)S(1)}, bf16[256,768]{1,0:T(8,128)(2,1)S(1)}, u32[]{:S(2)}, u32[]{:S(2)}) collective-permute-start(bf16[256,768]{1,0:T(8,128)(2,1)S(1)} %get-tuple-element.53), channel_id=1, source_target_pairs={{4,0},{6,2},{8,4},{10,6},{12,8},{14,10},{5,1},{7,3},{9,5},{11,7},{... | collective-permute-start | bytes 1179656 | tf_op jit(solution)/shard_map/ppermute | solution.py:351
  75.8 24.4 %collective-permute-start.16 = (bf16[256,1536]{1,0:T(8,128)(2,1)S(1)}, bf16[256,1536]{1,0:T(8,128)(2,1)S(1)}, u32[]{:S(2)}, u32[]{:S(2)}) collective-permute-start(bf16[256,1536]{1,0:T(8,128)(2,1)S(1)} %get-tuple-element.55.refs_0_), channel_id=1, source_target_pairs={{4,0},{6,2},{8,4},{10,6},{12,8},{14,10},{5,1},{7,3},{9,5},{11,7},{... | collective-permute-start | bytes 2359304 | tf_op jit(solution)/shard_map/ppermute | solution.py:351
  77.1 15.6 %collective-permute-start.22 = (bf16[1024,256]{1,0:T(8,128)(2,1)S(1)}, bf16[1024,256]{1,0:T(8,128)(2,1)S(1)}, u32[]{:S(2)}, u32[]{:S(2)}) collective-permute-start(bf16[1024,256]{1,0:T(8,128)(2,1)S(1)} %get-tuple-element.48.odd_ref.refs_2_), channel_id=1, source_target_pairs={{0,1},{1,0},{2,3},{3,2},{4,5},{5,4},{6,7},{7,6},{8,9},{9,8},{10,11... | collective-permute-start | bytes 1572872 | tf_op jit(solution)/shard_map/ppermute | solution.py:361
  83.4 1.6 %collective-permute-start.18 = (bf16[1024,128]{1,0:T(8,128)(2,1)S(1)}, bf16[1024,128]{1,0:T(8,128)(2,1)S(1)}, u32[]{:S(2)}, u32[]{:S(2)}) collective-permute-start(bf16[1024,128]{1,0:T(8,128)(2,1)S(1)} %get-tuple-element.57.refs_2_), channel_id=1, source_target_pairs={{0,1},{1,0},{2,3},{3,2},{4,5},{5,4},{6,7},{7,6},{8,9},{9,8},{10,11... | collective-permute-start | bytes 786440 | tf_op jit(solution)/shard_map/ppermute | solution.py:361
  83.5 1.9 %collective-permute-start.19 = (bf16[1024,128]{1,0:T(8,128)(2,1)S(1)}, bf16[1024,128]{1,0:T(8,128)(2,1)S(1)}, u32[]{:S(2)}, u32[]{:S(2)}) collective-permute-start(bf16[1024,128]{1,0:T(8,128)(2,1)S(1)} %get-tuple-element.58.refs_4_), channel_id=1, source_target_pairs={{0,1},{1,0},{2,3},{3,2},{4,5},{5,4},{6,7},{7,6},{8,9},{9,8},{10,11... | collective-permute-start | bytes 786440 | tf_op jit(solution)/shard_map/ppermute | solution.py:361
  84.0 12.6 %collective-permute-start.21 = (bf16[1024,256]{1,0:T(8,128)(2,1)S(1)}, bf16[1024,256]{1,0:T(8,128)(2,1)S(1)}, u32[]{:S(2)}, u32[]{:S(2)}) collective-permute-start(bf16[1024,256]{1,0:T(8,128)(2,1)S(1)} %get-tuple-element.61.refs_2_), channel_id=1, source_target_pairs={{0,1},{1,0},{2,3},{3,2},{4,5},{5,4},{6,7},{7,6},{8,9},{9,8},{10,11... | collective-permute-start | bytes 1572872 | tf_op jit(solution)/shard_map/ppermute | solution.py:361
  86.6 18.4 %collective-permute-start.20 = (bf16[512,256]{1,0:T(8,128)(2,1)S(1)}, bf16[512,256]{1,0:T(8,128)(2,1)S(1)}, u32[]{:S(2)}, u32[]{:S(2)}) collective-permute-start(bf16[512,256]{1,0:T(8,128)(2,1)S(1)} %get-tuple-element.60), channel_id=1, source_target_pairs={{4,0},{6,2},{8,4},{10,6},{12,8},{14,10},{5,1},{7,3},{9,5},{11,7},{... | collective-permute-start | bytes 786440 | tf_op jit(solution)/shard_map/ppermute | solution.py:351

commit v12 on v10

--- a/solution.py
+++ b/solution.py
@@ -11,7 +11,7 @@
 PIECES = (4, 2, 2)
 ROWS = (1, 1)
 PARTS = 2
-BLOCKS = 8
+BLOCKS = 16
 STATS_VMEM = 50
 epsilon = 1e-05
 
@@ -284,40 +284,38 @@
     )(piece, *after)
 
 
-def last_kernel(place_ref, top2, top3, bottom, side, out_ref, two, three, sems):
-    keep2, keep3 = 2 < place_ref[2], 3 < place_ref[2]
+def put_kernel(place_ref, top2, top3, bottom, out_ref, two, three, sems):
     part, wide = top2.shape
-    first, after = wide - wide * PIECES[2] // (PIECES[0] + PIECES[2]), side.shape[1]
-
-    def kept(keep, block):
-        return jnp.where(keep, block, 0.0).astype(out_ref.dtype)
-
-    two[0:part, 0:wide] = kept(keep2, top2[...])
-    two[part:, 0:wide] = kept(keep2, bottom[:, wide:])
-    copies = [
-        pltpu.make_async_copy(two.at[:, 0:first], out_ref.at[2, :, 0:first], sems.at[0]),
-        pltpu.make_async_copy(two.at[:, first:], out_ref.at[2, :, first + after :], sems.at[1]),
-        pltpu.make_async_copy(three, out_ref.at[3], sems.at[2]),
-    ]
-    copies[0].start()
-    copies[1].start()
-    for at, columns in ((0, slice(0, first)), (first, slice(first + after, None))):
-        received = slice(at, first if at == 0 else wide)
-        three[0:part, columns] = kept(keep3, top3[:, received])
-        three[part:, columns] = kept(keep3, bottom[:, received])
-    three[:, first : first + after] = kept(keep3, side[...])
-    copies[2].start()
+    first = wide * PIECES[0] // (PIECES[0] + PIECES[2])
+    end = out_ref.shape[2]
+    after = end - wide + first
+    copies = []
+    for k, scratch, upper, lower in (
+        (2, two, top2, bottom[:, wide:]),
+        (3, three, top3, bottom[:, 0:wide]),
+    ):
+        keep = k < place_ref[2]
+        scratch[0:part, :] = jnp.where(keep, upper[...], 0.0).astype(scratch.dtype)
+        scratch[part:, :] = jnp.where(keep, lower, 0.0).astype(scratch.dtype)
+        for n, (here, there) in enumerate(
+            ((pl.ds(0, first), pl.ds(0, first)), (pl.ds(first, wide - first), pl.ds(after, end - after)))
+        ):
+            copy = pltpu.make_async_copy(
+                scratch.at[:, here], out_ref.at[k, :, there], sems.at[k - 2, n]
+            )
+            copy.start()
+            copies.append(copy)
     for copy in copies:
         copy.wait()
 
 
-def last(place, buffer, top2, top3, bottom, side):
-    operands = [place, top2, top3, bottom, side, buffer]
-    count, width = buffer.shape[1:]
+def put(place, buffer, top2, top3, bottom):
+    operands = [place, top2, top3, bottom, buffer]
+    shape = (buffer.shape[1], top2.shape[1])
 
     def kernel(*refs):
         n = len(operands)
-        last_kernel(*refs[: n - 1], *refs[n:])
+        put_kernel(*refs[: n - 1], *refs[n:])
 
     return pl.pallas_call(
         kernel,
@@ -325,14 +323,32 @@
         out_specs=ANY,
         out_shape=jax.ShapeDtypeStruct(buffer.shape, buffer.dtype),
         scratch_shapes=[
-            pltpu.VMEM((count, top2.shape[1]), buffer.dtype),
-            pltpu.VMEM((count, width), buffer.dtype),
-            pltpu.SemaphoreType.DMA((3,)),
+            pltpu.VMEM(shape, buffer.dtype),
+            pltpu.VMEM(shape, buffer.dtype),
+            pltpu.SemaphoreType.DMA((2, 2)),
         ],
         input_output_aliases={len(operands) - 1: 0},
         compiler_params=PARAMS,
         cost_estimate=COST,
     )(*operands)
+
+
+def last_kernel(place_ref, side, buffer_ref, out_ref):
+    out_ref[0] = jnp.where(3 < place_ref[2], side[...], 0.0).astype(out_ref.dtype)
+
+
+def last(place, buffer, side, column):
+    count, width = side.shape
+    return pl.pallas_call(
+        last_kernel,
+        grid=(1,),
+        in_specs=[SMEM, VMEM, ANY],
+        out_specs=pl.BlockSpec((1, count, width), lambda i: (3, 0, column)),
+        out_shape=jax.ShapeDtypeStruct(buffer.shape, buffer.dtype),
+        input_output_aliases={2: 0},
+        compiler_params=PARAMS,
+        cost_estimate=COST,
+    )(place, side, buffer)
 
 
 def per_device(dosage, observed, counts):
@@ -407,7 +423,8 @@
     buffer = tile(place, buffer, 0, 2, rows, [relayed, mate(relayed)], samples)
     buffer = tile(place, buffer, 1, 2, rows, low, samples)
     buffer = tile(place, buffer, 2, 2, rows, [above, mate(above)], samples)
-    buffer = last(place, buffer, top2, top3, bottom, side)
+    buffer = put(place, buffer, top2, top3, bottom)
+    buffer = last(place, buffer, side, 2)
     return buffer[None]
 
 

time: 96.5 us -> 95.8 us (level)
  waiting for transfers between devices: 39.4 us -> 37.2 us
  Pallas kernels: 29.7 us -> 31 us
    ppermute x11, waiting for transfers between devices: 37.9 us -> 35.6 us  [send(): return lax.ppermute(shard, 'var', pairs)]
    pallas_call x1 -> x2, Pallas kernels: 1.85 us -> 3.03 us  [the longest x1 1.76 us: put(): pl.pallas_call(kernel, in_specs=[SMEM] + [VMEM] * (len(operands) - 2) + [...]
  transfers between devices with their start and end apart: 23 -> 23, of which waited for: 12 -> 12; matrix products, arithmetic and copies ran while one was open for 0% -> 0% of each run, Pallas kernels for 24% -> 26%
where the time goes in v12:
time: 95.8 us; the launch traced here: 95.5 us
  waiting for transfers between devices  37.2 us (39%)
  Pallas kernels  31 us (32%)
  starting transfers between devices  26.4 us (28%)
    ppermute x11, waiting for transfers between devices, send(): return lax.ppermute(shard, 'var', pairs)  35.6 us
    ppermute x11, starting transfers between devices, send(): return lax.ppermute(shard, 'var', pairs)  23.5 us
    pallas_call x7, Pallas kernels, tile(): pl.pallas_call(functools.partial(tile_kernel, k, len(rows), len(rights),...  14.9 us
    pallas_call x4, Pallas kernels, far(): pl.pallas_call(functools.partial(far_kernel, 1.0 / samples, len(rows), le...  6.6 us
    pallas_call x1, Pallas kernels, stats(): pl.pallas_call(stats_kernel, in_specs=[pl.BlockSpec(memory_space=pltpu.HB...  3.16 us
    ppermute x12, starting transfers between devices, mate(): return lax.ppermute(shard, 'samp', [(0, 1), (1, 0)])  2.92 us
  transfers between devices with their start and end apart: 23, of which 12 were waited for; matrix products, arithmetic and copies ran while one was open for 0% of the time, Pallas kernels for 26%

profile of v12, /device:TPU:0, one launch (start us, length us, event | category | flops | bytes accessed | tf_op | source)
XLA Modules:
  0.0 95.5 jit_solution(13854894330435020786)
XLA Ops:
  0.0 3.2 %shard_map.37 = (f32[8,1024]{1,0:T(8,128)S(1)}, bf16[1024,1024]{1,0:T(8,128)(2,1)S(1)}) custom-call(bf16[1024,1024]{1,0:T(8,128)(2,1)} %dosage_hbm.1, s32[1024,1024]{1,0:T(8,128)} %observed_hbm.1), custom_call_target="tpu_custom_call" | custom-call | flops 1000 | bytes 1000 | tf_op jit(solution)/shard_map/pallas_call | solution.py:60
  3.2 0.5 collective-permute-start
  4.3 0.1 pad_add_fusion.place_ref.refs_0_
  4.4 0.1 collective-permute-done.sums_other_ref
  4.5 1.7 %shard_map.38 = (bf16[1024,512]{1,0:T(8,128)(2,1)S(1)}, bf16[1024,256]{1,0:T(8,128)(2,1)S(1)}, bf16[1024,256]{1,0:T(8,128)(2,1)S(1)}, bf16[1024,512]{1,0:T(8,128...) custom-call(s32[3]{0:T(128)S(1)} %pad_add_fusion.place_ref.refs_0_, ...), custom_call_target="tpu_custom_call" | custom-call | flops 1000 | bytes 1000 | tf_op jit(solution)/shard_map/pallas_call | solution.py:118
  6.3 0.4 collective-permute-start.1
  6.7 2.7 %collective-permute-start.6 = (bf16[1024,256]{1,0:T(8,128)(2,1)S(1)}, bf16[1024,256]{1,0:T(8,128)(2,1)S(1)}, u32[]{:S(2)}, u32[]{:S(2)}) collective-permute-start(bf16[1024,256]{1,0:T(8,128)(2,1)S(1)} %get-tuple-element.42.refs_2_.refs_3_.refs_9_), channel_id=1, source_target_pairs={{2,0},{6,4},{10,8},{14,12},{0,2},{4,6},{8,10},{12,14},{3,1},{7,5},... | collective-permute-start | bytes 1572872 | tf_op jit(solution)/shard_map/ppermute | solution.py:367
  9.4 0.1 collective-permute-start.8
  9.5 1.3 %collective-permute-start.5 = (bf16[1024,256]{1,0:T(8,128)(2,1)S(1)}, bf16[1024,256]{1,0:T(8,128)(2,1)S(1)}, u32[]{:S(2)}, u32[]{:S(2)}) collective-permute-start(bf16[1024,256]{1,0:T(8,128)(2,1)S(1)} %get-tuple-element.41.odd_ref.refs_2_), channel_id=1, source_target_pairs={{4,0},{6,2},{8,4},{10,6},{12,8},{14,10},{5,1},{7,3},{9,5},{11,7},{... | collective-permute-start | bytes 1572872 | tf_op jit(solution)/shard_map/ppermute | solution.py:367
  10.7 0.0 collective-permute-done.1.arrived_ref
  10.8 0.1 shard_map.39
  10.8 4.6 %collective-permute-start.2 = (bf16[512,1024]{1,0:T(8,128)(2,1)S(1)}, bf16[512,1024]{1,0:T(8,128)(2,1)S(1)}, u32[]{:S(2)}, u32[]{:S(2)}) collective-permute-start(bf16[512,1024]{1,0:T(8,128)(2,1)S(1)} %get-tuple-element.38.refs_0_), channel_id=1, source_target_pairs={{0,4},{2,6},{4,8},{6,10},{8,12},{10,14},{1,5},{3,7},{5,9},{7,11},{... | collective-permute-start | bytes 3145736 | tf_op jit(solution)/shard_map/ppermute | solution.py:367
  15.5 6.4 %collective-permute-done.6.refs_1_.refs_0_ = bf16[1024,256]{1,0:T(8,128)(2,1)S(1)} collective-permute-done((bf16[1024,256]{1,0:T(8,128)(2,1)S(1)}, bf16[1024,256]{1,0:T(8,128)(2,1)S(1)}, u32[]{:S(2)}, u32[]{:S(2)}) %collective-permute-start.6) | collective-permute-done | bytes 524320 | tf_op jit(solution)/shard_map/ppermute | solution.py:367
  21.8 1.3 %collective-permute-start.11 = (bf16[1024,512]{1,0:T(8,128)(2,1)S(1)}, bf16[1024,512]{1,0:T(8,128)(2,1)S(1)}, u32[]{:S(2)}, u32[]{:S(2)}) collective-permute-start(bf16[1024,512]{1,0:T(8,128)(2,1)S(1)} %shard_map.48), channel_id=1, source_target_pairs={{2,0},{4,2},{6,4},{8,6},{10,8},{12,10},{14,12},{3,1},{5,3},{7,5},{... | collective-permute-start | bytes 3145736 | tf_op jit(solution)/shard_map/ppermute | solution.py:367
  23.1 0.1 collective-permute-start.3
  23.2 2.4 %collective-permute-done.5.refs_0_.even_ref = bf16[1024,256]{1,0:T(8,128)(2,1)S(1)} collective-permute-done((bf16[1024,256]{1,0:T(8,128)(2,1)S(1)}, bf16[1024,256]{1,0:T(8,128)(2,1)S(1)}, u32[]{:S(2)}, u32[]{:S(2)}) %collective-permute-start.5) | collective-permute-done | bytes 524320 | tf_op jit(solution)/shard_map/ppermute | solution.py:367
  25.6 0.0 collective-permute-start.9
  25.6 0.0 collective-permute-done.3.arrived_ref
  25.6 0.7 collective-permute-start.7
  26.3 0.1 shard_map.40.refs_1_
  26.4 0.0 collective-permute-done.8.refs_3_.refs_2_.refs_8_
  26.4 5.3 %collective-permute-start.4 = (bf16[512,1024]{1,0:T(8,128)(2,1)S(1)}, bf16[512,1024]{1,0:T(8,128)(2,1)S(1)}, u32[]{:S(2)}, u32[]{:S(2)}) collective-permute-start(bf16[512,1024]{1,0:T(8,128)(2,1)S(1)} %shard_map.40.refs_1_), channel_id=1, source_target_pairs={{0,4},{2,6},{4,8},{6,10},{8,12},{10,14},{1,5},{3,7},{5,9},{7,11},{... | collective-permute-start | bytes 3145736 | tf_op jit(solution)/shard_map/ppermute | solution.py:367
  31.7 2.6 %shard_map.42.refs_4_ = bf16[4,512,1024]{2,1,0:T(8,128)(2,1)} custom-call(s32[3]{0:T(128)S(1)} %pad_add_fusion.place_ref.refs_0_, bf16[512,1024]{1,0:T(8,128)(2,1)S(1)} %get-tuple-element.38.refs_0_, bf16[512,1024]{1,0:T(8,128)(2,1)S(1)} %shard_map.40.refs_1_, ...), custom_call_target="tpu_custom_call", output_to_operand_aliasing={{}: (5, {})} | custom-call | flops 1000 | bytes 1000 | tf_op jit(solution)/shard_map/pallas_call | solution.py:192
  34.3 0.0 collective-permute-done.9.refs_3_.refs_4_.refs_10_
  34.3 2.0 %shard_map.43.refs_1_ = bf16[4,512,1024]{2,1,0:T(8,128)(2,1)} custom-call(s32[3]{0:T(128)S(1)} %pad_add_fusion.place_ref.refs_0_, bf16[512,1024]{1,0:T(8,128)(2,1)S(1)} %get-tuple-element.38.refs_0_, bf16[512,1024]{1,0:T(8,128)(2,1)S(1)} %shard_map.40.refs_1_, ...), custom_call_target="tpu_custom_call", output_to_operand_aliasing={{}: (5, {})} | custom-call | flops 1000 | bytes 1000 | tf_op jit(solution)/shard_map/pallas_call | solution.py:192
  36.2 2.7 %collective-permute-done.2.refs_0_ = bf16[512,1024]{1,0:T(8,128)(2,1)S(1)} collective-permute-done((bf16[512,1024]{1,0:T(8,128)(2,1)S(1)}, bf16[512,1024]{1,0:T(8,128)(2,1)S(1)}, u32[]{:S(2)}, u32[]{:S(2)}) %collective-permute-start.2) | collective-permute-done | bytes 1048608 | tf_op jit(solution)/shard_map/ppermute | solution.py:367
  38.9 1.5 %shard_map.45 = (bf16[256,768]{1,0:T(8,128)(2,1)S(1)}, bf16[4,512,1024]{2,1,0:T(8,128)(2,1)}) custom-call(s32[3]{0:T(128)S(1)} %pad_add_fusion.place_ref.refs_0_, bf16[512,1024]{1,0:T(8,128)(2,1)S(1)} %collective-permute-done.2.refs_0_, bf16[1024,512]{1,0:T(8,128)(2,1)S(1)} %get-tuple-element.43.refs_2_.refs_1_.refs_7_, ...), custom_call_target="tpu_custom_call", output_to_operand_aliasing={{1}: (6, {})} | custom-call | flops 1000 | bytes 1000 | tf_op jit(solution)/shard_map/pallas_call | solution.py:213
  40.4 8.2 %collective-permute-done.11.whole_ref = bf16[1024,512]{1,0:T(8,128)(2,1)S(1)} collective-permute-done((bf16[1024,512]{1,0:T(8,128)(2,1)S(1)}, bf16[1024,512]{1,0:T(8,128)(2,1)S(1)}, u32[]{:S(2)}, u32[]{:S(2)}) %collective-permute-start.11) | collective-permute-done | bytes 1048608 | tf_op jit(solution)/shard_map/ppermute | solution.py:367
  48.6 0.1 shard_map.49
  48.7 0.1 collective-permute-start.12
  48.8 0.5 collective-permute-start.13
  49.3 0.0 collective-permute-done.7.odd_ref
  49.3 0.6 shard_map.46
  49.9 0.1 collective-permute-start.14
  50.0 1.3 %collective-permute-start.15 = (bf16[256,768]{1,0:T(8,128)(2,1)S(1)}, bf16[256,768]{1,0:T(8,128)(2,1)S(1)}, u32[]{:S(2)}, u32[]{:S(2)}) collective-permute-start(bf16[256,768]{1,0:T(8,128)(2,1)S(1)} %get-tuple-element.49.refs_0_), channel_id=1, source_target_pairs={{4,0},{6,2},{8,4},{10,6},{12,8},{14,10},{5,1},{7,3},{9,5},{11,7},{... | collective-permute-start | bytes 1179656 | tf_op jit(solution)/shard_map/ppermute | solution.py:367
  51.3 0.6 shard_map.47
  51.9 2.4 %collective-permute-start.10 = (bf16[1024,256]{1,0:T(8,128)(2,1)S(1)}, bf16[1024,256]{1,0:T(8,128)(2,1)S(1)}, u32[]{:S(2)}, u32[]{:S(2)}) collective-permute-start(bf16[1024,256]{1,0:T(8,128)(2,1)S(1)} %get-tuple-element.47), channel_id=1, source_target_pairs={{2,0},{6,4},{10,8},{14,12},{0,2},{4,6},{8,10},{12,14},{3,1},{7,5},... | collective-permute-start | bytes 1572872 | tf_op jit(solution)/shard_map/ppermute | solution.py:367
  54.3 1.5 %shard_map.50 = (bf16[256,768]{1,0:T(8,128)(2,1)S(1)}, bf16[4,512,1024]{2,1,0:T(8,128)(2,1)}) custom-call(s32[3]{0:T(128)S(1)} %pad_add_fusion.place_ref.refs_0_, bf16[512,1024]{1,0:T(8,128)(2,1)S(1)} %collective-permute-done.2.refs_0_, bf16[1024,256]{1,0:T(8,128)(2,1)S(1)} %get-tuple-element.50.refs_1_.refs_2_, ...), custom_call_target="tpu_custom_call", output_to_operand_aliasing={{1}: (8, {})} | custom-call | flops 1000 | bytes 1000 | tf_op jit(solution)/shard_map/pallas_call | solution.py:213
  55.8 1.3 %collective-permute-start.16 = (bf16[256,768]{1,0:T(8,128)(2,1)S(1)}, bf16[256,768]{1,0:T(8,128)(2,1)S(1)}, u32[]{:S(2)}, u32[]{:S(2)}) collective-permute-start(bf16[256,768]{1,0:T(8,128)(2,1)S(1)} %get-tuple-element.56), channel_id=1, source_target_pairs={{4,0},{6,2},{8,4},{10,6},{12,8},{14,10},{5,1},{7,3},{9,5},{11,7},{... | collective-permute-start | bytes 1179656 | tf_op jit(solution)/shard_map/ppermute | solution.py:367
  57.1 3.5 %collective-permute-done.4.refs_0_.refs_1_ = bf16[512,1024]{1,0:T(8,128)(2,1)S(1)} collective-permute-done((bf16[512,1024]{1,0:T(8,128)(2,1)S(1)}, bf16[512,1024]{1,0:T(8,128)(2,1)S(1)}, u32[]{:S(2)}, u32[]{:S(2)}) %collective-permute-start.4) | collective-permute-done | bytes 1048608 | tf_op jit(solution)/shard_map/ppermute | solution.py:367
  60.6 3.2 %collective-permute-done.15.refs_1_ = bf16[256,768]{1,0:T(8,128)(2,1)S(1)} collective-permute-done((bf16[256,768]{1,0:T(8,128)(2,1)S(1)}, bf16[256,768]{1,0:T(8,128)(2,1)S(1)}, u32[]{:S(2)}, u32[]{:S(2)}) %collective-permute-start.15) | collective-permute-done | bytes 393248 | tf_op jit(solution)/shard_map/ppermute | solution.py:367
  63.8 2.3 %shard_map.52 = (bf16[256,1536]{1,0:T(8,128)(2,1)S(1)}, bf16[4,512,1024]{2,1,0:T(8,128)(2,1)}) custom-call(s32[3]{0:T(128)S(1)} %pad_add_fusion.place_ref.refs_0_, bf16[512,1024]{1,0:T(8,128)(2,1)S(1)} %collective-permute-done.4.refs_0_.refs_1_, bf16[1024,256]{1,0:T(8,128)(2,1)S(1)} %get-tuple-element.50.refs_1_.refs_2_, ...), custom_call_target="tpu_custom_call", output_to_operand_aliasing={{1}: (12, {})} | custom-call | flops 1000 | bytes 1000 | tf_op jit(solution)/shard_map/pallas_call | solution.py:213
  66.2 1.3 %collective-permute-start.20 = (bf16[256,1536]{1,0:T(8,128)(2,1)S(1)}, bf16[256,1536]{1,0:T(8,128)(2,1)S(1)}, u32[]{:S(2)}, u32[]{:S(2)}) collective-permute-start(bf16[256,1536]{1,0:T(8,128)(2,1)S(1)} %get-tuple-element.55.refs_0_), channel_id=1, source_target_pairs={{4,0},{6,2},{8,4},{10,6},{12,8},{14,10},{5,1},{7,3},{9,5},{11,7},{... | collective-permute-start | bytes 2359304 | tf_op jit(solution)/shard_map/ppermute | solution.py:367
  67.5 0.1 collective-permute-start.22
  67.5 0.5 collective-permute-start.21
  68.0 0.0 collective-permute-done.10.whole_ref
  68.0 4.2 %collective-permute-done.16.refs_1_.refs_2_ = bf16[256,768]{1,0:T(8,128)(2,1)S(1)} collective-permute-done((bf16[256,768]{1,0:T(8,128)(2,1)S(1)}, bf16[256,768]{1,0:T(8,128)(2,1)S(1)}, u32[]{:S(2)}, u32[]{:S(2)}) %collective-permute-start.16) | collective-permute-done | bytes 393248 | tf_op jit(solution)/shard_map/ppermute | solution.py:367
  72.2 0.1 shard_map.53
  72.3 0.1 collective-permute-start.17
  72.4 0.5 collective-permute-start.18
  72.9 1.0 %collective-permute-done.17.refs_3_ = bf16[1024,128]{1,0:T(8,128)(2,1)S(1)} collective-permute-done((bf16[1024,128]{1,0:T(8,128)(2,1)S(1)}, bf16[1024,128]{1,0:T(8,128)(2,1)S(1)}, u32[]{:S(2)}, u32[]{:S(2)}) %collective-permute-start.17) | collective-permute-done | bytes 262176 | tf_op jit(solution)/shard_map/ppermute | solution.py:377
  73.9 0.4 collective-permute-done.18.refs_5_
  74.3 1.2 %shard_map.54 = (bf16[512,256]{1,0:T(8,128)(2,1)S(1)}, bf16[4,512,1024]{2,1,0:T(8,128)(2,1)}) custom-call(s32[3]{0:T(128)S(1)} %pad_add_fusion.place_ref.refs_0_, bf16[512,1024]{1,0:T(8,128)(2,1)S(1)} %collective-permute-done.2.refs_0_, bf16[512,1024]{1,0:T(8,128)(2,1)S(1)} %collective-permute-done.4.refs_0_.refs_1_, ...), custom_call_target="tpu_custom_call", output_to_operand_aliasing={{1}: (7, {})} | custom-call | flops 1000 | bytes 1000 | tf_op jit(solution)/shard_map/pallas_call | solution.py:213
  75.6 1.5 %collective-permute-start.19 = (bf16[512,256]{1,0:T(8,128)(2,1)S(1)}, bf16[512,256]{1,0:T(8,128)(2,1)S(1)}, u32[]{:S(2)}, u32[]{:S(2)}) collective-permute-start(bf16[512,256]{1,0:T(8,128)(2,1)S(1)} %get-tuple-element.60), channel_id=1, source_target_pairs={{4,0},{6,2},{8,4},{10,6},{12,8},{14,10},{5,1},{7,3},{9,5},{11,7},{... | collective-permute-start | bytes 786440 | tf_op jit(solution)/shard_map/ppermute | solution.py:367
  77.0 2.6 %shard_map.55.refs_4_ = bf16[4,512,1024]{2,1,0:T(8,128)(2,1)} custom-call(s32[3]{0:T(128)S(1)} %pad_add_fusion.place_ref.refs_0_, bf16[512,1024]{1,0:T(8,128)(2,1)S(1)} %get-tuple-element.38.refs_0_, bf16[512,1024]{1,0:T(8,128)(2,1)S(1)} %shard_map.40.refs_1_, ...), custom_call_target="tpu_custom_call", output_to_operand_aliasing={{}: (7, {})} | custom-call | flops 1000 | bytes 1000 | tf_op jit(solution)/shard_map/pallas_call | solution.py:192
  79.6 2.0 %shard_map.56.refs_4_ = bf16[4,512,1024]{2,1,0:T(8,128)(2,1)} custom-call(s32[3]{0:T(128)S(1)} %pad_add_fusion.place_ref.refs_0_, bf16[512,1024]{1,0:T(8,128)(2,1)S(1)} %get-tuple-element.38.refs_0_, bf16[512,1024]{1,0:T(8,128)(2,1)S(1)} %shard_map.40.refs_1_, ...), custom_call_target="tpu_custom_call", output_to_operand_aliasing={{}: (5, {})} | custom-call | flops 1000 | bytes 1000 | tf_op jit(solution)/shard_map/pallas_call | solution.py:192
  81.6 0.0 collective-permute-done.22.refs_3_
  81.6 2.0 %shard_map.57.refs_6_ = bf16[4,512,1024]{2,1,0:T(8,128)(2,1)} custom-call(s32[3]{0:T(128)S(1)} %pad_add_fusion.place_ref.refs_0_, bf16[512,1024]{1,0:T(8,128)(2,1)S(1)} %get-tuple-element.38.refs_0_, bf16[512,1024]{1,0:T(8,128)(2,1)S(1)} %shard_map.40.refs_1_, ...), custom_call_target="tpu_custom_call", output_to_operand_aliasing={{}: (5, {})} | custom-call | flops 1000 | bytes 1000 | tf_op jit(solution)/shard_map/pallas_call | solution.py:192
  83.5 2.0 %shard_map.58.refs_4_ = bf16[4,512,1024]{2,1,0:T(8,128)(2,1)} custom-call(s32[3]{0:T(128)S(1)} %pad_add_fusion.place_ref.refs_0_, bf16[512,1024]{1,0:T(8,128)(2,1)S(1)} %get-tuple-element.38.refs_0_, bf16[512,1024]{1,0:T(8,128)(2,1)S(1)} %shard_map.40.refs_1_, bf16[1024,128]{1,0:T(8,128)(2,1)S(1)} %get-tuple-element.57.refs_2_, ...), custom_call_target="tpu_custom_call", output_to_operand_aliasing={{}: (7, {})} | custom-call | flops 1000 | bytes 1000 | tf_op jit(solution)/shard_map/pallas_call | solution.py:192
  85.5 2.0 %shard_map.59.refs_4_ = bf16[4,512,1024]{2,1,0:T(8,128)(2,1)} custom-call(s32[3]{0:T(128)S(1)} %pad_add_fusion.place_ref.refs_0_, bf16[512,1024]{1,0:T(8,128)(2,1)S(1)} %get-tuple-element.38.refs_0_, bf16[512,1024]{1,0:T(8,128)(2,1)S(1)} %shard_map.40.refs_1_, bf16[1024,256]{1,0:T(8,128)(2,1)S(1)} %get-tuple-element.61.refs_2_, ...), custom_call_target="tpu_custom_call", output_to_operand_aliasing={{}: (5, {})} | custom-call | flops 1000 | bytes 1000 | tf_op jit(solution)/shard_map/pallas_call | solution.py:192
  87.4 1.6 %collective-permute-done.20.refs_3_ = bf16[256,1536]{1,0:T(8,128)(2,1)S(1)} collective-permute-done((bf16[256,1536]{1,0:T(8,128)(2,1)S(1)}, bf16[256,1536]{1,0:T(8,128)(2,1)S(1)}, u32[]{:S(2)}, u32[]{:S(2)}) %collective-permute-start.20) | collective-permute-done | bytes 786464 | tf_op jit(solution)/shard_map/ppermute | solution.py:367
  89.1 1.8 %shard_map.60.buffer_ref = bf16[4,512,1024]{2,1,0:T(8,128)(2,1)} custom-call(s32[3]{0:T(128)S(1)} %pad_add_fusion.place_ref.refs_0_, bf16[256,768]{1,0:T(8,128)(2,1)S(1)} %collective-permute-done.15.refs_1_, bf16[256,768]{1,0:T(8,128)(2,1)S(1)} %collective-permute-done.16.refs_1_.refs_2_, ...), custom_call_target="tpu_custom_call", output_to_operand_aliasing={{}: (4, {})} | custom-call | flops 1000 | bytes 1000 | tf_op jit(solution)/shard_map/pallas_call | solution.py:320
  90.9 3.4 %collective-permute-done.19.side = bf16[512,256]{1,0:T(8,128)(2,1)S(1)} collective-permute-done((bf16[512,256]{1,0:T(8,128)(2,1)S(1)}, bf16[512,256]{1,0:T(8,128)(2,1)S(1)}, u32[]{:S(2)}, u32[]{:S(2)}) %collective-permute-start.19) | collective-permute-done | bytes 262176 | tf_op jit(solution)/shard_map/ppermute | solution.py:367
  94.3 1.3 %shard_map.61 = bf16[4,512,1024]{2,1,0:T(8,128)(2,1)} custom-call(s32[3]{0:T(128)S(1)} %pad_add_fusion.place_ref.refs_0_, bf16[512,256]{1,0:T(8,128)(2,1)S(1)} %collective-permute-done.19.side, bf16[4,512,1024]{2,1,0:T(8,128)(2,1)} %shard_map.60.buffer_ref), custom_call_target="tpu_custom_call", output_to_operand_aliasing={{}: (2, {})} | custom-call | flops 1000 | bytes 1000 | tf_op jit(solution)/shard_map/pallas_call | solution.py:342
  (8 shorter events, 0.0 us)
Async XLA Ops:
  3.2 1.4 %collective-permute-start = (f32[8,1024]{1,0:T(8,128)S(1)}, f32[8,1024]{1,0:T(8,128)S(1)}, u32[]{:S(2)}, u32[]{:S(2)}) collective-permute-start(f32[8,1024]{1,0:T(8,128)S(1)} %get-tuple-element.35.sums_ref), channel_id=1, source_target_pairs={{0,1},{1,0},{2,3},{3,2},{4,5},{5,4},{6,7},{7,6},{8,9},{9,8},{10,11... | collective-permute-start | bytes 98312 | tf_op jit(solution)/shard_map/ppermute | solution.py:377
  6.3 4.4 %collective-permute-start.1 = (bf16[256,1024]{1,0:T(8,128)(2,1)S(1)}, bf16[256,1024]{1,0:T(8,128)(2,1)S(1)}, u32[]{:S(2)}, u32[]{:S(2)}) collective-permute-start(bf16[256,1024]{1,0:T(8,128)(2,1)S(1)} %get-tuple-element.37), channel_id=1, source_target_pairs={{0,1},{1,0},{2,3},{3,2},{4,5},{5,4},{6,7},{7,6},{8,9},{9,8},{10,11... | collective-permute-start | bytes 1572872 | tf_op jit(solution)/shard_map/ppermute | solution.py:377
  6.7 15.1 %collective-permute-start.6 = (bf16[1024,256]{1,0:T(8,128)(2,1)S(1)}, bf16[1024,256]{1,0:T(8,128)(2,1)S(1)}, u32[]{:S(2)}, u32[]{:S(2)}) collective-permute-start(bf16[1024,256]{1,0:T(8,128)(2,1)S(1)} %get-tuple-element.42.refs_2_.refs_3_.refs_9_), channel_id=1, source_target_pairs={{2,0},{6,4},{10,8},{14,12},{0,2},{4,6},{8,10},{12,14},{3,1},{7,5},... | collective-permute-start | bytes 1572872 | tf_op jit(solution)/shard_map/ppermute | solution.py:367
  9.4 17.0 %collective-permute-start.8 = (bf16[1024,512]{1,0:T(8,128)(2,1)S(1)}, bf16[1024,512]{1,0:T(8,128)(2,1)S(1)}, u32[]{:S(2)}, u32[]{:S(2)}) collective-permute-start(bf16[1024,512]{1,0:T(8,128)(2,1)S(1)} %get-tuple-element.43.refs_2_.refs_1_.refs_7_), channel_id=1, source_target_pairs={{0,1},{1,0},{2,3},{3,2},{4,5},{5,4},{6,7},{7,6},{8,9},{9,8},{10,11... | collective-permute-start | bytes 3145736 | tf_op jit(solution)/shard_map/ppermute | solution.py:377
  9.5 16.2 %collective-permute-start.5 = (bf16[1024,256]{1,0:T(8,128)(2,1)S(1)}, bf16[1024,256]{1,0:T(8,128)(2,1)S(1)}, u32[]{:S(2)}, u32[]{:S(2)}) collective-permute-start(bf16[1024,256]{1,0:T(8,128)(2,1)S(1)} %get-tuple-element.41.odd_ref.refs_2_), channel_id=1, source_target_pairs={{4,0},{6,2},{8,4},{10,6},{12,8},{14,10},{5,1},{7,3},{9,5},{11,7},{... | collective-permute-start | bytes 1572872 | tf_op jit(solution)/shard_map/ppermute | solution.py:367
  10.8 28.1 %collective-permute-start.2 = (bf16[512,1024]{1,0:T(8,128)(2,1)S(1)}, bf16[512,1024]{1,0:T(8,128)(2,1)S(1)}, u32[]{:S(2)}, u32[]{:S(2)}) collective-permute-start(bf16[512,1024]{1,0:T(8,128)(2,1)S(1)} %get-tuple-element.38.refs_0_), channel_id=1, source_target_pairs={{0,4},{2,6},{4,8},{6,10},{8,12},{10,14},{1,5},{3,7},{5,9},{7,11},{... | collective-permute-start | bytes 3145736 | tf_op jit(solution)/shard_map/ppermute | solution.py:367
  21.8 26.8 %collective-permute-start.11 = (bf16[1024,512]{1,0:T(8,128)(2,1)S(1)}, bf16[1024,512]{1,0:T(8,128)(2,1)S(1)}, u32[]{:S(2)}, u32[]{:S(2)}) collective-permute-start(bf16[1024,512]{1,0:T(8,128)(2,1)S(1)} %shard_map.48), channel_id=1, source_target_pairs={{2,0},{4,2},{6,4},{8,6},{10,8},{12,10},{14,12},{3,1},{5,3},{7,5},{... | collective-permute-start | bytes 3145736 | tf_op jit(solution)/shard_map/ppermute | solution.py:367
  23.1 2.5 %collective-permute-start.3 = (bf16[256,1024]{1,0:T(8,128)(2,1)S(1)}, bf16[256,1024]{1,0:T(8,128)(2,1)S(1)}, u32[]{:S(2)}, u32[]{:S(2)}) collective-permute-start(bf16[256,1024]{1,0:T(8,128)(2,1)S(1)} %get-tuple-element.40), channel_id=1, source_target_pairs={{0,1},{1,0},{2,3},{3,2},{4,5},{5,4},{6,7},{7,6},{8,9},{9,8},{10,11... | collective-permute-start | bytes 1572872 | tf_op jit(solution)/shard_map/ppermute | solution.py:377
  25.6 8.6 %collective-permute-start.9 = (bf16[1024,256]{1,0:T(8,128)(2,1)S(1)}, bf16[1024,256]{1,0:T(8,128)(2,1)S(1)}, u32[]{:S(2)}, u32[]{:S(2)}) collective-permute-start(bf16[1024,256]{1,0:T(8,128)(2,1)S(1)} %get-tuple-element.42.refs_2_.refs_3_.refs_9_), channel_id=1, source_target_pairs={{0,1},{1,0},{2,3},{3,2},{4,5},{5,4},{6,7},{7,6},{8,9},{9,8},{10,11... | collective-permute-start | bytes 1572872 | tf_op jit(solution)/shard_map/ppermute | solution.py:377
  25.6 23.7 %collective-permute-start.7 = (bf16[1024,256]{1,0:T(8,128)(2,1)S(1)}, bf16[1024,256]{1,0:T(8,128)(2,1)S(1)}, u32[]{:S(2)}, u32[]{:S(2)}) collective-permute-start(bf16[1024,256]{1,0:T(8,128)(2,1)S(1)} %shard_map.41.even_ref), channel_id=1, source_target_pairs={{6,2},{10,6},{14,10},{7,3},{11,7},{15,11},{22,18},{26,22},{30,26},... | collective-permute-start | bytes 1572872 | tf_op jit(solution)/shard_map/ppermute | solution.py:367
  26.4 34.2 %collective-permute-start.4 = (bf16[512,1024]{1,0:T(8,128)(2,1)S(1)}, bf16[512,1024]{1,0:T(8,128)(2,1)S(1)}, u32[]{:S(2)}, u32[]{:S(2)}) collective-permute-start(bf16[512,1024]{1,0:T(8,128)(2,1)S(1)} %shard_map.40.refs_1_), channel_id=1, source_target_pairs={{0,4},{2,6},{4,8},{6,10},{8,12},{10,14},{1,5},{3,7},{5,9},{7,11},{... | collective-permute-start | bytes 3145736 | tf_op jit(solution)/shard_map/ppermute | solution.py:367
  48.7 3.2 %collective-permute-start.12 = (bf16[1024,256]{1,0:T(8,128)(2,1)S(1)}, bf16[1024,256]{1,0:T(8,128)(2,1)S(1)}, u32[]{:S(2)}, u32[]{:S(2)}) collective-permute-start(bf16[1024,256]{1,0:T(8,128)(2,1)S(1)} %get-tuple-element.50.refs_1_.refs_2_), channel_id=1, source_target_pairs={{0,1},{1,0},{2,3},{3,2},{4,5},{5,4},{6,7},{7,6},{8,9},{9,8},{10,11... | collective-permute-start | bytes 1572872 | tf_op jit(solution)/shard_map/ppermute | solution.py:377
  48.8 5.5 %collective-permute-start.13 = (bf16[1024,256]{1,0:T(8,128)(2,1)S(1)}, bf16[1024,256]{1,0:T(8,128)(2,1)S(1)}, u32[]{:S(2)}, u32[]{:S(2)}) collective-permute-start(bf16[1024,256]{1,0:T(8,128)(2,1)S(1)} %get-tuple-element.51.refs_3_.refs_4_), channel_id=1, source_target_pairs={{0,1},{1,0},{2,3},{3,2},{4,5},{5,4},{6,7},{7,6},{8,9},{9,8},{10,11... | collective-permute-start | bytes 1572872 | tf_op jit(solution)/shard_map/ppermute | solution.py:377
  49.9 4.4 %collective-permute-start.14 = (bf16[1024,256]{1,0:T(8,128)(2,1)S(1)}, bf16[1024,256]{1,0:T(8,128)(2,1)S(1)}, u32[]{:S(2)}, u32[]{:S(2)}) collective-permute-start(bf16[1024,256]{1,0:T(8,128)(2,1)S(1)} %get-tuple-element.52.refs_5_.refs_2_), channel_id=1, source_target_pairs={{0,1},{1,0},{2,3},{3,2},{4,5},{5,4},{6,7},{7,6},{8,9},{9,8},{10,11... | collective-permute-start | bytes 1572872 | tf_op jit(solution)/shard_map/ppermute | solution.py:377
  50.0 13.8 %collective-permute-start.15 = (bf16[256,768]{1,0:T(8,128)(2,1)S(1)}, bf16[256,768]{1,0:T(8,128)(2,1)S(1)}, u32[]{:S(2)}, u32[]{:S(2)}) collective-permute-start(bf16[256,768]{1,0:T(8,128)(2,1)S(1)} %get-tuple-element.49.refs_0_), channel_id=1, source_target_pairs={{4,0},{6,2},{8,4},{10,6},{12,8},{14,10},{5,1},{7,3},{9,5},{11,7},{... | collective-permute-start | bytes 1179656 | tf_op jit(solution)/shard_map/ppermute | solution.py:367
  51.9 16.1 %collective-permute-start.10 = (bf16[1024,256]{1,0:T(8,128)(2,1)S(1)}, bf16[1024,256]{1,0:T(8,128)(2,1)S(1)}, u32[]{:S(2)}, u32[]{:S(2)}) collective-permute-start(bf16[1024,256]{1,0:T(8,128)(2,1)S(1)} %get-tuple-element.47), channel_id=1, source_target_pairs={{2,0},{6,4},{10,8},{14,12},{0,2},{4,6},{8,10},{12,14},{3,1},{7,5},... | collective-permute-start | bytes 1572872 | tf_op jit(solution)/shard_map/ppermute | solution.py:367
  55.8 16.4 %collective-permute-start.16 = (bf16[256,768]{1,0:T(8,128)(2,1)S(1)}, bf16[256,768]{1,0:T(8,128)(2,1)S(1)}, u32[]{:S(2)}, u32[]{:S(2)}) collective-permute-start(bf16[256,768]{1,0:T(8,128)(2,1)S(1)} %get-tuple-element.56), channel_id=1, source_target_pairs={{4,0},{6,2},{8,4},{10,6},{12,8},{14,10},{5,1},{7,3},{9,5},{11,7},{... | collective-permute-start | bytes 1179656 | tf_op jit(solution)/shard_map/ppermute | solution.py:367
  66.2 22.9 %collective-permute-start.20 = (bf16[256,1536]{1,0:T(8,128)(2,1)S(1)}, bf16[256,1536]{1,0:T(8,128)(2,1)S(1)}, u32[]{:S(2)}, u32[]{:S(2)}) collective-permute-start(bf16[256,1536]{1,0:T(8,128)(2,1)S(1)} %get-tuple-element.55.refs_0_), channel_id=1, source_target_pairs={{4,0},{6,2},{8,4},{10,6},{12,8},{14,10},{5,1},{7,3},{9,5},{11,7},{... | collective-permute-start | bytes 2359304 | tf_op jit(solution)/shard_map/ppermute | solution.py:367
  67.5 14.1 %collective-permute-start.22 = (bf16[1024,256]{1,0:T(8,128)(2,1)S(1)}, bf16[1024,256]{1,0:T(8,128)(2,1)S(1)}, u32[]{:S(2)}, u32[]{:S(2)}) collective-permute-start(bf16[1024,256]{1,0:T(8,128)(2,1)S(1)} %get-tuple-element.41.odd_ref.refs_2_), channel_id=1, source_target_pairs={{0,1},{1,0},{2,3},{3,2},{4,5},{5,4},{6,7},{7,6},{8,9},{9,8},{10,11... | collective-permute-start | bytes 1572872 | tf_op jit(solution)/shard_map/ppermute | solution.py:377
  67.5 18.0 %collective-permute-start.21 = (bf16[1024,256]{1,0:T(8,128)(2,1)S(1)}, bf16[1024,256]{1,0:T(8,128)(2,1)S(1)}, u32[]{:S(2)}, u32[]{:S(2)}) collective-permute-start(bf16[1024,256]{1,0:T(8,128)(2,1)S(1)} %get-tuple-element.61.refs_2_), channel_id=1, source_target_pairs={{0,1},{1,0},{2,3},{3,2},{4,5},{5,4},{6,7},{7,6},{8,9},{9,8},{10,11... | collective-permute-start | bytes 1572872 | tf_op jit(solution)/shard_map/ppermute | solution.py:377
  72.3 1.6 %collective-permute-start.17 = (bf16[1024,128]{1,0:T(8,128)(2,1)S(1)}, bf16[1024,128]{1,0:T(8,128)(2,1)S(1)}, u32[]{:S(2)}, u32[]{:S(2)}) collective-permute-start(bf16[1024,128]{1,0:T(8,128)(2,1)S(1)} %get-tuple-element.57.refs_2_), channel_id=1, source_target_pairs={{0,1},{1,0},{2,3},{3,2},{4,5},{5,4},{6,7},{7,6},{8,9},{9,8},{10,11... | collective-permute-start | bytes 786440 | tf_op jit(solution)/shard_map/ppermute | solution.py:377
  72.4 1.9 %collective-permute-start.18 = (bf16[1024,128]{1,0:T(8,128)(2,1)S(1)}, bf16[1024,128]{1,0:T(8,128)(2,1)S(1)}, u32[]{:S(2)}, u32[]{:S(2)}) collective-permute-start(bf16[1024,128]{1,0:T(8,128)(2,1)S(1)} %get-tuple-element.58.refs_4_), channel_id=1, source_target_pairs={{0,1},{1,0},{2,3},{3,2},{4,5},{5,4},{6,7},{7,6},{8,9},{9,8},{10,11... | collective-permute-start | bytes 786440 | tf_op jit(solution)/shard_map/ppermute | solution.py:377
  75.6 18.7 %collective-permute-start.19 = (bf16[512,256]{1,0:T(8,128)(2,1)S(1)}, bf16[512,256]{1,0:T(8,128)(2,1)S(1)}, u32[]{:S(2)}, u32[]{:S(2)}) collective-permute-start(bf16[512,256]{1,0:T(8,128)(2,1)S(1)} %get-tuple-element.60), channel_id=1, source_target_pairs={{4,0},{6,2},{8,4},{10,6},{12,8},{14,10},{5,1},{7,3},{9,5},{11,7},{... | collective-permute-start | bytes 786440 | tf_op jit(solution)/shard_map/ppermute | solution.py:367

commit v13 on v12

--- a/solution.py
+++ b/solution.py
@@ -8,10 +8,10 @@
 from jax.sharding import PartitionSpec as P
 
 WIN = 4
-PIECES = (4, 2, 2)
-ROWS = (1, 1)
+PIECES = (3, 3, 2)
+ROWS = (9, 7)
 PARTS = 2
-BLOCKS = 16
+BLOCKS = 8
 STATS_VMEM = 50
 epsilon = 1e-05
 
@@ -309,25 +309,25 @@
         copy.wait()
 
 
-def put(place, buffer, top2, top3, bottom):
-    operands = [place, top2, top3, bottom, buffer]
+def put(place, buffer, top2, top3, bottom, passed):
+    operands = [place, top2, top3, bottom, passed, buffer]
     shape = (buffer.shape[1], top2.shape[1])
 
     def kernel(*refs):
         n = len(operands)
-        put_kernel(*refs[: n - 1], *refs[n:])
+        put_kernel(*refs[: n - 2], *refs[n + 1 :])
 
     return pl.pallas_call(
         kernel,
-        in_specs=[SMEM] + [VMEM] * (len(operands) - 2) + [ANY],
-        out_specs=ANY,
-        out_shape=jax.ShapeDtypeStruct(buffer.shape, buffer.dtype),
+        in_specs=[SMEM] + [VMEM] * (len(operands) - 3) + [ANY] * 2,
+        out_specs=[ANY] * 2,
+        out_shape=[jax.ShapeDtypeStruct(x.shape, x.dtype) for x in (passed, buffer)],
         scratch_shapes=[
             pltpu.VMEM(shape, buffer.dtype),
             pltpu.VMEM(shape, buffer.dtype),
             pltpu.SemaphoreType.DMA((2, 2)),
         ],
-        input_output_aliases={len(operands) - 1: 0},
+        input_output_aliases={len(operands) - 2: 0, len(operands) - 1: 1},
         compiler_params=PARAMS,
         cost_estimate=COST,
     )(*operands)
@@ -404,7 +404,7 @@
     above, buffer, swapped = choose(place, relayed, above, (buffer,))
     next_relayed = send(swapped, swap)
     high = []
-    for piece in split(next_direct, (made,), 2):
+    for piece in split(next_direct, (made, next_detoured, swapped), 3):
         high += [piece, mate(piece)]
     high += [next_detoured, mate(next_detoured)]
     made, buffer = far(place, buffer, [below0], high, samples)
@@ -414,17 +414,19 @@
     made, buffer = far(place, buffer, [below1], high + own, samples)
     bottom = send(made, down)
     low = []
-    for piece in split(next_relayed, (made, top3), 2):
+    for piece in split(next_relayed, (made, top3), 3):
         low += [piece, mate(piece)]
     made, buffer = far(place, buffer, [below0, below1], low, samples)
     side = send(made, down)
     buffer = tile(place, buffer, 1, 0, rows, high[:-2], samples)
     buffer = tile(place, buffer, 1, 3, rows, high[-2:], samples)
-    buffer = tile(place, buffer, 0, 2, rows, [relayed, mate(relayed)], samples)
-    buffer = tile(place, buffer, 1, 2, rows, low, samples)
-    buffer = tile(place, buffer, 2, 2, rows, [above, mate(above)], samples)
-    buffer = put(place, buffer, top2, top3, bottom)
-    buffer = last(place, buffer, side, 2)
+    buffer = tile(place, buffer, 0, 1, rows, [relayed, mate(relayed)], samples)
+    buffer = tile(place, buffer, 1, 1, rows, low, samples)
+    pieces = list(split(above, (), 3))
+    pieces[2], buffer = put(place, buffer, top2, top3, bottom, pieces[2])
+    home = [array for piece in pieces for array in (piece, mate(piece))]
+    buffer = tile(place, buffer, 2, 1, rows, home, samples)
+    buffer = last(place, buffer, side, 1)
     return buffer[None]
 
 

time: 95.8 us -> 94.5 us (0.986)
  waiting for transfers between devices: 37.2 us -> 31.5 us
  Pallas kernels: 31 us -> 33.5 us
  starting transfers between devices: 26.4 us -> 27.9 us
    ppermute x11, waiting for transfers between devices: 35.6 us -> 28.2 us  [send(): return lax.ppermute(shard, 'var', pairs)]
    ppermute x12 -> x16, waiting for transfers between devices: 1.55 us -> 3.32 us  [mate(): return lax.ppermute(shard, 'samp', [(0, 1), (1, 0)])]
    pallas_call x7, Pallas kernels: 14.9 us -> 16.7 us  [tile(): pl.pallas_call(functools.partial(tile_kernel, k, len(rows), len(rights),...]
    ppermute x12 -> x16, starting transfers between devices: 2.92 us -> 4.02 us  [mate(): return lax.ppermute(shard, 'samp', [(0, 1), (1, 0)])]
  transfers between devices with their start and end apart: 23 -> 27, of which waited for: 12 -> 13; matrix products, arithmetic and copies ran while one was open for 0% -> 0% of each run, Pallas kernels for 26% -> 29%
where the time goes in v13:
time: 94.5 us; the launch traced here: 93.9 us
  Pallas kernels  33.5 us (35%)
  waiting for transfers between devices  31.5 us (33%)
  starting transfers between devices  27.9 us (30%)
    ppermute x11, waiting for transfers between devices, send(): return lax.ppermute(shard, 'var', pairs)  28.2 us
    ppermute x11, starting transfers between devices, send(): return lax.ppermute(shard, 'var', pairs)  23.9 us
    pallas_call x7, Pallas kernels, tile(): pl.pallas_call(functools.partial(tile_kernel, k, len(rows), len(rights),...  16.7 us
    pallas_call x4, Pallas kernels, far(): pl.pallas_call(functools.partial(far_kernel, 1.0 / samples, len(rows), le...  7.18 us
    ppermute x16, starting transfers between devices, mate(): return lax.ppermute(shard, 'samp', [(0, 1), (1, 0)])  4.02 us
    ppermute x16, waiting for transfers between devices, mate(): return lax.ppermute(shard, 'samp', [(0, 1), (1, 0)])  3.32 us
    pallas_call x1, Pallas kernels, stats(): pl.pallas_call(stats_kernel, in_specs=[pl.BlockSpec(memory_space=pltpu.HB...  3.08 us
  transfers between devices with their start and end apart: 27, of which 13 were waited for; matrix products, arithmetic and copies ran while one was open for 0% of the time, Pallas kernels for 29%

profile of v13, /device:TPU:0, one launch (start us, length us, event | category | flops | bytes accessed | tf_op | source)
XLA Modules:
  0.0 93.9 jit_solution(16147740030434566454)
XLA Ops:
  0.0 3.1 %shard_map.37 = (f32[8,1024]{1,0:T(8,128)S(1)}, bf16[1024,1024]{1,0:T(8,128)(2,1)S(1)}) custom-call(bf16[1024,1024]{1,0:T(8,128)(2,1)} %dosage_hbm.1, s32[1024,1024]{1,0:T(8,128)} %observed_hbm.1), custom_call_target="tpu_custom_call" | custom-call | flops 1000 | bytes 1000 | tf_op jit(solution)/shard_map/pallas_call | solution.py:60
  3.1 0.5 collective-permute-start
  4.3 0.1 pad_add_fusion.place_ref.refs_0_
  4.3 0.1 collective-permute-done.sums_other_ref
  4.5 1.8 %shard_map.38 = (bf16[1024,384]{1,0:T(8,128)(2,1)S(1)}, bf16[1024,384]{1,0:T(8,128)(2,1)S(1)}, bf16[1024,256]{1,0:T(8,128)(2,1)S(1)}, bf16[1024,384]{1,0:T(8,128...) custom-call(s32[3]{0:T(128)S(1)} %pad_add_fusion.place_ref.refs_0_, ...), custom_call_target="tpu_custom_call" | custom-call | flops 1000 | bytes 1000 | tf_op jit(solution)/shard_map/pallas_call | solution.py:118
  6.2 0.4 collective-permute-start.1
  6.7 1.3 %collective-permute-start.5 = (bf16[1024,384]{1,0:T(8,128)(2,1)S(1)}, bf16[1024,384]{1,0:T(8,128)(2,1)S(1)}, u32[]{:S(2)}, u32[]{:S(2)}) collective-permute-start(bf16[1024,384]{1,0:T(8,128)(2,1)S(1)} %get-tuple-element.48.odd_ref.refs_2_), channel_id=1, source_target_pairs={{4,0},{6,2},{8,4},{10,6},{12,8},{14,10},{5,1},{7,3},{9,5},{11,7},{... | collective-permute-start | bytes 2359304 | tf_op jit(solution)/shard_map/ppermute | solution.py:367
  7.9 2.7 %collective-permute-start.6 = (bf16[1024,256]{1,0:T(8,128)(2,1)S(1)}, bf16[1024,256]{1,0:T(8,128)(2,1)S(1)}, u32[]{:S(2)}, u32[]{:S(2)}) collective-permute-start(bf16[1024,256]{1,0:T(8,128)(2,1)S(1)} %get-tuple-element.49.refs_2_.refs_3_.refs_11_), channel_id=1, source_target_pairs={{2,0},{6,4},{10,8},{14,12},{0,2},{4,6},{8,10},{12,14},{3,1},{7,5},... | collective-permute-start | bytes 1572872 | tf_op jit(solution)/shard_map/ppermute | solution.py:367
  10.7 0.0 collective-permute-done.1.arrived_ref
  10.7 0.1 shard_map.39
  10.8 4.6 %collective-permute-start.2 = (bf16[576,1024]{1,0:T(8,128)(2,1)S(1)}, bf16[576,1024]{1,0:T(8,128)(2,1)S(1)}, u32[]{:S(2)}, u32[]{:S(2)}) collective-permute-start(bf16[576,1024]{1,0:T(8,128)(2,1)S(1)} %get-tuple-element.45.refs_0_), channel_id=1, source_target_pairs={{0,4},{2,6},{4,8},{6,10},{8,12},{10,14},{1,5},{3,7},{5,9},{7,11},{... | collective-permute-start | bytes 3538952 | tf_op jit(solution)/shard_map/ppermute | solution.py:367
  15.4 0.1 collective-permute-start.3
  15.5 0.5 collective-permute-start.8
  16.0 7.1 %collective-permute-done.6.refs_1_.refs_0_ = bf16[1024,256]{1,0:T(8,128)(2,1)S(1)} collective-permute-done((bf16[1024,256]{1,0:T(8,128)(2,1)S(1)}, bf16[1024,256]{1,0:T(8,128)(2,1)S(1)}, u32[]{:S(2)}, u32[]{:S(2)}) %collective-permute-start.6) | collective-permute-done | bytes 524320 | tf_op jit(solution)/shard_map/ppermute | solution.py:367
  23.1 1.3 %collective-permute-start.11 = (bf16[1024,384]{1,0:T(8,128)(2,1)S(1)}, bf16[1024,384]{1,0:T(8,128)(2,1)S(1)}, u32[]{:S(2)}, u32[]{:S(2)}) collective-permute-start(bf16[1024,384]{1,0:T(8,128)(2,1)S(1)} %shard_map.48), channel_id=1, source_target_pairs={{2,0},{4,2},{6,4},{8,6},{10,8},{12,10},{14,12},{3,1},{5,3},{7,5},{... | collective-permute-start | bytes 2359304 | tf_op jit(solution)/shard_map/ppermute | solution.py:367
  24.4 5.2 %collective-permute-done.5.refs_0_.even_ref = bf16[1024,384]{1,0:T(8,128)(2,1)S(1)} collective-permute-done((bf16[1024,384]{1,0:T(8,128)(2,1)S(1)}, bf16[1024,384]{1,0:T(8,128)(2,1)S(1)}, u32[]{:S(2)}, u32[]{:S(2)}) %collective-permute-start.5) | collective-permute-done | bytes 786464 | tf_op jit(solution)/shard_map/ppermute | solution.py:367
  29.6 0.0 collective-permute-done.3.arrived_ref
  29.6 0.7 collective-permute-start.7
  30.3 0.1 shard_map.40.refs_1_
  30.4 4.0 %collective-permute-start.4 = (bf16[448,1024]{1,0:T(8,128)(2,1)S(1)}, bf16[448,1024]{1,0:T(8,128)(2,1)S(1)}, u32[]{:S(2)}, u32[]{:S(2)}) collective-permute-start(bf16[448,1024]{1,0:T(8,128)(2,1)S(1)} %shard_map.40.refs_1_), channel_id=1, source_target_pairs={{0,4},{2,6},{4,8},{6,10},{8,12},{10,14},{1,5},{3,7},{5,9},{7,11},{... | collective-permute-start | bytes 2752520 | tf_op jit(solution)/shard_map/ppermute | solution.py:367
  34.4 2.5 %shard_map.42.refs_4_ = bf16[4,512,1024]{2,1,0:T(8,128)(2,1)} custom-call(s32[3]{0:T(128)S(1)} %pad_add_fusion.place_ref.refs_0_, bf16[576,1024]{1,0:T(8,128)(2,1)S(1)} %get-tuple-element.45.refs_0_, bf16[448,1024]{1,0:T(8,128)(2,1)S(1)} %shard_map.40.refs_1_, ...), custom_call_target="tpu_custom_call", output_to_operand_aliasing={{}: (5, {})} | custom-call | flops 1000 | bytes 1000 | tf_op jit(solution)/shard_map/pallas_call | solution.py:192
  36.9 2.0 %shard_map.43.refs_1_ = bf16[4,512,1024]{2,1,0:T(8,128)(2,1)} custom-call(s32[3]{0:T(128)S(1)} %pad_add_fusion.place_ref.refs_0_, bf16[576,1024]{1,0:T(8,128)(2,1)S(1)} %get-tuple-element.45.refs_0_, bf16[448,1024]{1,0:T(8,128)(2,1)S(1)} %shard_map.40.refs_1_, ...), custom_call_target="tpu_custom_call", output_to_operand_aliasing={{}: (5, {})} | custom-call | flops 1000 | bytes 1000 | tf_op jit(solution)/shard_map/pallas_call | solution.py:192
  38.9 2.8 %collective-permute-done.2.refs_0_ = bf16[576,1024]{1,0:T(8,128)(2,1)S(1)} collective-permute-done((bf16[576,1024]{1,0:T(8,128)(2,1)S(1)}, bf16[576,1024]{1,0:T(8,128)(2,1)S(1)}, u32[]{:S(2)}, u32[]{:S(2)}) %collective-permute-start.2) | collective-permute-done | bytes 1179680 | tf_op jit(solution)/shard_map/ppermute | solution.py:367
  41.7 1.6 %shard_map.45 = (bf16[288,640]{1,0:T(8,128)(2,1)S(1)}, bf16[4,512,1024]{2,1,0:T(8,128)(2,1)}) custom-call(s32[3]{0:T(128)S(1)} %pad_add_fusion.place_ref.refs_0_, bf16[576,1024]{1,0:T(8,128)(2,1)S(1)} %collective-permute-done.2.refs_0_, bf16[1024,384]{1,0:T(8,128)(2,1)S(1)} %get-tuple-element.50.refs_2_.refs_1_.refs_9_, ...), custom_call_target="tpu_custom_call", output_to_operand_aliasing={{1}: (6, {})} | custom-call | flops 1000 | bytes 1000 | tf_op jit(solution)/shard_map/pallas_call | solution.py:213
  43.3 0.6 shard_map.46
  43.9 0.6 shard_map.47
  44.6 0.1 shard_map.49
  44.7 0.1 collective-permute-start.12
  44.8 0.5 collective-permute-start.15
  45.3 0.1 collective-permute-start.13
  45.4 3.9 %collective-permute-start.10 = (bf16[1024,384]{1,0:T(8,128)(2,1)S(1)}, bf16[1024,384]{1,0:T(8,128)(2,1)S(1)}, u32[]{:S(2)}, u32[]{:S(2)}) collective-permute-start(bf16[1024,384]{1,0:T(8,128)(2,1)S(1)} %get-tuple-element.54.refs_2_), channel_id=1, source_target_pairs={{2,0},{6,4},{10,8},{14,12},{0,2},{4,6},{8,10},{12,14},{3,1},{7,5},... | collective-permute-start | bytes 2359304 | tf_op jit(solution)/shard_map/ppermute | solution.py:367
  49.3 0.2 collective-permute-start.14
  49.4 1.3 %collective-permute-start.16 = (bf16[288,640]{1,0:T(8,128)(2,1)S(1)}, bf16[288,640]{1,0:T(8,128)(2,1)S(1)}, u32[]{:S(2)}, u32[]{:S(2)}) collective-permute-start(bf16[288,640]{1,0:T(8,128)(2,1)S(1)} %get-tuple-element.56.refs_0_), channel_id=1, source_target_pairs={{4,0},{6,2},{8,4},{10,6},{12,8},{14,10},{5,1},{7,3},{9,5},{11,7},{... | collective-permute-start | bytes 1105928 | tf_op jit(solution)/shard_map/ppermute | solution.py:367
  50.7 0.1 collective-permute-done.14.refs_6_.refs_7_
  50.8 0.3 collective-permute-start.25
  51.2 1.6 %shard_map.50 = (bf16[288,640]{1,0:T(8,128)(2,1)S(1)}, bf16[4,512,1024]{2,1,0:T(8,128)(2,1)}) custom-call(s32[3]{0:T(128)S(1)} %pad_add_fusion.place_ref.refs_0_, bf16[576,1024]{1,0:T(8,128)(2,1)S(1)} %collective-permute-done.2.refs_0_, bf16[1024,128]{1,0:T(8,128)(2,1)S(1)} %get-tuple-element.58.refs_1_.refs_2_, ...), custom_call_target="tpu_custom_call", output_to_operand_aliasing={{1}: (10, {})} | custom-call | flops 1000 | bytes 1000 | tf_op jit(solution)/shard_map/pallas_call | solution.py:213
  52.8 1.3 %collective-permute-start.17 = (bf16[288,640]{1,0:T(8,128)(2,1)S(1)}, bf16[288,640]{1,0:T(8,128)(2,1)S(1)}, u32[]{:S(2)}, u32[]{:S(2)}) collective-permute-start(bf16[288,640]{1,0:T(8,128)(2,1)S(1)} %get-tuple-element.64), channel_id=1, source_target_pairs={{4,0},{6,2},{8,4},{10,6},{12,8},{14,10},{5,1},{7,3},{9,5},{11,7},{... | collective-permute-start | bytes 1105928 | tf_op jit(solution)/shard_map/ppermute | solution.py:367
  54.1 6.1 %collective-permute-done.4.refs_0_.refs_1_ = bf16[448,1024]{1,0:T(8,128)(2,1)S(1)} collective-permute-done((bf16[448,1024]{1,0:T(8,128)(2,1)S(1)}, bf16[448,1024]{1,0:T(8,128)(2,1)S(1)}, u32[]{:S(2)}, u32[]{:S(2)}) %collective-permute-start.4) | collective-permute-done | bytes 917536 | tf_op jit(solution)/shard_map/ppermute | solution.py:367
  60.1 2.6 %collective-permute-done.16.refs_1_ = bf16[288,640]{1,0:T(8,128)(2,1)S(1)} collective-permute-done((bf16[288,640]{1,0:T(8,128)(2,1)S(1)}, bf16[288,640]{1,0:T(8,128)(2,1)S(1)}, u32[]{:S(2)}, u32[]{:S(2)}) %collective-permute-start.16) | collective-permute-done | bytes 368672 | tf_op jit(solution)/shard_map/ppermute | solution.py:367
  62.7 2.1 %shard_map.52 = (bf16[224,1280]{1,0:T(8,128)(2,1)S(1)}, bf16[4,512,1024]{2,1,0:T(8,128)(2,1)}) custom-call(s32[3]{0:T(128)S(1)} %pad_add_fusion.place_ref.refs_0_, bf16[448,1024]{1,0:T(8,128)(2,1)S(1)} %collective-permute-done.4.refs_0_.refs_1_, bf16[1024,128]{1,0:T(8,128)(2,1)S(1)} %get-tuple-element.58.refs_1_.refs_2_, ...), custom_call_target="tpu_custom_call", output_to_operand_aliasing={{1}: (14, {})} | custom-call | flops 1000 | bytes 1000 | tf_op jit(solution)/shard_map/pallas_call | solution.py:213
  64.9 1.3 %collective-permute-start.24 = (bf16[224,1280]{1,0:T(8,128)(2,1)S(1)}, bf16[224,1280]{1,0:T(8,128)(2,1)S(1)}, u32[]{:S(2)}, u32[]{:S(2)}) collective-permute-start(bf16[224,1280]{1,0:T(8,128)(2,1)S(1)} %get-tuple-element.63.refs_0_), channel_id=1, source_target_pairs={{4,0},{6,2},{8,4},{10,6},{12,8},{14,10},{5,1},{7,3},{9,5},{11,7},{... | collective-permute-start | bytes 1720328 | tf_op jit(solution)/shard_map/ppermute | solution.py:367
  66.2 1.2 %collective-permute-done.10.whole_ref = bf16[1024,384]{1,0:T(8,128)(2,1)S(1)} collective-permute-done((bf16[1024,384]{1,0:T(8,128)(2,1)S(1)}, bf16[1024,384]{1,0:T(8,128)(2,1)S(1)}, u32[]{:S(2)}, u32[]{:S(2)}) %collective-permute-start.10) | collective-permute-done | bytes 786464 | tf_op jit(solution)/shard_map/ppermute | solution.py:367
  67.4 3.2 %collective-permute-done.17.refs_1_.refs_2_ = bf16[288,640]{1,0:T(8,128)(2,1)S(1)} collective-permute-done((bf16[288,640]{1,0:T(8,128)(2,1)S(1)}, bf16[288,640]{1,0:T(8,128)(2,1)S(1)}, u32[]{:S(2)}, u32[]{:S(2)}) %collective-permute-start.17) | collective-permute-done | bytes 368672 | tf_op jit(solution)/shard_map/ppermute | solution.py:367
  70.6 0.1 shard_map.53
  70.8 0.1 collective-permute-start.18
  70.8 0.5 collective-permute-start.19
  71.3 0.1 collective-permute-start.20
  71.4 0.9 %collective-permute-done.18.refs_3_ = bf16[1024,128]{1,0:T(8,128)(2,1)S(1)} collective-permute-done((bf16[1024,128]{1,0:T(8,128)(2,1)S(1)}, bf16[1024,128]{1,0:T(8,128)(2,1)S(1)}, u32[]{:S(2)}, u32[]{:S(2)}) %collective-permute-start.18) | collective-permute-done | bytes 262176 | tf_op jit(solution)/shard_map/ppermute | solution.py:377
  72.4 0.4 collective-permute-done.19.refs_5_
  72.7 0.4 collective-permute-done.20.refs_7_
  73.1 1.8 %shard_map.54 = (bf16[512,384]{1,0:T(8,128)(2,1)S(1)}, bf16[4,512,1024]{2,1,0:T(8,128)(2,1)}) custom-call(s32[3]{0:T(128)S(1)} %pad_add_fusion.place_ref.refs_0_, bf16[576,1024]{1,0:T(8,128)(2,1)S(1)} %collective-permute-done.2.refs_0_, bf16[448,1024]{1,0:T(8,128)(2,1)S(1)} %collective-permute-done.4.refs_0_.refs_1_, ...), custom_call_target="tpu_custom_call", output_to_operand_aliasing={{1}: (9, {})} | custom-call | flops 1000 | bytes 1000 | tf_op jit(solution)/shard_map/pallas_call | solution.py:213
  74.9 1.5 %collective-permute-start.21 = (bf16[512,384]{1,0:T(8,128)(2,1)S(1)}, bf16[512,384]{1,0:T(8,128)(2,1)S(1)}, u32[]{:S(2)}, u32[]{:S(2)}) collective-permute-start(bf16[512,384]{1,0:T(8,128)(2,1)S(1)} %get-tuple-element.69), channel_id=1, source_target_pairs={{4,0},{6,2},{8,4},{10,6},{12,8},{14,10},{5,1},{7,3},{9,5},{11,7},{... | collective-permute-start | bytes 1179656 | tf_op jit(solution)/shard_map/ppermute | solution.py:367
  76.4 0.1 shard_map.55
  76.6 2.6 %shard_map.56.refs_4_ = bf16[4,512,1024]{2,1,0:T(8,128)(2,1)} custom-call(s32[3]{0:T(128)S(1)} %pad_add_fusion.place_ref.refs_0_, bf16[576,1024]{1,0:T(8,128)(2,1)S(1)} %get-tuple-element.45.refs_0_, bf16[448,1024]{1,0:T(8,128)(2,1)S(1)} %shard_map.40.refs_1_, ...), custom_call_target="tpu_custom_call", output_to_operand_aliasing={{}: (9, {})} | custom-call | flops 1000 | bytes 1000 | tf_op jit(solution)/shard_map/pallas_call | solution.py:192
  79.1 0.1 collective-permute-start.22
  79.3 2.0 %shard_map.57.refs_4_ = bf16[4,512,1024]{2,1,0:T(8,128)(2,1)} custom-call(s32[3]{0:T(128)S(1)} %pad_add_fusion.place_ref.refs_0_, bf16[576,1024]{1,0:T(8,128)(2,1)S(1)} %get-tuple-element.45.refs_0_, bf16[448,1024]{1,0:T(8,128)(2,1)S(1)} %shard_map.40.refs_1_, ...), custom_call_target="tpu_custom_call", output_to_operand_aliasing={{}: (5, {})} | custom-call | flops 1000 | bytes 1000 | tf_op jit(solution)/shard_map/pallas_call | solution.py:192
  81.2 2.6 %shard_map.58.refs_8_ = bf16[4,512,1024]{2,1,0:T(8,128)(2,1)} custom-call(s32[3]{0:T(128)S(1)} %pad_add_fusion.place_ref.refs_0_, bf16[576,1024]{1,0:T(8,128)(2,1)S(1)} %get-tuple-element.45.refs_0_, bf16[448,1024]{1,0:T(8,128)(2,1)S(1)} %shard_map.40.refs_1_, ...), custom_call_target="tpu_custom_call", output_to_operand_aliasing={{}: (5, {})} | custom-call | flops 1000 | bytes 1000 | tf_op jit(solution)/shard_map/pallas_call | solution.py:192
  83.8 0.4 collective-permute-start.23
  84.1 2.6 %shard_map.59.refs_5_ = bf16[4,512,1024]{2,1,0:T(8,128)(2,1)} custom-call(s32[3]{0:T(128)S(1)} %pad_add_fusion.place_ref.refs_0_, bf16[576,1024]{1,0:T(8,128)(2,1)S(1)} %get-tuple-element.45.refs_0_, bf16[448,1024]{1,0:T(8,128)(2,1)S(1)} %shard_map.40.refs_1_, bf16[1024,128]{1,0:T(8,128)(2,1)S(1)} %get-tuple-element.65.refs_2_, ...), custom_call_target="tpu_custom_call", output_to_operand_aliasing={{}: (9, {})} | custom-call | flops 1000 | bytes 1000 | tf_op jit(solution)/shard_map/pallas_call | solution.py:192
  86.7 1.7 %shard_map.60 = (bf16[1024,128]{1,0:T(8,128)(2,1)S(1)}, bf16[4,512,1024]{2,1,0:T(8,128)(2,1)}) custom-call(s32[3]{0:T(128)S(1)} %pad_add_fusion.place_ref.refs_0_, bf16[288,640]{1,0:T(8,128)(2,1)S(1)} %collective-permute-done.16.refs_1_, bf16[288,640]{1,0:T(8,128)(2,1)S(1)} %collective-permute-done.17.refs_1_.refs_2_, ...), custom_call_target="tpu_custom_call", output_to_operand_aliasing={{0}: (4, {}), {1}: (5, {})} | custom-call | flops 1000 | bytes 1000 | tf_op jit(solution)/shard_map/pallas_call | solution.py:320
  88.4 0.2 collective-permute-start.26
  88.6 1.4 %collective-permute-done.26.refs_7_ = bf16[1024,128]{1,0:T(8,128)(2,1)S(1)} collective-permute-done((bf16[1024,128]{1,0:T(8,128)(2,1)S(1)}, bf16[1024,128]{1,0:T(8,128)(2,1)S(1)}, u32[]{:S(2)}, u32[]{:S(2)}) %collective-permute-start.26) | collective-permute-done | bytes 262176 | tf_op jit(solution)/shard_map/ppermute | solution.py:377
  90.0 2.6 %shard_map.61.buffer_ref = bf16[4,512,1024]{2,1,0:T(8,128)(2,1)} custom-call(s32[3]{0:T(128)S(1)} %pad_add_fusion.place_ref.refs_0_, bf16[576,1024]{1,0:T(8,128)(2,1)S(1)} %get-tuple-element.45.refs_0_, bf16[448,1024]{1,0:T(8,128)(2,1)S(1)} %shard_map.40.refs_1_, bf16[1024,128]{1,0:T(8,128)(2,1)S(1)} %get-tuple-element.71.refs_2_, ...), custom_call_target="tpu_custom_call", output_to_operand_aliasing={{}: (9, {})} | custom-call | flops 1000 | bytes 1000 | tf_op jit(solution)/shard_map/pallas_call | solution.py:192
  92.6 1.3 %shard_map.62 = bf16[4,512,1024]{2,1,0:T(8,128)(2,1)} custom-call(s32[3]{0:T(128)S(1)} %pad_add_fusion.place_ref.refs_0_, bf16[512,384]{1,0:T(8,128)(2,1)S(1)} %collective-permute-done.21.side, bf16[4,512,1024]{2,1,0:T(8,128)(2,1)} %shard_map.61.buffer_ref), custom_call_target="tpu_custom_call", output_to_operand_aliasing={{}: (2, {})} | custom-call | flops 1000 | bytes 1000 | tf_op jit(solution)/shard_map/pallas_call | solution.py:342
  (17 shorter events, 0.0 us)
Async XLA Ops:
  3.1 1.4 %collective-permute-start = (f32[8,1024]{1,0:T(8,128)S(1)}, f32[8,1024]{1,0:T(8,128)S(1)}, u32[]{:S(2)}, u32[]{:S(2)}) collective-permute-start(f32[8,1024]{1,0:T(8,128)S(1)} %get-tuple-element.42.sums_ref), channel_id=1, source_target_pairs={{0,1},{1,0},{2,3},{3,2},{4,5},{5,4},{6,7},{7,6},{8,9},{9,8},{10,11... | collective-permute-start | bytes 98312 | tf_op jit(solution)/shard_map/ppermute | solution.py:377
  6.2 4.5 %collective-permute-start.1 = (bf16[288,1024]{1,0:T(8,128)(2,1)S(1)}, bf16[288,1024]{1,0:T(8,128)(2,1)S(1)}, u32[]{:S(2)}, u32[]{:S(2)}) collective-permute-start(bf16[288,1024]{1,0:T(8,128)(2,1)S(1)} %get-tuple-element.44), channel_id=1, source_target_pairs={{0,1},{1,0},{2,3},{3,2},{4,5},{5,4},{6,7},{7,6},{8,9},{9,8},{10,11... | collective-permute-start | bytes 1769480 | tf_op jit(solution)/shard_map/ppermute | solution.py:377
  6.7 22.9 %collective-permute-start.5 = (bf16[1024,384]{1,0:T(8,128)(2,1)S(1)}, bf16[1024,384]{1,0:T(8,128)(2,1)S(1)}, u32[]{:S(2)}, u32[]{:S(2)}) collective-permute-start(bf16[1024,384]{1,0:T(8,128)(2,1)S(1)} %get-tuple-element.48.odd_ref.refs_2_), channel_id=1, source_target_pairs={{4,0},{6,2},{8,4},{10,6},{12,8},{14,10},{5,1},{7,3},{9,5},{11,7},{... | collective-permute-start | bytes 2359304 | tf_op jit(solution)/shard_map/ppermute | solution.py:367
  7.9 15.2 %collective-permute-start.6 = (bf16[1024,256]{1,0:T(8,128)(2,1)S(1)}, bf16[1024,256]{1,0:T(8,128)(2,1)S(1)}, u32[]{:S(2)}, u32[]{:S(2)}) collective-permute-start(bf16[1024,256]{1,0:T(8,128)(2,1)S(1)} %get-tuple-element.49.refs_2_.refs_3_.refs_11_), channel_id=1, source_target_pairs={{2,0},{6,4},{10,8},{14,12},{0,2},{4,6},{8,10},{12,14},{3,1},{7,5},... | collective-permute-start | bytes 1572872 | tf_op jit(solution)/shard_map/ppermute | solution.py:367
  10.8 30.9 %collective-permute-start.2 = (bf16[576,1024]{1,0:T(8,128)(2,1)S(1)}, bf16[576,1024]{1,0:T(8,128)(2,1)S(1)}, u32[]{:S(2)}, u32[]{:S(2)}) collective-permute-start(bf16[576,1024]{1,0:T(8,128)(2,1)S(1)} %get-tuple-element.45.refs_0_), channel_id=1, source_target_pairs={{0,4},{2,6},{4,8},{6,10},{8,12},{10,14},{1,5},{3,7},{5,9},{7,11},{... | collective-permute-start | bytes 3538952 | tf_op jit(solution)/shard_map/ppermute | solution.py:367
  15.4 14.2 %collective-permute-start.3 = (bf16[224,1024]{1,0:T(8,128)(2,1)S(1)}, bf16[224,1024]{1,0:T(8,128)(2,1)S(1)}, u32[]{:S(2)}, u32[]{:S(2)}) collective-permute-start(bf16[224,1024]{1,0:T(8,128)(2,1)S(1)} %get-tuple-element.47), channel_id=1, source_target_pairs={{0,1},{1,0},{2,3},{3,2},{4,5},{5,4},{6,7},{7,6},{8,9},{9,8},{10,11... | collective-permute-start | bytes 1376264 | tf_op jit(solution)/shard_map/ppermute | solution.py:377
  15.5 14.9 %collective-permute-start.8 = (bf16[1024,384]{1,0:T(8,128)(2,1)S(1)}, bf16[1024,384]{1,0:T(8,128)(2,1)S(1)}, u32[]{:S(2)}, u32[]{:S(2)}) collective-permute-start(bf16[1024,384]{1,0:T(8,128)(2,1)S(1)} %get-tuple-element.50.refs_2_.refs_1_.refs_9_), channel_id=1, source_target_pairs={{0,1},{1,0},{2,3},{3,2},{4,5},{5,4},{6,7},{7,6},{8,9},{9,8},{10,11... | collective-permute-start | bytes 2359304 | tf_op jit(solution)/shard_map/ppermute | solution.py:377
  23.1 21.4 %collective-permute-start.11 = (bf16[1024,384]{1,0:T(8,128)(2,1)S(1)}, bf16[1024,384]{1,0:T(8,128)(2,1)S(1)}, u32[]{:S(2)}, u32[]{:S(2)}) collective-permute-start(bf16[1024,384]{1,0:T(8,128)(2,1)S(1)} %shard_map.48), channel_id=1, source_target_pairs={{2,0},{4,2},{6,4},{8,6},{10,8},{12,10},{14,12},{3,1},{5,3},{7,5},{... | collective-permute-start | bytes 2359304 | tf_op jit(solution)/shard_map/ppermute | solution.py:367
  29.6 7.4 %collective-permute-start.9 = (bf16[1024,256]{1,0:T(8,128)(2,1)S(1)}, bf16[1024,256]{1,0:T(8,128)(2,1)S(1)}, u32[]{:S(2)}, u32[]{:S(2)}) collective-permute-start(bf16[1024,256]{1,0:T(8,128)(2,1)S(1)} %get-tuple-element.49.refs_2_.refs_3_.refs_11_), channel_id=1, source_target_pairs={{0,1},{1,0},{2,3},{3,2},{4,5},{5,4},{6,7},{7,6},{8,9},{9,8},{10,11... | collective-permute-start | bytes 1572872 | tf_op jit(solution)/shard_map/ppermute | solution.py:377
  29.6 13.7 %collective-permute-start.7 = (bf16[1024,256]{1,0:T(8,128)(2,1)S(1)}, bf16[1024,256]{1,0:T(8,128)(2,1)S(1)}, u32[]{:S(2)}, u32[]{:S(2)}) collective-permute-start(bf16[1024,256]{1,0:T(8,128)(2,1)S(1)} %shard_map.41.even_ref), channel_id=1, source_target_pairs={{6,2},{10,6},{14,10},{7,3},{11,7},{15,11},{22,18},{26,22},{30,26},... | collective-permute-start | bytes 1572872 | tf_op jit(solution)/shard_map/ppermute | solution.py:367
  30.4 29.8 %collective-permute-start.4 = (bf16[448,1024]{1,0:T(8,128)(2,1)S(1)}, bf16[448,1024]{1,0:T(8,128)(2,1)S(1)}, u32[]{:S(2)}, u32[]{:S(2)}) collective-permute-start(bf16[448,1024]{1,0:T(8,128)(2,1)S(1)} %shard_map.40.refs_1_), channel_id=1, source_target_pairs={{0,4},{2,6},{4,8},{6,10},{8,12},{10,14},{1,5},{3,7},{5,9},{7,11},{... | collective-permute-start | bytes 2752520 | tf_op jit(solution)/shard_map/ppermute | solution.py:367
  44.7 4.6 %collective-permute-start.12 = (bf16[1024,128]{1,0:T(8,128)(2,1)S(1)}, bf16[1024,128]{1,0:T(8,128)(2,1)S(1)}, u32[]{:S(2)}, u32[]{:S(2)}) collective-permute-start(bf16[1024,128]{1,0:T(8,128)(2,1)S(1)} %get-tuple-element.58.refs_1_.refs_2_), channel_id=1, source_target_pairs={{0,1},{1,0},{2,3},{3,2},{4,5},{5,4},{6,7},{7,6},{8,9},{9,8},{10,11... | collective-permute-start | bytes 786440 | tf_op jit(solution)/shard_map/ppermute | solution.py:377
  44.8 6.4 %collective-permute-start.15 = (bf16[1024,256]{1,0:T(8,128)(2,1)S(1)}, bf16[1024,256]{1,0:T(8,128)(2,1)S(1)}, u32[]{:S(2)}, u32[]{:S(2)}) collective-permute-start(bf16[1024,256]{1,0:T(8,128)(2,1)S(1)} %get-tuple-element.57.refs_1_.refs_7_.refs_2_), channel_id=1, source_target_pairs={{0,1},{1,0},{2,3},{3,2},{4,5},{5,4},{6,7},{7,6},{8,9},{9,8},{10,11... | collective-permute-start | bytes 1572872 | tf_op jit(solution)/shard_map/ppermute | solution.py:377
  45.3 4.2 %collective-permute-start.13 = (bf16[1024,128]{1,0:T(8,128)(2,1)S(1)}, bf16[1024,128]{1,0:T(8,128)(2,1)S(1)}, u32[]{:S(2)}, u32[]{:S(2)}) collective-permute-start(bf16[1024,128]{1,0:T(8,128)(2,1)S(1)} %get-tuple-element.59.refs_3_.refs_4_), channel_id=1, source_target_pairs={{0,1},{1,0},{2,3},{3,2},{4,5},{5,4},{6,7},{7,6},{8,9},{9,8},{10,11... | collective-permute-start | bytes 786440 | tf_op jit(solution)/shard_map/ppermute | solution.py:377
  45.4 22.0 %collective-permute-start.10 = (bf16[1024,384]{1,0:T(8,128)(2,1)S(1)}, bf16[1024,384]{1,0:T(8,128)(2,1)S(1)}, u32[]{:S(2)}, u32[]{:S(2)}) collective-permute-start(bf16[1024,384]{1,0:T(8,128)(2,1)S(1)} %get-tuple-element.54.refs_2_), channel_id=1, source_target_pairs={{2,0},{6,4},{10,8},{14,12},{0,2},{4,6},{8,10},{12,14},{3,1},{7,5},... | collective-permute-start | bytes 2359304 | tf_op jit(solution)/shard_map/ppermute | solution.py:367
  49.3 1.5 %collective-permute-start.14 = (bf16[1024,128]{1,0:T(8,128)(2,1)S(1)}, bf16[1024,128]{1,0:T(8,128)(2,1)S(1)}, u32[]{:S(2)}, u32[]{:S(2)}) collective-permute-start(bf16[1024,128]{1,0:T(8,128)(2,1)S(1)} %get-tuple-element.60.refs_5_.refs_6_), channel_id=1, source_target_pairs={{0,1},{1,0},{2,3},{3,2},{4,5},{5,4},{6,7},{7,6},{8,9},{9,8},{10,11... | collective-permute-start | bytes 786440 | tf_op jit(solution)/shard_map/ppermute | solution.py:377
  49.4 13.3 %collective-permute-start.16 = (bf16[288,640]{1,0:T(8,128)(2,1)S(1)}, bf16[288,640]{1,0:T(8,128)(2,1)S(1)}, u32[]{:S(2)}, u32[]{:S(2)}) collective-permute-start(bf16[288,640]{1,0:T(8,128)(2,1)S(1)} %get-tuple-element.56.refs_0_), channel_id=1, source_target_pairs={{4,0},{6,2},{8,4},{10,6},{12,8},{14,10},{5,1},{7,3},{9,5},{11,7},{... | collective-permute-start | bytes 1105928 | tf_op jit(solution)/shard_map/ppermute | solution.py:367
  50.8 30.4 %collective-permute-start.25 = (bf16[1024,384]{1,0:T(8,128)(2,1)S(1)}, bf16[1024,384]{1,0:T(8,128)(2,1)S(1)}, u32[]{:S(2)}, u32[]{:S(2)}) collective-permute-start(bf16[1024,384]{1,0:T(8,128)(2,1)S(1)} %get-tuple-element.48.odd_ref.refs_2_), channel_id=1, source_target_pairs={{0,1},{1,0},{2,3},{3,2},{4,5},{5,4},{6,7},{7,6},{8,9},{9,8},{10,11... | collective-permute-start | bytes 2359304 | tf_op jit(solution)/shard_map/ppermute | solution.py:377
  52.8 17.8 %collective-permute-start.17 = (bf16[288,640]{1,0:T(8,128)(2,1)S(1)}, bf16[288,640]{1,0:T(8,128)(2,1)S(1)}, u32[]{:S(2)}, u32[]{:S(2)}) collective-permute-start(bf16[288,640]{1,0:T(8,128)(2,1)S(1)} %get-tuple-element.64), channel_id=1, source_target_pairs={{4,0},{6,2},{8,4},{10,6},{12,8},{14,10},{5,1},{7,3},{9,5},{11,7},{... | collective-permute-start | bytes 1105928 | tf_op jit(solution)/shard_map/ppermute | solution.py:367
  64.9 21.8 %collective-permute-start.24 = (bf16[224,1280]{1,0:T(8,128)(2,1)S(1)}, bf16[224,1280]{1,0:T(8,128)(2,1)S(1)}, u32[]{:S(2)}, u32[]{:S(2)}) collective-permute-start(bf16[224,1280]{1,0:T(8,128)(2,1)S(1)} %get-tuple-element.63.refs_0_), channel_id=1, source_target_pairs={{4,0},{6,2},{8,4},{10,6},{12,8},{14,10},{5,1},{7,3},{9,5},{11,7},{... | collective-permute-start | bytes 1720328 | tf_op jit(solution)/shard_map/ppermute | solution.py:367
  70.8 1.6 %collective-permute-start.18 = (bf16[1024,128]{1,0:T(8,128)(2,1)S(1)}, bf16[1024,128]{1,0:T(8,128)(2,1)S(1)}, u32[]{:S(2)}, u32[]{:S(2)}) collective-permute-start(bf16[1024,128]{1,0:T(8,128)(2,1)S(1)} %get-tuple-element.65.refs_2_), channel_id=1, source_target_pairs={{0,1},{1,0},{2,3},{3,2},{4,5},{5,4},{6,7},{7,6},{8,9},{9,8},{10,11... | collective-permute-start | bytes 786440 | tf_op jit(solution)/shard_map/ppermute | solution.py:377
  70.8 1.9 %collective-permute-start.19 = (bf16[1024,128]{1,0:T(8,128)(2,1)S(1)}, bf16[1024,128]{1,0:T(8,128)(2,1)S(1)}, u32[]{:S(2)}, u32[]{:S(2)}) collective-permute-start(bf16[1024,128]{1,0:T(8,128)(2,1)S(1)} %get-tuple-element.66.refs_4_), channel_id=1, source_target_pairs={{0,1},{1,0},{2,3},{3,2},{4,5},{5,4},{6,7},{7,6},{8,9},{9,8},{10,11... | collective-permute-start | bytes 786440 | tf_op jit(solution)/shard_map/ppermute | solution.py:377
  71.3 1.8 %collective-permute-start.20 = (bf16[1024,128]{1,0:T(8,128)(2,1)S(1)}, bf16[1024,128]{1,0:T(8,128)(2,1)S(1)}, u32[]{:S(2)}, u32[]{:S(2)}) collective-permute-start(bf16[1024,128]{1,0:T(8,128)(2,1)S(1)} %get-tuple-element.67.refs_6_), channel_id=1, source_target_pairs={{0,1},{1,0},{2,3},{3,2},{4,5},{5,4},{6,7},{7,6},{8,9},{9,8},{10,11... | collective-permute-start | bytes 786440 | tf_op jit(solution)/shard_map/ppermute | solution.py:377
  74.9 17.6 %collective-permute-start.21 = (bf16[512,384]{1,0:T(8,128)(2,1)S(1)}, bf16[512,384]{1,0:T(8,128)(2,1)S(1)}, u32[]{:S(2)}, u32[]{:S(2)}) collective-permute-start(bf16[512,384]{1,0:T(8,128)(2,1)S(1)} %get-tuple-element.69), channel_id=1, source_target_pairs={{4,0},{6,2},{8,4},{10,6},{12,8},{14,10},{5,1},{7,3},{9,5},{11,7},{... | collective-permute-start | bytes 1179656 | tf_op jit(solution)/shard_map/ppermute | solution.py:367
  79.1 9.5 %collective-permute-start.22 = (bf16[1024,128]{1,0:T(8,128)(2,1)S(1)}, bf16[1024,128]{1,0:T(8,128)(2,1)S(1)}, u32[]{:S(2)}, u32[]{:S(2)}) collective-permute-start(bf16[1024,128]{1,0:T(8,128)(2,1)S(1)} %get-tuple-element.71.refs_2_), channel_id=1, source_target_pairs={{0,1},{1,0},{2,3},{3,2},{4,5},{5,4},{6,7},{7,6},{8,9},{9,8},{10,11... | collective-permute-start | bytes 786440 | tf_op jit(solution)/shard_map/ppermute | solution.py:377
  83.8 4.8 %collective-permute-start.23 = (bf16[1024,128]{1,0:T(8,128)(2,1)S(1)}, bf16[1024,128]{1,0:T(8,128)(2,1)S(1)}, u32[]{:S(2)}, u32[]{:S(2)}) collective-permute-start(bf16[1024,128]{1,0:T(8,128)(2,1)S(1)} %get-tuple-element.72.refs_4_), channel_id=1, source_target_pairs={{0,1},{1,0},{2,3},{3,2},{4,5},{5,4},{6,7},{7,6},{8,9},{9,8},{10,11... | collective-permute-start | bytes 786440 | tf_op jit(solution)/shard_map/ppermute | solution.py:377
  88.4 1.6 %collective-permute-start.26 = (bf16[1024,128]{1,0:T(8,128)(2,1)S(1)}, bf16[1024,128]{1,0:T(8,128)(2,1)S(1)}, u32[]{:S(2)}, u32[]{:S(2)}) collective-permute-start(bf16[1024,128]{1,0:T(8,128)(2,1)S(1)} %get-tuple-element.75.refs_6_), channel_id=1, source_target_pairs={{0,1},{1,0},{2,3},{3,2},{4,5},{5,4},{6,7},{7,6},{8,9},{9,8},{10,11... | collective-permute-start | bytes 786440 | tf_op jit(solution)/shard_map/ppermute | solution.py:377

commit v14 on v13

--- a/solution.py
+++ b/solution.py
@@ -409,6 +409,8 @@
     high += [next_detoured, mate(next_detoured)]
     made, buffer = far(place, buffer, [below0], high, samples)
     top3 = send(made, down)
+    buffer = tile(place, buffer, 1, 0, rows, high[:-2], samples)
+    buffer = tile(place, buffer, 0, 1, rows, [relayed, mate(relayed)], samples)
 
     (buffer,) = hold((below1, top2), buffer)
     made, buffer = far(place, buffer, [below1], high + own, samples)
@@ -418,9 +420,7 @@
         low += [piece, mate(piece)]
     made, buffer = far(place, buffer, [below0, below1], low, samples)
     side = send(made, down)
-    buffer = tile(place, buffer, 1, 0, rows, high[:-2], samples)
     buffer = tile(place, buffer, 1, 3, rows, high[-2:], samples)
-    buffer = tile(place, buffer, 0, 1, rows, [relayed, mate(relayed)], samples)
     buffer = tile(place, buffer, 1, 1, rows, low, samples)
     pieces = list(split(above, (), 3))
     pieces[2], buffer = put(place, buffer, top2, top3, bottom, pieces[2])

time: 94.5 us -> 93.1 us (0.985)
  waiting for transfers between devices: 31.5 us -> 30.4 us
    ppermute x11, waiting for transfers between devices: 28.2 us -> 26.3 us  [send(): return lax.ppermute(shard, 'var', pairs)]
  transfers between devices with their start and end apart: 27 -> 27, of which waited for: 13 -> 15; matrix products, arithmetic and copies ran while one was open for 0% -> 0% of each run, Pallas kernels for 29% -> 29%
where the time goes in v14:
time: 93.1 us; the launch traced here: 92.8 us
  Pallas kernels  33.5 us (36%)
  waiting for transfers between devices  30.4 us (33%)
  starting transfers between devices  27.9 us (30%)
    ppermute x11, waiting for transfers between devices, send(): return lax.ppermute(shard, 'var', pairs)  26.3 us
    ppermute x11, starting transfers between devices, send(): return lax.ppermute(shard, 'var', pairs)  23.9 us
    pallas_call x7, Pallas kernels, tile(): pl.pallas_call(functools.partial(tile_kernel, k, len(rows), len(rights),...  16.7 us
    pallas_call x4, Pallas kernels, far(): pl.pallas_call(functools.partial(far_kernel, 1.0 / samples, len(rows), le...  7.22 us
    ppermute x16, waiting for transfers between devices, mate(): return lax.ppermute(shard, 'samp', [(0, 1), (1, 0)])  4.1 us
    ppermute x16, starting transfers between devices, mate(): return lax.ppermute(shard, 'samp', [(0, 1), (1, 0)])  4.01 us
    pallas_call x1, Pallas kernels, stats(): pl.pallas_call(stats_kernel, in_specs=[pl.BlockSpec(memory_space=pltpu.HB...  3.08 us
  transfers between devices with their start and end apart: 27, of which 15 were waited for; matrix products, arithmetic and copies ran while one was open for 0% of the time, Pallas kernels for 29%

profile of v14, /device:TPU:0, one launch (start us, length us, event | category | flops | bytes accessed | tf_op | source)
XLA Modules:
  0.0 92.8 jit_solution(8263054543771696088)
XLA Ops:
  0.0 3.1 %shard_map.37 = (f32[8,1024]{1,0:T(8,128)S(1)}, bf16[1024,1024]{1,0:T(8,128)(2,1)S(1)}) custom-call(bf16[1024,1024]{1,0:T(8,128)(2,1)} %dosage_hbm.1, s32[1024,1024]{1,0:T(8,128)} %observed_hbm.1), custom_call_target="tpu_custom_call" | custom-call | flops 1000 | bytes 1000 | tf_op jit(solution)/shard_map/pallas_call | solution.py:60
  3.1 0.5 collective-permute-start
  4.3 0.1 pad_add_fusion.place_ref.refs_0_
  4.3 0.1 collective-permute-done.sums_other_ref
  4.5 1.8 %shard_map.38 = (bf16[1024,384]{1,0:T(8,128)(2,1)S(1)}, bf16[1024,384]{1,0:T(8,128)(2,1)S(1)}, bf16[1024,256]{1,0:T(8,128)(2,1)S(1)}, bf16[1024,384]{1,0:T(8,128...) custom-call(s32[3]{0:T(128)S(1)} %pad_add_fusion.place_ref.refs_0_, ...), custom_call_target="tpu_custom_call" | custom-call | flops 1000 | bytes 1000 | tf_op jit(solution)/shard_map/pallas_call | solution.py:118
  6.2 0.4 collective-permute-start.1
  6.7 1.3 %collective-permute-start.5 = (bf16[1024,384]{1,0:T(8,128)(2,1)S(1)}, bf16[1024,384]{1,0:T(8,128)(2,1)S(1)}, u32[]{:S(2)}, u32[]{:S(2)}) collective-permute-start(bf16[1024,384]{1,0:T(8,128)(2,1)S(1)} %get-tuple-element.48.odd_ref.refs_2_), channel_id=1, source_target_pairs={{4,0},{6,2},{8,4},{10,6},{12,8},{14,10},{5,1},{7,3},{9,5},{11,7},{... | collective-permute-start | bytes 2359304 | tf_op jit(solution)/shard_map/ppermute | solution.py:367
  7.9 2.7 %collective-permute-start.6 = (bf16[1024,256]{1,0:T(8,128)(2,1)S(1)}, bf16[1024,256]{1,0:T(8,128)(2,1)S(1)}, u32[]{:S(2)}, u32[]{:S(2)}) collective-permute-start(bf16[1024,256]{1,0:T(8,128)(2,1)S(1)} %get-tuple-element.49.refs_2_.refs_3_.refs_11_), channel_id=1, source_target_pairs={{2,0},{6,4},{10,8},{14,12},{0,2},{4,6},{8,10},{12,14},{3,1},{7,5},... | collective-permute-start | bytes 1572872 | tf_op jit(solution)/shard_map/ppermute | solution.py:367
  10.7 0.1 shard_map.39
  10.8 4.6 %collective-permute-start.2 = (bf16[576,1024]{1,0:T(8,128)(2,1)S(1)}, bf16[576,1024]{1,0:T(8,128)(2,1)S(1)}, u32[]{:S(2)}, u32[]{:S(2)}) collective-permute-start(bf16[576,1024]{1,0:T(8,128)(2,1)S(1)} %get-tuple-element.45.refs_0_), channel_id=1, source_target_pairs={{0,4},{2,6},{4,8},{6,10},{8,12},{10,14},{1,5},{3,7},{5,9},{7,11},{... | collective-permute-start | bytes 3538952 | tf_op jit(solution)/shard_map/ppermute | solution.py:367
  15.4 0.1 collective-permute-start.3
  15.5 0.5 collective-permute-start.8
  16.0 7.1 %collective-permute-done.6.refs_1_.refs_0_ = bf16[1024,256]{1,0:T(8,128)(2,1)S(1)} collective-permute-done((bf16[1024,256]{1,0:T(8,128)(2,1)S(1)}, bf16[1024,256]{1,0:T(8,128)(2,1)S(1)}, u32[]{:S(2)}, u32[]{:S(2)}) %collective-permute-start.6) | collective-permute-done | bytes 524320 | tf_op jit(solution)/shard_map/ppermute | solution.py:367
  23.1 1.3 %collective-permute-start.11 = (bf16[1024,384]{1,0:T(8,128)(2,1)S(1)}, bf16[1024,384]{1,0:T(8,128)(2,1)S(1)}, u32[]{:S(2)}, u32[]{:S(2)}) collective-permute-start(bf16[1024,384]{1,0:T(8,128)(2,1)S(1)} %shard_map.48), channel_id=1, source_target_pairs={{2,0},{4,2},{6,4},{8,6},{10,8},{12,10},{14,12},{3,1},{5,3},{7,5},{... | collective-permute-start | bytes 2359304 | tf_op jit(solution)/shard_map/ppermute | solution.py:367
  24.4 5.2 %collective-permute-done.5.refs_0_.even_ref = bf16[1024,384]{1,0:T(8,128)(2,1)S(1)} collective-permute-done((bf16[1024,384]{1,0:T(8,128)(2,1)S(1)}, bf16[1024,384]{1,0:T(8,128)(2,1)S(1)}, u32[]{:S(2)}, u32[]{:S(2)}) %collective-permute-start.5) | collective-permute-done | bytes 786464 | tf_op jit(solution)/shard_map/ppermute | solution.py:367
  29.6 0.7 collective-permute-start.7
  30.3 0.1 shard_map.40.refs_1_
  30.4 4.0 %collective-permute-start.4 = (bf16[448,1024]{1,0:T(8,128)(2,1)S(1)}, bf16[448,1024]{1,0:T(8,128)(2,1)S(1)}, u32[]{:S(2)}, u32[]{:S(2)}) collective-permute-start(bf16[448,1024]{1,0:T(8,128)(2,1)S(1)} %shard_map.40.refs_1_), channel_id=1, source_target_pairs={{0,4},{2,6},{4,8},{6,10},{8,12},{10,14},{1,5},{3,7},{5,9},{7,11},{... | collective-permute-start | bytes 2752520 | tf_op jit(solution)/shard_map/ppermute | solution.py:367
  34.4 2.5 %shard_map.42.refs_4_ = bf16[4,512,1024]{2,1,0:T(8,128)(2,1)} custom-call(s32[3]{0:T(128)S(1)} %pad_add_fusion.place_ref.refs_0_, bf16[576,1024]{1,0:T(8,128)(2,1)S(1)} %get-tuple-element.45.refs_0_, bf16[448,1024]{1,0:T(8,128)(2,1)S(1)} %shard_map.40.refs_1_, ...), custom_call_target="tpu_custom_call", output_to_operand_aliasing={{}: (5, {})} | custom-call | flops 1000 | bytes 1000 | tf_op jit(solution)/shard_map/pallas_call | solution.py:192
  36.9 2.0 %shard_map.43.refs_1_ = bf16[4,512,1024]{2,1,0:T(8,128)(2,1)} custom-call(s32[3]{0:T(128)S(1)} %pad_add_fusion.place_ref.refs_0_, bf16[576,1024]{1,0:T(8,128)(2,1)S(1)} %get-tuple-element.45.refs_0_, bf16[448,1024]{1,0:T(8,128)(2,1)S(1)} %shard_map.40.refs_1_, ...), custom_call_target="tpu_custom_call", output_to_operand_aliasing={{}: (5, {})} | custom-call | flops 1000 | bytes 1000 | tf_op jit(solution)/shard_map/pallas_call | solution.py:192
  38.9 2.8 %collective-permute-done.2.refs_0_ = bf16[576,1024]{1,0:T(8,128)(2,1)S(1)} collective-permute-done((bf16[576,1024]{1,0:T(8,128)(2,1)S(1)}, bf16[576,1024]{1,0:T(8,128)(2,1)S(1)}, u32[]{:S(2)}, u32[]{:S(2)}) %collective-permute-start.2) | collective-permute-done | bytes 1179680 | tf_op jit(solution)/shard_map/ppermute | solution.py:367
  41.7 1.6 %shard_map.45 = (bf16[288,640]{1,0:T(8,128)(2,1)S(1)}, bf16[4,512,1024]{2,1,0:T(8,128)(2,1)}) custom-call(s32[3]{0:T(128)S(1)} %pad_add_fusion.place_ref.refs_0_, bf16[576,1024]{1,0:T(8,128)(2,1)S(1)} %collective-permute-done.2.refs_0_, bf16[1024,384]{1,0:T(8,128)(2,1)S(1)} %get-tuple-element.50.refs_2_.refs_1_.refs_9_, ...), custom_call_target="tpu_custom_call", output_to_operand_aliasing={{1}: (6, {})} | custom-call | flops 1000 | bytes 1000 | tf_op jit(solution)/shard_map/pallas_call | solution.py:213
  43.3 0.6 shard_map.46
  43.9 0.6 shard_map.47
  44.6 0.1 shard_map.49
  44.7 0.1 collective-permute-start.12
  44.8 0.5 collective-permute-start.13
  45.3 0.1 collective-permute-start.17
  45.4 0.4 collective-permute-start.15
  45.8 0.5 collective-permute-done.12.refs_2_.refs_3_
  46.3 0.1 collective-permute-start.14
  46.4 0.2 collective-permute-done.13.refs_4_.refs_5_
  46.7 3.9 %collective-permute-start.10 = (bf16[1024,384]{1,0:T(8,128)(2,1)S(1)}, bf16[1024,384]{1,0:T(8,128)(2,1)S(1)}, u32[]{:S(2)}, u32[]{:S(2)}) collective-permute-start(bf16[1024,384]{1,0:T(8,128)(2,1)S(1)} %get-tuple-element.54.refs_2_), channel_id=1, source_target_pairs={{2,0},{6,4},{10,8},{14,12},{0,2},{4,6},{8,10},{12,14},{3,1},{7,5},... | collective-permute-start | bytes 2359304 | tf_op jit(solution)/shard_map/ppermute | solution.py:367
  50.6 1.3 %collective-permute-start.16 = (bf16[288,640]{1,0:T(8,128)(2,1)S(1)}, bf16[288,640]{1,0:T(8,128)(2,1)S(1)}, u32[]{:S(2)}, u32[]{:S(2)}) collective-permute-start(bf16[288,640]{1,0:T(8,128)(2,1)S(1)} %get-tuple-element.56.refs_0_), channel_id=1, source_target_pairs={{4,0},{6,2},{8,4},{10,6},{12,8},{14,10},{5,1},{7,3},{9,5},{11,7},{... | collective-permute-start | bytes 1105928 | tf_op jit(solution)/shard_map/ppermute | solution.py:367
  51.9 1.6 %shard_map.50 = (bf16[288,640]{1,0:T(8,128)(2,1)S(1)}, bf16[4,512,1024]{2,1,0:T(8,128)(2,1)}) custom-call(s32[3]{0:T(128)S(1)} %pad_add_fusion.place_ref.refs_0_, bf16[576,1024]{1,0:T(8,128)(2,1)S(1)} %collective-permute-done.2.refs_0_, bf16[1024,128]{1,0:T(8,128)(2,1)S(1)} %get-tuple-element.58.refs_1_.refs_2_, ...), custom_call_target="tpu_custom_call", output_to_operand_aliasing={{1}: (10, {})} | custom-call | flops 1000 | bytes 1000 | tf_op jit(solution)/shard_map/pallas_call | solution.py:213
  53.5 1.5 %collective-permute-start.18 = (bf16[288,640]{1,0:T(8,128)(2,1)S(1)}, bf16[288,640]{1,0:T(8,128)(2,1)S(1)}, u32[]{:S(2)}, u32[]{:S(2)}) collective-permute-start(bf16[288,640]{1,0:T(8,128)(2,1)S(1)} %get-tuple-element.64), channel_id=1, source_target_pairs={{4,0},{6,2},{8,4},{10,6},{12,8},{14,10},{5,1},{7,3},{9,5},{11,7},{... | collective-permute-start | bytes 1105928 | tf_op jit(solution)/shard_map/ppermute | solution.py:367
  55.0 2.6 %shard_map.51.refs_4_ = bf16[4,512,1024]{2,1,0:T(8,128)(2,1)} custom-call(s32[3]{0:T(128)S(1)} %pad_add_fusion.place_ref.refs_0_, bf16[576,1024]{1,0:T(8,128)(2,1)S(1)} %get-tuple-element.45.refs_0_, bf16[448,1024]{1,0:T(8,128)(2,1)S(1)} %shard_map.40.refs_1_, ...), custom_call_target="tpu_custom_call", output_to_operand_aliasing={{}: (9, {})} | custom-call | flops 1000 | bytes 1000 | tf_op jit(solution)/shard_map/pallas_call | solution.py:192
  57.6 2.6 %shard_map.52.refs_2_ = bf16[4,512,1024]{2,1,0:T(8,128)(2,1)} custom-call(s32[3]{0:T(128)S(1)} %pad_add_fusion.place_ref.refs_0_, bf16[576,1024]{1,0:T(8,128)(2,1)S(1)} %get-tuple-element.45.refs_0_, bf16[448,1024]{1,0:T(8,128)(2,1)S(1)} %shard_map.40.refs_1_, ...), custom_call_target="tpu_custom_call", output_to_operand_aliasing={{}: (5, {})} | custom-call | flops 1000 | bytes 1000 | tf_op jit(solution)/shard_map/pallas_call | solution.py:192
  60.1 3.8 %collective-permute-done.16.refs_1_ = bf16[288,640]{1,0:T(8,128)(2,1)S(1)} collective-permute-done((bf16[288,640]{1,0:T(8,128)(2,1)S(1)}, bf16[288,640]{1,0:T(8,128)(2,1)S(1)}, u32[]{:S(2)}, u32[]{:S(2)}) %collective-permute-start.16) | collective-permute-done | bytes 368672 | tf_op jit(solution)/shard_map/ppermute | solution.py:367
  63.9 2.1 %shard_map.54 = (bf16[224,1280]{1,0:T(8,128)(2,1)S(1)}, bf16[4,512,1024]{2,1,0:T(8,128)(2,1)}) custom-call(s32[3]{0:T(128)S(1)} %pad_add_fusion.place_ref.refs_0_, bf16[448,1024]{1,0:T(8,128)(2,1)S(1)} %collective-permute-done.4.refs_0_.refs_1_, bf16[1024,128]{1,0:T(8,128)(2,1)S(1)} %get-tuple-element.58.refs_1_.refs_2_, ...), custom_call_target="tpu_custom_call", output_to_operand_aliasing={{1}: (14, {})} | custom-call | flops 1000 | bytes 1000 | tf_op jit(solution)/shard_map/pallas_call | solution.py:213
  66.1 1.3 %collective-permute-start.25 = (bf16[224,1280]{1,0:T(8,128)(2,1)S(1)}, bf16[224,1280]{1,0:T(8,128)(2,1)S(1)}, u32[]{:S(2)}, u32[]{:S(2)}) collective-permute-start(bf16[224,1280]{1,0:T(8,128)(2,1)S(1)} %get-tuple-element.63.refs_0_), channel_id=1, source_target_pairs={{4,0},{6,2},{8,4},{10,6},{12,8},{14,10},{5,1},{7,3},{9,5},{11,7},{... | collective-permute-start | bytes 1720328 | tf_op jit(solution)/shard_map/ppermute | solution.py:367
  67.4 1.0 %collective-permute-done.10.whole_ref = bf16[1024,384]{1,0:T(8,128)(2,1)S(1)} collective-permute-done((bf16[1024,384]{1,0:T(8,128)(2,1)S(1)}, bf16[1024,384]{1,0:T(8,128)(2,1)S(1)}, u32[]{:S(2)}, u32[]{:S(2)}) %collective-permute-start.10) | collective-permute-done | bytes 786464 | tf_op jit(solution)/shard_map/ppermute | solution.py:367
  68.4 3.4 %collective-permute-done.18.refs_1_.refs_2_ = bf16[288,640]{1,0:T(8,128)(2,1)S(1)} collective-permute-done((bf16[288,640]{1,0:T(8,128)(2,1)S(1)}, bf16[288,640]{1,0:T(8,128)(2,1)S(1)}, u32[]{:S(2)}, u32[]{:S(2)}) %collective-permute-start.18) | collective-permute-done | bytes 368672 | tf_op jit(solution)/shard_map/ppermute | solution.py:367
  71.8 0.1 shard_map.55
  72.0 0.1 collective-permute-start.19
  72.1 0.5 collective-permute-start.20
  72.6 0.1 collective-permute-start.21
  72.6 0.9 %collective-permute-done.19.refs_3_ = bf16[1024,128]{1,0:T(8,128)(2,1)S(1)} collective-permute-done((bf16[1024,128]{1,0:T(8,128)(2,1)S(1)}, bf16[1024,128]{1,0:T(8,128)(2,1)S(1)}, u32[]{:S(2)}, u32[]{:S(2)}) %collective-permute-start.19) | collective-permute-done | bytes 262176 | tf_op jit(solution)/shard_map/ppermute | solution.py:377
  73.6 0.4 collective-permute-done.20.refs_5_
  74.0 0.4 collective-permute-done.21.refs_7_
  74.3 1.8 %shard_map.56 = (bf16[512,384]{1,0:T(8,128)(2,1)S(1)}, bf16[4,512,1024]{2,1,0:T(8,128)(2,1)}) custom-call(s32[3]{0:T(128)S(1)} %pad_add_fusion.place_ref.refs_0_, bf16[576,1024]{1,0:T(8,128)(2,1)S(1)} %collective-permute-done.2.refs_0_, bf16[448,1024]{1,0:T(8,128)(2,1)S(1)} %collective-permute-done.4.refs_0_.refs_1_, ...), custom_call_target="tpu_custom_call", output_to_operand_aliasing={{1}: (9, {})} | custom-call | flops 1000 | bytes 1000 | tf_op jit(solution)/shard_map/pallas_call | solution.py:213
  76.2 1.3 %collective-permute-start.22 = (bf16[512,384]{1,0:T(8,128)(2,1)S(1)}, bf16[512,384]{1,0:T(8,128)(2,1)S(1)}, u32[]{:S(2)}, u32[]{:S(2)}) collective-permute-start(bf16[512,384]{1,0:T(8,128)(2,1)S(1)} %get-tuple-element.69), channel_id=1, source_target_pairs={{4,0},{6,2},{8,4},{10,6},{12,8},{14,10},{5,1},{7,3},{9,5},{11,7},{... | collective-permute-start | bytes 1179656 | tf_op jit(solution)/shard_map/ppermute | solution.py:367
  77.5 0.1 shard_map.57
  77.6 0.2 collective-permute-start.23
  77.8 2.0 %shard_map.58.refs_8_ = bf16[4,512,1024]{2,1,0:T(8,128)(2,1)} custom-call(s32[3]{0:T(128)S(1)} %pad_add_fusion.place_ref.refs_0_, bf16[576,1024]{1,0:T(8,128)(2,1)S(1)} %get-tuple-element.45.refs_0_, bf16[448,1024]{1,0:T(8,128)(2,1)S(1)} %shard_map.40.refs_1_, ...), custom_call_target="tpu_custom_call", output_to_operand_aliasing={{}: (5, {})} | custom-call | flops 1000 | bytes 1000 | tf_op jit(solution)/shard_map/pallas_call | solution.py:192
  79.8 0.4 collective-permute-start.24
  80.1 2.6 %shard_map.59.refs_5_ = bf16[4,512,1024]{2,1,0:T(8,128)(2,1)} custom-call(s32[3]{0:T(128)S(1)} %pad_add_fusion.place_ref.refs_0_, bf16[576,1024]{1,0:T(8,128)(2,1)S(1)} %get-tuple-element.45.refs_0_, bf16[448,1024]{1,0:T(8,128)(2,1)S(1)} %shard_map.40.refs_1_, bf16[1024,128]{1,0:T(8,128)(2,1)S(1)} %get-tuple-element.65.refs_2_, ...), custom_call_target="tpu_custom_call", output_to_operand_aliasing={{}: (9, {})} | custom-call | flops 1000 | bytes 1000 | tf_op jit(solution)/shard_map/pallas_call | solution.py:192
  82.7 1.4 %collective-permute-done.25.refs_3_ = bf16[224,1280]{1,0:T(8,128)(2,1)S(1)} collective-permute-done((bf16[224,1280]{1,0:T(8,128)(2,1)S(1)}, bf16[224,1280]{1,0:T(8,128)(2,1)S(1)}, u32[]{:S(2)}, u32[]{:S(2)}) %collective-permute-start.25) | collective-permute-done | bytes 573472 | tf_op jit(solution)/shard_map/ppermute | solution.py:367
  84.1 1.7 %shard_map.60 = (bf16[1024,128]{1,0:T(8,128)(2,1)S(1)}, bf16[4,512,1024]{2,1,0:T(8,128)(2,1)}) custom-call(s32[3]{0:T(128)S(1)} %pad_add_fusion.place_ref.refs_0_, bf16[288,640]{1,0:T(8,128)(2,1)S(1)} %collective-permute-done.16.refs_1_, bf16[288,640]{1,0:T(8,128)(2,1)S(1)} %collective-permute-done.18.refs_1_.refs_2_, ...), custom_call_target="tpu_custom_call", output_to_operand_aliasing={{0}: (4, {}), {1}: (5, {})} | custom-call | flops 1000 | bytes 1000 | tf_op jit(solution)/shard_map/pallas_call | solution.py:320
  85.8 0.1 collective-permute-start.26
  85.9 1.5 %collective-permute-done.26.refs_7_ = bf16[1024,128]{1,0:T(8,128)(2,1)S(1)} collective-permute-done((bf16[1024,128]{1,0:T(8,128)(2,1)S(1)}, bf16[1024,128]{1,0:T(8,128)(2,1)S(1)}, u32[]{:S(2)}, u32[]{:S(2)}) %collective-permute-start.26) | collective-permute-done | bytes 262176 | tf_op jit(solution)/shard_map/ppermute | solution.py:377
  87.4 2.5 %shard_map.61.buffer_ref = bf16[4,512,1024]{2,1,0:T(8,128)(2,1)} custom-call(s32[3]{0:T(128)S(1)} %pad_add_fusion.place_ref.refs_0_, bf16[576,1024]{1,0:T(8,128)(2,1)S(1)} %get-tuple-element.45.refs_0_, bf16[448,1024]{1,0:T(8,128)(2,1)S(1)} %shard_map.40.refs_1_, bf16[1024,128]{1,0:T(8,128)(2,1)S(1)} %get-tuple-element.71.refs_2_, ...), custom_call_target="tpu_custom_call", output_to_operand_aliasing={{}: (9, {})} | custom-call | flops 1000 | bytes 1000 | tf_op jit(solution)/shard_map/pallas_call | solution.py:192
  90.0 1.5 %collective-permute-done.22.side = bf16[512,384]{1,0:T(8,128)(2,1)S(1)} collective-permute-done((bf16[512,384]{1,0:T(8,128)(2,1)S(1)}, bf16[512,384]{1,0:T(8,128)(2,1)S(1)}, u32[]{:S(2)}, u32[]{:S(2)}) %collective-permute-start.22) | collective-permute-done | bytes 393248 | tf_op jit(solution)/shard_map/ppermute | solution.py:367
  91.4 1.3 %shard_map.62 = bf16[4,512,1024]{2,1,0:T(8,128)(2,1)} custom-call(s32[3]{0:T(128)S(1)} %pad_add_fusion.place_ref.refs_0_, bf16[512,384]{1,0:T(8,128)(2,1)S(1)} %collective-permute-done.22.side, bf16[4,512,1024]{2,1,0:T(8,128)(2,1)} %shard_map.61.buffer_ref), custom_call_target="tpu_custom_call", output_to_operand_aliasing={{}: (2, {})} | custom-call | flops 1000 | bytes 1000 | tf_op jit(solution)/shard_map/pallas_call | solution.py:342
  (17 shorter events, 0.0 us)
Async XLA Ops:
  3.1 1.4 %collective-permute-start = (f32[8,1024]{1,0:T(8,128)S(1)}, f32[8,1024]{1,0:T(8,128)S(1)}, u32[]{:S(2)}, u32[]{:S(2)}) collective-permute-start(f32[8,1024]{1,0:T(8,128)S(1)} %get-tuple-element.42.sums_ref), channel_id=1, source_target_pairs={{0,1},{1,0},{2,3},{3,2},{4,5},{5,4},{6,7},{7,6},{8,9},{9,8},{10,11... | collective-permute-start | bytes 98312 | tf_op jit(solution)/shard_map/ppermute | solution.py:377
  6.2 4.5 %collective-permute-start.1 = (bf16[288,1024]{1,0:T(8,128)(2,1)S(1)}, bf16[288,1024]{1,0:T(8,128)(2,1)S(1)}, u32[]{:S(2)}, u32[]{:S(2)}) collective-permute-start(bf16[288,1024]{1,0:T(8,128)(2,1)S(1)} %get-tuple-element.44), channel_id=1, source_target_pairs={{0,1},{1,0},{2,3},{3,2},{4,5},{5,4},{6,7},{7,6},{8,9},{9,8},{10,11... | collective-permute-start | bytes 1769480 | tf_op jit(solution)/shard_map/ppermute | solution.py:377
  6.7 22.9 %collective-permute-start.5 = (bf16[1024,384]{1,0:T(8,128)(2,1)S(1)}, bf16[1024,384]{1,0:T(8,128)(2,1)S(1)}, u32[]{:S(2)}, u32[]{:S(2)}) collective-permute-start(bf16[1024,384]{1,0:T(8,128)(2,1)S(1)} %get-tuple-element.48.odd_ref.refs_2_), channel_id=1, source_target_pairs={{4,0},{6,2},{8,4},{10,6},{12,8},{14,10},{5,1},{7,3},{9,5},{11,7},{... | collective-permute-start | bytes 2359304 | tf_op jit(solution)/shard_map/ppermute | solution.py:367
  7.9 15.2 %collective-permute-start.6 = (bf16[1024,256]{1,0:T(8,128)(2,1)S(1)}, bf16[1024,256]{1,0:T(8,128)(2,1)S(1)}, u32[]{:S(2)}, u32[]{:S(2)}) collective-permute-start(bf16[1024,256]{1,0:T(8,128)(2,1)S(1)} %get-tuple-element.49.refs_2_.refs_3_.refs_11_), channel_id=1, source_target_pairs={{2,0},{6,4},{10,8},{14,12},{0,2},{4,6},{8,10},{12,14},{3,1},{7,5},... | collective-permute-start | bytes 1572872 | tf_op jit(solution)/shard_map/ppermute | solution.py:367
  10.8 30.9 %collective-permute-start.2 = (bf16[576,1024]{1,0:T(8,128)(2,1)S(1)}, bf16[576,1024]{1,0:T(8,128)(2,1)S(1)}, u32[]{:S(2)}, u32[]{:S(2)}) collective-permute-start(bf16[576,1024]{1,0:T(8,128)(2,1)S(1)} %get-tuple-element.45.refs_0_), channel_id=1, source_target_pairs={{0,4},{2,6},{4,8},{6,10},{8,12},{10,14},{1,5},{3,7},{5,9},{7,11},{... | collective-permute-start | bytes 3538952 | tf_op jit(solution)/shard_map/ppermute | solution.py:367
  15.4 14.2 %collective-permute-start.3 = (bf16[224,1024]{1,0:T(8,128)(2,1)S(1)}, bf16[224,1024]{1,0:T(8,128)(2,1)S(1)}, u32[]{:S(2)}, u32[]{:S(2)}) collective-permute-start(bf16[224,1024]{1,0:T(8,128)(2,1)S(1)} %get-tuple-element.47), channel_id=1, source_target_pairs={{0,1},{1,0},{2,3},{3,2},{4,5},{5,4},{6,7},{7,6},{8,9},{9,8},{10,11... | collective-permute-start | bytes 1376264 | tf_op jit(solution)/shard_map/ppermute | solution.py:377
  15.5 14.9 %collective-permute-start.8 = (bf16[1024,384]{1,0:T(8,128)(2,1)S(1)}, bf16[1024,384]{1,0:T(8,128)(2,1)S(1)}, u32[]{:S(2)}, u32[]{:S(2)}) collective-permute-start(bf16[1024,384]{1,0:T(8,128)(2,1)S(1)} %get-tuple-element.50.refs_2_.refs_1_.refs_9_), channel_id=1, source_target_pairs={{0,1},{1,0},{2,3},{3,2},{4,5},{5,4},{6,7},{7,6},{8,9},{9,8},{10,11... | collective-permute-start | bytes 2359304 | tf_op jit(solution)/shard_map/ppermute | solution.py:377
  23.1 21.4 %collective-permute-start.11 = (bf16[1024,384]{1,0:T(8,128)(2,1)S(1)}, bf16[1024,384]{1,0:T(8,128)(2,1)S(1)}, u32[]{:S(2)}, u32[]{:S(2)}) collective-permute-start(bf16[1024,384]{1,0:T(8,128)(2,1)S(1)} %shard_map.48), channel_id=1, source_target_pairs={{2,0},{4,2},{6,4},{8,6},{10,8},{12,10},{14,12},{3,1},{5,3},{7,5},{... | collective-permute-start | bytes 2359304 | tf_op jit(solution)/shard_map/ppermute | solution.py:367
  29.6 7.4 %collective-permute-start.9 = (bf16[1024,256]{1,0:T(8,128)(2,1)S(1)}, bf16[1024,256]{1,0:T(8,128)(2,1)S(1)}, u32[]{:S(2)}, u32[]{:S(2)}) collective-permute-start(bf16[1024,256]{1,0:T(8,128)(2,1)S(1)} %get-tuple-element.49.refs_2_.refs_3_.refs_11_), channel_id=1, source_target_pairs={{0,1},{1,0},{2,3},{3,2},{4,5},{5,4},{6,7},{7,6},{8,9},{9,8},{10,11... | collective-permute-start | bytes 1572872 | tf_op jit(solution)/shard_map/ppermute | solution.py:377
  29.6 13.7 %collective-permute-start.7 = (bf16[1024,256]{1,0:T(8,128)(2,1)S(1)}, bf16[1024,256]{1,0:T(8,128)(2,1)S(1)}, u32[]{:S(2)}, u32[]{:S(2)}) collective-permute-start(bf16[1024,256]{1,0:T(8,128)(2,1)S(1)} %shard_map.41.even_ref), channel_id=1, source_target_pairs={{6,2},{10,6},{14,10},{7,3},{11,7},{15,11},{22,18},{26,22},{30,26},... | collective-permute-start | bytes 1572872 | tf_op jit(solution)/shard_map/ppermute | solution.py:367
  30.4 29.8 %collective-permute-start.4 = (bf16[448,1024]{1,0:T(8,128)(2,1)S(1)}, bf16[448,1024]{1,0:T(8,128)(2,1)S(1)}, u32[]{:S(2)}, u32[]{:S(2)}) collective-permute-start(bf16[448,1024]{1,0:T(8,128)(2,1)S(1)} %shard_map.40.refs_1_), channel_id=1, source_target_pairs={{0,4},{2,6},{4,8},{6,10},{8,12},{10,14},{1,5},{3,7},{5,9},{7,11},{... | collective-permute-start | bytes 2752520 | tf_op jit(solution)/shard_map/ppermute | solution.py:367
  44.7 1.6 %collective-permute-start.12 = (bf16[1024,128]{1,0:T(8,128)(2,1)S(1)}, bf16[1024,128]{1,0:T(8,128)(2,1)S(1)}, u32[]{:S(2)}, u32[]{:S(2)}) collective-permute-start(bf16[1024,128]{1,0:T(8,128)(2,1)S(1)} %get-tuple-element.58.refs_1_.refs_2_), channel_id=1, source_target_pairs={{0,1},{1,0},{2,3},{3,2},{4,5},{5,4},{6,7},{7,6},{8,9},{9,8},{10,11... | collective-permute-start | bytes 786440 | tf_op jit(solution)/shard_map/ppermute | solution.py:377
  44.8 1.9 %collective-permute-start.13 = (bf16[1024,128]{1,0:T(8,128)(2,1)S(1)}, bf16[1024,128]{1,0:T(8,128)(2,1)S(1)}, u32[]{:S(2)}, u32[]{:S(2)}) collective-permute-start(bf16[1024,128]{1,0:T(8,128)(2,1)S(1)} %get-tuple-element.59.refs_3_.refs_4_), channel_id=1, source_target_pairs={{0,1},{1,0},{2,3},{3,2},{4,5},{5,4},{6,7},{7,6},{8,9},{9,8},{10,11... | collective-permute-start | bytes 786440 | tf_op jit(solution)/shard_map/ppermute | solution.py:377
  45.3 12.3 %collective-permute-start.17 = (bf16[1024,384]{1,0:T(8,128)(2,1)S(1)}, bf16[1024,384]{1,0:T(8,128)(2,1)S(1)}, u32[]{:S(2)}, u32[]{:S(2)}) collective-permute-start(bf16[1024,384]{1,0:T(8,128)(2,1)S(1)} %get-tuple-element.48.odd_ref.refs_2_), channel_id=1, source_target_pairs={{0,1},{1,0},{2,3},{3,2},{4,5},{5,4},{6,7},{7,6},{8,9},{9,8},{10,11... | collective-permute-start | bytes 2359304 | tf_op jit(solution)/shard_map/ppermute | solution.py:377
  45.4 6.5 %collective-permute-start.15 = (bf16[1024,256]{1,0:T(8,128)(2,1)S(1)}, bf16[1024,256]{1,0:T(8,128)(2,1)S(1)}, u32[]{:S(2)}, u32[]{:S(2)}) collective-permute-start(bf16[1024,256]{1,0:T(8,128)(2,1)S(1)} %get-tuple-element.57.refs_1_.refs_7_.refs_2_), channel_id=1, source_target_pairs={{0,1},{1,0},{2,3},{3,2},{4,5},{5,4},{6,7},{7,6},{8,9},{9,8},{10,11... | collective-permute-start | bytes 1572872 | tf_op jit(solution)/shard_map/ppermute | solution.py:377
  46.3 4.3 %collective-permute-start.14 = (bf16[1024,128]{1,0:T(8,128)(2,1)S(1)}, bf16[1024,128]{1,0:T(8,128)(2,1)S(1)}, u32[]{:S(2)}, u32[]{:S(2)}) collective-permute-start(bf16[1024,128]{1,0:T(8,128)(2,1)S(1)} %get-tuple-element.60.refs_5_.refs_6_), channel_id=1, source_target_pairs={{0,1},{1,0},{2,3},{3,2},{4,5},{5,4},{6,7},{7,6},{8,9},{9,8},{10,11... | collective-permute-start | bytes 786440 | tf_op jit(solution)/shard_map/ppermute | solution.py:377
  46.7 21.7 %collective-permute-start.10 = (bf16[1024,384]{1,0:T(8,128)(2,1)S(1)}, bf16[1024,384]{1,0:T(8,128)(2,1)S(1)}, u32[]{:S(2)}, u32[]{:S(2)}) collective-permute-start(bf16[1024,384]{1,0:T(8,128)(2,1)S(1)} %get-tuple-element.54.refs_2_), channel_id=1, source_target_pairs={{2,0},{6,4},{10,8},{14,12},{0,2},{4,6},{8,10},{12,14},{3,1},{7,5},... | collective-permute-start | bytes 2359304 | tf_op jit(solution)/shard_map/ppermute | solution.py:367
  50.6 13.4 %collective-permute-start.16 = (bf16[288,640]{1,0:T(8,128)(2,1)S(1)}, bf16[288,640]{1,0:T(8,128)(2,1)S(1)}, u32[]{:S(2)}, u32[]{:S(2)}) collective-permute-start(bf16[288,640]{1,0:T(8,128)(2,1)S(1)} %get-tuple-element.56.refs_0_), channel_id=1, source_target_pairs={{4,0},{6,2},{8,4},{10,6},{12,8},{14,10},{5,1},{7,3},{9,5},{11,7},{... | collective-permute-start | bytes 1105928 | tf_op jit(solution)/shard_map/ppermute | solution.py:367
  53.5 18.3 %collective-permute-start.18 = (bf16[288,640]{1,0:T(8,128)(2,1)S(1)}, bf16[288,640]{1,0:T(8,128)(2,1)S(1)}, u32[]{:S(2)}, u32[]{:S(2)}) collective-permute-start(bf16[288,640]{1,0:T(8,128)(2,1)S(1)} %get-tuple-element.64), channel_id=1, source_target_pairs={{4,0},{6,2},{8,4},{10,6},{12,8},{14,10},{5,1},{7,3},{9,5},{11,7},{... | collective-permute-start | bytes 1105928 | tf_op jit(solution)/shard_map/ppermute | solution.py:367
  66.1 18.0 %collective-permute-start.25 = (bf16[224,1280]{1,0:T(8,128)(2,1)S(1)}, bf16[224,1280]{1,0:T(8,128)(2,1)S(1)}, u32[]{:S(2)}, u32[]{:S(2)}) collective-permute-start(bf16[224,1280]{1,0:T(8,128)(2,1)S(1)} %get-tuple-element.63.refs_0_), channel_id=1, source_target_pairs={{4,0},{6,2},{8,4},{10,6},{12,8},{14,10},{5,1},{7,3},{9,5},{11,7},{... | collective-permute-start | bytes 1720328 | tf_op jit(solution)/shard_map/ppermute | solution.py:367
  72.0 1.6 %collective-permute-start.19 = (bf16[1024,128]{1,0:T(8,128)(2,1)S(1)}, bf16[1024,128]{1,0:T(8,128)(2,1)S(1)}, u32[]{:S(2)}, u32[]{:S(2)}) collective-permute-start(bf16[1024,128]{1,0:T(8,128)(2,1)S(1)} %get-tuple-element.65.refs_2_), channel_id=1, source_target_pairs={{0,1},{1,0},{2,3},{3,2},{4,5},{5,4},{6,7},{7,6},{8,9},{9,8},{10,11... | collective-permute-start | bytes 786440 | tf_op jit(solution)/shard_map/ppermute | solution.py:377
  72.1 1.9 %collective-permute-start.20 = (bf16[1024,128]{1,0:T(8,128)(2,1)S(1)}, bf16[1024,128]{1,0:T(8,128)(2,1)S(1)}, u32[]{:S(2)}, u32[]{:S(2)}) collective-permute-start(bf16[1024,128]{1,0:T(8,128)(2,1)S(1)} %get-tuple-element.66.refs_4_), channel_id=1, source_target_pairs={{0,1},{1,0},{2,3},{3,2},{4,5},{5,4},{6,7},{7,6},{8,9},{9,8},{10,11... | collective-permute-start | bytes 786440 | tf_op jit(solution)/shard_map/ppermute | solution.py:377
  72.6 1.8 %collective-permute-start.21 = (bf16[1024,128]{1,0:T(8,128)(2,1)S(1)}, bf16[1024,128]{1,0:T(8,128)(2,1)S(1)}, u32[]{:S(2)}, u32[]{:S(2)}) collective-permute-start(bf16[1024,128]{1,0:T(8,128)(2,1)S(1)} %get-tuple-element.67.refs_6_), channel_id=1, source_target_pairs={{0,1},{1,0},{2,3},{3,2},{4,5},{5,4},{6,7},{7,6},{8,9},{9,8},{10,11... | collective-permute-start | bytes 786440 | tf_op jit(solution)/shard_map/ppermute | solution.py:377
  76.2 15.3 %collective-permute-start.22 = (bf16[512,384]{1,0:T(8,128)(2,1)S(1)}, bf16[512,384]{1,0:T(8,128)(2,1)S(1)}, u32[]{:S(2)}, u32[]{:S(2)}) collective-permute-start(bf16[512,384]{1,0:T(8,128)(2,1)S(1)} %get-tuple-element.69), channel_id=1, source_target_pairs={{4,0},{6,2},{8,4},{10,6},{12,8},{14,10},{5,1},{7,3},{9,5},{11,7},{... | collective-permute-start | bytes 1179656 | tf_op jit(solution)/shard_map/ppermute | solution.py:367
  77.6 8.3 %collective-permute-start.23 = (bf16[1024,128]{1,0:T(8,128)(2,1)S(1)}, bf16[1024,128]{1,0:T(8,128)(2,1)S(1)}, u32[]{:S(2)}, u32[]{:S(2)}) collective-permute-start(bf16[1024,128]{1,0:T(8,128)(2,1)S(1)} %get-tuple-element.71.refs_2_), channel_id=1, source_target_pairs={{0,1},{1,0},{2,3},{3,2},{4,5},{5,4},{6,7},{7,6},{8,9},{9,8},{10,11... | collective-permute-start | bytes 786440 | tf_op jit(solution)/shard_map/ppermute | solution.py:377
  79.8 6.2 %collective-permute-start.24 = (bf16[1024,128]{1,0:T(8,128)(2,1)S(1)}, bf16[1024,128]{1,0:T(8,128)(2,1)S(1)}, u32[]{:S(2)}, u32[]{:S(2)}) collective-permute-start(bf16[1024,128]{1,0:T(8,128)(2,1)S(1)} %get-tuple-element.72.refs_4_), channel_id=1, source_target_pairs={{0,1},{1,0},{2,3},{3,2},{4,5},{5,4},{6,7},{7,6},{8,9},{9,8},{10,11... | collective-permute-start | bytes 786440 | tf_op jit(solution)/shard_map/ppermute | solution.py:377
  85.8 1.6 %collective-permute-start.26 = (bf16[1024,128]{1,0:T(8,128)(2,1)S(1)}, bf16[1024,128]{1,0:T(8,128)(2,1)S(1)}, u32[]{:S(2)}, u32[]{:S(2)}) collective-permute-start(bf16[1024,128]{1,0:T(8,128)(2,1)S(1)} %get-tuple-element.75.refs_6_), channel_id=1, source_target_pairs={{0,1},{1,0},{2,3},{3,2},{4,5},{5,4},{6,7},{7,6},{8,9},{9,8},{10,11... | collective-permute-start | bytes 786440 | tf_op jit(solution)/shard_map/ppermute | solution.py:377

commit v15 on v14

--- a/solution.py
+++ b/solution.py
@@ -9,7 +9,7 @@
 
 WIN = 4
 PIECES = (3, 3, 2)
-ROWS = (9, 7)
+ROWS = (17, 15)
 PARTS = 2
 BLOCKS = 8
 STATS_VMEM = 50
@@ -397,12 +397,12 @@
 
     buffer = tile(place, buffer, 0, 0, rows, own[:2], samples)
     buffer = tile(place, buffer, 0, 3, rows, own[2:], samples)
+    above, buffer, swapped = choose(place, relayed, above, (buffer,))
+    next_relayed = send(swapped, swap)
     (buffer,) = hold((below0,), buffer)
     made, buffer = far(place, buffer, [below0], own, samples)
     top2 = send(made, down)
     across, buffer, next_detoured = choose(place, around, across, (buffer,))
-    above, buffer, swapped = choose(place, relayed, above, (buffer,))
-    next_relayed = send(swapped, swap)
     high = []
     for piece in split(next_direct, (made, next_detoured, swapped), 3):
         high += [piece, mate(piece)]

time: 93.1 us -> 92.5 us (level)
  transfers between devices with their start and end apart: 27 -> 27, of which waited for: 15 -> 17; matrix products, arithmetic and copies ran while one was open for 0% -> 0% of each run, Pallas kernels for 29% -> 30%
where the time goes in v15:
time: 92.5 us; the launch traced here: 92.1 us
  Pallas kernels  33.6 us (36%)
  waiting for transfers between devices  30.1 us (33%)
  starting transfers between devices  27.5 us (30%)
    ppermute x11, waiting for transfers between devices, send(): return lax.ppermute(shard, 'var', pairs)  26 us
    ppermute x11, starting transfers between devices, send(): return lax.ppermute(shard, 'var', pairs)  23.5 us
    pallas_call x7, Pallas kernels, tile(): pl.pallas_call(functools.partial(tile_kernel, k, len(rows), len(rights),...  16.7 us
    pallas_call x4, Pallas kernels, far(): pl.pallas_call(functools.partial(far_kernel, 1.0 / samples, len(rows), le...  7.24 us
    ppermute x16, waiting for transfers between devices, mate(): return lax.ppermute(shard, 'samp', [(0, 1), (1, 0)])  4.1 us
    ppermute x16, starting transfers between devices, mate(): return lax.ppermute(shard, 'samp', [(0, 1), (1, 0)])  4.01 us
    pallas_call x1, Pallas kernels, stats(): pl.pallas_call(stats_kernel, in_specs=[pl.BlockSpec(memory_space=pltpu.HB...  3.08 us
  transfers between devices with their start and end apart: 27, of which 17 were waited for; matrix products, arithmetic and copies ran while one was open for 0% of the time, Pallas kernels for 30%

profile of v15, /device:TPU:0, one launch (start us, length us, event | category | flops | bytes accessed | tf_op | source)
XLA Modules:
  0.0 92.1 jit_solution(11339810791703637176)
XLA Ops:
  0.0 3.1 %shard_map.37 = (f32[8,1024]{1,0:T(8,128)S(1)}, bf16[1024,1024]{1,0:T(8,128)(2,1)S(1)}) custom-call(bf16[1024,1024]{1,0:T(8,128)(2,1)} %dosage_hbm.1, s32[1024,1024]{1,0:T(8,128)} %observed_hbm.1), custom_call_target="tpu_custom_call" | custom-call | flops 1000 | bytes 1000 | tf_op jit(solution)/shard_map/pallas_call | solution.py:60
  3.1 0.5 collective-permute-start
  4.3 0.1 pad_add_fusion.place_ref.refs_0_
  4.3 0.1 collective-permute-done.sums_other_ref
  4.5 1.8 %shard_map.38 = (bf16[1024,384]{1,0:T(8,128)(2,1)S(1)}, bf16[1024,384]{1,0:T(8,128)(2,1)S(1)}, bf16[1024,256]{1,0:T(8,128)(2,1)S(1)}, bf16[1024,384]{1,0:T(8,128...) custom-call(s32[3]{0:T(128)S(1)} %pad_add_fusion.place_ref.refs_0_, ...), custom_call_target="tpu_custom_call" | custom-call | flops 1000 | bytes 1000 | tf_op jit(solution)/shard_map/pallas_call | solution.py:118
  6.2 0.4 collective-permute-start.1
  6.7 1.3 %collective-permute-start.5 = (bf16[1024,384]{1,0:T(8,128)(2,1)S(1)}, bf16[1024,384]{1,0:T(8,128)(2,1)S(1)}, u32[]{:S(2)}, u32[]{:S(2)}) collective-permute-start(bf16[1024,384]{1,0:T(8,128)(2,1)S(1)} %get-tuple-element.48.odd_ref.refs_2_), channel_id=1, source_target_pairs={{4,0},{6,2},{8,4},{10,6},{12,8},{14,10},{5,1},{7,3},{9,5},{11,7},{... | collective-permute-start | bytes 2359304 | tf_op jit(solution)/shard_map/ppermute | solution.py:367
  7.9 2.7 %collective-permute-start.9 = (bf16[1024,256]{1,0:T(8,128)(2,1)S(1)}, bf16[1024,256]{1,0:T(8,128)(2,1)S(1)}, u32[]{:S(2)}, u32[]{:S(2)}) collective-permute-start(bf16[1024,256]{1,0:T(8,128)(2,1)S(1)} %get-tuple-element.49.refs_2_.refs_3_.refs_11_), channel_id=1, source_target_pairs={{2,0},{6,4},{10,8},{14,12},{0,2},{4,6},{8,10},{12,14},{3,1},{7,5},... | collective-permute-start | bytes 1572872 | tf_op jit(solution)/shard_map/ppermute | solution.py:367
  10.7 0.1 shard_map.39
  10.8 4.6 %collective-permute-start.2 = (bf16[544,1024]{1,0:T(8,128)(2,1)S(1)}, bf16[544,1024]{1,0:T(8,128)(2,1)S(1)}, u32[]{:S(2)}, u32[]{:S(2)}) collective-permute-start(bf16[544,1024]{1,0:T(8,128)(2,1)S(1)} %get-tuple-element.45.refs_0_), channel_id=1, source_target_pairs={{0,4},{2,6},{4,8},{6,10},{8,12},{10,14},{1,5},{3,7},{5,9},{7,11},{... | collective-permute-start | bytes 3342344 | tf_op jit(solution)/shard_map/ppermute | solution.py:367
  15.4 0.1 collective-permute-start.3
  15.5 0.5 collective-permute-start.7
  16.0 7.1 %collective-permute-done.9.refs_0_.refs_1_ = bf16[1024,256]{1,0:T(8,128)(2,1)S(1)} collective-permute-done((bf16[1024,256]{1,0:T(8,128)(2,1)S(1)}, bf16[1024,256]{1,0:T(8,128)(2,1)S(1)}, u32[]{:S(2)}, u32[]{:S(2)}) %collective-permute-start.9) | collective-permute-done | bytes 524320 | tf_op jit(solution)/shard_map/ppermute | solution.py:367
  23.1 1.3 %collective-permute-start.10 = (bf16[1024,384]{1,0:T(8,128)(2,1)S(1)}, bf16[1024,384]{1,0:T(8,128)(2,1)S(1)}, u32[]{:S(2)}, u32[]{:S(2)}) collective-permute-start(bf16[1024,384]{1,0:T(8,128)(2,1)S(1)} %shard_map.44), channel_id=1, source_target_pairs={{2,0},{4,2},{6,4},{8,6},{10,8},{12,10},{14,12},{3,1},{5,3},{7,5},{... | collective-permute-start | bytes 2359304 | tf_op jit(solution)/shard_map/ppermute | solution.py:367
  24.4 5.2 %collective-permute-done.5.even_ref.refs_0_ = bf16[1024,384]{1,0:T(8,128)(2,1)S(1)} collective-permute-done((bf16[1024,384]{1,0:T(8,128)(2,1)S(1)}, bf16[1024,384]{1,0:T(8,128)(2,1)S(1)}, u32[]{:S(2)}, u32[]{:S(2)}) %collective-permute-start.5) | collective-permute-done | bytes 786464 | tf_op jit(solution)/shard_map/ppermute | solution.py:367
  29.6 0.7 collective-permute-start.11
  30.4 4.0 %collective-permute-start.4 = (bf16[480,1024]{1,0:T(8,128)(2,1)S(1)}, bf16[480,1024]{1,0:T(8,128)(2,1)S(1)}, u32[]{:S(2)}, u32[]{:S(2)}) collective-permute-start(bf16[480,1024]{1,0:T(8,128)(2,1)S(1)} %shard_map.40.refs_1_), channel_id=1, source_target_pairs={{0,4},{2,6},{4,8},{6,10},{8,12},{10,14},{1,5},{3,7},{5,9},{7,11},{... | collective-permute-start | bytes 2949128 | tf_op jit(solution)/shard_map/ppermute | solution.py:367
  34.4 2.5 %shard_map.41.refs_4_ = bf16[4,512,1024]{2,1,0:T(8,128)(2,1)} custom-call(s32[3]{0:T(128)S(1)} %pad_add_fusion.place_ref.refs_0_, bf16[544,1024]{1,0:T(8,128)(2,1)S(1)} %get-tuple-element.45.refs_0_, bf16[480,1024]{1,0:T(8,128)(2,1)S(1)} %shard_map.40.refs_1_, ...), custom_call_target="tpu_custom_call", output_to_operand_aliasing={{}: (5, {})} | custom-call | flops 1000 | bytes 1000 | tf_op jit(solution)/shard_map/pallas_call | solution.py:192
  36.9 2.0 %shard_map.42.refs_0_ = bf16[4,512,1024]{2,1,0:T(8,128)(2,1)} custom-call(s32[3]{0:T(128)S(1)} %pad_add_fusion.place_ref.refs_0_, bf16[544,1024]{1,0:T(8,128)(2,1)S(1)} %get-tuple-element.45.refs_0_, bf16[480,1024]{1,0:T(8,128)(2,1)S(1)} %shard_map.40.refs_1_, ...), custom_call_target="tpu_custom_call", output_to_operand_aliasing={{}: (5, {})} | custom-call | flops 1000 | bytes 1000 | tf_op jit(solution)/shard_map/pallas_call | solution.py:192
  38.9 0.6 shard_map.43
  39.5 0.7 collective-permute-done.2.refs_0_
  40.3 1.6 %shard_map.46 = (bf16[272,640]{1,0:T(8,128)(2,1)S(1)}, bf16[4,512,1024]{2,1,0:T(8,128)(2,1)}) custom-call(s32[3]{0:T(128)S(1)} %pad_add_fusion.place_ref.refs_0_, bf16[544,1024]{1,0:T(8,128)(2,1)S(1)} %collective-permute-done.2.refs_0_, bf16[1024,384]{1,0:T(8,128)(2,1)S(1)} %get-tuple-element.50.refs_2_.refs_1_.refs_9_, ...), custom_call_target="tpu_custom_call", output_to_operand_aliasing={{1}: (6, {})} | custom-call | flops 1000 | bytes 1000 | tf_op jit(solution)/shard_map/pallas_call | solution.py:213
  41.9 0.6 shard_map.48
  42.5 1.8 %collective-permute-done.10.whole_ref = bf16[1024,384]{1,0:T(8,128)(2,1)S(1)} collective-permute-done((bf16[1024,384]{1,0:T(8,128)(2,1)S(1)}, bf16[1024,384]{1,0:T(8,128)(2,1)S(1)}, u32[]{:S(2)}, u32[]{:S(2)}) %collective-permute-start.10) | collective-permute-done | bytes 786464 | tf_op jit(solution)/shard_map/ppermute | solution.py:367
  44.3 0.1 shard_map.49
  44.4 0.1 collective-permute-start.12
  44.5 0.5 collective-permute-start.13
  45.0 0.1 collective-permute-start.17
  45.1 0.4 collective-permute-start.15
  45.5 0.5 collective-permute-done.12.refs_2_.refs_3_
  46.0 0.1 collective-permute-start.14
  46.2 0.2 collective-permute-done.13.refs_4_.refs_5_
  46.4 3.5 %collective-permute-start.8 = (bf16[1024,384]{1,0:T(8,128)(2,1)S(1)}, bf16[1024,384]{1,0:T(8,128)(2,1)S(1)}, u32[]{:S(2)}, u32[]{:S(2)}) collective-permute-start(bf16[1024,384]{1,0:T(8,128)(2,1)S(1)} %get-tuple-element.52.refs_2_), channel_id=1, source_target_pairs={{2,0},{6,4},{10,8},{14,12},{0,2},{4,6},{8,10},{12,14},{3,1},{7,5},... | collective-permute-start | bytes 2359304 | tf_op jit(solution)/shard_map/ppermute | solution.py:367
  50.0 1.3 %collective-permute-start.16 = (bf16[272,640]{1,0:T(8,128)(2,1)S(1)}, bf16[272,640]{1,0:T(8,128)(2,1)S(1)}, u32[]{:S(2)}, u32[]{:S(2)}) collective-permute-start(bf16[272,640]{1,0:T(8,128)(2,1)S(1)} %get-tuple-element.55.refs_0_), channel_id=1, source_target_pairs={{4,0},{6,2},{8,4},{10,6},{12,8},{14,10},{5,1},{7,3},{9,5},{11,7},{... | collective-permute-start | bytes 1044488 | tf_op jit(solution)/shard_map/ppermute | solution.py:367
  51.3 1.6 %shard_map.50 = (bf16[272,640]{1,0:T(8,128)(2,1)S(1)}, bf16[4,512,1024]{2,1,0:T(8,128)(2,1)}) custom-call(s32[3]{0:T(128)S(1)} %pad_add_fusion.place_ref.refs_0_, bf16[544,1024]{1,0:T(8,128)(2,1)S(1)} %collective-permute-done.2.refs_0_, bf16[1024,128]{1,0:T(8,128)(2,1)S(1)} %get-tuple-element.58.refs_1_.refs_2_, ...), custom_call_target="tpu_custom_call", output_to_operand_aliasing={{1}: (10, {})} | custom-call | flops 1000 | bytes 1000 | tf_op jit(solution)/shard_map/pallas_call | solution.py:213
  52.9 1.5 %collective-permute-start.18 = (bf16[272,640]{1,0:T(8,128)(2,1)S(1)}, bf16[272,640]{1,0:T(8,128)(2,1)S(1)}, u32[]{:S(2)}, u32[]{:S(2)}) collective-permute-start(bf16[272,640]{1,0:T(8,128)(2,1)S(1)} %get-tuple-element.64), channel_id=1, source_target_pairs={{4,0},{6,2},{8,4},{10,6},{12,8},{14,10},{5,1},{7,3},{9,5},{11,7},{... | collective-permute-start | bytes 1044488 | tf_op jit(solution)/shard_map/ppermute | solution.py:367
  54.3 2.6 %shard_map.51.refs_4_ = bf16[4,512,1024]{2,1,0:T(8,128)(2,1)} custom-call(s32[3]{0:T(128)S(1)} %pad_add_fusion.place_ref.refs_0_, bf16[544,1024]{1,0:T(8,128)(2,1)S(1)} %get-tuple-element.45.refs_0_, bf16[480,1024]{1,0:T(8,128)(2,1)S(1)} %shard_map.40.refs_1_, ...), custom_call_target="tpu_custom_call", output_to_operand_aliasing={{}: (9, {})} | custom-call | flops 1000 | bytes 1000 | tf_op jit(solution)/shard_map/pallas_call | solution.py:192
  56.9 2.6 %shard_map.52.refs_2_ = bf16[4,512,1024]{2,1,0:T(8,128)(2,1)} custom-call(s32[3]{0:T(128)S(1)} %pad_add_fusion.place_ref.refs_0_, bf16[544,1024]{1,0:T(8,128)(2,1)S(1)} %get-tuple-element.45.refs_0_, bf16[480,1024]{1,0:T(8,128)(2,1)S(1)} %shard_map.40.refs_1_, ...), custom_call_target="tpu_custom_call", output_to_operand_aliasing={{}: (5, {})} | custom-call | flops 1000 | bytes 1000 | tf_op jit(solution)/shard_map/pallas_call | solution.py:192
  59.5 0.7 collective-permute-done.4.refs_0_.refs_1_
  60.1 2.7 %collective-permute-done.16.refs_1_ = bf16[272,640]{1,0:T(8,128)(2,1)S(1)} collective-permute-done((bf16[272,640]{1,0:T(8,128)(2,1)S(1)}, bf16[272,640]{1,0:T(8,128)(2,1)S(1)}, u32[]{:S(2)}, u32[]{:S(2)}) %collective-permute-start.16) | collective-permute-done | bytes 348192 | tf_op jit(solution)/shard_map/ppermute | solution.py:367
  62.9 2.3 %shard_map.54 = (bf16[240,1280]{1,0:T(8,128)(2,1)S(1)}, bf16[4,512,1024]{2,1,0:T(8,128)(2,1)}) custom-call(s32[3]{0:T(128)S(1)} %pad_add_fusion.place_ref.refs_0_, bf16[480,1024]{1,0:T(8,128)(2,1)S(1)} %collective-permute-done.4.refs_0_.refs_1_, bf16[1024,128]{1,0:T(8,128)(2,1)S(1)} %get-tuple-element.58.refs_1_.refs_2_, ...), custom_call_target="tpu_custom_call", output_to_operand_aliasing={{1}: (14, {})} | custom-call | flops 1000 | bytes 1000 | tf_op jit(solution)/shard_map/pallas_call | solution.py:213
  65.2 1.3 %collective-permute-start.25 = (bf16[240,1280]{1,0:T(8,128)(2,1)S(1)}, bf16[240,1280]{1,0:T(8,128)(2,1)S(1)}, u32[]{:S(2)}, u32[]{:S(2)}) collective-permute-start(bf16[240,1280]{1,0:T(8,128)(2,1)S(1)} %get-tuple-element.63.refs_0_), channel_id=1, source_target_pairs={{4,0},{6,2},{8,4},{10,6},{12,8},{14,10},{5,1},{7,3},{9,5},{11,7},{... | collective-permute-start | bytes 1843208 | tf_op jit(solution)/shard_map/ppermute | solution.py:367
  66.5 1.3 %collective-permute-done.8.whole_ref = bf16[1024,384]{1,0:T(8,128)(2,1)S(1)} collective-permute-done((bf16[1024,384]{1,0:T(8,128)(2,1)S(1)}, bf16[1024,384]{1,0:T(8,128)(2,1)S(1)}, u32[]{:S(2)}, u32[]{:S(2)}) %collective-permute-start.8) | collective-permute-done | bytes 786464 | tf_op jit(solution)/shard_map/ppermute | solution.py:367
  67.8 2.5 %collective-permute-done.18.refs_1_.refs_2_ = bf16[272,640]{1,0:T(8,128)(2,1)S(1)} collective-permute-done((bf16[272,640]{1,0:T(8,128)(2,1)S(1)}, bf16[272,640]{1,0:T(8,128)(2,1)S(1)}, u32[]{:S(2)}, u32[]{:S(2)}) %collective-permute-start.18) | collective-permute-done | bytes 348192 | tf_op jit(solution)/shard_map/ppermute | solution.py:367
  70.3 0.1 shard_map.55
  70.5 0.1 collective-permute-start.19
  70.6 0.5 collective-permute-start.20
  71.1 0.1 collective-permute-start.21
  71.1 0.9 %collective-permute-done.19.refs_3_ = bf16[1024,128]{1,0:T(8,128)(2,1)S(1)} collective-permute-done((bf16[1024,128]{1,0:T(8,128)(2,1)S(1)}, bf16[1024,128]{1,0:T(8,128)(2,1)S(1)}, u32[]{:S(2)}, u32[]{:S(2)}) %collective-permute-start.19) | collective-permute-done | bytes 262176 | tf_op jit(solution)/shard_map/ppermute | solution.py:377
  72.1 0.4 collective-permute-done.20.refs_5_
  72.5 0.4 collective-permute-done.21.refs_7_
  72.8 1.8 %shard_map.56 = (bf16[512,384]{1,0:T(8,128)(2,1)S(1)}, bf16[4,512,1024]{2,1,0:T(8,128)(2,1)}) custom-call(s32[3]{0:T(128)S(1)} %pad_add_fusion.place_ref.refs_0_, bf16[544,1024]{1,0:T(8,128)(2,1)S(1)} %collective-permute-done.2.refs_0_, bf16[480,1024]{1,0:T(8,128)(2,1)S(1)} %collective-permute-done.4.refs_0_.refs_1_, ...), custom_call_target="tpu_custom_call", output_to_operand_aliasing={{1}: (9, {})} | custom-call | flops 1000 | bytes 1000 | tf_op jit(solution)/shard_map/pallas_call | solution.py:213
  74.6 1.3 %collective-permute-start.22 = (bf16[512,384]{1,0:T(8,128)(2,1)S(1)}, bf16[512,384]{1,0:T(8,128)(2,1)S(1)}, u32[]{:S(2)}, u32[]{:S(2)}) collective-permute-start(bf16[512,384]{1,0:T(8,128)(2,1)S(1)} %get-tuple-element.69), channel_id=1, source_target_pairs={{4,0},{6,2},{8,4},{10,6},{12,8},{14,10},{5,1},{7,3},{9,5},{11,7},{... | collective-permute-start | bytes 1179656 | tf_op jit(solution)/shard_map/ppermute | solution.py:367
  75.9 0.1 shard_map.57
  76.1 0.2 collective-permute-start.23
  76.3 2.0 %shard_map.58.refs_8_ = bf16[4,512,1024]{2,1,0:T(8,128)(2,1)} custom-call(s32[3]{0:T(128)S(1)} %pad_add_fusion.place_ref.refs_0_, bf16[544,1024]{1,0:T(8,128)(2,1)S(1)} %get-tuple-element.45.refs_0_, bf16[480,1024]{1,0:T(8,128)(2,1)S(1)} %shard_map.40.refs_1_, ...), custom_call_target="tpu_custom_call", output_to_operand_aliasing={{}: (5, {})} | custom-call | flops 1000 | bytes 1000 | tf_op jit(solution)/shard_map/pallas_call | solution.py:192
  78.3 0.4 collective-permute-start.24
  78.6 2.5 %shard_map.59.refs_5_ = bf16[4,512,1024]{2,1,0:T(8,128)(2,1)} custom-call(s32[3]{0:T(128)S(1)} %pad_add_fusion.place_ref.refs_0_, bf16[544,1024]{1,0:T(8,128)(2,1)S(1)} %get-tuple-element.45.refs_0_, bf16[480,1024]{1,0:T(8,128)(2,1)S(1)} %shard_map.40.refs_1_, bf16[1024,128]{1,0:T(8,128)(2,1)S(1)} %get-tuple-element.65.refs_2_, ...), custom_call_target="tpu_custom_call", output_to_operand_aliasing={{}: (9, {})} | custom-call | flops 1000 | bytes 1000 | tf_op jit(solution)/shard_map/pallas_call | solution.py:192
  81.2 2.7 %collective-permute-done.25.refs_3_ = bf16[240,1280]{1,0:T(8,128)(2,1)S(1)} collective-permute-done((bf16[240,1280]{1,0:T(8,128)(2,1)S(1)}, bf16[240,1280]{1,0:T(8,128)(2,1)S(1)}, u32[]{:S(2)}, u32[]{:S(2)}) %collective-permute-start.25) | collective-permute-done | bytes 614432 | tf_op jit(solution)/shard_map/ppermute | solution.py:367
  83.8 1.7 %shard_map.60 = (bf16[1024,128]{1,0:T(8,128)(2,1)S(1)}, bf16[4,512,1024]{2,1,0:T(8,128)(2,1)}) custom-call(s32[3]{0:T(128)S(1)} %pad_add_fusion.place_ref.refs_0_, bf16[272,640]{1,0:T(8,128)(2,1)S(1)} %collective-permute-done.16.refs_1_, bf16[272,640]{1,0:T(8,128)(2,1)S(1)} %collective-permute-done.18.refs_1_.refs_2_, ...), custom_call_target="tpu_custom_call", output_to_operand_aliasing={{0}: (4, {}), {1}: (5, {})} | custom-call | flops 1000 | bytes 1000 | tf_op jit(solution)/shard_map/pallas_call | solution.py:320
  85.6 1.5 %collective-permute-done.26.refs_7_ = bf16[1024,128]{1,0:T(8,128)(2,1)S(1)} collective-permute-done((bf16[1024,128]{1,0:T(8,128)(2,1)S(1)}, bf16[1024,128]{1,0:T(8,128)(2,1)S(1)}, u32[]{:S(2)}, u32[]{:S(2)}) %collective-permute-start.26) | collective-permute-done | bytes 262176 | tf_op jit(solution)/shard_map/ppermute | solution.py:377
  87.1 2.6 %shard_map.61.buffer_ref = bf16[4,512,1024]{2,1,0:T(8,128)(2,1)} custom-call(s32[3]{0:T(128)S(1)} %pad_add_fusion.place_ref.refs_0_, bf16[544,1024]{1,0:T(8,128)(2,1)S(1)} %get-tuple-element.45.refs_0_, bf16[480,1024]{1,0:T(8,128)(2,1)S(1)} %shard_map.40.refs_1_, bf16[1024,128]{1,0:T(8,128)(2,1)S(1)} %get-tuple-element.71.refs_2_, ...), custom_call_target="tpu_custom_call", output_to_operand_aliasing={{}: (9, {})} | custom-call | flops 1000 | bytes 1000 | tf_op jit(solution)/shard_map/pallas_call | solution.py:192
  89.7 1.1 %collective-permute-done.22.side = bf16[512,384]{1,0:T(8,128)(2,1)S(1)} collective-permute-done((bf16[512,384]{1,0:T(8,128)(2,1)S(1)}, bf16[512,384]{1,0:T(8,128)(2,1)S(1)}, u32[]{:S(2)}, u32[]{:S(2)}) %collective-permute-start.22) | collective-permute-done | bytes 393248 | tf_op jit(solution)/shard_map/ppermute | solution.py:367
  90.8 1.3 %shard_map.62 = bf16[4,512,1024]{2,1,0:T(8,128)(2,1)} custom-call(s32[3]{0:T(128)S(1)} %pad_add_fusion.place_ref.refs_0_, bf16[512,384]{1,0:T(8,128)(2,1)S(1)} %collective-permute-done.22.side, bf16[4,512,1024]{2,1,0:T(8,128)(2,1)} %shard_map.61.buffer_ref), custom_call_target="tpu_custom_call", output_to_operand_aliasing={{}: (2, {})} | custom-call | flops 1000 | bytes 1000 | tf_op jit(solution)/shard_map/pallas_call | solution.py:342
  (17 shorter events, 0.2 us)
Async XLA Ops:
  3.1 1.4 %collective-permute-start = (f32[8,1024]{1,0:T(8,128)S(1)}, f32[8,1024]{1,0:T(8,128)S(1)}, u32[]{:S(2)}, u32[]{:S(2)}) collective-permute-start(f32[8,1024]{1,0:T(8,128)S(1)} %get-tuple-element.42.sums_ref), channel_id=1, source_target_pairs={{0,1},{1,0},{2,3},{3,2},{4,5},{5,4},{6,7},{7,6},{8,9},{9,8},{10,11... | collective-permute-start | bytes 98312 | tf_op jit(solution)/shard_map/ppermute | solution.py:377
  6.2 4.5 %collective-permute-start.1 = (bf16[272,1024]{1,0:T(8,128)(2,1)S(1)}, bf16[272,1024]{1,0:T(8,128)(2,1)S(1)}, u32[]{:S(2)}, u32[]{:S(2)}) collective-permute-start(bf16[272,1024]{1,0:T(8,128)(2,1)S(1)} %get-tuple-element.44), channel_id=1, source_target_pairs={{0,1},{1,0},{2,3},{3,2},{4,5},{5,4},{6,7},{7,6},{8,9},{9,8},{10,11... | collective-permute-start | bytes 1671176 | tf_op jit(solution)/shard_map/ppermute | solution.py:377
  6.7 22.9 %collective-permute-start.5 = (bf16[1024,384]{1,0:T(8,128)(2,1)S(1)}, bf16[1024,384]{1,0:T(8,128)(2,1)S(1)}, u32[]{:S(2)}, u32[]{:S(2)}) collective-permute-start(bf16[1024,384]{1,0:T(8,128)(2,1)S(1)} %get-tuple-element.48.odd_ref.refs_2_), channel_id=1, source_target_pairs={{4,0},{6,2},{8,4},{10,6},{12,8},{14,10},{5,1},{7,3},{9,5},{11,7},{... | collective-permute-start | bytes 2359304 | tf_op jit(solution)/shard_map/ppermute | solution.py:367
  7.9 15.2 %collective-permute-start.9 = (bf16[1024,256]{1,0:T(8,128)(2,1)S(1)}, bf16[1024,256]{1,0:T(8,128)(2,1)S(1)}, u32[]{:S(2)}, u32[]{:S(2)}) collective-permute-start(bf16[1024,256]{1,0:T(8,128)(2,1)S(1)} %get-tuple-element.49.refs_2_.refs_3_.refs_11_), channel_id=1, source_target_pairs={{2,0},{6,4},{10,8},{14,12},{0,2},{4,6},{8,10},{12,14},{3,1},{7,5},... | collective-permute-start | bytes 1572872 | tf_op jit(solution)/shard_map/ppermute | solution.py:367
  10.8 29.5 %collective-permute-start.2 = (bf16[544,1024]{1,0:T(8,128)(2,1)S(1)}, bf16[544,1024]{1,0:T(8,128)(2,1)S(1)}, u32[]{:S(2)}, u32[]{:S(2)}) collective-permute-start(bf16[544,1024]{1,0:T(8,128)(2,1)S(1)} %get-tuple-element.45.refs_0_), channel_id=1, source_target_pairs={{0,4},{2,6},{4,8},{6,10},{8,12},{10,14},{1,5},{3,7},{5,9},{7,11},{... | collective-permute-start | bytes 3342344 | tf_op jit(solution)/shard_map/ppermute | solution.py:367
  15.4 14.2 %collective-permute-start.3 = (bf16[240,1024]{1,0:T(8,128)(2,1)S(1)}, bf16[240,1024]{1,0:T(8,128)(2,1)S(1)}, u32[]{:S(2)}, u32[]{:S(2)}) collective-permute-start(bf16[240,1024]{1,0:T(8,128)(2,1)S(1)} %get-tuple-element.47), channel_id=1, source_target_pairs={{0,1},{1,0},{2,3},{3,2},{4,5},{5,4},{6,7},{7,6},{8,9},{9,8},{10,11... | collective-permute-start | bytes 1474568 | tf_op jit(solution)/shard_map/ppermute | solution.py:377
  15.5 14.9 %collective-permute-start.7 = (bf16[1024,384]{1,0:T(8,128)(2,1)S(1)}, bf16[1024,384]{1,0:T(8,128)(2,1)S(1)}, u32[]{:S(2)}, u32[]{:S(2)}) collective-permute-start(bf16[1024,384]{1,0:T(8,128)(2,1)S(1)} %get-tuple-element.50.refs_2_.refs_1_.refs_9_), channel_id=1, source_target_pairs={{0,1},{1,0},{2,3},{3,2},{4,5},{5,4},{6,7},{7,6},{8,9},{9,8},{10,11... | collective-permute-start | bytes 2359304 | tf_op jit(solution)/shard_map/ppermute | solution.py:377
  23.1 21.2 %collective-permute-start.10 = (bf16[1024,384]{1,0:T(8,128)(2,1)S(1)}, bf16[1024,384]{1,0:T(8,128)(2,1)S(1)}, u32[]{:S(2)}, u32[]{:S(2)}) collective-permute-start(bf16[1024,384]{1,0:T(8,128)(2,1)S(1)} %shard_map.44), channel_id=1, source_target_pairs={{2,0},{4,2},{6,4},{8,6},{10,8},{12,10},{14,12},{3,1},{5,3},{7,5},{... | collective-permute-start | bytes 2359304 | tf_op jit(solution)/shard_map/ppermute | solution.py:367
  29.6 7.4 %collective-permute-start.6 = (bf16[1024,256]{1,0:T(8,128)(2,1)S(1)}, bf16[1024,256]{1,0:T(8,128)(2,1)S(1)}, u32[]{:S(2)}, u32[]{:S(2)}) collective-permute-start(bf16[1024,256]{1,0:T(8,128)(2,1)S(1)} %get-tuple-element.49.refs_2_.refs_3_.refs_11_), channel_id=1, source_target_pairs={{0,1},{1,0},{2,3},{3,2},{4,5},{5,4},{6,7},{7,6},{8,9},{9,8},{10,11... | collective-permute-start | bytes 1572872 | tf_op jit(solution)/shard_map/ppermute | solution.py:377
  29.6 12.3 %collective-permute-start.11 = (bf16[1024,256]{1,0:T(8,128)(2,1)S(1)}, bf16[1024,256]{1,0:T(8,128)(2,1)S(1)}, u32[]{:S(2)}, u32[]{:S(2)}) collective-permute-start(bf16[1024,256]{1,0:T(8,128)(2,1)S(1)} %shard_map.47.even_ref), channel_id=1, source_target_pairs={{6,2},{10,6},{14,10},{7,3},{11,7},{15,11},{22,18},{26,22},{30,26},... | collective-permute-start | bytes 1572872 | tf_op jit(solution)/shard_map/ppermute | solution.py:367
  30.4 29.8 %collective-permute-start.4 = (bf16[480,1024]{1,0:T(8,128)(2,1)S(1)}, bf16[480,1024]{1,0:T(8,128)(2,1)S(1)}, u32[]{:S(2)}, u32[]{:S(2)}) collective-permute-start(bf16[480,1024]{1,0:T(8,128)(2,1)S(1)} %shard_map.40.refs_1_), channel_id=1, source_target_pairs={{0,4},{2,6},{4,8},{6,10},{8,12},{10,14},{1,5},{3,7},{5,9},{7,11},{... | collective-permute-start | bytes 2949128 | tf_op jit(solution)/shard_map/ppermute | solution.py:367
  44.4 1.6 %collective-permute-start.12 = (bf16[1024,128]{1,0:T(8,128)(2,1)S(1)}, bf16[1024,128]{1,0:T(8,128)(2,1)S(1)}, u32[]{:S(2)}, u32[]{:S(2)}) collective-permute-start(bf16[1024,128]{1,0:T(8,128)(2,1)S(1)} %get-tuple-element.58.refs_1_.refs_2_), channel_id=1, source_target_pairs={{0,1},{1,0},{2,3},{3,2},{4,5},{5,4},{6,7},{7,6},{8,9},{9,8},{10,11... | collective-permute-start | bytes 786440 | tf_op jit(solution)/shard_map/ppermute | solution.py:377
  44.5 1.9 %collective-permute-start.13 = (bf16[1024,128]{1,0:T(8,128)(2,1)S(1)}, bf16[1024,128]{1,0:T(8,128)(2,1)S(1)}, u32[]{:S(2)}, u32[]{:S(2)}) collective-permute-start(bf16[1024,128]{1,0:T(8,128)(2,1)S(1)} %get-tuple-element.59.refs_3_.refs_4_), channel_id=1, source_target_pairs={{0,1},{1,0},{2,3},{3,2},{4,5},{5,4},{6,7},{7,6},{8,9},{9,8},{10,11... | collective-permute-start | bytes 786440 | tf_op jit(solution)/shard_map/ppermute | solution.py:377
  45.0 11.9 %collective-permute-start.17 = (bf16[1024,384]{1,0:T(8,128)(2,1)S(1)}, bf16[1024,384]{1,0:T(8,128)(2,1)S(1)}, u32[]{:S(2)}, u32[]{:S(2)}) collective-permute-start(bf16[1024,384]{1,0:T(8,128)(2,1)S(1)} %get-tuple-element.48.odd_ref.refs_2_), channel_id=1, source_target_pairs={{0,1},{1,0},{2,3},{3,2},{4,5},{5,4},{6,7},{7,6},{8,9},{9,8},{10,11... | collective-permute-start | bytes 2359304 | tf_op jit(solution)/shard_map/ppermute | solution.py:377
  45.1 6.2 %collective-permute-start.15 = (bf16[1024,256]{1,0:T(8,128)(2,1)S(1)}, bf16[1024,256]{1,0:T(8,128)(2,1)S(1)}, u32[]{:S(2)}, u32[]{:S(2)}) collective-permute-start(bf16[1024,256]{1,0:T(8,128)(2,1)S(1)} %get-tuple-element.57.refs_1_.refs_7_.refs_2_), channel_id=1, source_target_pairs={{0,1},{1,0},{2,3},{3,2},{4,5},{5,4},{6,7},{7,6},{8,9},{9,8},{10,11... | collective-permute-start | bytes 1572872 | tf_op jit(solution)/shard_map/ppermute | solution.py:377
  46.0 3.9 %collective-permute-start.14 = (bf16[1024,128]{1,0:T(8,128)(2,1)S(1)}, bf16[1024,128]{1,0:T(8,128)(2,1)S(1)}, u32[]{:S(2)}, u32[]{:S(2)}) collective-permute-start(bf16[1024,128]{1,0:T(8,128)(2,1)S(1)} %get-tuple-element.60.refs_5_.refs_6_), channel_id=1, source_target_pairs={{0,1},{1,0},{2,3},{3,2},{4,5},{5,4},{6,7},{7,6},{8,9},{9,8},{10,11... | collective-permute-start | bytes 786440 | tf_op jit(solution)/shard_map/ppermute | solution.py:377
  46.4 21.4 %collective-permute-start.8 = (bf16[1024,384]{1,0:T(8,128)(2,1)S(1)}, bf16[1024,384]{1,0:T(8,128)(2,1)S(1)}, u32[]{:S(2)}, u32[]{:S(2)}) collective-permute-start(bf16[1024,384]{1,0:T(8,128)(2,1)S(1)} %get-tuple-element.52.refs_2_), channel_id=1, source_target_pairs={{2,0},{6,4},{10,8},{14,12},{0,2},{4,6},{8,10},{12,14},{3,1},{7,5},... | collective-permute-start | bytes 2359304 | tf_op jit(solution)/shard_map/ppermute | solution.py:367
  50.0 12.9 %collective-permute-start.16 = (bf16[272,640]{1,0:T(8,128)(2,1)S(1)}, bf16[272,640]{1,0:T(8,128)(2,1)S(1)}, u32[]{:S(2)}, u32[]{:S(2)}) collective-permute-start(bf16[272,640]{1,0:T(8,128)(2,1)S(1)} %get-tuple-element.55.refs_0_), channel_id=1, source_target_pairs={{4,0},{6,2},{8,4},{10,6},{12,8},{14,10},{5,1},{7,3},{9,5},{11,7},{... | collective-permute-start | bytes 1044488 | tf_op jit(solution)/shard_map/ppermute | solution.py:367
  52.9 17.5 %collective-permute-start.18 = (bf16[272,640]{1,0:T(8,128)(2,1)S(1)}, bf16[272,640]{1,0:T(8,128)(2,1)S(1)}, u32[]{:S(2)}, u32[]{:S(2)}) collective-permute-start(bf16[272,640]{1,0:T(8,128)(2,1)S(1)} %get-tuple-element.64), channel_id=1, source_target_pairs={{4,0},{6,2},{8,4},{10,6},{12,8},{14,10},{5,1},{7,3},{9,5},{11,7},{... | collective-permute-start | bytes 1044488 | tf_op jit(solution)/shard_map/ppermute | solution.py:367
  65.2 18.7 %collective-permute-start.25 = (bf16[240,1280]{1,0:T(8,128)(2,1)S(1)}, bf16[240,1280]{1,0:T(8,128)(2,1)S(1)}, u32[]{:S(2)}, u32[]{:S(2)}) collective-permute-start(bf16[240,1280]{1,0:T(8,128)(2,1)S(1)} %get-tuple-element.63.refs_0_), channel_id=1, source_target_pairs={{4,0},{6,2},{8,4},{10,6},{12,8},{14,10},{5,1},{7,3},{9,5},{11,7},{... | collective-permute-start | bytes 1843208 | tf_op jit(solution)/shard_map/ppermute | solution.py:367
  70.5 1.6 %collective-permute-start.19 = (bf16[1024,128]{1,0:T(8,128)(2,1)S(1)}, bf16[1024,128]{1,0:T(8,128)(2,1)S(1)}, u32[]{:S(2)}, u32[]{:S(2)}) collective-permute-start(bf16[1024,128]{1,0:T(8,128)(2,1)S(1)} %get-tuple-element.65.refs_2_), channel_id=1, source_target_pairs={{0,1},{1,0},{2,3},{3,2},{4,5},{5,4},{6,7},{7,6},{8,9},{9,8},{10,11... | collective-permute-start | bytes 786440 | tf_op jit(solution)/shard_map/ppermute | solution.py:377
  70.6 1.9 %collective-permute-start.20 = (bf16[1024,128]{1,0:T(8,128)(2,1)S(1)}, bf16[1024,128]{1,0:T(8,128)(2,1)S(1)}, u32[]{:S(2)}, u32[]{:S(2)}) collective-permute-start(bf16[1024,128]{1,0:T(8,128)(2,1)S(1)} %get-tuple-element.66.refs_4_), channel_id=1, source_target_pairs={{0,1},{1,0},{2,3},{3,2},{4,5},{5,4},{6,7},{7,6},{8,9},{9,8},{10,11... | collective-permute-start | bytes 786440 | tf_op jit(solution)/shard_map/ppermute | solution.py:377
  71.1 1.8 %collective-permute-start.21 = (bf16[1024,128]{1,0:T(8,128)(2,1)S(1)}, bf16[1024,128]{1,0:T(8,128)(2,1)S(1)}, u32[]{:S(2)}, u32[]{:S(2)}) collective-permute-start(bf16[1024,128]{1,0:T(8,128)(2,1)S(1)} %get-tuple-element.67.refs_6_), channel_id=1, source_target_pairs={{0,1},{1,0},{2,3},{3,2},{4,5},{5,4},{6,7},{7,6},{8,9},{9,8},{10,11... | collective-permute-start | bytes 786440 | tf_op jit(solution)/shard_map/ppermute | solution.py:377
  74.6 16.2 %collective-permute-start.22 = (bf16[512,384]{1,0:T(8,128)(2,1)S(1)}, bf16[512,384]{1,0:T(8,128)(2,1)S(1)}, u32[]{:S(2)}, u32[]{:S(2)}) collective-permute-start(bf16[512,384]{1,0:T(8,128)(2,1)S(1)} %get-tuple-element.69), channel_id=1, source_target_pairs={{4,0},{6,2},{8,4},{10,6},{12,8},{14,10},{5,1},{7,3},{9,5},{11,7},{... | collective-permute-start | bytes 1179656 | tf_op jit(solution)/shard_map/ppermute | solution.py:367
  76.1 9.5 %collective-permute-start.23 = (bf16[1024,128]{1,0:T(8,128)(2,1)S(1)}, bf16[1024,128]{1,0:T(8,128)(2,1)S(1)}, u32[]{:S(2)}, u32[]{:S(2)}) collective-permute-start(bf16[1024,128]{1,0:T(8,128)(2,1)S(1)} %get-tuple-element.71.refs_2_), channel_id=1, source_target_pairs={{0,1},{1,0},{2,3},{3,2},{4,5},{5,4},{6,7},{7,6},{8,9},{9,8},{10,11... | collective-permute-start | bytes 786440 | tf_op jit(solution)/shard_map/ppermute | solution.py:377
  78.3 7.4 %collective-permute-start.24 = (bf16[1024,128]{1,0:T(8,128)(2,1)S(1)}, bf16[1024,128]{1,0:T(8,128)(2,1)S(1)}, u32[]{:S(2)}, u32[]{:S(2)}) collective-permute-start(bf16[1024,128]{1,0:T(8,128)(2,1)S(1)} %get-tuple-element.72.refs_4_), channel_id=1, source_target_pairs={{0,1},{1,0},{2,3},{3,2},{4,5},{5,4},{6,7},{7,6},{8,9},{9,8},{10,11... | collective-permute-start | bytes 786440 | tf_op jit(solution)/shard_map/ppermute | solution.py:377
  85.5 1.6 %collective-permute-start.26 = (bf16[1024,128]{1,0:T(8,128)(2,1)S(1)}, bf16[1024,128]{1,0:T(8,128)(2,1)S(1)}, u32[]{:S(2)}, u32[]{:S(2)}) collective-permute-start(bf16[1024,128]{1,0:T(8,128)(2,1)S(1)} %get-tuple-element.75.refs_6_), channel_id=1, source_target_pairs={{0,1},{1,0},{2,3},{3,2},{4,5},{5,4},{6,7},{7,6},{8,9},{9,8},{10,11... | collective-permute-start | bytes 786440 | tf_op jit(solution)/shard_map/ppermute | solution.py:377

commit v16 on v15

--- a/solution.py
+++ b/solution.py
@@ -403,9 +403,8 @@
     made, buffer = far(place, buffer, [below0], own, samples)
     top2 = send(made, down)
     across, buffer, next_detoured = choose(place, around, across, (buffer,))
-    high = []
-    for piece in split(next_direct, (made, next_detoured, swapped), 3):
-        high += [piece, mate(piece)]
+    (next_direct,) = hold((made, next_detoured, swapped), next_direct)
+    high = [next_direct, mate(next_direct)]
     high += [next_detoured, mate(next_detoured)]
     made, buffer = far(place, buffer, [below0], high, samples)
     top3 = send(made, down)

time: 92.5 us -> 91.3 us (0.987)
    ppermute x16 -> x14, waiting for transfers between devices: 4.1 us -> 3.35 us  [mate(): return lax.ppermute(shard, 'samp', [(0, 1), (1, 0)])]
    ppermute x16 -> x14, starting transfers between devices: 4.01 us -> 3.31 us  [mate(): return lax.ppermute(shard, 'samp', [(0, 1), (1, 0)])]
  transfers between devices with their start and end apart: 27 -> 25, of which waited for: 17 -> 15; matrix products, arithmetic and copies ran while one was open for 0% -> 0% of each run, Pallas kernels for 30% -> 30%
where the time goes in v16:
time: 91.3 us; the launch traced here: 91 us
  Pallas kernels  33.4 us (37%)
  waiting for transfers between devices  29.6 us (32%)
  starting transfers between devices  27 us (30%)
    ppermute x11, waiting for transfers between devices, send(): return lax.ppermute(shard, 'var', pairs)  26.3 us
    ppermute x11, starting transfers between devices, send(): return lax.ppermute(shard, 'var', pairs)  23.6 us
    pallas_call x7, Pallas kernels, tile(): pl.pallas_call(functools.partial(tile_kernel, k, len(rows), len(rights),...  16.7 us
    pallas_call x4, Pallas kernels, far(): pl.pallas_call(functools.partial(far_kernel, 1.0 / samples, len(rows), le...  7.26 us
    ppermute x14, waiting for transfers between devices, mate(): return lax.ppermute(shard, 'samp', [(0, 1), (1, 0)])  3.35 us
    ppermute x14, starting transfers between devices, mate(): return lax.ppermute(shard, 'samp', [(0, 1), (1, 0)])  3.31 us
    pallas_call x1, Pallas kernels, stats(): pl.pallas_call(stats_kernel, in_specs=[pl.BlockSpec(memory_space=pltpu.HB...  3.08 us
  transfers between devices with their start and end apart: 25, of which 15 were waited for; matrix products, arithmetic and copies ran while one was open for 0% of the time, Pallas kernels for 30%

profile of v16, /device:TPU:0, one launch (start us, length us, event | category | flops | bytes accessed | tf_op | source)
XLA Modules:
  0.0 91.0 jit_solution(14033378598464633709)
XLA Ops:
  0.0 3.1 %shard_map.37 = (f32[8,1024]{1,0:T(8,128)S(1)}, bf16[1024,1024]{1,0:T(8,128)(2,1)S(1)}) custom-call(bf16[1024,1024]{1,0:T(8,128)(2,1)} %dosage_hbm.1, s32[1024,1024]{1,0:T(8,128)} %observed_hbm.1), custom_call_target="tpu_custom_call" | custom-call | flops 1000 | bytes 1000 | tf_op jit(solution)/shard_map/pallas_call | solution.py:60
  3.1 0.5 collective-permute-start
  4.3 0.1 pad_add_fusion.place_ref.refs_0_
  4.3 0.1 collective-permute-done.sums_other_ref
  4.5 1.8 %shard_map.38 = (bf16[1024,384]{1,0:T(8,128)(2,1)S(1)}, bf16[1024,384]{1,0:T(8,128)(2,1)S(1)}, bf16[1024,256]{1,0:T(8,128)(2,1)S(1)}, bf16[1024,384]{1,0:T(8,128...) custom-call(s32[3]{0:T(128)S(1)} %pad_add_fusion.place_ref.refs_0_, ...), custom_call_target="tpu_custom_call" | custom-call | flops 1000 | bytes 1000 | tf_op jit(solution)/shard_map/pallas_call | solution.py:118
  6.2 0.4 collective-permute-start.1
  6.7 1.3 %collective-permute-start.5 = (bf16[1024,384]{1,0:T(8,128)(2,1)S(1)}, bf16[1024,384]{1,0:T(8,128)(2,1)S(1)}, u32[]{:S(2)}, u32[]{:S(2)}) collective-permute-start(bf16[1024,384]{1,0:T(8,128)(2,1)S(1)} %get-tuple-element.45.odd_ref.refs_2_), channel_id=1, source_target_pairs={{4,0},{6,2},{8,4},{10,6},{12,8},{14,10},{5,1},{7,3},{9,5},{11,7},{... | collective-permute-start | bytes 2359304 | tf_op jit(solution)/shard_map/ppermute | solution.py:367
  7.9 2.7 %collective-permute-start.9 = (bf16[1024,256]{1,0:T(8,128)(2,1)S(1)}, bf16[1024,256]{1,0:T(8,128)(2,1)S(1)}, u32[]{:S(2)}, u32[]{:S(2)}) collective-permute-start(bf16[1024,256]{1,0:T(8,128)(2,1)S(1)} %get-tuple-element.46.refs_2_.refs_3_.refs_7_), channel_id=1, source_target_pairs={{2,0},{6,4},{10,8},{14,12},{0,2},{4,6},{8,10},{12,14},{3,1},{7,5},... | collective-permute-start | bytes 1572872 | tf_op jit(solution)/shard_map/ppermute | solution.py:367
  10.7 0.0 collective-permute-done.1.arrived_ref
  10.7 0.1 shard_map.39
  10.8 4.6 %collective-permute-start.2 = (bf16[544,1024]{1,0:T(8,128)(2,1)S(1)}, bf16[544,1024]{1,0:T(8,128)(2,1)S(1)}, u32[]{:S(2)}, u32[]{:S(2)}) collective-permute-start(bf16[544,1024]{1,0:T(8,128)(2,1)S(1)} %get-tuple-element.42.refs_0_), channel_id=1, source_target_pairs={{0,4},{2,6},{4,8},{6,10},{8,12},{10,14},{1,5},{3,7},{5,9},{7,11},{... | collective-permute-start | bytes 3342344 | tf_op jit(solution)/shard_map/ppermute | solution.py:367
  15.4 0.1 collective-permute-start.3
  15.5 0.5 collective-permute-start.7
  16.0 7.1 %collective-permute-done.9.refs_1_.refs_0_ = bf16[1024,256]{1,0:T(8,128)(2,1)S(1)} collective-permute-done((bf16[1024,256]{1,0:T(8,128)(2,1)S(1)}, bf16[1024,256]{1,0:T(8,128)(2,1)S(1)}, u32[]{:S(2)}, u32[]{:S(2)}) %collective-permute-start.9) | collective-permute-done | bytes 524320 | tf_op jit(solution)/shard_map/ppermute | solution.py:367
  23.1 1.3 %collective-permute-start.11 = (bf16[1024,384]{1,0:T(8,128)(2,1)S(1)}, bf16[1024,384]{1,0:T(8,128)(2,1)S(1)}, u32[]{:S(2)}, u32[]{:S(2)}) collective-permute-start(bf16[1024,384]{1,0:T(8,128)(2,1)S(1)} %shard_map.48), channel_id=1, source_target_pairs={{2,0},{4,2},{6,4},{8,6},{10,8},{12,10},{14,12},{3,1},{5,3},{7,5},{... | collective-permute-start | bytes 2359304 | tf_op jit(solution)/shard_map/ppermute | solution.py:367
  24.4 5.2 %collective-permute-done.5.even_ref.refs_0_ = bf16[1024,384]{1,0:T(8,128)(2,1)S(1)} collective-permute-done((bf16[1024,384]{1,0:T(8,128)(2,1)S(1)}, bf16[1024,384]{1,0:T(8,128)(2,1)S(1)}, u32[]{:S(2)}, u32[]{:S(2)}) %collective-permute-start.5) | collective-permute-done | bytes 786464 | tf_op jit(solution)/shard_map/ppermute | solution.py:367
  29.6 0.0 collective-permute-start.6
  29.6 0.0 collective-permute-done.3.arrived_ref
  29.6 0.7 collective-permute-start.10
  30.3 0.1 shard_map.40.refs_1_
  30.4 0.0 collective-permute-done.7.refs_3_.refs_2_.refs_6_
  30.4 4.0 %collective-permute-start.4 = (bf16[480,1024]{1,0:T(8,128)(2,1)S(1)}, bf16[480,1024]{1,0:T(8,128)(2,1)S(1)}, u32[]{:S(2)}, u32[]{:S(2)}) collective-permute-start(bf16[480,1024]{1,0:T(8,128)(2,1)S(1)} %shard_map.40.refs_1_), channel_id=1, source_target_pairs={{0,4},{2,6},{4,8},{6,10},{8,12},{10,14},{1,5},{3,7},{5,9},{7,11},{... | collective-permute-start | bytes 2949128 | tf_op jit(solution)/shard_map/ppermute | solution.py:367
  34.4 2.5 %shard_map.41.refs_4_ = bf16[4,512,1024]{2,1,0:T(8,128)(2,1)} custom-call(s32[3]{0:T(128)S(1)} %pad_add_fusion.place_ref.refs_0_, bf16[544,1024]{1,0:T(8,128)(2,1)S(1)} %get-tuple-element.42.refs_0_, bf16[480,1024]{1,0:T(8,128)(2,1)S(1)} %shard_map.40.refs_1_, ...), custom_call_target="tpu_custom_call", output_to_operand_aliasing={{}: (5, {})} | custom-call | flops 1000 | bytes 1000 | tf_op jit(solution)/shard_map/pallas_call | solution.py:192
  36.9 2.0 %shard_map.42.refs_0_ = bf16[4,512,1024]{2,1,0:T(8,128)(2,1)} custom-call(s32[3]{0:T(128)S(1)} %pad_add_fusion.place_ref.refs_0_, bf16[544,1024]{1,0:T(8,128)(2,1)S(1)} %get-tuple-element.42.refs_0_, bf16[480,1024]{1,0:T(8,128)(2,1)S(1)} %shard_map.40.refs_1_, ...), custom_call_target="tpu_custom_call", output_to_operand_aliasing={{}: (5, {})} | custom-call | flops 1000 | bytes 1000 | tf_op jit(solution)/shard_map/pallas_call | solution.py:192
  38.9 0.6 shard_map.43
  39.5 0.7 collective-permute-done.2.refs_0_
  40.3 1.6 %shard_map.45 = (bf16[272,640]{1,0:T(8,128)(2,1)S(1)}, bf16[4,512,1024]{2,1,0:T(8,128)(2,1)}) custom-call(s32[3]{0:T(128)S(1)} %pad_add_fusion.place_ref.refs_0_, bf16[544,1024]{1,0:T(8,128)(2,1)S(1)} %collective-permute-done.2.refs_0_, bf16[1024,384]{1,0:T(8,128)(2,1)S(1)} %get-tuple-element.47.refs_2_.refs_1_.refs_5_, ...), custom_call_target="tpu_custom_call", output_to_operand_aliasing={{1}: (6, {})} | custom-call | flops 1000 | bytes 1000 | tf_op jit(solution)/shard_map/pallas_call | solution.py:213
  41.9 0.6 shard_map.47
  42.5 1.8 %collective-permute-done.11.refs_3_ = bf16[1024,384]{1,0:T(8,128)(2,1)S(1)} collective-permute-done((bf16[1024,384]{1,0:T(8,128)(2,1)S(1)}, bf16[1024,384]{1,0:T(8,128)(2,1)S(1)}, u32[]{:S(2)}, u32[]{:S(2)}) %collective-permute-start.11) | collective-permute-done | bytes 786464 | tf_op jit(solution)/shard_map/ppermute | solution.py:367
  44.3 0.5 collective-permute-start.13
  44.8 0.0 collective-permute-start.15
  44.8 3.7 %collective-permute-start.8 = (bf16[1024,384]{1,0:T(8,128)(2,1)S(1)}, bf16[1024,384]{1,0:T(8,128)(2,1)S(1)}, u32[]{:S(2)}, u32[]{:S(2)}) collective-permute-start(bf16[1024,384]{1,0:T(8,128)(2,1)S(1)} %get-tuple-element.49.refs_2_), channel_id=1, source_target_pairs={{2,0},{6,4},{10,8},{14,12},{0,2},{4,6},{8,10},{12,14},{3,1},{7,5},... | collective-permute-start | bytes 2359304 | tf_op jit(solution)/shard_map/ppermute | solution.py:367
  48.5 1.3 %collective-permute-start.14 = (bf16[272,640]{1,0:T(8,128)(2,1)S(1)}, bf16[272,640]{1,0:T(8,128)(2,1)S(1)}, u32[]{:S(2)}, u32[]{:S(2)}) collective-permute-start(bf16[272,640]{1,0:T(8,128)(2,1)S(1)} %get-tuple-element.51.refs_0_), channel_id=1, source_target_pairs={{4,0},{6,2},{8,4},{10,6},{12,8},{14,10},{5,1},{7,3},{9,5},{11,7},{... | collective-permute-start | bytes 1044488 | tf_op jit(solution)/shard_map/ppermute | solution.py:367
  49.8 1.6 %shard_map.50 = (bf16[272,640]{1,0:T(8,128)(2,1)S(1)}, bf16[4,512,1024]{2,1,0:T(8,128)(2,1)}) custom-call(s32[3]{0:T(128)S(1)} %pad_add_fusion.place_ref.refs_0_, bf16[544,1024]{1,0:T(8,128)(2,1)S(1)} %collective-permute-done.2.refs_0_, bf16[1024,384]{1,0:T(8,128)(2,1)S(1)} %shard_map.49.refs_1_.refs_2_, ...), custom_call_target="tpu_custom_call", output_to_operand_aliasing={{1}: (6, {})} | custom-call | flops 1000 | bytes 1000 | tf_op jit(solution)/shard_map/pallas_call | solution.py:213
  51.4 1.5 %collective-permute-start.16 = (bf16[272,640]{1,0:T(8,128)(2,1)S(1)}, bf16[272,640]{1,0:T(8,128)(2,1)S(1)}, u32[]{:S(2)}, u32[]{:S(2)}) collective-permute-start(bf16[272,640]{1,0:T(8,128)(2,1)S(1)} %get-tuple-element.58), channel_id=1, source_target_pairs={{4,0},{6,2},{8,4},{10,6},{12,8},{14,10},{5,1},{7,3},{9,5},{11,7},{... | collective-permute-start | bytes 1044488 | tf_op jit(solution)/shard_map/ppermute | solution.py:367
  52.9 2.5 %shard_map.51.refs_4_ = bf16[4,512,1024]{2,1,0:T(8,128)(2,1)} custom-call(s32[3]{0:T(128)S(1)} %pad_add_fusion.place_ref.refs_0_, bf16[544,1024]{1,0:T(8,128)(2,1)S(1)} %get-tuple-element.42.refs_0_, bf16[480,1024]{1,0:T(8,128)(2,1)S(1)} %shard_map.40.refs_1_, bf16[1024,384]{1,0:T(8,128)(2,1)S(1)} %shard_map.49.refs_1_.refs_2_, ...), custom_call_target="tpu_custom_call", output_to_operand_aliasing={{}: (5, {})} | custom-call | flops 1000 | bytes 1000 | tf_op jit(solution)/shard_map/pallas_call | solution.py:192
  55.4 2.6 %shard_map.52.refs_2_ = bf16[4,512,1024]{2,1,0:T(8,128)(2,1)} custom-call(s32[3]{0:T(128)S(1)} %pad_add_fusion.place_ref.refs_0_, bf16[544,1024]{1,0:T(8,128)(2,1)S(1)} %get-tuple-element.42.refs_0_, bf16[480,1024]{1,0:T(8,128)(2,1)S(1)} %shard_map.40.refs_1_, ...), custom_call_target="tpu_custom_call", output_to_operand_aliasing={{}: (5, {})} | custom-call | flops 1000 | bytes 1000 | tf_op jit(solution)/shard_map/pallas_call | solution.py:192
  58.0 2.2 %collective-permute-done.4.refs_0_.refs_1_ = bf16[480,1024]{1,0:T(8,128)(2,1)S(1)} collective-permute-done((bf16[480,1024]{1,0:T(8,128)(2,1)S(1)}, bf16[480,1024]{1,0:T(8,128)(2,1)S(1)}, u32[]{:S(2)}, u32[]{:S(2)}) %collective-permute-start.4) | collective-permute-done | bytes 983072 | tf_op jit(solution)/shard_map/ppermute | solution.py:367
  60.1 1.2 %collective-permute-done.14.refs_1_ = bf16[272,640]{1,0:T(8,128)(2,1)S(1)} collective-permute-done((bf16[272,640]{1,0:T(8,128)(2,1)S(1)}, bf16[272,640]{1,0:T(8,128)(2,1)S(1)}, u32[]{:S(2)}, u32[]{:S(2)}) %collective-permute-start.14) | collective-permute-done | bytes 348192 | tf_op jit(solution)/shard_map/ppermute | solution.py:367
  61.4 2.3 %shard_map.54 = (bf16[240,1280]{1,0:T(8,128)(2,1)S(1)}, bf16[4,512,1024]{2,1,0:T(8,128)(2,1)}) custom-call(s32[3]{0:T(128)S(1)} %pad_add_fusion.place_ref.refs_0_, bf16[480,1024]{1,0:T(8,128)(2,1)S(1)} %collective-permute-done.4.refs_0_.refs_1_, bf16[1024,384]{1,0:T(8,128)(2,1)S(1)} %shard_map.49.refs_1_.refs_2_, ...), custom_call_target="tpu_custom_call", output_to_operand_aliasing={{1}: (10, {})} | custom-call | flops 1000 | bytes 1000 | tf_op jit(solution)/shard_map/pallas_call | solution.py:213
  63.7 1.3 %collective-permute-start.23 = (bf16[240,1280]{1,0:T(8,128)(2,1)S(1)}, bf16[240,1280]{1,0:T(8,128)(2,1)S(1)}, u32[]{:S(2)}, u32[]{:S(2)}) collective-permute-start(bf16[240,1280]{1,0:T(8,128)(2,1)S(1)} %get-tuple-element.57.refs_0_), channel_id=1, source_target_pairs={{4,0},{6,2},{8,4},{10,6},{12,8},{14,10},{5,1},{7,3},{9,5},{11,7},{... | collective-permute-start | bytes 1843208 | tf_op jit(solution)/shard_map/ppermute | solution.py:367
  65.0 1.7 %collective-permute-done.8.whole_ref = bf16[1024,384]{1,0:T(8,128)(2,1)S(1)} collective-permute-done((bf16[1024,384]{1,0:T(8,128)(2,1)S(1)}, bf16[1024,384]{1,0:T(8,128)(2,1)S(1)}, u32[]{:S(2)}, u32[]{:S(2)}) %collective-permute-start.8) | collective-permute-done | bytes 786464 | tf_op jit(solution)/shard_map/ppermute | solution.py:367
  66.6 2.2 %collective-permute-done.16.refs_1_.refs_2_ = bf16[272,640]{1,0:T(8,128)(2,1)S(1)} collective-permute-done((bf16[272,640]{1,0:T(8,128)(2,1)S(1)}, bf16[272,640]{1,0:T(8,128)(2,1)S(1)}, u32[]{:S(2)}, u32[]{:S(2)}) %collective-permute-start.16) | collective-permute-done | bytes 348192 | tf_op jit(solution)/shard_map/ppermute | solution.py:367
  68.8 0.1 shard_map.55
  69.0 0.1 collective-permute-start.17
  69.1 0.5 collective-permute-start.18
  69.6 0.1 collective-permute-start.19
  69.6 0.9 %collective-permute-done.17.refs_3_ = bf16[1024,128]{1,0:T(8,128)(2,1)S(1)} collective-permute-done((bf16[1024,128]{1,0:T(8,128)(2,1)S(1)}, bf16[1024,128]{1,0:T(8,128)(2,1)S(1)}, u32[]{:S(2)}, u32[]{:S(2)}) %collective-permute-start.17) | collective-permute-done | bytes 262176 | tf_op jit(solution)/shard_map/ppermute | solution.py:377
  70.6 0.4 collective-permute-done.18.refs_5_
  71.0 0.4 collective-permute-done.19.refs_7_
  71.3 1.8 %shard_map.56 = (bf16[512,384]{1,0:T(8,128)(2,1)S(1)}, bf16[4,512,1024]{2,1,0:T(8,128)(2,1)}) custom-call(s32[3]{0:T(128)S(1)} %pad_add_fusion.place_ref.refs_0_, bf16[544,1024]{1,0:T(8,128)(2,1)S(1)} %collective-permute-done.2.refs_0_, bf16[480,1024]{1,0:T(8,128)(2,1)S(1)} %collective-permute-done.4.refs_0_.refs_1_, ...), custom_call_target="tpu_custom_call", output_to_operand_aliasing={{1}: (9, {})} | custom-call | flops 1000 | bytes 1000 | tf_op jit(solution)/shard_map/pallas_call | solution.py:213
  73.1 1.3 %collective-permute-start.20 = (bf16[512,384]{1,0:T(8,128)(2,1)S(1)}, bf16[512,384]{1,0:T(8,128)(2,1)S(1)}, u32[]{:S(2)}, u32[]{:S(2)}) collective-permute-start(bf16[512,384]{1,0:T(8,128)(2,1)S(1)} %get-tuple-element.63), channel_id=1, source_target_pairs={{4,0},{6,2},{8,4},{10,6},{12,8},{14,10},{5,1},{7,3},{9,5},{11,7},{... | collective-permute-start | bytes 1179656 | tf_op jit(solution)/shard_map/ppermute | solution.py:367
  74.4 0.1 shard_map.57
  74.6 0.2 collective-permute-start.21
  74.8 2.0 %shard_map.58.refs_8_ = bf16[4,512,1024]{2,1,0:T(8,128)(2,1)} custom-call(s32[3]{0:T(128)S(1)} %pad_add_fusion.place_ref.refs_0_, bf16[544,1024]{1,0:T(8,128)(2,1)S(1)} %get-tuple-element.42.refs_0_, bf16[480,1024]{1,0:T(8,128)(2,1)S(1)} %shard_map.40.refs_1_, ...), custom_call_target="tpu_custom_call", output_to_operand_aliasing={{}: (5, {})} | custom-call | flops 1000 | bytes 1000 | tf_op jit(solution)/shard_map/pallas_call | solution.py:192
  76.8 0.4 collective-permute-start.22
  77.1 2.6 %shard_map.59.refs_5_ = bf16[4,512,1024]{2,1,0:T(8,128)(2,1)} custom-call(s32[3]{0:T(128)S(1)} %pad_add_fusion.place_ref.refs_0_, bf16[544,1024]{1,0:T(8,128)(2,1)S(1)} %get-tuple-element.42.refs_0_, bf16[480,1024]{1,0:T(8,128)(2,1)S(1)} %shard_map.40.refs_1_, bf16[1024,128]{1,0:T(8,128)(2,1)S(1)} %get-tuple-element.59.refs_2_, ...), custom_call_target="tpu_custom_call", output_to_operand_aliasing={{}: (9, {})} | custom-call | flops 1000 | bytes 1000 | tf_op jit(solution)/shard_map/pallas_call | solution.py:192
  79.7 2.7 %collective-permute-done.23.refs_3_ = bf16[240,1280]{1,0:T(8,128)(2,1)S(1)} collective-permute-done((bf16[240,1280]{1,0:T(8,128)(2,1)S(1)}, bf16[240,1280]{1,0:T(8,128)(2,1)S(1)}, u32[]{:S(2)}, u32[]{:S(2)}) %collective-permute-start.23) | collective-permute-done | bytes 614432 | tf_op jit(solution)/shard_map/ppermute | solution.py:367
  82.4 1.7 %shard_map.60 = (bf16[1024,128]{1,0:T(8,128)(2,1)S(1)}, bf16[4,512,1024]{2,1,0:T(8,128)(2,1)}) custom-call(s32[3]{0:T(128)S(1)} %pad_add_fusion.place_ref.refs_0_, bf16[272,640]{1,0:T(8,128)(2,1)S(1)} %collective-permute-done.14.refs_1_, bf16[272,640]{1,0:T(8,128)(2,1)S(1)} %collective-permute-done.16.refs_1_.refs_2_, ...), custom_call_target="tpu_custom_call", output_to_operand_aliasing={{0}: (4, {}), {1}: (5, {})} | custom-call | flops 1000 | bytes 1000 | tf_op jit(solution)/shard_map/pallas_call | solution.py:320
  84.0 0.1 collective-permute-start.24
  84.1 1.5 %collective-permute-done.24.refs_7_ = bf16[1024,128]{1,0:T(8,128)(2,1)S(1)} collective-permute-done((bf16[1024,128]{1,0:T(8,128)(2,1)S(1)}, bf16[1024,128]{1,0:T(8,128)(2,1)S(1)}, u32[]{:S(2)}, u32[]{:S(2)}) %collective-permute-start.24) | collective-permute-done | bytes 262176 | tf_op jit(solution)/shard_map/ppermute | solution.py:377
  85.6 2.6 %shard_map.61.buffer_ref = bf16[4,512,1024]{2,1,0:T(8,128)(2,1)} custom-call(s32[3]{0:T(128)S(1)} %pad_add_fusion.place_ref.refs_0_, bf16[544,1024]{1,0:T(8,128)(2,1)S(1)} %get-tuple-element.42.refs_0_, bf16[480,1024]{1,0:T(8,128)(2,1)S(1)} %shard_map.40.refs_1_, bf16[1024,128]{1,0:T(8,128)(2,1)S(1)} %get-tuple-element.65.refs_2_, ...), custom_call_target="tpu_custom_call", output_to_operand_aliasing={{}: (9, {})} | custom-call | flops 1000 | bytes 1000 | tf_op jit(solution)/shard_map/pallas_call | solution.py:192
  88.2 1.4 %collective-permute-done.20.side = bf16[512,384]{1,0:T(8,128)(2,1)S(1)} collective-permute-done((bf16[512,384]{1,0:T(8,128)(2,1)S(1)}, bf16[512,384]{1,0:T(8,128)(2,1)S(1)}, u32[]{:S(2)}, u32[]{:S(2)}) %collective-permute-start.20) | collective-permute-done | bytes 393248 | tf_op jit(solution)/shard_map/ppermute | solution.py:367
  89.7 1.3 %shard_map.62 = bf16[4,512,1024]{2,1,0:T(8,128)(2,1)} custom-call(s32[3]{0:T(128)S(1)} %pad_add_fusion.place_ref.refs_0_, bf16[512,384]{1,0:T(8,128)(2,1)S(1)} %collective-permute-done.20.side, bf16[4,512,1024]{2,1,0:T(8,128)(2,1)} %shard_map.61.buffer_ref), custom_call_target="tpu_custom_call", output_to_operand_aliasing={{}: (2, {})} | custom-call | flops 1000 | bytes 1000 | tf_op jit(solution)/shard_map/pallas_call | solution.py:342
  (13 shorter events, 0.0 us)
Async XLA Ops:
  3.1 1.4 %collective-permute-start = (f32[8,1024]{1,0:T(8,128)S(1)}, f32[8,1024]{1,0:T(8,128)S(1)}, u32[]{:S(2)}, u32[]{:S(2)}) collective-permute-start(f32[8,1024]{1,0:T(8,128)S(1)} %get-tuple-element.39.sums_ref), channel_id=1, source_target_pairs={{0,1},{1,0},{2,3},{3,2},{4,5},{5,4},{6,7},{7,6},{8,9},{9,8},{10,11... | collective-permute-start | bytes 98312 | tf_op jit(solution)/shard_map/ppermute | solution.py:377
  6.2 4.5 %collective-permute-start.1 = (bf16[272,1024]{1,0:T(8,128)(2,1)S(1)}, bf16[272,1024]{1,0:T(8,128)(2,1)S(1)}, u32[]{:S(2)}, u32[]{:S(2)}) collective-permute-start(bf16[272,1024]{1,0:T(8,128)(2,1)S(1)} %get-tuple-element.41), channel_id=1, source_target_pairs={{0,1},{1,0},{2,3},{3,2},{4,5},{5,4},{6,7},{7,6},{8,9},{9,8},{10,11... | collective-permute-start | bytes 1671176 | tf_op jit(solution)/shard_map/ppermute | solution.py:377
  6.7 22.9 %collective-permute-start.5 = (bf16[1024,384]{1,0:T(8,128)(2,1)S(1)}, bf16[1024,384]{1,0:T(8,128)(2,1)S(1)}, u32[]{:S(2)}, u32[]{:S(2)}) collective-permute-start(bf16[1024,384]{1,0:T(8,128)(2,1)S(1)} %get-tuple-element.45.odd_ref.refs_2_), channel_id=1, source_target_pairs={{4,0},{6,2},{8,4},{10,6},{12,8},{14,10},{5,1},{7,3},{9,5},{11,7},{... | collective-permute-start | bytes 2359304 | tf_op jit(solution)/shard_map/ppermute | solution.py:367
  7.9 15.2 %collective-permute-start.9 = (bf16[1024,256]{1,0:T(8,128)(2,1)S(1)}, bf16[1024,256]{1,0:T(8,128)(2,1)S(1)}, u32[]{:S(2)}, u32[]{:S(2)}) collective-permute-start(bf16[1024,256]{1,0:T(8,128)(2,1)S(1)} %get-tuple-element.46.refs_2_.refs_3_.refs_7_), channel_id=1, source_target_pairs={{2,0},{6,4},{10,8},{14,12},{0,2},{4,6},{8,10},{12,14},{3,1},{7,5},... | collective-permute-start | bytes 1572872 | tf_op jit(solution)/shard_map/ppermute | solution.py:367
  10.8 29.5 %collective-permute-start.2 = (bf16[544,1024]{1,0:T(8,128)(2,1)S(1)}, bf16[544,1024]{1,0:T(8,128)(2,1)S(1)}, u32[]{:S(2)}, u32[]{:S(2)}) collective-permute-start(bf16[544,1024]{1,0:T(8,128)(2,1)S(1)} %get-tuple-element.42.refs_0_), channel_id=1, source_target_pairs={{0,4},{2,6},{4,8},{6,10},{8,12},{10,14},{1,5},{3,7},{5,9},{7,11},{... | collective-permute-start | bytes 3342344 | tf_op jit(solution)/shard_map/ppermute | solution.py:367
  15.4 14.2 %collective-permute-start.3 = (bf16[240,1024]{1,0:T(8,128)(2,1)S(1)}, bf16[240,1024]{1,0:T(8,128)(2,1)S(1)}, u32[]{:S(2)}, u32[]{:S(2)}) collective-permute-start(bf16[240,1024]{1,0:T(8,128)(2,1)S(1)} %get-tuple-element.44), channel_id=1, source_target_pairs={{0,1},{1,0},{2,3},{3,2},{4,5},{5,4},{6,7},{7,6},{8,9},{9,8},{10,11... | collective-permute-start | bytes 1474568 | tf_op jit(solution)/shard_map/ppermute | solution.py:377
  15.5 14.9 %collective-permute-start.7 = (bf16[1024,384]{1,0:T(8,128)(2,1)S(1)}, bf16[1024,384]{1,0:T(8,128)(2,1)S(1)}, u32[]{:S(2)}, u32[]{:S(2)}) collective-permute-start(bf16[1024,384]{1,0:T(8,128)(2,1)S(1)} %get-tuple-element.47.refs_2_.refs_1_.refs_5_), channel_id=1, source_target_pairs={{0,1},{1,0},{2,3},{3,2},{4,5},{5,4},{6,7},{7,6},{8,9},{9,8},{10,11... | collective-permute-start | bytes 2359304 | tf_op jit(solution)/shard_map/ppermute | solution.py:377
  23.1 21.2 %collective-permute-start.11 = (bf16[1024,384]{1,0:T(8,128)(2,1)S(1)}, bf16[1024,384]{1,0:T(8,128)(2,1)S(1)}, u32[]{:S(2)}, u32[]{:S(2)}) collective-permute-start(bf16[1024,384]{1,0:T(8,128)(2,1)S(1)} %shard_map.48), channel_id=1, source_target_pairs={{2,0},{4,2},{6,4},{8,6},{10,8},{12,10},{14,12},{3,1},{5,3},{7,5},{... | collective-permute-start | bytes 2359304 | tf_op jit(solution)/shard_map/ppermute | solution.py:367
  29.6 7.4 %collective-permute-start.6 = (bf16[1024,256]{1,0:T(8,128)(2,1)S(1)}, bf16[1024,256]{1,0:T(8,128)(2,1)S(1)}, u32[]{:S(2)}, u32[]{:S(2)}) collective-permute-start(bf16[1024,256]{1,0:T(8,128)(2,1)S(1)} %get-tuple-element.46.refs_2_.refs_3_.refs_7_), channel_id=1, source_target_pairs={{0,1},{1,0},{2,3},{3,2},{4,5},{5,4},{6,7},{7,6},{8,9},{9,8},{10,11... | collective-permute-start | bytes 1572872 | tf_op jit(solution)/shard_map/ppermute | solution.py:377
  29.6 12.3 %collective-permute-start.10 = (bf16[1024,256]{1,0:T(8,128)(2,1)S(1)}, bf16[1024,256]{1,0:T(8,128)(2,1)S(1)}, u32[]{:S(2)}, u32[]{:S(2)}) collective-permute-start(bf16[1024,256]{1,0:T(8,128)(2,1)S(1)} %shard_map.46.even_ref), channel_id=1, source_target_pairs={{6,2},{10,6},{14,10},{7,3},{11,7},{15,11},{22,18},{26,22},{30,26},... | collective-permute-start | bytes 1572872 | tf_op jit(solution)/shard_map/ppermute | solution.py:367
  30.4 29.8 %collective-permute-start.4 = (bf16[480,1024]{1,0:T(8,128)(2,1)S(1)}, bf16[480,1024]{1,0:T(8,128)(2,1)S(1)}, u32[]{:S(2)}, u32[]{:S(2)}) collective-permute-start(bf16[480,1024]{1,0:T(8,128)(2,1)S(1)} %shard_map.40.refs_1_), channel_id=1, source_target_pairs={{0,4},{2,6},{4,8},{6,10},{8,12},{10,14},{1,5},{3,7},{5,9},{7,11},{... | collective-permute-start | bytes 2949128 | tf_op jit(solution)/shard_map/ppermute | solution.py:367
  44.3 5.5 %collective-permute-start.12 = (bf16[1024,384]{1,0:T(8,128)(2,1)S(1)}, bf16[1024,384]{1,0:T(8,128)(2,1)S(1)}, u32[]{:S(2)}, u32[]{:S(2)}) collective-permute-start(bf16[1024,384]{1,0:T(8,128)(2,1)S(1)} %shard_map.49.refs_1_.refs_2_), channel_id=1, source_target_pairs={{0,1},{1,0},{2,3},{3,2},{4,5},{5,4},{6,7},{7,6},{8,9},{9,8},{10,11... | collective-permute-start | bytes 2359304 | tf_op jit(solution)/shard_map/ppermute | solution.py:377
  44.3 4.2 %collective-permute-start.13 = (bf16[1024,256]{1,0:T(8,128)(2,1)S(1)}, bf16[1024,256]{1,0:T(8,128)(2,1)S(1)}, u32[]{:S(2)}, u32[]{:S(2)}) collective-permute-start(bf16[1024,256]{1,0:T(8,128)(2,1)S(1)} %get-tuple-element.53.refs_1_.refs_3_.refs_2_), channel_id=1, source_target_pairs={{0,1},{1,0},{2,3},{3,2},{4,5},{5,4},{6,7},{7,6},{8,9},{9,8},{10,11... | collective-permute-start | bytes 1572872 | tf_op jit(solution)/shard_map/ppermute | solution.py:377
  44.8 10.6 %collective-permute-start.15 = (bf16[1024,384]{1,0:T(8,128)(2,1)S(1)}, bf16[1024,384]{1,0:T(8,128)(2,1)S(1)}, u32[]{:S(2)}, u32[]{:S(2)}) collective-permute-start(bf16[1024,384]{1,0:T(8,128)(2,1)S(1)} %get-tuple-element.45.odd_ref.refs_2_), channel_id=1, source_target_pairs={{0,1},{1,0},{2,3},{3,2},{4,5},{5,4},{6,7},{7,6},{8,9},{9,8},{10,11... | collective-permute-start | bytes 2359304 | tf_op jit(solution)/shard_map/ppermute | solution.py:377
  44.8 21.8 %collective-permute-start.8 = (bf16[1024,384]{1,0:T(8,128)(2,1)S(1)}, bf16[1024,384]{1,0:T(8,128)(2,1)S(1)}, u32[]{:S(2)}, u32[]{:S(2)}) collective-permute-start(bf16[1024,384]{1,0:T(8,128)(2,1)S(1)} %get-tuple-element.49.refs_2_), channel_id=1, source_target_pairs={{2,0},{6,4},{10,8},{14,12},{0,2},{4,6},{8,10},{12,14},{3,1},{7,5},... | collective-permute-start | bytes 2359304 | tf_op jit(solution)/shard_map/ppermute | solution.py:367
  48.5 12.9 %collective-permute-start.14 = (bf16[272,640]{1,0:T(8,128)(2,1)S(1)}, bf16[272,640]{1,0:T(8,128)(2,1)S(1)}, u32[]{:S(2)}, u32[]{:S(2)}) collective-permute-start(bf16[272,640]{1,0:T(8,128)(2,1)S(1)} %get-tuple-element.51.refs_0_), channel_id=1, source_target_pairs={{4,0},{6,2},{8,4},{10,6},{12,8},{14,10},{5,1},{7,3},{9,5},{11,7},{... | collective-permute-start | bytes 1044488 | tf_op jit(solution)/shard_map/ppermute | solution.py:367
  51.4 17.4 %collective-permute-start.16 = (bf16[272,640]{1,0:T(8,128)(2,1)S(1)}, bf16[272,640]{1,0:T(8,128)(2,1)S(1)}, u32[]{:S(2)}, u32[]{:S(2)}) collective-permute-start(bf16[272,640]{1,0:T(8,128)(2,1)S(1)} %get-tuple-element.58), channel_id=1, source_target_pairs={{4,0},{6,2},{8,4},{10,6},{12,8},{14,10},{5,1},{7,3},{9,5},{11,7},{... | collective-permute-start | bytes 1044488 | tf_op jit(solution)/shard_map/ppermute | solution.py:367
  63.7 18.7 %collective-permute-start.23 = (bf16[240,1280]{1,0:T(8,128)(2,1)S(1)}, bf16[240,1280]{1,0:T(8,128)(2,1)S(1)}, u32[]{:S(2)}, u32[]{:S(2)}) collective-permute-start(bf16[240,1280]{1,0:T(8,128)(2,1)S(1)} %get-tuple-element.57.refs_0_), channel_id=1, source_target_pairs={{4,0},{6,2},{8,4},{10,6},{12,8},{14,10},{5,1},{7,3},{9,5},{11,7},{... | collective-permute-start | bytes 1843208 | tf_op jit(solution)/shard_map/ppermute | solution.py:367
  69.0 1.6 %collective-permute-start.17 = (bf16[1024,128]{1,0:T(8,128)(2,1)S(1)}, bf16[1024,128]{1,0:T(8,128)(2,1)S(1)}, u32[]{:S(2)}, u32[]{:S(2)}) collective-permute-start(bf16[1024,128]{1,0:T(8,128)(2,1)S(1)} %get-tuple-element.59.refs_2_), channel_id=1, source_target_pairs={{0,1},{1,0},{2,3},{3,2},{4,5},{5,4},{6,7},{7,6},{8,9},{9,8},{10,11... | collective-permute-start | bytes 786440 | tf_op jit(solution)/shard_map/ppermute | solution.py:377
  69.1 1.9 %collective-permute-start.18 = (bf16[1024,128]{1,0:T(8,128)(2,1)S(1)}, bf16[1024,128]{1,0:T(8,128)(2,1)S(1)}, u32[]{:S(2)}, u32[]{:S(2)}) collective-permute-start(bf16[1024,128]{1,0:T(8,128)(2,1)S(1)} %get-tuple-element.60.refs_4_), channel_id=1, source_target_pairs={{0,1},{1,0},{2,3},{3,2},{4,5},{5,4},{6,7},{7,6},{8,9},{9,8},{10,11... | collective-permute-start | bytes 786440 | tf_op jit(solution)/shard_map/ppermute | solution.py:377
  69.6 1.8 %collective-permute-start.19 = (bf16[1024,128]{1,0:T(8,128)(2,1)S(1)}, bf16[1024,128]{1,0:T(8,128)(2,1)S(1)}, u32[]{:S(2)}, u32[]{:S(2)}) collective-permute-start(bf16[1024,128]{1,0:T(8,128)(2,1)S(1)} %get-tuple-element.61.refs_6_), channel_id=1, source_target_pairs={{0,1},{1,0},{2,3},{3,2},{4,5},{5,4},{6,7},{7,6},{8,9},{9,8},{10,11... | collective-permute-start | bytes 786440 | tf_op jit(solution)/shard_map/ppermute | solution.py:377
  73.1 16.5 %collective-permute-start.20 = (bf16[512,384]{1,0:T(8,128)(2,1)S(1)}, bf16[512,384]{1,0:T(8,128)(2,1)S(1)}, u32[]{:S(2)}, u32[]{:S(2)}) collective-permute-start(bf16[512,384]{1,0:T(8,128)(2,1)S(1)} %get-tuple-element.63), channel_id=1, source_target_pairs={{4,0},{6,2},{8,4},{10,6},{12,8},{14,10},{5,1},{7,3},{9,5},{11,7},{... | collective-permute-start | bytes 1179656 | tf_op jit(solution)/shard_map/ppermute | solution.py:367
  74.6 9.5 %collective-permute-start.21 = (bf16[1024,128]{1,0:T(8,128)(2,1)S(1)}, bf16[1024,128]{1,0:T(8,128)(2,1)S(1)}, u32[]{:S(2)}, u32[]{:S(2)}) collective-permute-start(bf16[1024,128]{1,0:T(8,128)(2,1)S(1)} %get-tuple-element.65.refs_2_), channel_id=1, source_target_pairs={{0,1},{1,0},{2,3},{3,2},{4,5},{5,4},{6,7},{7,6},{8,9},{9,8},{10,11... | collective-permute-start | bytes 786440 | tf_op jit(solution)/shard_map/ppermute | solution.py:377
  76.8 7.4 %collective-permute-start.22 = (bf16[1024,128]{1,0:T(8,128)(2,1)S(1)}, bf16[1024,128]{1,0:T(8,128)(2,1)S(1)}, u32[]{:S(2)}, u32[]{:S(2)}) collective-permute-start(bf16[1024,128]{1,0:T(8,128)(2,1)S(1)} %get-tuple-element.66.refs_4_), channel_id=1, source_target_pairs={{0,1},{1,0},{2,3},{3,2},{4,5},{5,4},{6,7},{7,6},{8,9},{9,8},{10,11... | collective-permute-start | bytes 786440 | tf_op jit(solution)/shard_map/ppermute | solution.py:377
  84.0 1.6 %collective-permute-start.24 = (bf16[1024,128]{1,0:T(8,128)(2,1)S(1)}, bf16[1024,128]{1,0:T(8,128)(2,1)S(1)}, u32[]{:S(2)}, u32[]{:S(2)}) collective-permute-start(bf16[1024,128]{1,0:T(8,128)(2,1)S(1)} %get-tuple-element.69.refs_6_), channel_id=1, source_target_pairs={{0,1},{1,0},{2,3},{3,2},{4,5},{5,4},{6,7},{7,6},{8,9},{9,8},{10,11... | collective-permute-start | bytes 786440 | tf_op jit(solution)/shard_map/ppermute | solution.py:377

commit v17 on v16

--- a/solution.py
+++ b/solution.py
@@ -48,7 +48,7 @@
         present = observed_ref[at, :] > 0
         kept = jnp.where(present, values, 0.0)
         masked_ref[at, :] = jnp.where(present, values, -1.0).astype(masked_ref.dtype)
-        terms = [jnp.where(present, 1.0, 0.0), kept, kept * kept]
+        terms = [observed_ref[at, :].astype(jnp.float32), kept, kept * kept]
         totals = [total + fold(term) for total, term in zip(totals, terms)]
     for n in range(3):
         sums_ref[n : n + 1, :] = jnp.sum(totals[n], axis=0, keepdims=True)

time: 91.3 us -> 91.3 us (level)
  no operation moved by 1% of the time
where the time goes in v17:
time: 91.3 us; the launch traced here: 91 us
  Pallas kernels  33.4 us (37%)
  waiting for transfers between devices  29.6 us (32%)
  starting transfers between devices  27 us (30%)
    ppermute x11, waiting for transfers between devices, send(): return lax.ppermute(shard, 'var', pairs)  26.3 us
    ppermute x11, starting transfers between devices, send(): return lax.ppermute(shard, 'var', pairs)  23.6 us
    pallas_call x7, Pallas kernels, tile(): pl.pallas_call(functools.partial(tile_kernel, k, len(rows), len(rights),...  16.7 us
    pallas_call x4, Pallas kernels, far(): pl.pallas_call(functools.partial(far_kernel, 1.0 / samples, len(rows), le...  7.26 us
    ppermute x14, waiting for transfers between devices, mate(): return lax.ppermute(shard, 'samp', [(0, 1), (1, 0)])  3.35 us
    ppermute x14, starting transfers between devices, mate(): return lax.ppermute(shard, 'samp', [(0, 1), (1, 0)])  3.31 us
    pallas_call x1, Pallas kernels, stats(): pl.pallas_call(stats_kernel, in_specs=[pl.BlockSpec(memory_space=pltpu.HB...  3.09 us
  transfers between devices with their start and end apart: 25, of which 15 were waited for; matrix products, arithmetic and copies ran while one was open for 0% of the time, Pallas kernels for 30%

profile of v17, /device:TPU:0, one launch (start us, length us, event | category | flops | bytes accessed | tf_op | source)
XLA Modules:
  0.0 91.0 jit_solution(9881474504275923833)
XLA Ops:
  0.0 3.1 %shard_map.37 = (f32[8,1024]{1,0:T(8,128)S(1)}, bf16[1024,1024]{1,0:T(8,128)(2,1)S(1)}) custom-call(bf16[1024,1024]{1,0:T(8,128)(2,1)} %dosage_hbm.1, s32[1024,1024]{1,0:T(8,128)} %observed_hbm.1), custom_call_target="tpu_custom_call" | custom-call | flops 1000 | bytes 1000 | tf_op jit(solution)/shard_map/pallas_call | solution.py:60
  3.1 0.5 collective-permute-start
  4.3 0.1 pad_add_fusion.place_ref.refs_0_
  4.3 0.1 collective-permute-done.sums_other_ref
  4.5 1.8 %shard_map.38 = (bf16[1024,384]{1,0:T(8,128)(2,1)S(1)}, bf16[1024,384]{1,0:T(8,128)(2,1)S(1)}, bf16[1024,256]{1,0:T(8,128)(2,1)S(1)}, bf16[1024,384]{1,0:T(8,128...) custom-call(s32[3]{0:T(128)S(1)} %pad_add_fusion.place_ref.refs_0_, ...), custom_call_target="tpu_custom_call" | custom-call | flops 1000 | bytes 1000 | tf_op jit(solution)/shard_map/pallas_call | solution.py:118
  6.2 0.4 collective-permute-start.1
  6.7 1.3 %collective-permute-start.5 = (bf16[1024,384]{1,0:T(8,128)(2,1)S(1)}, bf16[1024,384]{1,0:T(8,128)(2,1)S(1)}, u32[]{:S(2)}, u32[]{:S(2)}) collective-permute-start(bf16[1024,384]{1,0:T(8,128)(2,1)S(1)} %get-tuple-element.45.odd_ref.refs_2_), channel_id=1, source_target_pairs={{4,0},{6,2},{8,4},{10,6},{12,8},{14,10},{5,1},{7,3},{9,5},{11,7},{... | collective-permute-start | bytes 2359304 | tf_op jit(solution)/shard_map/ppermute | solution.py:367
  8.0 2.7 %collective-permute-start.9 = (bf16[1024,256]{1,0:T(8,128)(2,1)S(1)}, bf16[1024,256]{1,0:T(8,128)(2,1)S(1)}, u32[]{:S(2)}, u32[]{:S(2)}) collective-permute-start(bf16[1024,256]{1,0:T(8,128)(2,1)S(1)} %get-tuple-element.46.refs_2_.refs_3_.refs_7_), channel_id=1, source_target_pairs={{2,0},{6,4},{10,8},{14,12},{0,2},{4,6},{8,10},{12,14},{3,1},{7,5},... | collective-permute-start | bytes 1572872 | tf_op jit(solution)/shard_map/ppermute | solution.py:367
  10.7 0.0 collective-permute-done.1.arrived_ref
  10.7 0.1 shard_map.39
  10.8 4.6 %collective-permute-start.2 = (bf16[544,1024]{1,0:T(8,128)(2,1)S(1)}, bf16[544,1024]{1,0:T(8,128)(2,1)S(1)}, u32[]{:S(2)}, u32[]{:S(2)}) collective-permute-start(bf16[544,1024]{1,0:T(8,128)(2,1)S(1)} %get-tuple-element.42.refs_0_), channel_id=1, source_target_pairs={{0,4},{2,6},{4,8},{6,10},{8,12},{10,14},{1,5},{3,7},{5,9},{7,11},{... | collective-permute-start | bytes 3342344 | tf_op jit(solution)/shard_map/ppermute | solution.py:367
  15.4 0.1 collective-permute-start.3
  15.5 0.5 collective-permute-start.7
  16.0 7.1 %collective-permute-done.9.refs_1_.refs_0_ = bf16[1024,256]{1,0:T(8,128)(2,1)S(1)} collective-permute-done((bf16[1024,256]{1,0:T(8,128)(2,1)S(1)}, bf16[1024,256]{1,0:T(8,128)(2,1)S(1)}, u32[]{:S(2)}, u32[]{:S(2)}) %collective-permute-start.9) | collective-permute-done | bytes 524320 | tf_op jit(solution)/shard_map/ppermute | solution.py:367
  23.1 1.3 %collective-permute-start.11 = (bf16[1024,384]{1,0:T(8,128)(2,1)S(1)}, bf16[1024,384]{1,0:T(8,128)(2,1)S(1)}, u32[]{:S(2)}, u32[]{:S(2)}) collective-permute-start(bf16[1024,384]{1,0:T(8,128)(2,1)S(1)} %shard_map.48), channel_id=1, source_target_pairs={{2,0},{4,2},{6,4},{8,6},{10,8},{12,10},{14,12},{3,1},{5,3},{7,5},{... | collective-permute-start | bytes 2359304 | tf_op jit(solution)/shard_map/ppermute | solution.py:367
  24.4 5.2 %collective-permute-done.5.even_ref.refs_0_ = bf16[1024,384]{1,0:T(8,128)(2,1)S(1)} collective-permute-done((bf16[1024,384]{1,0:T(8,128)(2,1)S(1)}, bf16[1024,384]{1,0:T(8,128)(2,1)S(1)}, u32[]{:S(2)}, u32[]{:S(2)}) %collective-permute-start.5) | collective-permute-done | bytes 786464 | tf_op jit(solution)/shard_map/ppermute | solution.py:367
  29.6 0.0 collective-permute-done.3.arrived_ref
  29.6 0.7 collective-permute-start.10
  30.3 0.1 shard_map.40.refs_1_
  30.4 4.0 %collective-permute-start.4 = (bf16[480,1024]{1,0:T(8,128)(2,1)S(1)}, bf16[480,1024]{1,0:T(8,128)(2,1)S(1)}, u32[]{:S(2)}, u32[]{:S(2)}) collective-permute-start(bf16[480,1024]{1,0:T(8,128)(2,1)S(1)} %shard_map.40.refs_1_), channel_id=1, source_target_pairs={{0,4},{2,6},{4,8},{6,10},{8,12},{10,14},{1,5},{3,7},{5,9},{7,11},{... | collective-permute-start | bytes 2949128 | tf_op jit(solution)/shard_map/ppermute | solution.py:367
  34.4 2.5 %shard_map.41.refs_4_ = bf16[4,512,1024]{2,1,0:T(8,128)(2,1)} custom-call(s32[3]{0:T(128)S(1)} %pad_add_fusion.place_ref.refs_0_, bf16[544,1024]{1,0:T(8,128)(2,1)S(1)} %get-tuple-element.42.refs_0_, bf16[480,1024]{1,0:T(8,128)(2,1)S(1)} %shard_map.40.refs_1_, ...), custom_call_target="tpu_custom_call", output_to_operand_aliasing={{}: (5, {})} | custom-call | flops 1000 | bytes 1000 | tf_op jit(solution)/shard_map/pallas_call | solution.py:192
  36.9 0.0 collective-permute-done.6.refs_3_.refs_4_.refs_8_
  37.0 2.0 %shard_map.42.refs_0_ = bf16[4,512,1024]{2,1,0:T(8,128)(2,1)} custom-call(s32[3]{0:T(128)S(1)} %pad_add_fusion.place_ref.refs_0_, bf16[544,1024]{1,0:T(8,128)(2,1)S(1)} %get-tuple-element.42.refs_0_, bf16[480,1024]{1,0:T(8,128)(2,1)S(1)} %shard_map.40.refs_1_, ...), custom_call_target="tpu_custom_call", output_to_operand_aliasing={{}: (5, {})} | custom-call | flops 1000 | bytes 1000 | tf_op jit(solution)/shard_map/pallas_call | solution.py:192
  38.9 0.6 shard_map.43
  39.5 0.7 collective-permute-done.2.refs_0_
  40.3 1.6 %shard_map.45 = (bf16[272,640]{1,0:T(8,128)(2,1)S(1)}, bf16[4,512,1024]{2,1,0:T(8,128)(2,1)}) custom-call(s32[3]{0:T(128)S(1)} %pad_add_fusion.place_ref.refs_0_, bf16[544,1024]{1,0:T(8,128)(2,1)S(1)} %collective-permute-done.2.refs_0_, bf16[1024,384]{1,0:T(8,128)(2,1)S(1)} %get-tuple-element.47.refs_2_.refs_1_.refs_5_, ...), custom_call_target="tpu_custom_call", output_to_operand_aliasing={{1}: (6, {})} | custom-call | flops 1000 | bytes 1000 | tf_op jit(solution)/shard_map/pallas_call | solution.py:213
  41.9 0.6 shard_map.47
  42.5 1.8 %collective-permute-done.11.refs_3_ = bf16[1024,384]{1,0:T(8,128)(2,1)S(1)} collective-permute-done((bf16[1024,384]{1,0:T(8,128)(2,1)S(1)}, bf16[1024,384]{1,0:T(8,128)(2,1)S(1)}, u32[]{:S(2)}, u32[]{:S(2)}) %collective-permute-start.11) | collective-permute-done | bytes 786464 | tf_op jit(solution)/shard_map/ppermute | solution.py:367
  44.3 0.5 collective-permute-start.13
  44.8 0.0 collective-permute-start.15
  44.8 3.7 %collective-permute-start.8 = (bf16[1024,384]{1,0:T(8,128)(2,1)S(1)}, bf16[1024,384]{1,0:T(8,128)(2,1)S(1)}, u32[]{:S(2)}, u32[]{:S(2)}) collective-permute-start(bf16[1024,384]{1,0:T(8,128)(2,1)S(1)} %get-tuple-element.49.refs_2_), channel_id=1, source_target_pairs={{2,0},{6,4},{10,8},{14,12},{0,2},{4,6},{8,10},{12,14},{3,1},{7,5},... | collective-permute-start | bytes 2359304 | tf_op jit(solution)/shard_map/ppermute | solution.py:367
  48.5 0.0 collective-permute-done.13.refs_4_.refs_3_
  48.5 1.3 %collective-permute-start.14 = (bf16[272,640]{1,0:T(8,128)(2,1)S(1)}, bf16[272,640]{1,0:T(8,128)(2,1)S(1)}, u32[]{:S(2)}, u32[]{:S(2)}) collective-permute-start(bf16[272,640]{1,0:T(8,128)(2,1)S(1)} %get-tuple-element.51.refs_0_), channel_id=1, source_target_pairs={{4,0},{6,2},{8,4},{10,6},{12,8},{14,10},{5,1},{7,3},{9,5},{11,7},{... | collective-permute-start | bytes 1044488 | tf_op jit(solution)/shard_map/ppermute | solution.py:367
  49.8 1.6 %shard_map.50 = (bf16[272,640]{1,0:T(8,128)(2,1)S(1)}, bf16[4,512,1024]{2,1,0:T(8,128)(2,1)}) custom-call(s32[3]{0:T(128)S(1)} %pad_add_fusion.place_ref.refs_0_, bf16[544,1024]{1,0:T(8,128)(2,1)S(1)} %collective-permute-done.2.refs_0_, bf16[1024,384]{1,0:T(8,128)(2,1)S(1)} %shard_map.49.refs_1_.refs_2_, ...), custom_call_target="tpu_custom_call", output_to_operand_aliasing={{1}: (6, {})} | custom-call | flops 1000 | bytes 1000 | tf_op jit(solution)/shard_map/pallas_call | solution.py:213
  51.4 1.5 %collective-permute-start.16 = (bf16[272,640]{1,0:T(8,128)(2,1)S(1)}, bf16[272,640]{1,0:T(8,128)(2,1)S(1)}, u32[]{:S(2)}, u32[]{:S(2)}) collective-permute-start(bf16[272,640]{1,0:T(8,128)(2,1)S(1)} %get-tuple-element.58), channel_id=1, source_target_pairs={{4,0},{6,2},{8,4},{10,6},{12,8},{14,10},{5,1},{7,3},{9,5},{11,7},{... | collective-permute-start | bytes 1044488 | tf_op jit(solution)/shard_map/ppermute | solution.py:367
  52.9 2.5 %shard_map.51.refs_4_ = bf16[4,512,1024]{2,1,0:T(8,128)(2,1)} custom-call(s32[3]{0:T(128)S(1)} %pad_add_fusion.place_ref.refs_0_, bf16[544,1024]{1,0:T(8,128)(2,1)S(1)} %get-tuple-element.42.refs_0_, bf16[480,1024]{1,0:T(8,128)(2,1)S(1)} %shard_map.40.refs_1_, bf16[1024,384]{1,0:T(8,128)(2,1)S(1)} %shard_map.49.refs_1_.refs_2_, ...), custom_call_target="tpu_custom_call", output_to_operand_aliasing={{}: (5, {})} | custom-call | flops 1000 | bytes 1000 | tf_op jit(solution)/shard_map/pallas_call | solution.py:192
  55.4 2.6 %shard_map.52.refs_2_ = bf16[4,512,1024]{2,1,0:T(8,128)(2,1)} custom-call(s32[3]{0:T(128)S(1)} %pad_add_fusion.place_ref.refs_0_, bf16[544,1024]{1,0:T(8,128)(2,1)S(1)} %get-tuple-element.42.refs_0_, bf16[480,1024]{1,0:T(8,128)(2,1)S(1)} %shard_map.40.refs_1_, ...), custom_call_target="tpu_custom_call", output_to_operand_aliasing={{}: (5, {})} | custom-call | flops 1000 | bytes 1000 | tf_op jit(solution)/shard_map/pallas_call | solution.py:192
  58.0 2.2 %collective-permute-done.4.refs_0_.refs_1_ = bf16[480,1024]{1,0:T(8,128)(2,1)S(1)} collective-permute-done((bf16[480,1024]{1,0:T(8,128)(2,1)S(1)}, bf16[480,1024]{1,0:T(8,128)(2,1)S(1)}, u32[]{:S(2)}, u32[]{:S(2)}) %collective-permute-start.4) | collective-permute-done | bytes 983072 | tf_op jit(solution)/shard_map/ppermute | solution.py:367
  60.1 1.2 %collective-permute-done.14.refs_1_ = bf16[272,640]{1,0:T(8,128)(2,1)S(1)} collective-permute-done((bf16[272,640]{1,0:T(8,128)(2,1)S(1)}, bf16[272,640]{1,0:T(8,128)(2,1)S(1)}, u32[]{:S(2)}, u32[]{:S(2)}) %collective-permute-start.14) | collective-permute-done | bytes 348192 | tf_op jit(solution)/shard_map/ppermute | solution.py:367
  61.4 2.3 %shard_map.54 = (bf16[240,1280]{1,0:T(8,128)(2,1)S(1)}, bf16[4,512,1024]{2,1,0:T(8,128)(2,1)}) custom-call(s32[3]{0:T(128)S(1)} %pad_add_fusion.place_ref.refs_0_, bf16[480,1024]{1,0:T(8,128)(2,1)S(1)} %collective-permute-done.4.refs_0_.refs_1_, bf16[1024,384]{1,0:T(8,128)(2,1)S(1)} %shard_map.49.refs_1_.refs_2_, ...), custom_call_target="tpu_custom_call", output_to_operand_aliasing={{1}: (10, {})} | custom-call | flops 1000 | bytes 1000 | tf_op jit(solution)/shard_map/pallas_call | solution.py:213
  63.7 1.3 %collective-permute-start.23 = (bf16[240,1280]{1,0:T(8,128)(2,1)S(1)}, bf16[240,1280]{1,0:T(8,128)(2,1)S(1)}, u32[]{:S(2)}, u32[]{:S(2)}) collective-permute-start(bf16[240,1280]{1,0:T(8,128)(2,1)S(1)} %get-tuple-element.57.refs_0_), channel_id=1, source_target_pairs={{4,0},{6,2},{8,4},{10,6},{12,8},{14,10},{5,1},{7,3},{9,5},{11,7},{... | collective-permute-start | bytes 1843208 | tf_op jit(solution)/shard_map/ppermute | solution.py:367
  65.0 1.7 %collective-permute-done.8.whole_ref = bf16[1024,384]{1,0:T(8,128)(2,1)S(1)} collective-permute-done((bf16[1024,384]{1,0:T(8,128)(2,1)S(1)}, bf16[1024,384]{1,0:T(8,128)(2,1)S(1)}, u32[]{:S(2)}, u32[]{:S(2)}) %collective-permute-start.8) | collective-permute-done | bytes 786464 | tf_op jit(solution)/shard_map/ppermute | solution.py:367
  66.6 2.2 %collective-permute-done.16.refs_1_.refs_2_ = bf16[272,640]{1,0:T(8,128)(2,1)S(1)} collective-permute-done((bf16[272,640]{1,0:T(8,128)(2,1)S(1)}, bf16[272,640]{1,0:T(8,128)(2,1)S(1)}, u32[]{:S(2)}, u32[]{:S(2)}) %collective-permute-start.16) | collective-permute-done | bytes 348192 | tf_op jit(solution)/shard_map/ppermute | solution.py:367
  68.8 0.1 shard_map.55
  69.0 0.1 collective-permute-start.17
  69.1 0.5 collective-permute-start.18
  69.6 0.1 collective-permute-start.19
  69.6 0.9 %collective-permute-done.17.refs_3_ = bf16[1024,128]{1,0:T(8,128)(2,1)S(1)} collective-permute-done((bf16[1024,128]{1,0:T(8,128)(2,1)S(1)}, bf16[1024,128]{1,0:T(8,128)(2,1)S(1)}, u32[]{:S(2)}, u32[]{:S(2)}) %collective-permute-start.17) | collective-permute-done | bytes 262176 | tf_op jit(solution)/shard_map/ppermute | solution.py:377
  70.6 0.4 collective-permute-done.18.refs_5_
  71.0 0.4 collective-permute-done.19.refs_7_
  71.3 1.8 %shard_map.56 = (bf16[512,384]{1,0:T(8,128)(2,1)S(1)}, bf16[4,512,1024]{2,1,0:T(8,128)(2,1)}) custom-call(s32[3]{0:T(128)S(1)} %pad_add_fusion.place_ref.refs_0_, bf16[544,1024]{1,0:T(8,128)(2,1)S(1)} %collective-permute-done.2.refs_0_, bf16[480,1024]{1,0:T(8,128)(2,1)S(1)} %collective-permute-done.4.refs_0_.refs_1_, ...), custom_call_target="tpu_custom_call", output_to_operand_aliasing={{1}: (9, {})} | custom-call | flops 1000 | bytes 1000 | tf_op jit(solution)/shard_map/pallas_call | solution.py:213
  73.2 1.3 %collective-permute-start.20 = (bf16[512,384]{1,0:T(8,128)(2,1)S(1)}, bf16[512,384]{1,0:T(8,128)(2,1)S(1)}, u32[]{:S(2)}, u32[]{:S(2)}) collective-permute-start(bf16[512,384]{1,0:T(8,128)(2,1)S(1)} %get-tuple-element.63), channel_id=1, source_target_pairs={{4,0},{6,2},{8,4},{10,6},{12,8},{14,10},{5,1},{7,3},{9,5},{11,7},{... | collective-permute-start | bytes 1179656 | tf_op jit(solution)/shard_map/ppermute | solution.py:367
  74.5 0.1 shard_map.57
  74.6 0.2 collective-permute-start.21
  74.8 2.0 %shard_map.58.refs_8_ = bf16[4,512,1024]{2,1,0:T(8,128)(2,1)} custom-call(s32[3]{0:T(128)S(1)} %pad_add_fusion.place_ref.refs_0_, bf16[544,1024]{1,0:T(8,128)(2,1)S(1)} %get-tuple-element.42.refs_0_, bf16[480,1024]{1,0:T(8,128)(2,1)S(1)} %shard_map.40.refs_1_, ...), custom_call_target="tpu_custom_call", output_to_operand_aliasing={{}: (5, {})} | custom-call | flops 1000 | bytes 1000 | tf_op jit(solution)/shard_map/pallas_call | solution.py:192
  76.8 0.4 collective-permute-start.22
  77.1 2.6 %shard_map.59.refs_5_ = bf16[4,512,1024]{2,1,0:T(8,128)(2,1)} custom-call(s32[3]{0:T(128)S(1)} %pad_add_fusion.place_ref.refs_0_, bf16[544,1024]{1,0:T(8,128)(2,1)S(1)} %get-tuple-element.42.refs_0_, bf16[480,1024]{1,0:T(8,128)(2,1)S(1)} %shard_map.40.refs_1_, bf16[1024,128]{1,0:T(8,128)(2,1)S(1)} %get-tuple-element.59.refs_2_, ...), custom_call_target="tpu_custom_call", output_to_operand_aliasing={{}: (9, {})} | custom-call | flops 1000 | bytes 1000 | tf_op jit(solution)/shard_map/pallas_call | solution.py:192
  79.7 2.7 %collective-permute-done.23.refs_3_ = bf16[240,1280]{1,0:T(8,128)(2,1)S(1)} collective-permute-done((bf16[240,1280]{1,0:T(8,128)(2,1)S(1)}, bf16[240,1280]{1,0:T(8,128)(2,1)S(1)}, u32[]{:S(2)}, u32[]{:S(2)}) %collective-permute-start.23) | collective-permute-done | bytes 614432 | tf_op jit(solution)/shard_map/ppermute | solution.py:367
  82.4 1.7 %shard_map.60 = (bf16[1024,128]{1,0:T(8,128)(2,1)S(1)}, bf16[4,512,1024]{2,1,0:T(8,128)(2,1)}) custom-call(s32[3]{0:T(128)S(1)} %pad_add_fusion.place_ref.refs_0_, bf16[272,640]{1,0:T(8,128)(2,1)S(1)} %collective-permute-done.14.refs_1_, bf16[272,640]{1,0:T(8,128)(2,1)S(1)} %collective-permute-done.16.refs_1_.refs_2_, ...), custom_call_target="tpu_custom_call", output_to_operand_aliasing={{0}: (4, {}), {1}: (5, {})} | custom-call | flops 1000 | bytes 1000 | tf_op jit(solution)/shard_map/pallas_call | solution.py:320
  84.1 0.1 collective-permute-start.24
  84.2 1.5 %collective-permute-done.24.refs_7_ = bf16[1024,128]{1,0:T(8,128)(2,1)S(1)} collective-permute-done((bf16[1024,128]{1,0:T(8,128)(2,1)S(1)}, bf16[1024,128]{1,0:T(8,128)(2,1)S(1)}, u32[]{:S(2)}, u32[]{:S(2)}) %collective-permute-start.24) | collective-permute-done | bytes 262176 | tf_op jit(solution)/shard_map/ppermute | solution.py:377
  85.7 2.6 %shard_map.61.buffer_ref = bf16[4,512,1024]{2,1,0:T(8,128)(2,1)} custom-call(s32[3]{0:T(128)S(1)} %pad_add_fusion.place_ref.refs_0_, bf16[544,1024]{1,0:T(8,128)(2,1)S(1)} %get-tuple-element.42.refs_0_, bf16[480,1024]{1,0:T(8,128)(2,1)S(1)} %shard_map.40.refs_1_, bf16[1024,128]{1,0:T(8,128)(2,1)S(1)} %get-tuple-element.65.refs_2_, ...), custom_call_target="tpu_custom_call", output_to_operand_aliasing={{}: (9, {})} | custom-call | flops 1000 | bytes 1000 | tf_op jit(solution)/shard_map/pallas_call | solution.py:192
  88.2 1.4 %collective-permute-done.20.side = bf16[512,384]{1,0:T(8,128)(2,1)S(1)} collective-permute-done((bf16[512,384]{1,0:T(8,128)(2,1)S(1)}, bf16[512,384]{1,0:T(8,128)(2,1)S(1)}, u32[]{:S(2)}, u32[]{:S(2)}) %collective-permute-start.20) | collective-permute-done | bytes 393248 | tf_op jit(solution)/shard_map/ppermute | solution.py:367
  89.7 1.3 %shard_map.62 = bf16[4,512,1024]{2,1,0:T(8,128)(2,1)} custom-call(s32[3]{0:T(128)S(1)} %pad_add_fusion.place_ref.refs_0_, bf16[512,384]{1,0:T(8,128)(2,1)S(1)} %collective-permute-done.20.side, bf16[4,512,1024]{2,1,0:T(8,128)(2,1)} %shard_map.61.buffer_ref), custom_call_target="tpu_custom_call", output_to_operand_aliasing={{}: (2, {})} | custom-call | flops 1000 | bytes 1000 | tf_op jit(solution)/shard_map/pallas_call | solution.py:342
  (13 shorter events, 0.0 us)
Async XLA Ops:
  3.1 1.4 %collective-permute-start = (f32[8,1024]{1,0:T(8,128)S(1)}, f32[8,1024]{1,0:T(8,128)S(1)}, u32[]{:S(2)}, u32[]{:S(2)}) collective-permute-start(f32[8,1024]{1,0:T(8,128)S(1)} %get-tuple-element.39.sums_ref), channel_id=1, source_target_pairs={{0,1},{1,0},{2,3},{3,2},{4,5},{5,4},{6,7},{7,6},{8,9},{9,8},{10,11... | collective-permute-start | bytes 98312 | tf_op jit(solution)/shard_map/ppermute | solution.py:377
  6.2 4.5 %collective-permute-start.1 = (bf16[272,1024]{1,0:T(8,128)(2,1)S(1)}, bf16[272,1024]{1,0:T(8,128)(2,1)S(1)}, u32[]{:S(2)}, u32[]{:S(2)}) collective-permute-start(bf16[272,1024]{1,0:T(8,128)(2,1)S(1)} %get-tuple-element.41), channel_id=1, source_target_pairs={{0,1},{1,0},{2,3},{3,2},{4,5},{5,4},{6,7},{7,6},{8,9},{9,8},{10,11... | collective-permute-start | bytes 1671176 | tf_op jit(solution)/shard_map/ppermute | solution.py:377
  6.7 22.9 %collective-permute-start.5 = (bf16[1024,384]{1,0:T(8,128)(2,1)S(1)}, bf16[1024,384]{1,0:T(8,128)(2,1)S(1)}, u32[]{:S(2)}, u32[]{:S(2)}) collective-permute-start(bf16[1024,384]{1,0:T(8,128)(2,1)S(1)} %get-tuple-element.45.odd_ref.refs_2_), channel_id=1, source_target_pairs={{4,0},{6,2},{8,4},{10,6},{12,8},{14,10},{5,1},{7,3},{9,5},{11,7},{... | collective-permute-start | bytes 2359304 | tf_op jit(solution)/shard_map/ppermute | solution.py:367
  8.0 15.2 %collective-permute-start.9 = (bf16[1024,256]{1,0:T(8,128)(2,1)S(1)}, bf16[1024,256]{1,0:T(8,128)(2,1)S(1)}, u32[]{:S(2)}, u32[]{:S(2)}) collective-permute-start(bf16[1024,256]{1,0:T(8,128)(2,1)S(1)} %get-tuple-element.46.refs_2_.refs_3_.refs_7_), channel_id=1, source_target_pairs={{2,0},{6,4},{10,8},{14,12},{0,2},{4,6},{8,10},{12,14},{3,1},{7,5},... | collective-permute-start | bytes 1572872 | tf_op jit(solution)/shard_map/ppermute | solution.py:367
  10.8 29.5 %collective-permute-start.2 = (bf16[544,1024]{1,0:T(8,128)(2,1)S(1)}, bf16[544,1024]{1,0:T(8,128)(2,1)S(1)}, u32[]{:S(2)}, u32[]{:S(2)}) collective-permute-start(bf16[544,1024]{1,0:T(8,128)(2,1)S(1)} %get-tuple-element.42.refs_0_), channel_id=1, source_target_pairs={{0,4},{2,6},{4,8},{6,10},{8,12},{10,14},{1,5},{3,7},{5,9},{7,11},{... | collective-permute-start | bytes 3342344 | tf_op jit(solution)/shard_map/ppermute | solution.py:367
  15.4 14.2 %collective-permute-start.3 = (bf16[240,1024]{1,0:T(8,128)(2,1)S(1)}, bf16[240,1024]{1,0:T(8,128)(2,1)S(1)}, u32[]{:S(2)}, u32[]{:S(2)}) collective-permute-start(bf16[240,1024]{1,0:T(8,128)(2,1)S(1)} %get-tuple-element.44), channel_id=1, source_target_pairs={{0,1},{1,0},{2,3},{3,2},{4,5},{5,4},{6,7},{7,6},{8,9},{9,8},{10,11... | collective-permute-start | bytes 1474568 | tf_op jit(solution)/shard_map/ppermute | solution.py:377
  15.5 14.9 %collective-permute-start.7 = (bf16[1024,384]{1,0:T(8,128)(2,1)S(1)}, bf16[1024,384]{1,0:T(8,128)(2,1)S(1)}, u32[]{:S(2)}, u32[]{:S(2)}) collective-permute-start(bf16[1024,384]{1,0:T(8,128)(2,1)S(1)} %get-tuple-element.47.refs_2_.refs_1_.refs_5_), channel_id=1, source_target_pairs={{0,1},{1,0},{2,3},{3,2},{4,5},{5,4},{6,7},{7,6},{8,9},{9,8},{10,11... | collective-permute-start | bytes 2359304 | tf_op jit(solution)/shard_map/ppermute | solution.py:377
  23.1 21.2 %collective-permute-start.11 = (bf16[1024,384]{1,0:T(8,128)(2,1)S(1)}, bf16[1024,384]{1,0:T(8,128)(2,1)S(1)}, u32[]{:S(2)}, u32[]{:S(2)}) collective-permute-start(bf16[1024,384]{1,0:T(8,128)(2,1)S(1)} %shard_map.48), channel_id=1, source_target_pairs={{2,0},{4,2},{6,4},{8,6},{10,8},{12,10},{14,12},{3,1},{5,3},{7,5},{... | collective-permute-start | bytes 2359304 | tf_op jit(solution)/shard_map/ppermute | solution.py:367
  29.6 7.4 %collective-permute-start.6 = (bf16[1024,256]{1,0:T(8,128)(2,1)S(1)}, bf16[1024,256]{1,0:T(8,128)(2,1)S(1)}, u32[]{:S(2)}, u32[]{:S(2)}) collective-permute-start(bf16[1024,256]{1,0:T(8,128)(2,1)S(1)} %get-tuple-element.46.refs_2_.refs_3_.refs_7_), channel_id=1, source_target_pairs={{0,1},{1,0},{2,3},{3,2},{4,5},{5,4},{6,7},{7,6},{8,9},{9,8},{10,11... | collective-permute-start | bytes 1572872 | tf_op jit(solution)/shard_map/ppermute | solution.py:377
  29.6 12.3 %collective-permute-start.10 = (bf16[1024,256]{1,0:T(8,128)(2,1)S(1)}, bf16[1024,256]{1,0:T(8,128)(2,1)S(1)}, u32[]{:S(2)}, u32[]{:S(2)}) collective-permute-start(bf16[1024,256]{1,0:T(8,128)(2,1)S(1)} %shard_map.46.even_ref), channel_id=1, source_target_pairs={{6,2},{10,6},{14,10},{7,3},{11,7},{15,11},{22,18},{26,22},{30,26},... | collective-permute-start | bytes 1572872 | tf_op jit(solution)/shard_map/ppermute | solution.py:367
  30.4 29.8 %collective-permute-start.4 = (bf16[480,1024]{1,0:T(8,128)(2,1)S(1)}, bf16[480,1024]{1,0:T(8,128)(2,1)S(1)}, u32[]{:S(2)}, u32[]{:S(2)}) collective-permute-start(bf16[480,1024]{1,0:T(8,128)(2,1)S(1)} %shard_map.40.refs_1_), channel_id=1, source_target_pairs={{0,4},{2,6},{4,8},{6,10},{8,12},{10,14},{1,5},{3,7},{5,9},{7,11},{... | collective-permute-start | bytes 2949128 | tf_op jit(solution)/shard_map/ppermute | solution.py:367
  44.3 5.5 %collective-permute-start.12 = (bf16[1024,384]{1,0:T(8,128)(2,1)S(1)}, bf16[1024,384]{1,0:T(8,128)(2,1)S(1)}, u32[]{:S(2)}, u32[]{:S(2)}) collective-permute-start(bf16[1024,384]{1,0:T(8,128)(2,1)S(1)} %shard_map.49.refs_1_.refs_2_), channel_id=1, source_target_pairs={{0,1},{1,0},{2,3},{3,2},{4,5},{5,4},{6,7},{7,6},{8,9},{9,8},{10,11... | collective-permute-start | bytes 2359304 | tf_op jit(solution)/shard_map/ppermute | solution.py:377
  44.3 4.2 %collective-permute-start.13 = (bf16[1024,256]{1,0:T(8,128)(2,1)S(1)}, bf16[1024,256]{1,0:T(8,128)(2,1)S(1)}, u32[]{:S(2)}, u32[]{:S(2)}) collective-permute-start(bf16[1024,256]{1,0:T(8,128)(2,1)S(1)} %get-tuple-element.53.refs_1_.refs_3_.refs_2_), channel_id=1, source_target_pairs={{0,1},{1,0},{2,3},{3,2},{4,5},{5,4},{6,7},{7,6},{8,9},{9,8},{10,11... | collective-permute-start | bytes 1572872 | tf_op jit(solution)/shard_map/ppermute | solution.py:377
  44.8 10.6 %collective-permute-start.15 = (bf16[1024,384]{1,0:T(8,128)(2,1)S(1)}, bf16[1024,384]{1,0:T(8,128)(2,1)S(1)}, u32[]{:S(2)}, u32[]{:S(2)}) collective-permute-start(bf16[1024,384]{1,0:T(8,128)(2,1)S(1)} %get-tuple-element.45.odd_ref.refs_2_), channel_id=1, source_target_pairs={{0,1},{1,0},{2,3},{3,2},{4,5},{5,4},{6,7},{7,6},{8,9},{9,8},{10,11... | collective-permute-start | bytes 2359304 | tf_op jit(solution)/shard_map/ppermute | solution.py:377
  44.8 21.8 %collective-permute-start.8 = (bf16[1024,384]{1,0:T(8,128)(2,1)S(1)}, bf16[1024,384]{1,0:T(8,128)(2,1)S(1)}, u32[]{:S(2)}, u32[]{:S(2)}) collective-permute-start(bf16[1024,384]{1,0:T(8,128)(2,1)S(1)} %get-tuple-element.49.refs_2_), channel_id=1, source_target_pairs={{2,0},{6,4},{10,8},{14,12},{0,2},{4,6},{8,10},{12,14},{3,1},{7,5},... | collective-permute-start | bytes 2359304 | tf_op jit(solution)/shard_map/ppermute | solution.py:367
  48.5 12.9 %collective-permute-start.14 = (bf16[272,640]{1,0:T(8,128)(2,1)S(1)}, bf16[272,640]{1,0:T(8,128)(2,1)S(1)}, u32[]{:S(2)}, u32[]{:S(2)}) collective-permute-start(bf16[272,640]{1,0:T(8,128)(2,1)S(1)} %get-tuple-element.51.refs_0_), channel_id=1, source_target_pairs={{4,0},{6,2},{8,4},{10,6},{12,8},{14,10},{5,1},{7,3},{9,5},{11,7},{... | collective-permute-start | bytes 1044488 | tf_op jit(solution)/shard_map/ppermute | solution.py:367
  51.4 17.4 %collective-permute-start.16 = (bf16[272,640]{1,0:T(8,128)(2,1)S(1)}, bf16[272,640]{1,0:T(8,128)(2,1)S(1)}, u32[]{:S(2)}, u32[]{:S(2)}) collective-permute-start(bf16[272,640]{1,0:T(8,128)(2,1)S(1)} %get-tuple-element.58), channel_id=1, source_target_pairs={{4,0},{6,2},{8,4},{10,6},{12,8},{14,10},{5,1},{7,3},{9,5},{11,7},{... | collective-permute-start | bytes 1044488 | tf_op jit(solution)/shard_map/ppermute | solution.py:367
  63.7 18.7 %collective-permute-start.23 = (bf16[240,1280]{1,0:T(8,128)(2,1)S(1)}, bf16[240,1280]{1,0:T(8,128)(2,1)S(1)}, u32[]{:S(2)}, u32[]{:S(2)}) collective-permute-start(bf16[240,1280]{1,0:T(8,128)(2,1)S(1)} %get-tuple-element.57.refs_0_), channel_id=1, source_target_pairs={{4,0},{6,2},{8,4},{10,6},{12,8},{14,10},{5,1},{7,3},{9,5},{11,7},{... | collective-permute-start | bytes 1843208 | tf_op jit(solution)/shard_map/ppermute | solution.py:367
  69.0 1.6 %collective-permute-start.17 = (bf16[1024,128]{1,0:T(8,128)(2,1)S(1)}, bf16[1024,128]{1,0:T(8,128)(2,1)S(1)}, u32[]{:S(2)}, u32[]{:S(2)}) collective-permute-start(bf16[1024,128]{1,0:T(8,128)(2,1)S(1)} %get-tuple-element.59.refs_2_), channel_id=1, source_target_pairs={{0,1},{1,0},{2,3},{3,2},{4,5},{5,4},{6,7},{7,6},{8,9},{9,8},{10,11... | collective-permute-start | bytes 786440 | tf_op jit(solution)/shard_map/ppermute | solution.py:377
  69.1 1.9 %collective-permute-start.18 = (bf16[1024,128]{1,0:T(8,128)(2,1)S(1)}, bf16[1024,128]{1,0:T(8,128)(2,1)S(1)}, u32[]{:S(2)}, u32[]{:S(2)}) collective-permute-start(bf16[1024,128]{1,0:T(8,128)(2,1)S(1)} %get-tuple-element.60.refs_4_), channel_id=1, source_target_pairs={{0,1},{1,0},{2,3},{3,2},{4,5},{5,4},{6,7},{7,6},{8,9},{9,8},{10,11... | collective-permute-start | bytes 786440 | tf_op jit(solution)/shard_map/ppermute | solution.py:377
  69.6 1.8 %collective-permute-start.19 = (bf16[1024,128]{1,0:T(8,128)(2,1)S(1)}, bf16[1024,128]{1,0:T(8,128)(2,1)S(1)}, u32[]{:S(2)}, u32[]{:S(2)}) collective-permute-start(bf16[1024,128]{1,0:T(8,128)(2,1)S(1)} %get-tuple-element.61.refs_6_), channel_id=1, source_target_pairs={{0,1},{1,0},{2,3},{3,2},{4,5},{5,4},{6,7},{7,6},{8,9},{9,8},{10,11... | collective-permute-start | bytes 786440 | tf_op jit(solution)/shard_map/ppermute | solution.py:377
  73.2 16.5 %collective-permute-start.20 = (bf16[512,384]{1,0:T(8,128)(2,1)S(1)}, bf16[512,384]{1,0:T(8,128)(2,1)S(1)}, u32[]{:S(2)}, u32[]{:S(2)}) collective-permute-start(bf16[512,384]{1,0:T(8,128)(2,1)S(1)} %get-tuple-element.63), channel_id=1, source_target_pairs={{4,0},{6,2},{8,4},{10,6},{12,8},{14,10},{5,1},{7,3},{9,5},{11,7},{... | collective-permute-start | bytes 1179656 | tf_op jit(solution)/shard_map/ppermute | solution.py:367
  74.6 9.5 %collective-permute-start.21 = (bf16[1024,128]{1,0:T(8,128)(2,1)S(1)}, bf16[1024,128]{1,0:T(8,128)(2,1)S(1)}, u32[]{:S(2)}, u32[]{:S(2)}) collective-permute-start(bf16[1024,128]{1,0:T(8,128)(2,1)S(1)} %get-tuple-element.65.refs_2_), channel_id=1, source_target_pairs={{0,1},{1,0},{2,3},{3,2},{4,5},{5,4},{6,7},{7,6},{8,9},{9,8},{10,11... | collective-permute-start | bytes 786440 | tf_op jit(solution)/shard_map/ppermute | solution.py:377
  76.8 7.4 %collective-permute-start.22 = (bf16[1024,128]{1,0:T(8,128)(2,1)S(1)}, bf16[1024,128]{1,0:T(8,128)(2,1)S(1)}, u32[]{:S(2)}, u32[]{:S(2)}) collective-permute-start(bf16[1024,128]{1,0:T(8,128)(2,1)S(1)} %get-tuple-element.66.refs_4_), channel_id=1, source_target_pairs={{0,1},{1,0},{2,3},{3,2},{4,5},{5,4},{6,7},{7,6},{8,9},{9,8},{10,11... | collective-permute-start | bytes 786440 | tf_op jit(solution)/shard_map/ppermute | solution.py:377
  84.1 1.6 %collective-permute-start.24 = (bf16[1024,128]{1,0:T(8,128)(2,1)S(1)}, bf16[1024,128]{1,0:T(8,128)(2,1)S(1)}, u32[]{:S(2)}, u32[]{:S(2)}) collective-permute-start(bf16[1024,128]{1,0:T(8,128)(2,1)S(1)} %get-tuple-element.69.refs_6_), channel_id=1, source_target_pairs={{0,1},{1,0},{2,3},{3,2},{4,5},{5,4},{6,7},{7,6},{8,9},{9,8},{10,11... | collective-permute-start | bytes 786440 | tf_op jit(solution)/shard_map/ppermute | solution.py:377
